TPU v7x, 32 devices: a whole 2x2x4 slice. The times are simulated.
32 devices in a mesh: gx: 4 (over y, core), gy: 8 (over z, x).
Axes of the slice: x: 2, y: 2, z: 4, core: 2. Of those that a mesh axis runs over, the one named last changes fastest.
Arguments:
- right_side: float32 [4096, 64, 128], P(('gx', 'gy')), may hold values from -24 to 24
- fine_coupling: bfloat16 [4096, 64, 4, 64], P(('gx', 'gy')), may hold values from -0.359375 to 0.359375
- fine_diagonal: bfloat16 [4096, 64, 64], P(('gx', 'gy')), may hold values from -0.41 to 6, as said below
- fine_inverse: bfloat16 [4096, 64, 64], P(('gx', 'gy')), may hold values from -1 to 1, as said below
- coarse_coupling: bfloat16 [2048, 64, 8, 64], P(('gx', 'gy')), may hold values from -0.23925781 to 0.23925781
- coarse_diagonal: bfloat16 [2048, 64, 64], P(('gx', 'gy')), may hold values from -0.41 to 6, as said below
- coarse_inverse: bfloat16 [2048, 64, 64], P(('gx', 'gy')), may hold values from -1 to 1, as said below
- coarse_pattern: int32 [2048, 8], P(('gx', 'gy')), may hold values from 0 to 2047, as said below
Outputs:
- fine_iterate: float32 [4096, 64, 128], P(('gx', 'gy'))
- coarse_iterate: float32 [2048, 64, 128], P(('gx', 'gy'))
- next_right_side: float32 [1024, 64, 128], P(('gx', 'gy'))
Inputs may be any that keep to these rules, and one draw needn't show every extreme that they name: `coarse_pattern`: the entries of cell c name the eight cells around c on the next level's grid, each once, in an order that differs from cell to cell; an entry whose cell would lie outside the grid names c itself. `fine_diagonal`: each block is a positive diagonal plus smaller off-diagonal entries. `fine_inverse`: each block is the bfloat16 rounding of the inverse of the corresponding diagonal block before its rounding. `coarse_diagonal`: each block is a positive diagonal plus smaller off-diagonal entries. `coarse_inverse`: each block is the bfloat16 rounding of the inverse of the corresponding diagonal block before its rounding.
All inputs are finite; a program needn't handle non-finite values.
Results may differ from a plain program's by a relative error of at most 0.00065.
Values sent between devices are 32-bit elements; how exact they have to be, the bound alone decides.
No kernel may reach another device: no remote copies, remote signals or barrier semaphores. Data moves between devices by JAX's collectives and lax.ppermute only.
A program may use at most 192 MiB of HBM per device.

v0:
```python
import jax
import jax.numpy as jnp
from jax import lax
from jax.sharding import PartitionSpec as P

BLOCK_X = 4
BLOCK_Y = 32


def with_halo(block, sides, width):
    for axis, dim in sides:
        count = lax.axis_size(axis)
        forward = [(i, i + 1) for i in range(count - 1)]
        backward = [(target, source) for source, target in forward]
        low = lax.ppermute(
            lax.slice_in_dim(block, block.shape[dim] - width, None, axis=dim), axis, forward
        )
        high = lax.ppermute(lax.slice_in_dim(block, 0, width, axis=dim), axis, backward)
        block = jnp.concatenate([low, block, high], axis=dim)
    return block


def window_index(pattern, rows_block, cols_block, anchor_rows, anchor_cols):
    per_block = rows_block * cols_block
    blocks_across = lax.axis_size("gy")
    owner_block = pattern // per_block
    inside = pattern % per_block
    row_place = owner_block // blocks_across * rows_block + inside // cols_block
    col_place = owner_block % blocks_across * cols_block + inside % cols_block
    return (row_place - anchor_rows + 1) * (cols_block + 2) + (col_place - anchor_cols + 1)


def product(matrix, vector_b):
    return jnp.einsum(
        "cij,cjv->civ", matrix.astype(jnp.float32), vector_b, precision=lax.Precision.HIGHEST
    )


def smooth(side, inverse, apply_fn):
    first_sweep = product(inverse, side)
    slack_part = side - apply_fn(first_sweep)
    second = first_sweep + product(inverse, slack_part)
    residue = side - apply_fn(second)
    return (second, residue)


def fine_near(vector_b):
    cells, species, vectors = vector_b.shape
    shaped = vector_b.reshape(BLOCK_X, BLOCK_Y, species, vectors)
    padded = with_halo(shaped, (("gx", 0), ("gy", 1)), 1)
    pieces = [padded[:-2, 1:-1], padded[2:, 1:-1], padded[1:-1, :-2], padded[1:-1, 2:]]
    return jnp.stack(pieces, axis=2).reshape(cells, 4, species, vectors)


def coarse_near(vector_b, indices):
    cells, species, vectors = vector_b.shape
    shaped = vector_b.reshape(BLOCK_X // 2, BLOCK_Y, species, vectors)
    padded = with_halo(shaped, (("gx", 0), ("gy", 1)), 1)
    return jnp.take(padded.reshape(-1, species, vectors), indices, axis=0)


def apply_blocks(near, coupling, diagonal, vector_b):
    coupling_wide = coupling.astype(jnp.float32)
    summed = jnp.einsum("cikj,ckjv->civ", coupling_wide, near, precision=lax.Precision.HIGHEST)
    return summed + jnp.einsum(
        "cij,cjv->civ", diagonal.astype(jnp.float32), vector_b, precision=lax.Precision.HIGHEST
    )


def on_device(
    right_side,
    fine_coupling,
    fine_diagonal,
    fine_inverse,
    coarse_coupling,
    coarse_diagonal,
    coarse_inverse,
    coarse_pattern,
):
    row_index = lax.axis_index("gx")
    col_index = lax.axis_index("gy")
    half_rows = BLOCK_X // 2
    coarse_indices = window_index(
        coarse_pattern, half_rows, BLOCK_Y, row_index * half_rows, col_index * BLOCK_Y
    )
    species, vectors = (right_side.shape[1], right_side.shape[2])

    def fine_apply(vector_b):
        return apply_blocks(fine_near(vector_b), fine_coupling, fine_diagonal, vector_b)

    def coarse_apply(vector_b):
        return apply_blocks(
            coarse_near(vector_b, coarse_indices), coarse_coupling, coarse_diagonal, vector_b
        )

    fine_iterate, fine_residue = smooth(right_side, fine_inverse, fine_apply)
    coarse_side = (
        fine_residue.reshape(half_rows, 2, BLOCK_Y, species, vectors)
        .sum(axis=1)
        .reshape(-1, species, vectors)
    )
    coarse_iterate, coarse_residue = smooth(coarse_side, coarse_inverse, coarse_apply)
    next_side = (
        coarse_residue.reshape(half_rows, BLOCK_Y // 2, 2, species, vectors)
        .sum(axis=2)
        .reshape(-1, species, vectors)
    )
    return (fine_iterate, coarse_iterate, next_side)


def solution(mesh):
    placed = (
        P(("gx", "gy"), None, None),
        P(("gx", "gy"), None, None, None),
        P(("gx", "gy"), None, None),
        P(("gx", "gy"), None, None),
        P(("gx", "gy"), None, None, None),
        P(("gx", "gy"), None, None),
        P(("gx", "gy"), None, None),
        P(("gx", "gy"), None),
    )
    return jax.shard_map(
        on_device,
        mesh=mesh,
        in_specs=placed,
        out_specs=(
            P(("gx", "gy"), None, None),
            P(("gx", "gy"), None, None),
            P(("gx", "gy"), None, None),
        ),
        check_vma=False,
    )
```

profile of v0, /device:TPU:1, one launch (start us, length us, event | category | flops | bytes accessed | tf_op | source)
XLA Modules:
  0.0 312.2 jit_solution(7007805135122402142)
XLA Ops:
  0.6 0.0 copy-start
  0.6 4.0 %copy.18 = bf16[128,64,64]{2,1,0:T(8,128)(2,1)S(1)} copy(bf16[128,64,64]{0,2,1:T(8,128)(2,1)} %param.13) | data formatting | bytes 2097152 | tf_op args[3]
  4.7 4.9 %fusion.58 = f32[128,64,128]{2,1,0:T(8,128)S(1)} fusion(bf16[128,64,64]{2,1,0:T(8,128)(2,1)S(1)} %copy.18, f32[128,64,128]{2,1,0:T(8,128)} %param.10), kind=kOutput, calls=%fused_computation.124 | convolution fusion | flops 805306368 | bytes 9437184 | tf_op jit(solution)/shard_map/cij,cjv->civ/dot_general | solution.py:34
  9.6 0.0 copy-start.1
  9.6 2.0 copy-done.1
  11.6 1.6 slice_bitcast_fusion.7
  13.2 4.5 %collective-permute-start = (f32[1,32,64,128]{3,2,1,0:T(8,128)}, f32[1,32,64,128]{3,2,1,0:T(8,128)}, u32[]{:S(2)}, u32[]{:S(2)}) collective-permute-start(f32[1,32,64,128]{3,2,1,0:T(8,128)} %get-tuple-element.24), channel_id=1, source_target_pairs={{0,8},{8,16},{16,24},{1,9},{9,17},{17,25},{2,10},{10,18},{18,26},{... | collective-permute-start | bytes 3145736 | tf_op jit(solution)/shard_map/ppermute | solution.py:15
  17.7 1.9 collective-permute-start.1
  19.7 3.9 %copy.21 = bf16[128,64,64]{2,1,0:T(8,128)(2,1)S(1)} copy(bf16[128,64,64]{0,2,1:T(8,128)(2,1)} %param.12) | data formatting | bytes 2097152 | tf_op args[2]
  23.6 0.0 copy-start.2
  23.6 6.1 %collective-permute-done = f32[1,32,64,128]{3,2,1,0:T(8,128)} collective-permute-done((f32[1,32,64,128]{3,2,1,0:T(8,128)}, f32[1,32,64,128]{3,2,1,0:T(8,128)}, u32[]{:S(2)}, u32[]{:S(2)}) %collective-permute-start) | collective-permute-done | bytes 1048608 | tf_op jit(solution)/shard_map/ppermute | solution.py:15
  29.8 4.6 %collective-permute-done.1 = f32[1,32,64,128]{3,2,1,0:T(8,128)} collective-permute-done((f32[1,32,64,128]{3,2,1,0:T(8,128)}, f32[1,32,64,128]{3,2,1,0:T(8,128)}, u32[]{:S(2)}, u32[]{:S(2)}) %collective-permute-start.1) | collective-permute-done | bytes 1048608 | tf_op jit(solution)/shard_map/ppermute | solution.py:18
  34.4 1.8 pad_maximum_fusion.23
  36.1 2.9 collective-permute-start.2
  39.1 1.5 collective-permute-start.3
  40.6 3.7 %fusion.59 = f32[128,128,64]{1,2,0:T(8,128)} fusion(f32[128,64,128]{2,1,0:T(8,128)S(1)} %copy-done.2, bf16[128,64,64]{2,1,0:T(8,128)(2,1)S(1)} %copy.21), kind=kOutput, calls=%fused_computation.125 | convolution fusion | flops 805306368 | bytes 9437184 | tf_op jit(solution)/shard_map/cij,cjv->civ/dot_general | solution.py:65
  44.3 15.7 %copy.27 = bf16[128,64,4,64]{1,3,0,2:T(8,128)(2,1)} copy(bf16[128,64,4,64]{0,3,2,1:T(8,128)(2,1)} %param.11) | data formatting | bytes 8388608 | tf_op args[1]
  60.0 10.1 %pad_maximum_fusion.13 = (f32[4,32,64,128]{3,2,1,0:T(8,128)S(1)}, f32[4,32,64,128]{3,2,1,0:T(8,128)}, f32[4,32,64,128]{3,2,1,0:T(8,128)}, f32[4,32,64,128]{3,2,1,0:T(8,128)}) fusion(f32[6,1,64,128]{3,2,1,0:T(8,128)S(1)} %collective-permute-done.2, f32[1,32,64,128]{3,2,1,0:T(8,128)} %collective-permute-done.1, f32[4,32,64,128]{3,2,1,0:T(8,128)} %bitcast.102, ...), kind=kLoop, calls=%fused_computation.41 | loop fusion | flops 8388608 | bytes 23461888 | tf_op jit(solution)/shard_map/concatenate | solution.py:19
  70.1 16.7 %fusion = f32[128,128,64,1]{1,2,0,3:T(8,128)} fusion(bf16[128,64,4,64]{1,3,0,2:T(8,128)(2,1)} %copy.27, f32[128,1,64,128]{3,2,0,1:T(8,128)} %bitcast.123, f32[128,1,64,128]{3,2,0,1:T(8,128)S(1)} %bitcast.122, f32[128,1,64,128]{3,2,0,1:T(8,128)} %bitcast.125, f32[128,1,64,128]{3,2,0,1:T(8,128)} %bitcast.124), kind=kOutput, calls=%fused_computation.2 | convolution fusion | flops 3233808384 | bytes 25165824 | tf_op jit(solution)/shard_map/cikj,ckjv->civ/dot_general | solution.py:64
  86.8 8.4 %bitcast_add_fusion.1 = f32[128,64,128]{2,1,0:T(8,128)S(1)} fusion(f32[128,64,128]{2,1,0:T(8,128)S(1)} %copy-done.3, bf16[128,64,64]{2,1,0:T(8,128)(2,1)} %copy-done.11, f32[128,64,128]{2,1,0:T(8,128)} %param.10, f32[128,128,64]{1,2,0:T(8,128)} %fusion.59, f32[128,128,64,1]{1,2,0,3:T(8,128)} %fusion), kind=kOutput, calls=%fused_computation.48 | convolution fusion | flops 808452096 | bytes 22020096 | tf_op jit(solution)/shard_map/cij,cjv->civ/dot_general | solution.py:34
  95.2 2.0 copy-done.4
  97.2 1.6 slice_bitcast_fusion.5
  98.8 2.0 collective-permute-start.4
  100.8 2.6 collective-permute-start.5
  103.4 13.1 %copy.20 = bf16[128,64,4,64]{3,1,2,0:T(8,128)(2,1)} copy(bf16[128,64,4,64]{0,3,2,1:T(8,128)(2,1)} %param.11) | data formatting | bytes 8388608 | tf_op args[1]
  116.5 0.6 collective-permute-done.5
  117.1 1.3 pad_maximum_fusion.20
  118.4 4.4 %collective-permute-start.6 = (f32[6,1,64,128]{3,2,1,0:T(8,128)S(1)}, f32[6,1,64,128]{3,2,1,0:T(8,128)S(1)}, u32[]{:S(2)}, u32[]{:S(2)}) collective-permute-start(f32[6,1,64,128]{3,2,1,0:T(8,128)S(1)} %get-tuple-element.8), channel_id=1, source_target_pairs={{0,1},{1,2},{2,3},{3,4},{4,5},{5,6},{6,7},{8,9},{9,10},{10,11},{11... | collective-permute-start | bytes 589832 | tf_op jit(solution)/shard_map/ppermute | solution.py:15
  122.9 1.3 collective-permute-start.7
  124.2 3.7 %fusion.60 = f32[128,128,64]{1,2,0:T(8,128)} fusion(f32[128,64,128]{2,1,0:T(8,128)S(1)} %copy-done.5, bf16[128,64,64]{2,1,0:T(8,128)(2,1)S(1)} %copy-done.10), kind=kOutput, calls=%fused_computation.126 | convolution fusion | flops 805306368 | bytes 9437184 | tf_op jit(solution)/shard_map/cij,cjv->civ/dot_general | solution.py:65
  127.9 3.3 %collective-permute-done.7 = f32[6,1,64,128]{3,2,1,0:T(8,128)S(1)} collective-permute-done((f32[6,1,64,128]{3,2,1,0:T(8,128)S(1)}, f32[6,1,64,128]{3,2,1,0:T(8,128)S(1)}, u32[]{:S(2)}, u32[]{:S(2)}) %collective-permute-start.7) | collective-permute-done | bytes 196640 | tf_op jit(solution)/shard_map/ppermute | solution.py:18
  131.2 7.0 %pad_maximum_fusion.5 = (f32[4,32,64,128]{3,2,1,0:T(8,128)}, f32[4,32,64,128]{3,2,1,0:T(8,128)}, f32[4,32,64,128]{3,2,1,0:T(8,128)}, f32[4,32,64,128]{3,2,1,0:T(8,128)}) fusion(f32[6,1,64,128]{3,2,1,0:T(8,128)S(1)} %collective-permute-done.6, f32[1,32,64,128]{3,2,1,0:T(8,128)S(1)} %collective-permute-done.5, f32[4,32,64,128]{3,2,1,0:T(8,128)S(1)} %bitcast.106, ...), kind=kLoop, calls=%fused_computation.33 | loop fusion | flops 8388608 | bytes 23461888 | tf_op jit(solution)/shard_map/concatenate | solution.py:19
  138.1 17.6 %bitcast_subtract_fusion = f32[128,64,128]{2,1,0:T(8,128)} fusion(f32[128,64,128]{2,1,0:T(8,128)} %param.10, f32[128,128,64]{1,2,0:T(8,128)} %fusion.60, bf16[128,64,4,64]{3,1,2,0:T(8,128)(2,1)} %copy.20, f32[128,1,64,128]{3,2,1,0:T(8,128)} %bitcast.119, f32[128,1,64,128]{3,2,1,0:T(8,128)} %bitcast.118, f32[128,1,64,128]{3,2,1,0:T(8,128)} %bitcast.121, ...), kind=kOutput, calls=%fused_computation.46 | convolution fusion | flops 3235905536 | bytes 33554432 | tf_op jit(solution)/shard_map/cikj,ckjv->civ/dot_general | solution.py:64
  155.8 4.2 %reduce_sum.18 = f32[2,32,64,128]{3,2,1,0:T(8,128)} reduce(f32[2,2,32,64,128]{4,3,2,1,0:T(8,128)} %bitcast.117, f32[]{:T(128)} %constant.78.clone.1), dimensions={1}, to_apply=%region_0.1 | reduce | flops 524288 | bytes 6291460 | tf_op jit(solution)/shard_map/reduce_sum | solution.py:99
  159.9 2.8 fusion.61
  162.7 1.5 slice_bitcast_fusion.3
  164.2 2.5 collective-permute-start.8
  166.6 2.8 collective-permute-start.9
  169.5 0.1 copy.23
  169.6 0.1 reshape.97
  169.7 0.1 copy.22
  169.8 8.9 %collective-permute-done.8 = f32[1,32,64,128]{3,2,1,0:T(8,128)} collective-permute-done((f32[1,32,64,128]{3,2,1,0:T(8,128)}, f32[1,32,64,128]{3,2,1,0:T(8,128)}, u32[]{:S(2)}, u32[]{:S(2)}) %collective-permute-start.8) | collective-permute-done | bytes 1048608 | tf_op jit(solution)/shard_map/ppermute | solution.py:15
  178.7 4.4 %collective-permute-done.9 = f32[1,32,64,128]{3,2,1,0:T(8,128)} collective-permute-done((f32[1,32,64,128]{3,2,1,0:T(8,128)}, f32[1,32,64,128]{3,2,1,0:T(8,128)}, u32[]{:S(2)}, u32[]{:S(2)}) %collective-permute-start.9) | collective-permute-done | bytes 1048608 | tf_op jit(solution)/shard_map/ppermute | solution.py:18
  183.1 0.8 pad_maximum_fusion.29
  183.9 4.5 %collective-permute-start.10 = (f32[4,1,64,128]{3,2,1,0:T(8,128)S(1)}, f32[4,1,64,128]{3,2,1,0:T(8,128)S(1)}, u32[]{:S(2)}, u32[]{:S(2)}) collective-permute-start(f32[4,1,64,128]{3,2,1,0:T(8,128)S(1)} %get-tuple-element.20), channel_id=1, source_target_pairs={{0,1},{1,2},{2,3},{3,4},{4,5},{5,6},{6,7},{8,9},{9,10},{10,11},{11... | collective-permute-start | bytes 393224 | tf_op jit(solution)/shard_map/ppermute | solution.py:15
  188.5 1.7 collective-permute-start.11
  190.2 2.5 fusion.62
  192.7 2.0 collective-permute-done.11
  194.7 4.1 %pad_maximum_fusion = f32[4,34,64,128]{3,2,1,0:T(8,128)} fusion(f32[4,1,64,128]{3,2,1,0:T(8,128)S(1)} %collective-permute-done.11, f32[1,32,64,128]{3,2,1,0:T(8,128)} %collective-permute-done.9, f32[2,32,64,128]{3,2,1,0:T(8,128)S(1)} %bitcast.109, f32[1,32,64,128]{3,2,1,0:T(8,128)} %collective-permute-done.8, f32[4,1,64,128]{3,2,1,0:T(8,128)S(1)} %collective-permute-done.10), kind=kLoop, calls=%fused_computation.28 | loop fusion | flops 4456448 | bytes 8912896 | tf_op jit(solution)/shard_map/concatenate | solution.py:19
  198.8 23.3 %gather_fusion = f32[512,64,128]{2,1,0:T(8,128)} fusion(f32[136,64,128]{2,1,0:T(8,128)} %bitcast.104, s32[1024]{0:T(1024)S(1)} %pad_clamp_fusion), kind=kCustom, calls=%fused_computation.clone | custom fusion | bytes 33556480 | tf_op jit(solution)/shard_map/jit(_take)/gather | solution.py:59
  222.1 15.4 %fusion.18 = f32[64,128,64,1]{1,2,3,0:T(8,128)S(1)} fusion(f32[64,8,64,128]{3,2,1,0:T(8,128)} %bitcast.110, pred[64,8]{1,0:T(8,128)(4,1)S(1)} %copy.22, bf16[64,64,8,64]{3,2,1,0:T(8,128)(2,1)} %param.14), kind=kOutput, calls=%fused_computation.20 | convolution fusion | flops 3225419776 | bytes 23069184 | tf_op jit(solution)/shard_map/cikj,ckjv->civ/dot_general | solution.py:64
  237.6 1.5 bitcast_add_fusion.5
  239.1 0.1 slice_bitcast_fusion.1
  239.3 3.2 %collective-permute-start.12 = (f32[1,32,64,128]{3,2,1,0:T(8,128)S(1)}, f32[1,32,64,128]{3,2,1,0:T(8,128)S(1)}, u32[]{:S(2)}, u32[]{:S(2)}) collective-permute-start(f32[1,32,64,128]{3,2,1,0:T(8,128)S(1)} %get-tuple-element.26), channel_id=1, source_target_pairs={{0,8},{8,16},{16,24},{1,9},{9,17},{17,25},{2,10},{10,18},{18,26},{... | collective-permute-start | bytes 3145736 | tf_op jit(solution)/shard_map/ppermute | solution.py:15
  242.4 1.9 collective-permute-start.13
  244.4 9.8 %collective-permute-done.12 = f32[1,32,64,128]{3,2,1,0:T(8,128)S(1)} collective-permute-done((f32[1,32,64,128]{3,2,1,0:T(8,128)S(1)}, f32[1,32,64,128]{3,2,1,0:T(8,128)S(1)}, u32[]{:S(2)}, u32[]{:S(2)}) %collective-permute-start.12) | collective-permute-done | bytes 1048608 | tf_op jit(solution)/shard_map/ppermute | solution.py:15
  254.2 4.4 %collective-permute-done.13 = f32[1,32,64,128]{3,2,1,0:T(8,128)S(1)} collective-permute-done((f32[1,32,64,128]{3,2,1,0:T(8,128)S(1)}, f32[1,32,64,128]{3,2,1,0:T(8,128)S(1)}, u32[]{:S(2)}, u32[]{:S(2)}) %collective-permute-start.13) | collective-permute-done | bytes 1048608 | tf_op jit(solution)/shard_map/ppermute | solution.py:18
  258.6 4.5 %collective-permute-start.14 = (f32[4,1,64,128]{3,2,1,0:T(8,128)S(1)}, f32[4,1,64,128]{3,2,1,0:T(8,128)S(1)}, u32[]{:S(2)}, u32[]{:S(2)}) collective-permute-start(f32[4,1,64,128]{3,2,1,0:T(8,128)S(1)} %get-tuple-element.18), channel_id=1, source_target_pairs={{0,1},{1,2},{2,3},{3,4},{4,5},{5,6},{6,7},{8,9},{9,10},{10,11},{11... | collective-permute-start | bytes 393224 | tf_op jit(solution)/shard_map/ppermute | solution.py:15
  263.1 1.3 collective-permute-start.15
  264.4 2.6 fusion.63
  267.0 1.8 collective-permute-done.15
  268.8 2.5 pad_maximum_fusion.1
  271.4 23.7 %gather_fusion.1 = f32[512,64,128]{2,1,0:T(8,128)} fusion(f32[136,64,128]{2,1,0:T(8,128)} %bitcast.103, s32[1024]{0:T(1024)S(1)} %pad_clamp_fusion), kind=kCustom, calls=%fused_computation.1.clone | custom fusion | bytes 33556480 | tf_op jit(solution)/shard_map/jit(_take)/gather | solution.py:59
  295.1 16.9 %bitcast_reduce_fusion = f32[2,16,64,128]{3,2,1,0:T(8,128)} fusion(f32[64,64,128]{2,1,0:T(8,128)S(1)} %bitcast.116, f32[64,128,64]{1,2,0:T(8,128)} %fusion.63, bf16[64,64,8,64]{3,2,1,0:T(8,128)(2,1)} %param.14, f32[64,8,64,128]{3,2,1,0:T(8,128)} %bitcast.111, pred[64,8]{1,0:T(8,128)(4,1)S(1)} %copy.22), kind=kOutput, calls=%fused_computation.52 | convolution fusion | flops 3226730496 | bytes 26214912 | tf_op jit(solution)/shard_map/cikj,ckjv->civ/dot_general | solution.py:64
  (36 shorter events, 0.1 us)
Async XLA Ops:
  0.6 159.3 %copy-start = (bf16[64,64,64]{2,1,0:T(8,128)(2,1)S(1)}, bf16[64,64,64]{2,1,0:T(8,128)(2,1)}, u32[]{:S(2)}) copy-start(bf16[64,64,64]{2,1,0:T(8,128)(2,1)} %param.16) | copy-start | bytes 1572868
  4.7 4.9 %copy-start.11 = (bf16[128,64,64]{2,1,0:T(8,128)(2,1)}, bf16[128,64,64]{2,1,0:T(8,128)(2,1)S(1)}, u32[]{:S(2)}) copy-start(bf16[128,64,64]{2,1,0:T(8,128)(2,1)S(1)} %copy.18) | copy-start | bytes 3145732
  9.6 2.0 copy-start.1
  13.2 16.6 %collective-permute-start = (f32[1,32,64,128]{3,2,1,0:T(8,128)}, f32[1,32,64,128]{3,2,1,0:T(8,128)}, u32[]{:S(2)}, u32[]{:S(2)}) collective-permute-start(f32[1,32,64,128]{3,2,1,0:T(8,128)} %get-tuple-element.24), channel_id=1, source_target_pairs={{0,8},{8,16},{16,24},{1,9},{9,17},{17,25},{2,10},{10,18},{18,26},{... | collective-permute-start | bytes 3145736 | tf_op jit(solution)/shard_map/ppermute | solution.py:15
  17.7 16.6 %collective-permute-start.1 = (f32[1,32,64,128]{3,2,1,0:T(8,128)}, f32[1,32,64,128]{3,2,1,0:T(8,128)}, u32[]{:S(2)}, u32[]{:S(2)}) collective-permute-start(f32[1,32,64,128]{3,2,1,0:T(8,128)} %get-tuple-element.25), channel_id=1, source_target_pairs={{8,0},{16,8},{24,16},{9,1},{17,9},{25,17},{10,2},{18,10},{26,18},{... | collective-permute-start | bytes 3145736 | tf_op jit(solution)/shard_map/ppermute | solution.py:18
  23.6 20.7 %copy-start.9 = (bf16[128,64,64]{2,1,0:T(8,128)(2,1)}, bf16[128,64,64]{2,1,0:T(8,128)(2,1)S(1)}, u32[]{:S(2)}) copy-start(bf16[128,64,64]{2,1,0:T(8,128)(2,1)S(1)} %copy.21) | copy-start | bytes 3145732
  23.6 16.9 %copy-start.2 = (f32[128,64,128]{2,1,0:T(8,128)S(1)}, f32[128,64,128]{2,1,0:T(8,128)}, u32[]{:S(2)}) copy-start(f32[128,64,128]{2,1,0:T(8,128)} %copy-done.1) | copy-start | bytes 12582916
  36.1 23.8 %collective-permute-start.2 = (f32[6,1,64,128]{3,2,1,0:T(8,128)}, f32[6,1,64,128]{3,2,1,0:T(8,128)S(1)}, u32[]{:S(2)}, u32[]{:S(2)}) collective-permute-start(f32[6,1,64,128]{3,2,1,0:T(8,128)} %get-tuple-element.12), channel_id=1, source_target_pairs={{0,1},{1,2},{2,3},{3,4},{4,5},{5,6},{6,7},{8,9},{9,10},{10,11},{11... | collective-permute-start | bytes 589832 | tf_op jit(solution)/shard_map/ppermute | solution.py:15
  39.1 20.9 %collective-permute-start.3 = (f32[6,1,64,128]{3,2,1,0:T(8,128)}, f32[6,1,64,128]{3,2,1,0:T(8,128)S(1)}, u32[]{:S(2)}, u32[]{:S(2)}) collective-permute-start(f32[6,1,64,128]{3,2,1,0:T(8,128)} %get-tuple-element.13), channel_id=1, source_target_pairs={{1,0},{2,1},{3,2},{4,3},{5,4},{6,5},{7,6},{9,8},{10,9},{11,10},{12... | collective-permute-start | bytes 589832 | tf_op jit(solution)/shard_map/ppermute | solution.py:18
  70.1 16.7 %copy-start.3 = (f32[128,64,128]{2,1,0:T(8,128)S(1)}, f32[128,64,128]{2,1,0:T(8,128)}, u32[]{:S(2)}) copy-start(f32[128,64,128]{2,1,0:T(8,128)} %copy-done.1) | copy-start | bytes 12582916
  95.2 2.0 copy-start.4
  98.8 17.7 %collective-permute-start.4 = (f32[1,32,64,128]{3,2,1,0:T(8,128)}, f32[1,32,64,128]{3,2,1,0:T(8,128)S(1)}, u32[]{:S(2)}, u32[]{:S(2)}) collective-permute-start(f32[1,32,64,128]{3,2,1,0:T(8,128)} %get-tuple-element.22), channel_id=1, source_target_pairs={{0,8},{8,16},{16,24},{1,9},{9,17},{17,25},{2,10},{10,18},{18,26},{... | collective-permute-start | bytes 3145736 | tf_op jit(solution)/shard_map/ppermute | solution.py:15
  100.8 16.3 %collective-permute-start.5 = (f32[1,32,64,128]{3,2,1,0:T(8,128)}, f32[1,32,64,128]{3,2,1,0:T(8,128)S(1)}, u32[]{:S(2)}, u32[]{:S(2)}) collective-permute-start(f32[1,32,64,128]{3,2,1,0:T(8,128)} %get-tuple-element.23), channel_id=1, source_target_pairs={{8,0},{16,8},{24,16},{9,1},{17,9},{25,17},{10,2},{18,10},{26,18},{... | collective-permute-start | bytes 3145736 | tf_op jit(solution)/shard_map/ppermute | solution.py:18
  116.5 7.7 %copy-start.5 = (f32[128,64,128]{2,1,0:T(8,128)S(1)}, f32[128,64,128]{2,1,0:T(8,128)}, u32[]{:S(2)}) copy-start(f32[128,64,128]{2,1,0:T(8,128)} %copy-done.4) | copy-start | bytes 12582916
  116.5 7.7 %copy-start.10 = (bf16[128,64,64]{2,1,0:T(8,128)(2,1)S(1)}, bf16[128,64,64]{2,1,0:T(8,128)(2,1)}, u32[]{:S(2)}) copy-start(bf16[128,64,64]{2,1,0:T(8,128)(2,1)} %copy-done.9) | copy-start | bytes 3145732
  118.4 9.5 %collective-permute-start.6 = (f32[6,1,64,128]{3,2,1,0:T(8,128)S(1)}, f32[6,1,64,128]{3,2,1,0:T(8,128)S(1)}, u32[]{:S(2)}, u32[]{:S(2)}) collective-permute-start(f32[6,1,64,128]{3,2,1,0:T(8,128)S(1)} %get-tuple-element.8), channel_id=1, source_target_pairs={{0,1},{1,2},{2,3},{3,4},{4,5},{5,6},{6,7},{8,9},{9,10},{10,11},{11... | collective-permute-start | bytes 589832 | tf_op jit(solution)/shard_map/ppermute | solution.py:15
  122.9 8.3 %collective-permute-start.7 = (f32[6,1,64,128]{3,2,1,0:T(8,128)S(1)}, f32[6,1,64,128]{3,2,1,0:T(8,128)S(1)}, u32[]{:S(2)}, u32[]{:S(2)}) collective-permute-start(f32[6,1,64,128]{3,2,1,0:T(8,128)S(1)} %get-tuple-element.9), channel_id=1, source_target_pairs={{1,0},{2,1},{3,2},{4,3},{5,4},{6,5},{7,6},{9,8},{10,9},{11,10},{12... | collective-permute-start | bytes 589832 | tf_op jit(solution)/shard_map/ppermute | solution.py:18
  159.9 9.5 %copy-start.15 = (s32[64,8]{0,1:T(8,128)S(1)}, s32[64,8]{0,1:T(8,128)}, u32[]{:S(2)}) copy-start(s32[64,8]{0,1:T(8,128)} %param.17) | copy-start | bytes 6148
  164.2 14.5 %collective-permute-start.8 = (f32[1,32,64,128]{3,2,1,0:T(8,128)}, f32[1,32,64,128]{3,2,1,0:T(8,128)}, u32[]{:S(2)}, u32[]{:S(2)}) collective-permute-start(f32[1,32,64,128]{3,2,1,0:T(8,128)} %get-tuple-element.28), channel_id=1, source_target_pairs={{0,8},{8,16},{16,24},{1,9},{9,17},{17,25},{2,10},{10,18},{18,26},{... | collective-permute-start | bytes 3145736 | tf_op jit(solution)/shard_map/ppermute | solution.py:15
  166.6 16.4 %collective-permute-start.9 = (f32[1,32,64,128]{3,2,1,0:T(8,128)}, f32[1,32,64,128]{3,2,1,0:T(8,128)}, u32[]{:S(2)}, u32[]{:S(2)}) collective-permute-start(f32[1,32,64,128]{3,2,1,0:T(8,128)} %get-tuple-element.29), channel_id=1, source_target_pairs={{8,0},{16,8},{24,16},{9,1},{17,9},{25,17},{10,2},{18,10},{26,18},{... | collective-permute-start | bytes 3145736 | tf_op jit(solution)/shard_map/ppermute | solution.py:18
  169.8 20.4 %copy-start.13 = (bf16[64,64,64]{2,1,0:T(8,128)(2,1)S(1)}, bf16[64,64,64]{2,1,0:T(8,128)(2,1)}, u32[]{:S(2)}) copy-start(bf16[64,64,64]{2,1,0:T(8,128)(2,1)} %param.15) | copy-start | bytes 1572868
  183.9 8.8 %collective-permute-start.10 = (f32[4,1,64,128]{3,2,1,0:T(8,128)S(1)}, f32[4,1,64,128]{3,2,1,0:T(8,128)S(1)}, u32[]{:S(2)}, u32[]{:S(2)}) collective-permute-start(f32[4,1,64,128]{3,2,1,0:T(8,128)S(1)} %get-tuple-element.20), channel_id=1, source_target_pairs={{0,1},{1,2},{2,3},{3,4},{4,5},{5,6},{6,7},{8,9},{9,10},{10,11},{11... | collective-permute-start | bytes 393224 | tf_op jit(solution)/shard_map/ppermute | solution.py:15
  188.5 6.2 %collective-permute-start.11 = (f32[4,1,64,128]{3,2,1,0:T(8,128)S(1)}, f32[4,1,64,128]{3,2,1,0:T(8,128)S(1)}, u32[]{:S(2)}, u32[]{:S(2)}) collective-permute-start(f32[4,1,64,128]{3,2,1,0:T(8,128)S(1)} %get-tuple-element.21), channel_id=1, source_target_pairs={{1,0},{2,1},{3,2},{4,3},{5,4},{6,5},{7,6},{9,8},{10,9},{11,10},{12... | collective-permute-start | bytes 393224 | tf_op jit(solution)/shard_map/ppermute | solution.py:18
  222.1 15.5 %copy-start.7 = (f32[2,32,64,128]{3,2,1,0:T(8,128)S(1)}, f32[2,32,64,128]{3,2,1,0:T(8,128)}, u32[]{:S(2)}) copy-start(f32[2,32,64,128]{3,2,1,0:T(8,128)} %reduce_sum.18) | copy-start | bytes 6291460
  222.1 15.5 %copy-start.12 = (f32[64,128,64]{1,2,0:T(8,128)S(1)}, f32[64,128,64]{1,2,0:T(8,128)}, u32[]{:S(2)}) copy-start(f32[64,128,64]{1,2,0:T(8,128)} %fusion.62) | copy-start | bytes 6291460
  239.1 29.7 %copy-start.6 = (f32[64,64,128]{2,1,0:T(8,128)}, f32[64,64,128]{2,1,0:T(8,128)S(1)}, u32[]{:S(2)}) copy-start(f32[64,64,128]{2,1,0:T(8,128)S(1)} %bitcast_add_fusion.5) | copy-start | bytes 6291460
  239.1 25.3 %copy-start.14 = (bf16[64,64,64]{2,1,0:T(8,128)(2,1)S(1)}, bf16[64,64,64]{2,1,0:T(8,128)(2,1)}, u32[]{:S(2)}) copy-start(bf16[64,64,64]{2,1,0:T(8,128)(2,1)} %param.15) | copy-start | bytes 1572868
  239.3 14.9 %collective-permute-start.12 = (f32[1,32,64,128]{3,2,1,0:T(8,128)S(1)}, f32[1,32,64,128]{3,2,1,0:T(8,128)S(1)}, u32[]{:S(2)}, u32[]{:S(2)}) collective-permute-start(f32[1,32,64,128]{3,2,1,0:T(8,128)S(1)} %get-tuple-element.26), channel_id=1, source_target_pairs={{0,8},{8,16},{16,24},{1,9},{9,17},{17,25},{2,10},{10,18},{18,26},{... | collective-permute-start | bytes 3145736 | tf_op jit(solution)/shard_map/ppermute | solution.py:15
  242.4 16.1 %collective-permute-start.13 = (f32[1,32,64,128]{3,2,1,0:T(8,128)S(1)}, f32[1,32,64,128]{3,2,1,0:T(8,128)S(1)}, u32[]{:S(2)}, u32[]{:S(2)}) collective-permute-start(f32[1,32,64,128]{3,2,1,0:T(8,128)S(1)} %get-tuple-element.27), channel_id=1, source_target_pairs={{8,0},{16,8},{24,16},{9,1},{17,9},{25,17},{10,2},{18,10},{26,18},{... | collective-permute-start | bytes 3145736 | tf_op jit(solution)/shard_map/ppermute | solution.py:18
  258.6 8.4 %collective-permute-start.14 = (f32[4,1,64,128]{3,2,1,0:T(8,128)S(1)}, f32[4,1,64,128]{3,2,1,0:T(8,128)S(1)}, u32[]{:S(2)}, u32[]{:S(2)}) collective-permute-start(f32[4,1,64,128]{3,2,1,0:T(8,128)S(1)} %get-tuple-element.18), channel_id=1, source_target_pairs={{0,1},{1,2},{2,3},{3,4},{4,5},{5,6},{6,7},{8,9},{9,10},{10,11},{11... | collective-permute-start | bytes 393224 | tf_op jit(solution)/shard_map/ppermute | solution.py:15
  263.1 5.7 %collective-permute-start.15 = (f32[4,1,64,128]{3,2,1,0:T(8,128)S(1)}, f32[4,1,64,128]{3,2,1,0:T(8,128)S(1)}, u32[]{:S(2)}, u32[]{:S(2)}) collective-permute-start(f32[4,1,64,128]{3,2,1,0:T(8,128)S(1)} %get-tuple-element.19), channel_id=1, source_target_pairs={{1,0},{2,1},{3,2},{4,3},{5,4},{6,5},{7,6},{9,8},{10,9},{11,10},{12... | collective-permute-start | bytes 393224 | tf_op jit(solution)/shard_map/ppermute | solution.py:18
  271.4 23.7 %copy-start.8 = (f32[2,32,64,128]{3,2,1,0:T(8,128)S(1)}, f32[2,32,64,128]{3,2,1,0:T(8,128)}, u32[]{:S(2)}) copy-start(f32[2,32,64,128]{3,2,1,0:T(8,128)} %reduce_sum.18) | copy-start | bytes 6291460
where the time goes:
time: 317 us; the launch traced here: 312 us
  matrix products  96.7 us (31%)
  local copies, waits for them, and re-layouts  92.8 us (29%)
  waiting for transfers between devices  46 us (15%)
  starting transfers between devices  43.6 us (14%)
  other arithmetic  31.8 us (10%)
    dot_general x4, matrix products, apply_blocks(): jnp.einsum('cikj,ckjv->civ', coupling_wide, near, precision=lax.Precision...  66.6 us
    gather x2, local copies, waits for them, and re-layouts, coarse_near(): return jnp.take(padded.reshape(-1, species, vectors), indices, axis=0)  47 us
    unnamed x36, local copies, waits for them, and re-layouts  40.8 us
    ppermute x8, starting transfers between devices, with_halo(): lax.ppermute(lax.slice_in_dim(block, block.shape[dim] - width, None, axis...  28.6 us
    ppermute x8, waiting for transfers between devices, with_halo(): lax.ppermute(lax.slice_in_dim(block, block.shape[dim] - width, None, axis...  24.8 us
    concatenate x4, other arithmetic, with_halo(): block = jnp.concatenate([low, block, high], axis=dim)  23.7 us
    ppermute x8, waiting for transfers between devices, with_halo(): lax.ppermute(lax.slice_in_dim(block, 0, width, axis=dim), axis, backward)  21.1 us
    dot_general x4, matrix products, product(): jnp.einsum('cij,cjv->civ', matrix.astype(jnp.float32), vector_b, precisio...  17.6 us
  transfers between devices with their start and end apart: 16, of which 10 were waited for; matrix products, arithmetic and copies ran while one was open for 15% of the time, Pallas kernels for 0%

commit v1 on v0

v1 whole, which is shorter than its diff:
```python
import functools

import jax
import jax.numpy as jnp
from jax import lax
from jax.experimental import pallas as pl
from jax.experimental.pallas import tpu as pltpu
from jax.sharding import PartitionSpec as P

BLOCK_X = 4
BLOCK_Y = 32

WIDE = BLOCK_Y + 2
COARSE_X = BLOCK_X // 2
QUARTER = BLOCK_Y // 4
MIDDLE = tuple(range(QUARTER, BLOCK_Y - QUARTER))
ENDS = tuple(q for q in range(BLOCK_Y) if q not in MIDDLE)
UNROLL = 16

F32 = jnp.float32
BF16 = jnp.bfloat16
BOTH = ("gx", "gy")


def split(x):
    high = x.astype(BF16)
    low = (x - high.astype(F32)).astype(BF16)
    return jnp.concatenate([high, low], axis=1)


def fold(x):
    half = x.shape[1] // 2
    return x[:, :half].astype(F32) + x[:, half:].astype(F32)


def dot(*pairs):
    parts = [jnp.dot(a, b, preferred_element_type=F32) for a, b in pairs]
    return fold(functools.reduce(jnp.add, parts))


def row_parity():
    return lax.rem(lax.axis_index("gx"), 2)


def col_parity():
    return lax.rem(lax.axis_index("gy"), 2)


def place(rho, rows):
    parity = row_parity()
    return rho + parity * (rows - 1 - 2 * rho)


def spot(rho, q):
    return (rho + 1) * WIDE + q + 1


def swap_far(rows, cols):
    hop = 2 if cols % 4 == 0 else 1
    pairs = []
    for a in range(rows):
        for b in range(cols):
            partner = a - 1 if a % 2 == 0 else a + 1
            if 0 <= partner < rows:
                pairs.append((a * cols + b, partner * cols + b))
            else:
                pairs.append((a * cols + b, a * cols + (b ^ hop)))
    return pairs


def swap_near(rows, cols):
    return [(a * cols + b, (a ^ 1) * cols + b) for a in range(rows) for b in range(cols)]


def swap_even(rows, cols):
    return [(a * cols + b, a * cols + (b ^ 1)) for a in range(rows) for b in range(cols)]


def swap_odd(rows, cols):
    pairs = []
    for a in range(rows):
        for b in range(cols):
            partner = b - 1 if b % 2 == 0 else b + 1
            if 0 <= partner < cols:
                pairs.append((a * cols + b, a * cols + partner))
            else:
                pairs.append((a * cols + b, (a ^ 1) * cols + b))
    return pairs


def far_is_inside():
    gx = lax.axis_index("gx")
    return jnp.where(row_parity() == 0, gx > 0, gx < lax.axis_size("gx") - 1)


def odd_is_inside():
    gy = lax.axis_index("gy")
    return jnp.where(col_parity() == 0, gy > 0, gy < lax.axis_size("gy") - 1)


def write_sides(grid, even_halo, odd_halo, rows):
    parity = col_parity()
    even_col = jnp.where(parity == 0, BLOCK_Y, -1)
    odd_col = BLOCK_Y - 1 - even_col
    inside = odd_is_inside()
    for rho in range(rows):
        grid[spot(rho, even_col)] = split(even_halo[rho])
        grid[spot(rho, odd_col)] = split(jnp.where(inside, odd_halo[rho], 0.0))


def read_sides(grid, even_send, odd_send, rows):
    parity = col_parity()
    even_col = jnp.where(parity == 0, BLOCK_Y - 1, 0)
    odd_col = BLOCK_Y - 1 - even_col
    for rho in range(rows):
        even_send[rho] = fold(grid[spot(rho, even_col)])
        odd_send[rho] = fold(grid[spot(rho, odd_col)])


def write_row(grid, halo, rho, cols, inside=None):
    for n, q in enumerate(cols):
        value = halo[n]
        if inside is not None:
            value = jnp.where(inside, value, 0.0)
        grid[spot(rho, q)] = split(value)


def read_row(grid, send, rho, cols):
    for n, q in enumerate(cols):
        send[n] = fold(grid[spot(rho, q)])


def over_rows(first, last, body):
    parts = BLOCK_Y // UNROLL

    def step(n, carry):
        body(first + n // parts, lax.rem(n, parts) * UNROLL)
        return carry

    lax.fori_loop(0, (last - first) * parts, step, 0)


def send_out(scratch, n, out, first, count, sem):
    copy = pltpu.make_async_copy(scratch.at[pl.ds(n, count)], out.at[pl.ds(first, count)], sem)
    copy.start()
    return copy


def stretches(cols):
    found = []
    for n, q in enumerate(cols):
        if found and found[-1][1] + found[-1][2] == q:
            found[-1][2] += 1
        else:
            found.append([n, q, 1])
    return found


def with_zeros(own, after):
    none = jnp.zeros(own.shape, BF16)
    return jnp.concatenate([own, none] if after else [none, own], axis=0)


def smoothed(blocks, cell, side):
    species = side.shape[0]
    return dot((blocks[cell, :, -2 * species :], with_zeros(split(side), False)))


def fine_cell(rho, q):
    return place(rho, BLOCK_X) * BLOCK_Y + q


def fine_apply(rho, q, blocks, grid):
    cell = fine_cell(rho, q)
    species = blocks.shape[1]
    here = spot(rho, q)
    step = WIDE * (1 - 2 * row_parity())
    near = jnp.concatenate([grid[here - step], grid[here + step], grid[here - 1], grid[here + 1]], axis=0)
    return dot(
        (blocks[cell, :, : 4 * species], near), (blocks[cell, :, 4 * species :], with_zeros(grid[here], True))
    )


def fine_second(rho, cols, blocks, grid, side, change, iterate, n, far=None):
    for q in cols:
        cell = fine_cell(rho, q)
        side[cell] = side[cell] - fine_apply(rho, q, blocks, grid)
    for m, q in enumerate(cols):
        cell = fine_cell(rho, q)
        here = spot(rho, q)
        step = smoothed(blocks, cell, side[cell])
        change[here] = split(step)
        iterate[n + m] = fold(grid[here]) + step
        if far is not None:
            far[m] = step


def fine_left(rho, q, blocks, side, change):
    return side[fine_cell(rho, q)] - fine_apply(rho, q, blocks, change)


def start_kernel(right, inverse, blocks, grid, side, far_m, far_n, inverse_here, sems):
    species = inverse.shape[0]
    part = species // 2
    loads = [
        pltpu.make_async_copy(inverse.at[pl.ds(n * part, part)], inverse_here.at[pl.ds(n * part, part)], sems.at[n])
        for n in range(2)
    ]
    for rho in range(BLOCK_X):
        row = pl.ds(fine_cell(rho, 0), BLOCK_Y)
        loads.append(pltpu.make_async_copy(right.at[row], side.at[row], sems.at[2 + rho]))
    for load in loads:
        load.start()
    for n in range(2):
        loads[n].wait()
        some = inverse_here[n * part : (n + 1) * part]
        both = jnp.concatenate([jnp.zeros(some.shape, BF16), some], axis=1)
        blocks[:, n * part : (n + 1) * part, 4 * species :] = jnp.transpose(both, (2, 0, 1))
    loads[2].wait()
    for cols, send in ((MIDDLE, far_m), (ENDS, far_n)):
        for n, q in enumerate(cols):
            cell = fine_cell(0, q)
            first = smoothed(blocks, cell, side[cell])
            grid[spot(0, q)] = split(first)
            send[n] = first
    for load in loads[3:]:
        load.wait()


def first_kernel(side, blocks, grid_in, grid, near, even, odd):
    def body(rho, start):
        for q in range(UNROLL):
            cell = fine_cell(rho, start + q)
            grid[spot(rho, start + q)] = split(smoothed(blocks, cell, side[cell]))

    over_rows(1, BLOCK_X, body)
    read_row(grid, near, BLOCK_X - 1, range(BLOCK_Y))
    read_sides(grid, even, odd, BLOCK_X)


def fine_blocks_kernel(coupling, diagonal, inverse, blocks_in, blocks):
    species = coupling.shape[0]
    part = species // 2
    for first in range(0, species, part):
        rows = slice(first, first + part)
        blocks[:, rows, : 4 * species] = jnp.transpose(coupling[rows], (2, 0, 1))
        both = jnp.concatenate([diagonal[rows], inverse[rows]], axis=1)
        blocks[:, rows, 4 * species :] = jnp.transpose(both, (2, 0, 1))


def fine_inner_kernel(blocks, near_h, even_h, odd_h, grid_in, side_in, grid, side, change, out, near, iterate, sems):
    write_row(grid, near_h, BLOCK_X, range(BLOCK_Y))
    write_sides(grid, even_h, odd_h, BLOCK_X)

    def body(rho, start):
        n = (rho - 1) * BLOCK_Y + start
        fine_second(rho, [start + q for q in range(UNROLL)], blocks, grid, side, change, iterate, n)
        send_out(iterate, n, out, fine_cell(rho, start), UNROLL, sems.at[n // UNROLL])

    over_rows(1, BLOCK_X, body)
    read_row(change, near, BLOCK_X - 1, range(BLOCK_Y))
    for n in range((BLOCK_X - 1) * BLOCK_Y // UNROLL):
        part = iterate.at[pl.ds(n * UNROLL, UNROLL)]
        pltpu.make_async_copy(part, out.at[pl.ds(0, UNROLL)], sems.at[n]).wait()


def fine_outer_kernel(
    cols, sides, blocks, far_h, grid_in, side_in, change_in, out_in, grid, side, change, out, far, *rest
):
    *sends, iterate, sems = rest
    write_row(grid, far_h, -1, cols, far_is_inside())
    fine_second(0, cols, blocks, grid, side, change, iterate, 0, far)
    copies = [
        send_out(iterate, n, out, fine_cell(0, q), count, sems.at[k])
        for k, (n, q, count) in enumerate(stretches(cols))
    ]
    if sides:
        read_sides(change, *sends, BLOCK_X)
    for copy in copies:
        copy.wait()


def next_first(rho, cols, side, blocks, grid, far=None):
    for n, q in enumerate(cols):
        cell = place(rho, COARSE_X) * BLOCK_Y + q
        first = smoothed(blocks, cell, side[rho * BLOCK_Y + q])
        grid[spot(rho, q)] = split(first)
        if far is not None:
            far[n] = first


def left_inner_kernel(blocks, side, coarse_blocks, near_h, even_h, odd_h, change_in, change, coarse_side, coarse_grid):
    write_row(change, near_h, BLOCK_X, range(BLOCK_Y))
    write_sides(change, even_h, odd_h, BLOCK_X)

    def pairs(rho, start):
        for q in range(UNROLL):
            upper = fine_left(2 * rho, start + q, blocks, side, change)
            lower = fine_left(2 * rho + 1, start + q, blocks, side, change)
            coarse_side[rho * BLOCK_Y + start + q] = upper + lower
        next_first(rho, [start + q for q in range(UNROLL)], coarse_side, coarse_blocks, coarse_grid)

    over_rows(1, COARSE_X, pairs)

    def single(rho, start):
        for q in range(UNROLL):
            coarse_side[start + q] = fine_left(rho, start + q, blocks, side, change)

    over_rows(1, 2, single)


def left_outer_kernel(
    cols, sides, blocks, side, coarse_blocks, far_h, change_in, coarse_in, grid_in, change, coarse_side, coarse_grid, *sends
):
    write_row(change, far_h, -1, cols, far_is_inside())
    for q in cols:
        coarse_side[q] = coarse_side[q] + fine_left(0, q, blocks, side, change)
    next_first(0, cols, coarse_side, coarse_blocks, coarse_grid, None if sides else sends[0])
    if sides:
        read_sides(coarse_grid, *sends, COARSE_X)


def coarse_blocks_kernel(coupling, diagonal, inverse, after, blocks):
    species = coupling.shape[1]
    first = pl.program_id(0) * coupling.shape[0]
    for n in range(coupling.shape[0]):
        blocks[first + n, :, : 8 * species] = coupling[n].reshape(species, 8 * species)
        blocks[first + n, :, 8 * species :] = jnp.concatenate([diagonal[n], inverse[n]], axis=1)


def coarse_apply(rho, q, places, blocks, grid):
    cell = place(rho, COARSE_X) * BLOCK_Y + q
    species = blocks.shape[1]
    near = jnp.concatenate([grid[places[k, cell]] for k in range(8)], axis=0)
    return dot(
        (blocks[cell, :, : 8 * species], near), (blocks[cell, :, 8 * species :], with_zeros(grid[spot(rho, q)], True))
    )


def coarse_second(rho, cols, places, blocks, grid, side, change, iterate, n, far=None):
    for q in cols:
        here = rho * BLOCK_Y + q
        side[here] = side[here] - coarse_apply(rho, q, places, blocks, grid)
    for m, q in enumerate(cols):
        here = spot(rho, q)
        step = smoothed(blocks, place(rho, COARSE_X) * BLOCK_Y + q, side[rho * BLOCK_Y + q])
        change[here] = split(step)
        iterate[n + m] = fold(grid[here]) + step
        if far is not None:
            far[m] = step


def pack_kernel(cols, even_h, odd_h, grid_in, grid, far, near):
    write_sides(grid, even_h, odd_h, COARSE_X)
    read_row(grid, far, 0, cols + (-1, BLOCK_Y))
    read_row(grid, near, COARSE_X - 1, range(-1, BLOCK_Y + 1))


def coarse_inner_kernel(places, blocks, near_h, grid_in, side_in, grid, side, change, out, iterate, sems):
    write_row(grid, near_h, COARSE_X, range(-1, BLOCK_Y + 1))

    def body(rho, start):
        n = (rho - 1) * BLOCK_Y + start
        cell = place(rho, COARSE_X) * BLOCK_Y + start
        coarse_second(rho, [start + q for q in range(UNROLL)], places, blocks, grid, side, change, iterate, n)
        send_out(iterate, n, out, cell, UNROLL, sems.at[n // UNROLL])

    over_rows(1, COARSE_X, body)
    for n in range((COARSE_X - 1) * BLOCK_Y // UNROLL):
        part = iterate.at[pl.ds(n * UNROLL, UNROLL)]
        pltpu.make_async_copy(part, out.at[pl.ds(0, UNROLL)], sems.at[n]).wait()


def coarse_outer_kernel(
    came, cols, sides, places, blocks, far_h, grid_in, side_in, change_in, out_in, grid, side, change, out, *rest
):
    *sends, iterate, sems = rest
    write_row(grid, far_h, -1, came)
    coarse_second(0, cols, places, blocks, grid, side, change, iterate, 0, None if sides else sends[0])
    copies = [
        send_out(iterate, n, out, place(0, COARSE_X) * BLOCK_Y + q, count, sems.at[k])
        for k, (n, q, count) in enumerate(stretches(cols))
    ]
    if sides:
        read_sides(change, *sends, COARSE_X)
    for copy in copies:
        copy.wait()


def coarse_left(rho, q, places, blocks, side, change):
    return side[rho * BLOCK_Y + q] - coarse_apply(rho, q, places, blocks, change)


def last_pair(rho, q, places, blocks, side, change):
    return coarse_left(rho, q, places, blocks, side, change) + coarse_left(rho, q + 1, places, blocks, side, change)


def last_inner_kernel(places, blocks, side, near_h, change_in, change, out, below, sems):
    write_row(change, near_h, COARSE_X, range(-1, BLOCK_Y + 1))
    count = UNROLL // 2

    def body(rho, start):
        n = ((rho - 1) * BLOCK_Y + start) // 2
        for q in range(count):
            below[n + q] = last_pair(rho, start + 2 * q, places, blocks, side, change)
        send_out(below, n, out, (place(rho, COARSE_X) * BLOCK_Y + start) // 2, count, sems.at[n // count])

    over_rows(1, COARSE_X, body)
    for n in range((COARSE_X - 1) * BLOCK_Y // UNROLL):
        part = below.at[pl.ds(n * count, count)]
        pltpu.make_async_copy(part, out.at[pl.ds(0, count)], sems.at[n]).wait()


def last_outer_kernel(came, cols, places, blocks, side, far_h, change_in, out_in, change, out, below, sems):
    write_row(change, far_h, -1, came)
    pairs = [q // 2 for q in cols[::2]]
    for n, q in enumerate(pairs):
        below[n] = last_pair(0, 2 * q, places, blocks, side, change)
    copies = [
        send_out(below, n, out, place(0, COARSE_X) * BLOCK_Y // 2 + q, count, sems.at[k])
        for k, (n, q, count) in enumerate(stretches(pairs))
    ]
    for copy in copies:
        copy.wait()


IN_VMEM = pl.BlockSpec(memory_space=pltpu.VMEM)
IN_SMEM = pl.BlockSpec(memory_space=pltpu.SMEM)
IN_HBM = pl.BlockSpec(memory_space=pltpu.HBM)


def run(name, kernel, outs, args, aliases=(), scalars=(), far_args=(), far_outs=(), scratch=(), after=()):
    count = len(args)
    args = list(args) + list(after)
    specs = [IN_SMEM if n in scalars else IN_HBM if n in far_args else IN_VMEM for n in range(len(args))]
    args = [
        x if n in scalars or n in far_args else pltpu.with_memory_space_constraint(x, pltpu.VMEM)
        for n, x in enumerate(args)
    ]

    def body(*refs):
        kernel(*refs[:count], *refs[len(args) :])

    called = pl.pallas_call(
        body,
        out_shape=tuple(
            (pltpu.HBM if n in far_outs else pltpu.VMEM)(shape, dtype) for n, (shape, dtype) in enumerate(outs)
        ),
        in_specs=specs,
        out_specs=tuple(IN_HBM if n in far_outs else IN_VMEM for n in range(len(outs))),
        scratch_shapes=list(scratch),
        input_output_aliases=dict(aliases),
        compiler_params=pltpu.CompilerParams(vmem_limit_bytes=8 * 2**20),
        cost_estimate=pl.CostEstimate(flops=1, bytes_accessed=1, transcendentals=0),
        name=name,
    )
    return called(*args)


def coarse_blocks_call(coupling, diagonal, inverse, after):
    cells, species = coupling.shape[:2]
    part = cells // 8
    return pl.pallas_call(
        coarse_blocks_kernel,
        grid=(cells // part,),
        out_shape=pltpu.VMEM((cells, species, 10 * species), BF16),
        in_specs=[
            pl.BlockSpec((part,) + coupling.shape[1:], lambda n: (n, 0, 0, 0)),
            pl.BlockSpec((part,) + diagonal.shape[1:], lambda n: (n, 0, 0)),
            pl.BlockSpec((part,) + inverse.shape[1:], lambda n: (n, 0, 0)),
            IN_VMEM,
        ],
        out_specs=IN_VMEM,
        compiler_params=pltpu.CompilerParams(vmem_limit_bytes=8 * 2**20),
        cost_estimate=pl.CostEstimate(flops=1, bytes_accessed=1, transcendentals=0),
        name="coarse_blocks",
    )(coupling, diagonal, inverse, pltpu.with_memory_space_constraint(after, pltpu.VMEM))


def coarse_places(pattern):
    blocks_across = lax.axis_size("gy")
    pattern = pattern.T
    per_block = COARSE_X * BLOCK_Y
    owner = pattern // per_block
    inside = pattern % per_block
    row = owner // blocks_across * COARSE_X + inside // BLOCK_Y - lax.axis_index("gx") * COARSE_X
    col = owner % blocks_across * BLOCK_Y + inside % BLOCK_Y - lax.axis_index("gy") * BLOCK_Y
    rho = jnp.where(row_parity() == 0, row, COARSE_X - 1 - row)
    return (rho + 1) * WIDE + col + 1


def on_device(
    right_side,
    fine_coupling,
    fine_diagonal,
    fine_inverse,
    coarse_coupling,
    coarse_diagonal,
    coarse_inverse,
    coarse_pattern,
):
    cells, species, vectors = right_side.shape
    coarse_cells = coarse_coupling.shape[0]
    rows, cols = lax.axis_size("gx"), lax.axis_size("gy")
    far_pairs, near_pairs = swap_far(rows, cols), swap_near(rows, cols)
    even_pairs, odd_pairs = swap_even(rows, cols), swap_odd(rows, cols)

    def far(x):
        return lax.ppermute(x, BOTH, far_pairs)

    def near(x):
        return lax.ppermute(x, BOTH, near_pairs)

    def even(x):
        return lax.ppermute(x, BOTH, even_pairs)

    def odd(x):
        return lax.ppermute(x, BOTH, odd_pairs)

    def field(count):
        return ((count, species, vectors), F32)

    def row_scratch(count):
        return [pltpu.VMEM((count, species, vectors), F32), pltpu.SemaphoreType.DMA((max(2, count // 8),))]

    def padded(count):
        return (((count + 2) * WIDE, species, 2 * vectors), BF16)

    fine_blocks = ((cells, species, 6 * species), BF16)
    coupling = jnp.transpose(fine_coupling, (1, 2, 3, 0)).reshape(species, 4 * species, cells)
    diagonal = jnp.transpose(fine_diagonal, (1, 2, 0))
    inverse = jnp.transpose(fine_inverse, (1, 2, 0))
    places = coarse_places(coarse_pattern)
    middle, ends = len(MIDDLE), len(ENDS)

    blocks, grid, side, far_m, far_n = run(
        "start",
        start_kernel,
        [fine_blocks, padded(BLOCK_X), field(cells), field(middle), field(ends)],
        [right_side, inverse],
        far_args=(0, 1),
        scratch=[pltpu.VMEM(inverse.shape, BF16), pltpu.SemaphoreType.DMA((2 + BLOCK_X,))],
    )
    far_m, far_n = far(far_m), far(far_n)
    grid, near_s, even_s, odd_s = run(
        "first",
        first_kernel,
        [padded(BLOCK_X), field(BLOCK_Y), field(BLOCK_X), field(BLOCK_X)],
        [side, blocks, grid],
        [(2, 0)],
    )
    near_h, even_h, odd_h = near(near_s), even(even_s), odd(odd_s)
    (blocks,) = run(
        "fine_blocks",
        fine_blocks_kernel,
        [fine_blocks],
        [coupling, diagonal, inverse, blocks],
        [(3, 0)],
        after=[near_s],
    )
    grid, side, change, iterate, near_s = run(
        "fine_inner",
        fine_inner_kernel,
        [padded(BLOCK_X), field(cells), padded(BLOCK_X), field(cells), field(BLOCK_Y)],
        [blocks, near_h, even_h, odd_h, grid, side],
        [(4, 0), (5, 1)],
        far_outs=(3,),
        scratch=row_scratch((BLOCK_X - 1) * BLOCK_Y),
    )
    near_h = near(near_s)
    coarse_blocks = coarse_blocks_call(coarse_coupling, coarse_diagonal, coarse_inverse, near_s)
    state = [padded(BLOCK_X), field(cells), padded(BLOCK_X), field(cells)]
    same = [(2, 0), (3, 1), (4, 2), (5, 3)]
    grid, side, change, iterate, far_m = run(
        "fine_middle",
        functools.partial(fine_outer_kernel, MIDDLE, False),
        state + [field(middle)],
        [blocks, far_m, grid, side, change, iterate],
        same,
        far_args=(5,),
        far_outs=(3,),
        scratch=row_scratch(middle),
        after=[coarse_blocks],
    )
    far_m = far(far_m)
    grid, side, change, fine_iterate, far_n, even_s, odd_s = run(
        "fine_ends",
        functools.partial(fine_outer_kernel, ENDS, True),
        state + [field(ends), field(BLOCK_X), field(BLOCK_X)],
        [blocks, far_n, grid, side, change, iterate],
        same,
        far_args=(5,),
        far_outs=(3,),
        scratch=row_scratch(ends),
    )
    far_n = far(far_n)
    even_h, odd_h = even(even_s), odd(odd_s)

    state = [padded(BLOCK_X), field(coarse_cells), padded(COARSE_X)]
    change, coarse_side, coarse_grid = run(
        "left_inner",
        left_inner_kernel,
        state,
        [blocks, side, coarse_blocks, near_h, even_h, odd_h, change],
        [(6, 0)],
    )
    same = [(4, 0), (5, 1), (6, 2)]
    change, coarse_side, coarse_grid, far_m = run(
        "left_middle",
        functools.partial(left_outer_kernel, MIDDLE, False),
        state + [field(middle)],
        [blocks, side, coarse_blocks, far_m, change, coarse_side, coarse_grid],
        same,
    )
    far_m = far(far_m)
    change, coarse_side, coarse_grid, even_s, odd_s = run(
        "left_ends",
        functools.partial(left_outer_kernel, ENDS, True),
        state + [field(COARSE_X), field(COARSE_X)],
        [blocks, side, coarse_blocks, far_n, change, coarse_side, coarse_grid],
        same,
    )
    even_h, odd_h = even(even_s), odd(odd_s)
    coarse_grid, far_n, near_s = run(
        "pack_first",
        functools.partial(pack_kernel, ENDS),
        [padded(COARSE_X), field(ends + 2), field(BLOCK_Y + 2)],
        [even_h, odd_h, coarse_grid],
        [(2, 0)],
    )
    far_n, near_h = far(far_n), near(near_s)

    state = [padded(COARSE_X), field(coarse_cells), padded(COARSE_X), field(coarse_cells)]
    coarse_grid, coarse_side, coarse_change, iterate = run(
        "coarse_inner",
        coarse_inner_kernel,
        state,
        [places, coarse_blocks, near_h, coarse_grid, coarse_side],
        [(3, 0), (4, 1)],
        scalars=(0,),
        far_outs=(3,),
        scratch=row_scratch((COARSE_X - 1) * BLOCK_Y),
    )
    inner = MIDDLE[1:-1]
    outer = tuple(q for q in range(BLOCK_Y) if q not in inner)
    same = [(3, 0), (4, 1), (5, 2), (6, 3)]
    coarse_grid, coarse_side, coarse_change, iterate, far_m = run(
        "coarse_middle",
        functools.partial(coarse_outer_kernel, MIDDLE, inner, False),
        state + [field(len(inner))],
        [places, coarse_blocks, far_m, coarse_grid, coarse_side, coarse_change, iterate],
        same,
        scalars=(0,),
        far_args=(6,),
        far_outs=(3,),
        scratch=row_scratch(len(inner)),
    )
    far_m = far(far_m)
    coarse_grid, coarse_side, coarse_change, coarse_iterate, even_s, odd_s = run(
        "coarse_ends",
        functools.partial(coarse_outer_kernel, ENDS + (-1, BLOCK_Y), outer, True),
        state + [field(COARSE_X), field(COARSE_X)],
        [places, coarse_blocks, far_n, coarse_grid, coarse_side, coarse_change, iterate],
        same,
        scalars=(0,),
        far_args=(6,),
        far_outs=(3,),
        scratch=row_scratch(len(outer)),
    )
    even_h, odd_h = even(even_s), odd(odd_s)
    coarse_change, far_n, near_s = run(
        "pack_second",
        functools.partial(pack_kernel, outer),
        [padded(COARSE_X), field(len(outer) + 2), field(BLOCK_Y + 2)],
        [even_h, odd_h, coarse_change],
        [(2, 0)],
    )
    far_n, near_h = far(far_n), near(near_s)

    state = [padded(COARSE_X), field(coarse_cells // 2)]
    coarse_change, next_side = run(
        "last_inner",
        last_inner_kernel,
        state,
        [places, coarse_blocks, coarse_side, near_h, coarse_change],
        [(4, 0)],
        scalars=(0,),
        far_outs=(1,),
        scratch=row_scratch((COARSE_X - 1) * BLOCK_Y // 2),
    )
    core = inner[1:-1]
    rest = tuple(q for q in range(BLOCK_Y) if q not in core)
    coarse_change, next_side = run(
        "last_middle",
        functools.partial(last_outer_kernel, inner, core),
        state,
        [places, coarse_blocks, coarse_side, far_m, coarse_change, next_side],
        [(4, 0), (5, 1)],
        scalars=(0,),
        far_args=(5,),
        far_outs=(1,),
        scratch=row_scratch(len(core) // 2),
    )
    coarse_change, next_side = run(
        "last_ends",
        functools.partial(last_outer_kernel, outer + (-1, BLOCK_Y), rest),
        state,
        [places, coarse_blocks, coarse_side, far_n, coarse_change, next_side],
        [(4, 0), (5, 1)],
        scalars=(0,),
        far_args=(5,),
        far_outs=(1,),
        scratch=row_scratch(len(rest) // 2),
    )
    return (fine_iterate, coarse_iterate, next_side)


def solution(mesh):
    placed = (
        P(BOTH, None, None),
        P(BOTH, None, None, None),
        P(BOTH, None, None),
        P(BOTH, None, None),
        P(BOTH, None, None, None),
        P(BOTH, None, None),
        P(BOTH, None, None),
        P(BOTH, None),
    )
    return jax.shard_map(
        on_device,
        mesh=mesh,
        in_specs=placed,
        out_specs=(P(BOTH, None, None), P(BOTH, None, None), P(BOTH, None, None)),
        check_vma=False,
    )
```

time: 317 us -> 117 us (0.37)
  the two profiles are of different devices: /device:TPU:1 before, /device:TPU:0 now
where the time goes in v1:
time: 117 us
  Pallas kernels  46.4 us (40%)
  starting transfers between devices  29.3 us (25%)
  waiting for transfers between devices  27.1 us (23%)
  local copies, waits for them, and re-layouts  13 us (11%)
    pallas_call x17, Pallas kernels, run(): return called(*args)  43.2 us
    ppermute x8, waiting for transfers between devices, far(): return lax.ppermute(x, BOTH, far_pairs)  16.5 us
    ppermute x4, starting transfers between devices, even(): return lax.ppermute(x, BOTH, even_pairs)  14.3 us
    ppermute x8, starting transfers between devices, far(): return lax.ppermute(x, BOTH, far_pairs)  14.3 us
    unnamed x36, local copies, waits for them, and re-layouts  13 us
    ppermute x4, waiting for transfers between devices, even(): return lax.ppermute(x, BOTH, even_pairs)  10.6 us
    pallas_call x1, Pallas kernels, coarse_blocks_call(): pl.pallas_call(coarse_blocks_kernel, grid=(cells // part,), out_shape=plt...  3.24 us
  transfers between devices with their start and end apart: 20, of which 7 were waited for; matrix products, arithmetic and copies ran while one was open for 0% of the time, Pallas kernels for 29%

profile of v1, /device:TPU:0, one launch (start us, length us, event | category | flops | bytes accessed | tf_op | source)
XLA Modules:
  0.0 117.0 jit_solution(3562885628489027037)
XLA Ops:
  0.6 1.2 %copy-done.6 = bf16[128,64,64]{0,2,1:T(8,128)(2,1)S(1)} copy-done((bf16[128,64,64]{0,2,1:T(8,128)(2,1)S(1)}, bf16[128,64,64]{0,2,1:T(8,128)(2,1)}, u32[]{:S(2)}) %copy-start.6) | copy-done | bytes 1048600
  1.9 2.2 %copy-done.7 = f32[128,64,128]{2,1,0:T(8,128)S(1)} copy-done((f32[128,64,128]{2,1,0:T(8,128)S(1)}, f32[128,64,128]{2,1,0:T(8,128)}, u32[]{:S(2)}) %copy-start.7) | copy-done | bytes 4194328
  4.0 1.9 %start.1 = (bf16[128,64,384]{2,1,0:T(8,128)(2,1)S(1)}, bf16[204,64,256]{2,1,0:T(8,128)(2,1)S(1)}, f32[128,64,128]{2,1,0:T(8,128)S(1)}, f32[16,64,128]{2,1,0:T(8,128)S(1)}, f32[16,64,128]{2,1,0:T(8,128)S(1)}) custom-call(f32[128,64,128]{2,1,0:T(8,128)S(1)} %copy-done.7, bf16[64,64,128]{2,1,0:T(8,128)(2,1)S(1)} %bitcast.28), custom_call_target="tpu_custom_call" | custom-call | flops 1 | bytes 1 | tf_op jit(solution)/shard_map/start/pallas_call | solution.py:457
  5.9 0.0 copy-start.5
  5.9 0.0 copy-start.8
  5.9 2.0 %first.1 = (bf16[204,64,256]{2,1,0:T(8,128)(2,1)S(1)}, f32[32,64,128]{2,1,0:T(8,128)S(1)}, f32[4,64,128]{2,1,0:T(8,128)S(1)}, f32[4,64,128]{2,1,0:T(8,128)S(1)}) custom-call(f32[128,64,128]{2,1,0:T(8,128)S(1)} %get-tuple-element.65.refs_0_.refs_5_, bf16[128,64,384]{2,1,0:T(8,128)(2,1)S(1)} %get-tuple-element.64.refs_1_.refs_3_, ...), custom_call_target="tpu_custom_call", output_to_operand_aliasing={{0}: (2, {})} | custom-call | flops 1 | bytes 1 | tf_op jit(solution)/shard_map/first/pallas_call | solution.py:457
  7.9 0.5 collective-permute-start.2
  8.4 2.6 %collective-permute-start.3 = (f32[4,64,128]{2,1,0:T(8,128)S(1)}, f32[4,64,128]{2,1,0:T(8,128)S(1)}, u32[]{:S(2)}, u32[]{:S(2)}) collective-permute-start(f32[4,64,128]{2,1,0:T(8,128)S(1)} %get-tuple-element.70), channel_id=1, source_target_pairs={{0,1},{1,0},{2,3},{3,2},{4,5},{5,4},{6,7},{7,6},{8,9},{9,8},{10,11... | collective-permute-start | bytes 393224 | tf_op jit(solution)/shard_map/ppermute | solution.py:515
  11.0 0.2 collective-permute-start.4
  11.2 1.4 %collective-permute-start.1 = (f32[16,64,128]{2,1,0:T(8,128)S(1)}, f32[16,64,128]{2,1,0:T(8,128)S(1)}, u32[]{:S(2)}, u32[]{:S(2)}) collective-permute-start(f32[16,64,128]{2,1,0:T(8,128)S(1)} %get-tuple-element.69), channel_id=1, source_target_pairs={{0,2},{1,3},{2,0},{3,1},{4,6},{5,7},{6,4},{7,5},{8,16},{9,17},{10,... | collective-permute-start | bytes 1572872 | tf_op jit(solution)/shard_map/ppermute | solution.py:509
  12.6 2.5 %fine_blocks.1.refs_0_ = bf16[128,64,384]{2,1,0:T(8,128)(2,1)S(1)} custom-call(bf16[64,256,128]{2,1,0:T(8,128)(2,1)S(1)} %bitcast.27, bf16[64,64,128]{2,1,0:T(8,128)(2,1)S(1)} %bitcast.30, bf16[64,64,128]{2,1,0:T(8,128)(2,1)S(1)} %bitcast.29, bf16[128,64,384]{2,1,0:T(8,128)(2,1)S(1)} %get-tuple-element.64.refs_1_.refs_3_, ...), custom_call_target="tpu_custom_call", output_to_operand_aliasing={{}: (3, {})} | custom-call | flops 1 | bytes 1 | tf_op jit(solution)/shard_map/fine_blocks/pallas_call | solution.py:457
  15.1 2.1 %collective-permute-done.3.refs_2_ = f32[4,64,128]{2,1,0:T(8,128)S(1)} collective-permute-done((f32[4,64,128]{2,1,0:T(8,128)S(1)}, f32[4,64,128]{2,1,0:T(8,128)S(1)}, u32[]{:S(2)}, u32[]{:S(2)}) %collective-permute-start.3) | collective-permute-done | bytes 131104 | tf_op jit(solution)/shard_map/ppermute | solution.py:515
  17.2 0.0 collective-permute-done.4.refs_3_
  17.2 0.0 collective-permute-done.2.refs_1_
  17.2 0.0 copy-start.9
  17.2 0.0 copy-start.10
  17.2 6.0 %fine_inner.1 = (bf16[204,64,256]{2,1,0:T(8,128)(2,1)S(1)}, f32[128,64,128]{2,1,0:T(8,128)S(1)}, bf16[204,64,256]{2,1,0:T(8,128)(2,1)S(1)}, f32[128,64,128]{2,1,0:T(8,128)}, f32[32,64,128]{2,1,0:T(8,128)S(1)}) custom-call(bf16[128,64,384]{2,1,0:T(8,128)(2,1)S(1)} %fine_blocks.1.refs_0_, ...), custom_call_target="tpu_custom_call", output_to_operand_aliasing={{0}: (4, {}), {1}: (5, {})} | custom-call | flops 1 | bytes 1 | tf_op jit(solution)/shard_map/fine_inner/pallas_call | solution.py:457
  23.2 2.7 %copy-done.4 = bf16[204,64,256]{2,1,0:T(8,128)(2,1)} copy-done((bf16[204,64,256]{2,1,0:T(8,128)(2,1)}, bf16[204,64,256]{2,1,0:T(8,128)(2,1)S(1)}, u32[]{:S(2)}) %copy-start.4) | copy-done | bytes 6684696
  26.0 0.0 collective-permute-start.7
  26.0 2.6 %collective-permute-start = (f32[16,64,128]{2,1,0:T(8,128)S(1)}, f32[16,64,128]{2,1,0:T(8,128)S(1)}, u32[]{:S(2)}, u32[]{:S(2)}) collective-permute-start(f32[16,64,128]{2,1,0:T(8,128)S(1)} %get-tuple-element.68), channel_id=1, source_target_pairs={{0,2},{1,3},{2,0},{3,1},{4,6},{5,7},{6,4},{7,5},{8,16},{9,17},{10,... | collective-permute-start | bytes 1572872 | tf_op jit(solution)/shard_map/ppermute | solution.py:509
  28.6 3.2 %coarse_blocks.1.refs_6_.refs_2_.refs_1_ = bf16[64,64,640]{2,1,0:T(8,128)(2,1)S(1)} custom-call(bf16[64,64,8,64]{3,2,1,0:T(8,128)(2,1)S(1)} %bitcast.26, bf16[64,64,64]{2,1,0:T(8,128)(2,1)S(1)} %copy-done.9, bf16[64,64,64]{2,1,0:T(8,128)(2,1)S(1)} %copy-done.10, f32[32,64,128]{2,1,0:T(8,128)S(1)} %get-tuple-element.77.after), custom_call_target="tpu_custom_call" | custom-call | flops 1 | bytes 1 | tf_op jit(solution)/shard_map/coarse_blocks/pallas_call | solution.py:463
  31.9 2.2 %fine_middle.1 = (bf16[204,64,256]{2,1,0:T(8,128)(2,1)S(1)}, f32[128,64,128]{2,1,0:T(8,128)S(1)}, bf16[204,64,256]{2,1,0:T(8,128)(2,1)S(1)}, f32[128,64,128]{2,1,0:T(8,128)}, f32[16,64,128]{2,1,0:T(8,128)S(1)}) custom-call(bf16[128,64,384]{2,1,0:T(8,128)(2,1)S(1)} %fine_blocks.1.refs_0_, ...), custom_call_target="tpu_custom_call", output_to_operand_aliasing={{0}: (2, {}), {1}: (3, {}), {2}: (4, {}), {3}: (5, {})} | custom-call | flops 1 | bytes 1 | tf_op jit(solution)/shard_map/fine_middle/pallas_call | solution.py:457
  34.1 0.1 collective-permute-start.6
  34.2 1.5 %collective-permute-done.refs_1_ = f32[16,64,128]{2,1,0:T(8,128)S(1)} collective-permute-done((f32[16,64,128]{2,1,0:T(8,128)S(1)}, f32[16,64,128]{2,1,0:T(8,128)S(1)}, u32[]{:S(2)}, u32[]{:S(2)}) %collective-permute-start) | collective-permute-done | bytes 524320 | tf_op jit(solution)/shard_map/ppermute | solution.py:509
  35.7 1.7 %fine_ends.1 = (bf16[204,64,256]{2,1,0:T(8,128)(2,1)S(1)}, f32[128,64,128]{2,1,0:T(8,128)S(1)}, bf16[204,64,256]{2,1,0:T(8,128)(2,1)S(1)}, f32[128,64,128]{2,1,0...) custom-call(bf16[128,64,384]{2,1,0:T(8,128)(2,1)S(1)} %fine_blocks.1, ...), custom_call_target="tpu_custom_call", output_to_operand_aliasing={{0}: (2, {}), {1}: (3, {}), {2}: (4, {}), {3}: (5, {})} | custom-call | flops 1 | bytes 1 | tf_op jit(solution)/shard_map/fine_ends/pallas_call | solution.py:457
  37.4 2.1 %collective-permute-start.5 = (f32[16,64,128]{2,1,0:T(8,128)S(1)}, f32[16,64,128]{2,1,0:T(8,128)S(1)}, u32[]{:S(2)}, u32[]{:S(2)}) collective-permute-start(f32[16,64,128]{2,1,0:T(8,128)S(1)} %get-tuple-element.84), channel_id=1, source_target_pairs={{0,2},{1,3},{2,0},{3,1},{4,6},{5,7},{6,4},{7,5},{8,16},{9,17},{10,... | collective-permute-start | bytes 1572872 | tf_op jit(solution)/shard_map/ppermute | solution.py:509
  39.5 1.5 %collective-permute-start.8 = (f32[4,64,128]{2,1,0:T(8,128)S(1)}, f32[4,64,128]{2,1,0:T(8,128)S(1)}, u32[]{:S(2)}, u32[]{:S(2)}) collective-permute-start(f32[4,64,128]{2,1,0:T(8,128)S(1)} %get-tuple-element.86), channel_id=1, source_target_pairs={{0,1},{1,0},{2,3},{3,2},{4,5},{5,4},{6,7},{7,6},{8,9},{9,8},{10,11... | collective-permute-start | bytes 393224 | tf_op jit(solution)/shard_map/ppermute | solution.py:515
  41.0 3.9 %collective-permute-done.8.refs_4_ = f32[4,64,128]{2,1,0:T(8,128)S(1)} collective-permute-done((f32[4,64,128]{2,1,0:T(8,128)S(1)}, f32[4,64,128]{2,1,0:T(8,128)S(1)}, u32[]{:S(2)}, u32[]{:S(2)}) %collective-permute-start.8) | collective-permute-done | bytes 131104 | tf_op jit(solution)/shard_map/ppermute | solution.py:515
  44.9 0.0 collective-permute-done.7.refs_3_
  44.9 4.4 %left_inner.1 = (bf16[204,64,256]{2,1,0:T(8,128)(2,1)S(1)}, f32[64,64,128]{2,1,0:T(8,128)S(1)}, bf16[136,64,256]{2,1,0:T(8,128)(2,1)S(1)}) custom-call(bf16[128,64,384]{2,1,0:T(8,128)(2,1)S(1)} %fine_blocks.1.refs_0_, f32[128,64,128]{2,1,0:T(8,128)S(1)} %get-tuple-element.83.refs_1_, ...), custom_call_target="tpu_custom_call", output_to_operand_aliasing={{0}: (6, {})} | custom-call | flops 1 | bytes 1 | tf_op jit(solution)/shard_map/left_inner/pallas_call | solution.py:457
  49.3 0.0 collective-permute-done.6.refs_3_
  49.3 1.7 %left_middle.1 = (bf16[204,64,256]{2,1,0:T(8,128)(2,1)S(1)}, f32[64,64,128]{2,1,0:T(8,128)S(1)}, bf16[136,64,256]{2,1,0:T(8,128)(2,1)S(1)}, f32[16,64,128]{2,1,0:T(8,128)}) custom-call(bf16[128,64,384]{2,1,0:T(8,128)(2,1)S(1)} %fine_blocks.1.refs_0_, ...), custom_call_target="tpu_custom_call", output_to_operand_aliasing={{0}: (4, {}), {1}: (5, {}), {2}: (6, {})} | custom-call | flops 1 | bytes 1 | tf_op jit(solution)/shard_map/left_middle/pallas_call | solution.py:457
  50.9 0.0 collective-permute-done.5.refs_3_
  50.9 0.9 left_ends.1
  51.8 0.0 copy-start.11
  51.8 8.2 %collective-permute-start.10 = (f32[2,64,128]{2,1,0:T(8,128)S(1)}, f32[2,64,128]{2,1,0:T(8,128)S(1)}, u32[]{:S(2)}, u32[]{:S(2)}) collective-permute-start(f32[2,64,128]{2,1,0:T(8,128)S(1)} %get-tuple-element.95), channel_id=1, source_target_pairs={{0,1},{1,0},{2,3},{3,2},{4,5},{5,4},{6,7},{7,6},{8,9},{9,8},{10,11... | collective-permute-start | bytes 196616 | tf_op jit(solution)/shard_map/ppermute | solution.py:515
  60.1 0.0 collective-permute-start.11
  60.1 2.2 %collective-permute-done.10.refs_0_ = f32[2,64,128]{2,1,0:T(8,128)S(1)} collective-permute-done((f32[2,64,128]{2,1,0:T(8,128)S(1)}, f32[2,64,128]{2,1,0:T(8,128)S(1)}, u32[]{:S(2)}, u32[]{:S(2)}) %collective-permute-start.10) | collective-permute-done | bytes 65568 | tf_op jit(solution)/shard_map/ppermute | solution.py:515
  62.3 0.0 collective-permute-done.11.refs_1_
  62.3 1.3 %pack_first.1 = (bf16[136,64,256]{2,1,0:T(8,128)(2,1)S(1)}, f32[18,64,128]{2,1,0:T(8,128)}, f32[34,64,128]{2,1,0:T(8,128)}) custom-call(f32[2,64,128]{2,1,0:T(8,128)S(1)} %collective-permute-done.10.refs_0_, f32[2,64,128]{2,1,0:T(8,128)S(1)} %collective-permute-done.11.refs_1_, ...), custom_call_target="tpu_custom_call", output_to_operand_aliasing={{0}: (2, {})} | custom-call | flops 1 | bytes 1 | tf_op jit(solution)/shard_map/pack_first/pallas_call | solution.py:457
  63.6 2.1 %copy-done.2 = bf16[136,64,256]{2,1,0:T(8,128)(2,1)} copy-done((bf16[136,64,256]{2,1,0:T(8,128)(2,1)}, bf16[136,64,256]{2,1,0:T(8,128)(2,1)S(1)}, u32[]{:S(2)}) %copy-start.2) | copy-done | bytes 4456472
  65.7 3.1 %collective-permute-start.12 = (f32[18,64,128]{2,1,0:T(8,128)}, f32[18,64,128]{2,1,0:T(8,128)}, u32[]{:S(2)}, u32[]{:S(2)}) collective-permute-start(f32[18,64,128]{2,1,0:T(8,128)} %get-tuple-element.98), channel_id=1, source_target_pairs={{0,2},{1,3},{2,0},{3,1},{4,6},{5,7},{6,4},{7,5},{8,16},{9,17},{10,... | collective-permute-start | bytes 1769480 | tf_op jit(solution)/shard_map/ppermute | solution.py:509
  68.8 0.0 collective-permute-start.13
  68.8 0.0 collective-permute-done.14.refs_2_
  68.8 2.5 %copy-done.1 = bf16[64,64,640]{2,1,0:T(8,128)(2,1)S(1)} copy-done((bf16[64,64,640]{2,1,0:T(8,128)(2,1)S(1)}, bf16[64,64,640]{2,1,0:T(8,128)(2,1)}, u32[]{:S(2)}) %copy-start.1) | copy-done | bytes 5242904
  71.3 2.3 %copy-done.3 = bf16[136,64,256]{2,1,0:T(8,128)(2,1)S(1)} copy-done((bf16[136,64,256]{2,1,0:T(8,128)(2,1)S(1)}, bf16[136,64,256]{2,1,0:T(8,128)(2,1)}, u32[]{:S(2)}) %copy-start.3) | copy-done | bytes 4456472
  73.6 3.9 %coarse_inner.1 = (bf16[136,64,256]{2,1,0:T(8,128)(2,1)S(1)}, f32[64,64,128]{2,1,0:T(8,128)S(1)}, bf16[136,64,256]{2,1,0:T(8,128)(2,1)S(1)}, f32[64,64,128]{2,1,0:T(8,128)}) custom-call(s32[8,64]{1,0:T(8,128)S(1)} %fusion.6.refs_0_, bf16[64,64,640]{2,1,0:T(8,128)(2,1)S(1)} %copy-done.1, ...), custom_call_target="tpu_custom_call", output_to_operand_aliasing={{0}: (3, {}), {1}: (4, {})} | custom-call | flops 1 | bytes 1 | tf_op jit(solution)/shard_map/coarse_inner/pallas_call | solution.py:457
  77.5 5.1 %collective-permute-done.13.refs_2_ = f32[16,64,128]{2,1,0:T(8,128)} collective-permute-done((f32[16,64,128]{2,1,0:T(8,128)}, f32[16,64,128]{2,1,0:T(8,128)}, u32[]{:S(2)}, u32[]{:S(2)}) %collective-permute-start.13) | collective-permute-done | bytes 524320 | tf_op jit(solution)/shard_map/ppermute | solution.py:509
  82.6 2.9 %coarse_middle.1 = (bf16[136,64,256]{2,1,0:T(8,128)(2,1)S(1)}, f32[64,64,128]{2,1,0:T(8,128)S(1)}, bf16[136,64,256]{2,1,0:T(8,128)(2,1)S(1)}, f32[64,64,128]{2,1,0:T(8,128)}, f32[14,64,128]{2,1,0:T(8,128)S(1)}) custom-call(s32[8,64]{1,0:T(8,128)S(1)} %fusion.6.refs_0_, ...), custom_call_target="tpu_custom_call", output_to_operand_aliasing={{0}: (3, {}), {1}: (4, {}), {2}: (5, {}), {3}: (6, {})} | custom-call | flops 1 | bytes 1 | tf_op jit(solution)/shard_map/coarse_middle/pallas_call | solution.py:457
  85.5 0.0 collective-permute-done.12.refs_2_
  85.5 0.0 slice-start.1
  85.5 3.4 %coarse_ends.1 = (bf16[136,64,256]{2,1,0:T(8,128)(2,1)S(1)}, f32[64,64,128]{2,1,0:T(8,128)S(1)}, bf16[136,64,256]{2,1,0:T(8,128)(2,1)S(1)}, f32[64,64,128]{2,1,0...) custom-call(s32[8,64]{1,0:T(8,128)S(1)} %fusion.6.refs_0_, ...), custom_call_target="tpu_custom_call", output_to_operand_aliasing={{0}: (3, {}), {1}: (4, {}), {2}: (5, {}), {3}: (6, {})} | custom-call | flops 1 | bytes 1 | tf_op jit(solution)/shard_map/coarse_ends/pallas_call | solution.py:457
  89.0 2.0 %collective-permute-start.15 = (f32[2,64,128]{2,1,0:T(8,128)S(1)}, f32[2,64,128]{2,1,0:T(8,128)S(1)}, u32[]{:S(2)}, u32[]{:S(2)}) collective-permute-start(f32[2,64,128]{2,1,0:T(8,128)S(1)} %get-tuple-element.113), channel_id=1, source_target_pairs={{0,1},{1,0},{2,3},{3,2},{4,5},{5,4},{6,7},{7,6},{8,9},{9,8},{10,11... | collective-permute-start | bytes 196616 | tf_op jit(solution)/shard_map/ppermute | solution.py:515
  91.0 0.0 collective-permute-start.16
  91.0 2.4 %collective-permute-done.15.refs_0_ = f32[2,64,128]{2,1,0:T(8,128)S(1)} collective-permute-done((f32[2,64,128]{2,1,0:T(8,128)S(1)}, f32[2,64,128]{2,1,0:T(8,128)S(1)}, u32[]{:S(2)}, u32[]{:S(2)}) %collective-permute-start.15) | collective-permute-done | bytes 65568 | tf_op jit(solution)/shard_map/ppermute | solution.py:515
  93.4 0.0 collective-permute-done.16.refs_1_
  93.4 0.2 pack_second.1
  93.6 0.1 collective-permute-start.19
  93.7 4.9 %collective-permute-start.17 = (f32[20,64,128]{2,1,0:T(8,128)S(1)}, f32[20,64,128]{2,1,0:T(8,128)S(1)}, u32[]{:S(2)}, u32[]{:S(2)}) collective-permute-start(f32[20,64,128]{2,1,0:T(8,128)S(1)} %get-tuple-element.116), channel_id=1, source_target_pairs={{0,2},{1,3},{2,0},{3,1},{4,6},{5,7},{6,4},{7,5},{8,16},{9,17},{10,... | collective-permute-start | bytes 1966088 | tf_op jit(solution)/shard_map/ppermute | solution.py:509
  98.5 0.1 collective-permute-start.18
  98.6 3.5 %last_inner.1 = (bf16[136,64,256]{2,1,0:T(8,128)(2,1)S(1)}, f32[32,64,128]{2,1,0:T(8,128)}) custom-call(s32[8,64]{1,0:T(8,128)S(1)} %fusion.6.refs_0_, bf16[64,64,640]{2,1,0:T(8,128)(2,1)S(1)} %bitcast.22, f32[64,64,128]{2,1,0:T(8,128)S(1)} %get-tuple-element.112.refs_2_, ...), custom_call_target="tpu_custom_call", output_to_operand_aliasing={{0}: (4, {})} | custom-call | flops 1 | bytes 1 | tf_op jit(solution)/shard_map/last_inner/pallas_call | solution.py:457
  102.1 9.9 %collective-permute-done.18.refs_3_ = f32[14,64,128]{2,1,0:T(8,128)S(1)} collective-permute-done((f32[14,64,128]{2,1,0:T(8,128)S(1)}, f32[14,64,128]{2,1,0:T(8,128)S(1)}, u32[]{:S(2)}, u32[]{:S(2)}) %collective-permute-start.18) | collective-permute-done | bytes 458784 | tf_op jit(solution)/shard_map/ppermute | solution.py:509
  112.0 2.1 %last_middle.1 = (bf16[136,64,256]{2,1,0:T(8,128)(2,1)S(1)}, f32[32,64,128]{2,1,0:T(8,128)}) custom-call(s32[8,64]{1,0:T(8,128)S(1)} %fusion.6.refs_0_, bf16[64,64,640]{2,1,0:T(8,128)(2,1)S(1)} %bitcast.22, f32[64,64,128]{2,1,0:T(8,128)S(1)} %get-tuple-element.112.refs_2_, ...), custom_call_target="tpu_custom_call", output_to_operand_aliasing={{0}: (4, {}), {1}: (5, {})} | custom-call | flops 1 | bytes 1 | tf_op jit(solution)/shard_map/last_middle/pallas_call | solution.py:457
  114.2 2.6 %last_ends.1 = (bf16[136,64,256]{2,1,0:T(8,128)(2,1)S(1)}, f32[32,64,128]{2,1,0:T(8,128)}) custom-call(s32[8,64]{1,0:T(8,128)S(1)} %fusion.6.refs_0_, bf16[64,64,640]{2,1,0:T(8,128)(2,1)S(1)} %bitcast.22, f32[64,64,128]{2,1,0:T(8,128)S(1)} %get-tuple-element.112.refs_2_, ...), custom_call_target="tpu_custom_call", output_to_operand_aliasing={{0}: (4, {}), {1}: (5, {})} | custom-call | flops 1 | bytes 1 | tf_op jit(solution)/shard_map/last_ends/pallas_call | solution.py:457
  (34 shorter events, 0.1 us)
Async XLA Ops:
  0.6 1.2 %copy-start.6 = (bf16[128,64,64]{0,2,1:T(8,128)(2,1)S(1)}, bf16[128,64,64]{0,2,1:T(8,128)(2,1)}, u32[]{:S(2)}) copy-start(bf16[128,64,64]{0,2,1:T(8,128)(2,1)} %param.11) | copy-start | bytes 3145732
  1.9 2.2 %copy-start.7 = (f32[128,64,128]{2,1,0:T(8,128)S(1)}, f32[128,64,128]{2,1,0:T(8,128)}, u32[]{:S(2)}) copy-start(f32[128,64,128]{2,1,0:T(8,128)} %refs_0_.1) | copy-start | bytes 12582916
  5.9 6.7 %copy-start.5 = (bf16[128,64,4,64]{0,3,2,1:T(8,128)(2,1)S(1)}, bf16[128,64,4,64]{0,3,2,1:T(8,128)(2,1)}, u32[]{:S(2)}) copy-start(bf16[128,64,4,64]{0,3,2,1:T(8,128)(2,1)} %param.9) | copy-start | bytes 12582916
  5.9 6.7 %copy-start.8 = (bf16[128,64,64]{0,2,1:T(8,128)(2,1)S(1)}, bf16[128,64,64]{0,2,1:T(8,128)(2,1)}, u32[]{:S(2)}) copy-start(bf16[128,64,64]{0,2,1:T(8,128)(2,1)} %param.10) | copy-start | bytes 3145732
  7.9 9.3 %collective-permute-start.2 = (f32[32,64,128]{2,1,0:T(8,128)S(1)}, f32[32,64,128]{2,1,0:T(8,128)S(1)}, u32[]{:S(2)}, u32[]{:S(2)}) collective-permute-start(f32[32,64,128]{2,1,0:T(8,128)S(1)} %get-tuple-element.67.refs_4_), channel_id=1, source_target_pairs={{0,8},{1,9},{2,10},{3,11},{4,12},{5,13},{6,14},{7,15},{8,0},{9,1},... | collective-permute-start | bytes 3145736 | tf_op jit(solution)/shard_map/ppermute | solution.py:512
  8.4 8.7 %collective-permute-start.3 = (f32[4,64,128]{2,1,0:T(8,128)S(1)}, f32[4,64,128]{2,1,0:T(8,128)S(1)}, u32[]{:S(2)}, u32[]{:S(2)}) collective-permute-start(f32[4,64,128]{2,1,0:T(8,128)S(1)} %get-tuple-element.70), channel_id=1, source_target_pairs={{0,1},{1,0},{2,3},{3,2},{4,5},{5,4},{6,7},{7,6},{8,9},{9,8},{10,11... | collective-permute-start | bytes 393224 | tf_op jit(solution)/shard_map/ppermute | solution.py:515
  11.0 6.2 %collective-permute-start.4 = (f32[4,64,128]{2,1,0:T(8,128)S(1)}, f32[4,64,128]{2,1,0:T(8,128)S(1)}, u32[]{:S(2)}, u32[]{:S(2)}) collective-permute-start(f32[4,64,128]{2,1,0:T(8,128)S(1)} %get-tuple-element.71), channel_id=1, source_target_pairs={{0,8},{1,2},{2,1},{3,4},{4,3},{5,6},{6,5},{7,15},{8,0},{9,10},{10,... | collective-permute-start | bytes 393224 | tf_op jit(solution)/shard_map/ppermute | solution.py:518
  11.2 20.7 %collective-permute-start.1 = (f32[16,64,128]{2,1,0:T(8,128)S(1)}, f32[16,64,128]{2,1,0:T(8,128)S(1)}, u32[]{:S(2)}, u32[]{:S(2)}) collective-permute-start(f32[16,64,128]{2,1,0:T(8,128)S(1)} %get-tuple-element.69), channel_id=1, source_target_pairs={{0,2},{1,3},{2,0},{3,1},{4,6},{5,7},{6,4},{7,5},{8,16},{9,17},{10,... | collective-permute-start | bytes 1572872 | tf_op jit(solution)/shard_map/ppermute | solution.py:509
  17.2 11.4 %slice-start.4 = ((s8[8388608]{0:T(1024)(128)(4,1)}), s8[4194304]{0:T(1024)(128)(4,1)S(1)}, s32[]{:S(2)}) async-start(s8[8388608]{0:T(1024)(128)(4,1)} %bitcast.25), calls=%async_computation.4 | async-start | bytes 8388608
  17.2 11.4 %slice-start.5 = ((s8[8388608]{0:T(1024)(128)(4,1)}), s8[4194304]{0:T(1024)(128)(4,1)S(1)}, s32[]{:S(2)}) async-start(s8[8388608]{0:T(1024)(128)(4,1)} %bitcast.25), calls=%async_computation.5 | async-start | bytes 8388608
  17.2 11.4 %copy-start.9 = (bf16[64,64,64]{2,1,0:T(8,128)(2,1)S(1)}, bf16[64,64,64]{2,1,0:T(8,128)(2,1)}, u32[]{:S(2)}) copy-start(bf16[64,64,64]{2,1,0:T(8,128)(2,1)} %diagonal.1) | copy-start | bytes 1572868
  17.2 11.4 %copy-start.10 = (bf16[64,64,64]{2,1,0:T(8,128)(2,1)S(1)}, bf16[64,64,64]{2,1,0:T(8,128)(2,1)}, u32[]{:S(2)}) copy-start(bf16[64,64,64]{2,1,0:T(8,128)(2,1)} %inverse.1) | copy-start | bytes 1572868
  23.2 2.7 %copy-start.4 = (bf16[204,64,256]{2,1,0:T(8,128)(2,1)}, bf16[204,64,256]{2,1,0:T(8,128)(2,1)S(1)}, u32[]{:S(2)}) copy-start(bf16[204,64,256]{2,1,0:T(8,128)(2,1)S(1)} %get-tuple-element.73.refs_2_) | copy-start | bytes 20054020
  26.0 18.9 %collective-permute-start.7 = (f32[32,64,128]{2,1,0:T(8,128)S(1)}, f32[32,64,128]{2,1,0:T(8,128)S(1)}, u32[]{:S(2)}, u32[]{:S(2)}) collective-permute-start(f32[32,64,128]{2,1,0:T(8,128)S(1)} %get-tuple-element.77.after), channel_id=1, source_target_pairs={{0,8},{1,9},{2,10},{3,11},{4,12},{5,13},{6,14},{7,15},{8,0},{9,1},... | collective-permute-start | bytes 3145736 | tf_op jit(solution)/shard_map/ppermute | solution.py:512
  26.0 5.9 %slice-start.2 = ((s8[6684672]{0:T(1024)(128)(4,1)}), s8[4194304]{0:T(1024)(128)(4,1)S(1)}, s32[]{:S(2)}) async-start(s8[6684672]{0:T(1024)(128)(4,1)} %bitcast.23), calls=%async_computation.2 | async-start | bytes 8388608
  26.0 5.9 %slice-start.3 = ((s8[6684672]{0:T(1024)(128)(4,1)}), s8[2490368]{0:T(1024)(128)(4,1)S(1)}, s32[]{:S(2)}) async-start(s8[6684672]{0:T(1024)(128)(4,1)} %bitcast.23), calls=%async_computation.3 | async-start | bytes 4980736
  26.0 9.7 %collective-permute-start = (f32[16,64,128]{2,1,0:T(8,128)S(1)}, f32[16,64,128]{2,1,0:T(8,128)S(1)}, u32[]{:S(2)}, u32[]{:S(2)}) collective-permute-start(f32[16,64,128]{2,1,0:T(8,128)S(1)} %get-tuple-element.68), channel_id=1, source_target_pairs={{0,2},{1,3},{2,0},{3,1},{4,6},{5,7},{6,4},{7,5},{8,16},{9,17},{10,... | collective-permute-start | bytes 1572872 | tf_op jit(solution)/shard_map/ppermute | solution.py:509
  31.8 19.1 %copy-start = (bf16[64,64,640]{2,1,0:T(8,128)(2,1)}, bf16[64,64,640]{2,1,0:T(8,128)(2,1)S(1)}, u32[]{:S(2)}) copy-start(bf16[64,64,640]{2,1,0:T(8,128)(2,1)S(1)} %coarse_blocks.1.refs_6_.refs_2_.refs_1_) | copy-start | bytes 15728644
  34.1 15.2 %collective-permute-start.6 = (f32[16,64,128]{2,1,0:T(8,128)S(1)}, f32[16,64,128]{2,1,0:T(8,128)S(1)}, u32[]{:S(2)}, u32[]{:S(2)}) collective-permute-start(f32[16,64,128]{2,1,0:T(8,128)S(1)} %get-tuple-element.85), channel_id=1, source_target_pairs={{0,2},{1,3},{2,0},{3,1},{4,6},{5,7},{6,4},{7,5},{8,16},{9,17},{10,... | collective-permute-start | bytes 1572872 | tf_op jit(solution)/shard_map/ppermute | solution.py:509
  37.4 13.5 %collective-permute-start.5 = (f32[16,64,128]{2,1,0:T(8,128)S(1)}, f32[16,64,128]{2,1,0:T(8,128)S(1)}, u32[]{:S(2)}, u32[]{:S(2)}) collective-permute-start(f32[16,64,128]{2,1,0:T(8,128)S(1)} %get-tuple-element.84), channel_id=1, source_target_pairs={{0,2},{1,3},{2,0},{3,1},{4,6},{5,7},{6,4},{7,5},{8,16},{9,17},{10,... | collective-permute-start | bytes 1572872 | tf_op jit(solution)/shard_map/ppermute | solution.py:509
  39.5 5.3 %collective-permute-start.8 = (f32[4,64,128]{2,1,0:T(8,128)S(1)}, f32[4,64,128]{2,1,0:T(8,128)S(1)}, u32[]{:S(2)}, u32[]{:S(2)}) collective-permute-start(f32[4,64,128]{2,1,0:T(8,128)S(1)} %get-tuple-element.86), channel_id=1, source_target_pairs={{0,1},{1,0},{2,3},{3,2},{4,5},{5,4},{6,7},{7,6},{8,9},{9,8},{10,11... | collective-permute-start | bytes 393224 | tf_op jit(solution)/shard_map/ppermute | solution.py:515
  41.0 3.9 %collective-permute-start.9 = (f32[4,64,128]{2,1,0:T(8,128)S(1)}, f32[4,64,128]{2,1,0:T(8,128)S(1)}, u32[]{:S(2)}, u32[]{:S(2)}) collective-permute-start(f32[4,64,128]{2,1,0:T(8,128)S(1)} %get-tuple-element.87), channel_id=1, source_target_pairs={{0,8},{1,2},{2,1},{3,4},{4,3},{5,6},{6,5},{7,15},{8,0},{9,10},{10,... | collective-permute-start | bytes 393224 | tf_op jit(solution)/shard_map/ppermute | solution.py:518
  51.8 17.0 %copy-start.11 = (s32[64,8]{0,1:T(8,128)S(1)}, s32[64,8]{0,1:T(8,128)}, u32[]{:S(2)}) copy-start(s32[64,8]{0,1:T(8,128)} %param.15) | copy-start | bytes 6148
  51.8 10.5 %collective-permute-start.10 = (f32[2,64,128]{2,1,0:T(8,128)S(1)}, f32[2,64,128]{2,1,0:T(8,128)S(1)}, u32[]{:S(2)}, u32[]{:S(2)}) collective-permute-start(f32[2,64,128]{2,1,0:T(8,128)S(1)} %get-tuple-element.95), channel_id=1, source_target_pairs={{0,1},{1,0},{2,3},{3,2},{4,5},{5,4},{6,7},{7,6},{8,9},{9,8},{10,11... | collective-permute-start | bytes 196616 | tf_op jit(solution)/shard_map/ppermute | solution.py:515
  60.1 2.2 %collective-permute-start.11 = (f32[2,64,128]{2,1,0:T(8,128)S(1)}, f32[2,64,128]{2,1,0:T(8,128)S(1)}, u32[]{:S(2)}, u32[]{:S(2)}) collective-permute-start(f32[2,64,128]{2,1,0:T(8,128)S(1)} %get-tuple-element.96), channel_id=1, source_target_pairs={{0,8},{1,2},{2,1},{3,4},{4,3},{5,6},{6,5},{7,15},{8,0},{9,10},{10,... | collective-permute-start | bytes 196616 | tf_op jit(solution)/shard_map/ppermute | solution.py:518
  63.6 2.1 %copy-start.2 = (bf16[136,64,256]{2,1,0:T(8,128)(2,1)}, bf16[136,64,256]{2,1,0:T(8,128)(2,1)S(1)}, u32[]{:S(2)}) copy-start(bf16[136,64,256]{2,1,0:T(8,128)(2,1)S(1)} %get-tuple-element.101.refs_3_) | copy-start | bytes 13369348
  65.7 3.2 %collective-permute-start.14 = (f32[34,64,128]{2,1,0:T(8,128)}, f32[34,64,128]{2,1,0:T(8,128)S(1)}, u32[]{:S(2)}, u32[]{:S(2)}) collective-permute-start(f32[34,64,128]{2,1,0:T(8,128)} %get-tuple-element.100), channel_id=1, source_target_pairs={{0,8},{1,9},{2,10},{3,11},{4,12},{5,13},{6,14},{7,15},{8,0},{9,1},... | collective-permute-start | bytes 3342344 | tf_op jit(solution)/shard_map/ppermute | solution.py:512
  65.7 19.8 %collective-permute-start.12 = (f32[18,64,128]{2,1,0:T(8,128)}, f32[18,64,128]{2,1,0:T(8,128)}, u32[]{:S(2)}, u32[]{:S(2)}) collective-permute-start(f32[18,64,128]{2,1,0:T(8,128)} %get-tuple-element.98), channel_id=1, source_target_pairs={{0,2},{1,3},{2,0},{3,1},{4,6},{5,7},{6,4},{7,5},{8,16},{9,17},{10,... | collective-permute-start | bytes 1769480 | tf_op jit(solution)/shard_map/ppermute | solution.py:509
  68.8 13.8 %collective-permute-start.13 = (f32[16,64,128]{2,1,0:T(8,128)}, f32[16,64,128]{2,1,0:T(8,128)}, u32[]{:S(2)}, u32[]{:S(2)}) collective-permute-start(f32[16,64,128]{2,1,0:T(8,128)} %get-tuple-element.99), channel_id=1, source_target_pairs={{0,2},{1,3},{2,0},{3,1},{4,6},{5,7},{6,4},{7,5},{8,16},{9,17},{10,... | collective-permute-start | bytes 1572872 | tf_op jit(solution)/shard_map/ppermute | solution.py:509
  68.8 2.5 %copy-start.1 = (bf16[64,64,640]{2,1,0:T(8,128)(2,1)S(1)}, bf16[64,64,640]{2,1,0:T(8,128)(2,1)}, u32[]{:S(2)}) copy-start(bf16[64,64,640]{2,1,0:T(8,128)(2,1)} %copy-done) | copy-start | bytes 15728644
  71.3 2.3 %copy-start.3 = (bf16[136,64,256]{2,1,0:T(8,128)(2,1)S(1)}, bf16[136,64,256]{2,1,0:T(8,128)(2,1)}, u32[]{:S(2)}) copy-start(bf16[136,64,256]{2,1,0:T(8,128)(2,1)} %copy-done.2) | copy-start | bytes 13369348
  85.5 13.1 %slice-start = ((s8[5242880]{0:T(1024)(128)(4,1)}), s8[4194304]{0:T(1024)(128)(4,1)S(1)}, s32[]{:S(2)}) async-start(s8[5242880]{0:T(1024)(128)(4,1)} %bitcast.21), calls=%async_computation | async-start | bytes 8388608
  85.5 13.1 %slice-start.1 = ((s8[5242880]{0:T(1024)(128)(4,1)}), s8[1048576]{0:T(1024)(128)(4,1)S(1)}, s32[]{:S(2)}) async-start(s8[5242880]{0:T(1024)(128)(4,1)} %bitcast.21), calls=%async_computation.1 | async-start | bytes 2097152
  89.0 4.4 %collective-permute-start.15 = (f32[2,64,128]{2,1,0:T(8,128)S(1)}, f32[2,64,128]{2,1,0:T(8,128)S(1)}, u32[]{:S(2)}, u32[]{:S(2)}) collective-permute-start(f32[2,64,128]{2,1,0:T(8,128)S(1)} %get-tuple-element.113), channel_id=1, source_target_pairs={{0,1},{1,0},{2,3},{3,2},{4,5},{5,4},{6,7},{7,6},{8,9},{9,8},{10,11... | collective-permute-start | bytes 196616 | tf_op jit(solution)/shard_map/ppermute | solution.py:515
  91.0 2.4 %collective-permute-start.16 = (f32[2,64,128]{2,1,0:T(8,128)S(1)}, f32[2,64,128]{2,1,0:T(8,128)S(1)}, u32[]{:S(2)}, u32[]{:S(2)}) collective-permute-start(f32[2,64,128]{2,1,0:T(8,128)S(1)} %get-tuple-element.114), channel_id=1, source_target_pairs={{0,8},{1,2},{2,1},{3,4},{4,3},{5,6},{6,5},{7,15},{8,0},{9,10},{10,... | collective-permute-start | bytes 196616 | tf_op jit(solution)/shard_map/ppermute | solution.py:518
  93.6 5.0 %collective-permute-start.19 = (f32[34,64,128]{2,1,0:T(8,128)S(1)}, f32[34,64,128]{2,1,0:T(8,128)S(1)}, u32[]{:S(2)}, u32[]{:S(2)}) collective-permute-start(f32[34,64,128]{2,1,0:T(8,128)S(1)} %get-tuple-element.118), channel_id=1, source_target_pairs={{0,8},{1,9},{2,10},{3,11},{4,12},{5,13},{6,14},{7,15},{8,0},{9,1},... | collective-permute-start | bytes 3342344 | tf_op jit(solution)/shard_map/ppermute | solution.py:512
  93.7 20.5 %collective-permute-start.17 = (f32[20,64,128]{2,1,0:T(8,128)S(1)}, f32[20,64,128]{2,1,0:T(8,128)S(1)}, u32[]{:S(2)}, u32[]{:S(2)}) collective-permute-start(f32[20,64,128]{2,1,0:T(8,128)S(1)} %get-tuple-element.116), channel_id=1, source_target_pairs={{0,2},{1,3},{2,0},{3,1},{4,6},{5,7},{6,4},{7,5},{8,16},{9,17},{10,... | collective-permute-start | bytes 1966088 | tf_op jit(solution)/shard_map/ppermute | solution.py:509
  98.5 13.5 %collective-permute-start.18 = (f32[14,64,128]{2,1,0:T(8,128)S(1)}, f32[14,64,128]{2,1,0:T(8,128)S(1)}, u32[]{:S(2)}, u32[]{:S(2)}) collective-permute-start(f32[14,64,128]{2,1,0:T(8,128)S(1)} %get-tuple-element.117), channel_id=1, source_target_pairs={{0,2},{1,3},{2,0},{3,1},{4,6},{5,7},{6,4},{7,5},{8,16},{9,17},{10,... | collective-permute-start | bytes 1376264 | tf_op jit(solution)/shard_map/ppermute | solution.py:509

commit v2 on v1

--- a/solution.py
+++ b/solution.py
@@ -248,7 +248,9 @@
         blocks[:, rows, 4 * species :] = jnp.transpose(both, (2, 0, 1))
 
 
-def fine_inner_kernel(blocks, near_h, even_h, odd_h, grid_in, side_in, grid, side, change, out, near, iterate, sems):
+def fine_inner_kernel(
+    blocks, near_h, even_h, odd_h, grid_in, side_in, change_in, out_in, grid, side, change, out, near, iterate, sems
+):
     write_row(grid, near_h, BLOCK_X, range(BLOCK_Y))
     write_sides(grid, even_h, odd_h, BLOCK_X)
 
@@ -264,9 +266,15 @@
         pltpu.make_async_copy(part, out.at[pl.ds(0, UNROLL)], sems.at[n]).wait()
 
 
-def fine_outer_kernel(
-    cols, sides, blocks, far_h, grid_in, side_in, change_in, out_in, grid, side, change, out, far, *rest
-):
+def fine_middle_kernel(cols, blocks, far_h, grid_in, side_in, *rest):
+    fine_outer(cols, False, blocks, far_h, *rest)
+
+
+def fine_ends_kernel(cols, blocks, far_h, grid_in, side_in, change_in, out_in, *rest):
+    fine_outer(cols, True, blocks, far_h, *rest)
+
+
+def fine_outer(cols, sides, blocks, far_h, grid, side, change, out, far, *rest):
     *sends, iterate, sems = rest
     write_row(grid, far_h, -1, cols, far_is_inside())
     fine_second(0, cols, blocks, grid, side, change, iterate, 0, far)
@@ -289,80 +297,90 @@
             far[n] = first
 
 
-def left_inner_kernel(blocks, side, coarse_blocks, near_h, even_h, odd_h, change_in, change, coarse_side, coarse_grid):
+def left_pair(rho, cols, blocks, side, change, coarse_side, own_blocks, coarse_grid, far=None):
+    for q in cols:
+        upper = fine_left(2 * rho, q, blocks, side, change)
+        coarse_side[rho * BLOCK_Y + q] = upper + fine_left(2 * rho + 1, q, blocks, side, change)
+    for n, q in enumerate(cols):
+        cell = place(rho, COARSE_X) * BLOCK_Y + q
+        first = smoothed(own_blocks, cell, coarse_side[rho * BLOCK_Y + q])
+        coarse_grid[spot(rho, q)] = split(first)
+        if far is not None:
+            far[n] = first
+
+
+def left_middle_kernel(cols, blocks, side, own_blocks, far_h, change_in, change, coarse_side, coarse_grid, far):
+    write_row(change, far_h, -1, cols, far_is_inside())
+    left_pair(0, cols, blocks, side, change, coarse_side, own_blocks, coarse_grid, far)
+
+
+def left_inner_kernel(
+    blocks, side, own_blocks, near_h, even_h, odd_h, change_in, coarse_in, grid_in, change, coarse_side, coarse_grid
+):
     write_row(change, near_h, BLOCK_X, range(BLOCK_Y))
     write_sides(change, even_h, odd_h, BLOCK_X)
 
-    def pairs(rho, start):
-        for q in range(UNROLL):
-            upper = fine_left(2 * rho, start + q, blocks, side, change)
-            lower = fine_left(2 * rho + 1, start + q, blocks, side, change)
-            coarse_side[rho * BLOCK_Y + start + q] = upper + lower
-        next_first(rho, [start + q for q in range(UNROLL)], coarse_side, coarse_blocks, coarse_grid)
-
-    over_rows(1, COARSE_X, pairs)
-
-    def single(rho, start):
-        for q in range(UNROLL):
-            coarse_side[start + q] = fine_left(rho, start + q, blocks, side, change)
-
-    over_rows(1, 2, single)
-
-
-def left_outer_kernel(
-    cols, sides, blocks, side, coarse_blocks, far_h, change_in, coarse_in, grid_in, change, coarse_side, coarse_grid, *sends
+    def body(rho, start):
+        cols = [start + q for q in range(UNROLL)]
+        left_pair(rho, cols, blocks, side, change, coarse_side, own_blocks, coarse_grid)
+
+    over_rows(1, COARSE_X, body)
+
+
+def left_ends_kernel(
+    cols, blocks, side, own_blocks, far_h, change_in, coarse_in, grid_in, change, coarse_side, coarse_grid, far, *sends
 ):
     write_row(change, far_h, -1, cols, far_is_inside())
-    for q in cols:
-        coarse_side[q] = coarse_side[q] + fine_left(0, q, blocks, side, change)
-    next_first(0, cols, coarse_side, coarse_blocks, coarse_grid, None if sides else sends[0])
-    if sides:
-        read_sides(coarse_grid, *sends, COARSE_X)
-
-
-def coarse_blocks_kernel(coupling, diagonal, inverse, after, blocks):
+    left_pair(0, cols, blocks, side, change, coarse_side, own_blocks, coarse_grid, far)
+    read_sides(coarse_grid, *sends, COARSE_X)
+
+
+def own_blocks_kernel(diagonal, inverse, blocks):
+    for cell in range(diagonal.shape[0]):
+        blocks[cell] = jnp.concatenate([diagonal[cell], inverse[cell]], axis=1)
+
+
+def near_blocks_kernel(coupling, after, blocks):
     species = coupling.shape[1]
     first = pl.program_id(0) * coupling.shape[0]
     for n in range(coupling.shape[0]):
-        blocks[first + n, :, : 8 * species] = coupling[n].reshape(species, 8 * species)
-        blocks[first + n, :, 8 * species :] = jnp.concatenate([diagonal[n], inverse[n]], axis=1)
-
-
-def coarse_apply(rho, q, places, blocks, grid):
+        blocks[first + n] = coupling[n].reshape(species, 8 * species)
+
+
+def coarse_apply(rho, q, places, blocks, own_blocks, grid):
     cell = place(rho, COARSE_X) * BLOCK_Y + q
-    species = blocks.shape[1]
     near = jnp.concatenate([grid[places[k, cell]] for k in range(8)], axis=0)
-    return dot(
-        (blocks[cell, :, : 8 * species], near), (blocks[cell, :, 8 * species :], with_zeros(grid[spot(rho, q)], True))
-    )
-
-
-def coarse_second(rho, cols, places, blocks, grid, side, change, iterate, n, far=None):
+    return dot((blocks[cell], near), (own_blocks[cell], with_zeros(grid[spot(rho, q)], True)))
+
+
+def coarse_second(rho, cols, places, blocks, own_blocks, grid, side, change, iterate, n, far=None):
     for q in cols:
         here = rho * BLOCK_Y + q
-        side[here] = side[here] - coarse_apply(rho, q, places, blocks, grid)
+        side[here] = side[here] - coarse_apply(rho, q, places, blocks, own_blocks, grid)
     for m, q in enumerate(cols):
         here = spot(rho, q)
-        step = smoothed(blocks, place(rho, COARSE_X) * BLOCK_Y + q, side[rho * BLOCK_Y + q])
+        step = smoothed(own_blocks, place(rho, COARSE_X) * BLOCK_Y + q, side[rho * BLOCK_Y + q])
         change[here] = split(step)
         iterate[n + m] = fold(grid[here]) + step
         if far is not None:
             far[m] = step
 
 
-def pack_kernel(cols, even_h, odd_h, grid_in, grid, far, near):
+def pack_kernel(even_h, odd_h, grid_in, grid, corners, near):
     write_sides(grid, even_h, odd_h, COARSE_X)
-    read_row(grid, far, 0, cols + (-1, BLOCK_Y))
+    read_row(grid, corners, 0, (-1, BLOCK_Y))
     read_row(grid, near, COARSE_X - 1, range(-1, BLOCK_Y + 1))
 
 
-def coarse_inner_kernel(places, blocks, near_h, grid_in, side_in, grid, side, change, out, iterate, sems):
+def coarse_inner_kernel(
+    places, blocks, own_blocks, near_h, grid_in, side_in, change_in, out_in, grid, side, change, out, iterate, sems
+):
     write_row(grid, near_h, COARSE_X, range(-1, BLOCK_Y + 1))
 
     def body(rho, start):
         n = (rho - 1) * BLOCK_Y + start
         cell = place(rho, COARSE_X) * BLOCK_Y + start
-        coarse_second(rho, [start + q for q in range(UNROLL)], places, blocks, grid, side, change, iterate, n)
+        coarse_second(rho, [start + q for q in range(UNROLL)], places, blocks, own_blocks, grid, side, change, iterate, n)
         send_out(iterate, n, out, cell, UNROLL, sems.at[n // UNROLL])
 
     over_rows(1, COARSE_X, body)
@@ -371,12 +389,19 @@
         pltpu.make_async_copy(part, out.at[pl.ds(0, UNROLL)], sems.at[n]).wait()
 
 
-def coarse_outer_kernel(
-    came, cols, sides, places, blocks, far_h, grid_in, side_in, change_in, out_in, grid, side, change, out, *rest
-):
+def coarse_middle_kernel(came, cols, places, blocks, own_blocks, far_h, grid_in, side_in, *rest):
+    coarse_outer(came, cols, False, places, blocks, own_blocks, far_h, *rest)
+
+
+def coarse_ends_kernel(came, cols, places, blocks, own_blocks, far_h, corners_h, grid_in, side_in, change_in, out_in, grid, *rest):
+    write_row(grid, corners_h, -1, (-1, BLOCK_Y))
+    coarse_outer(came, cols, True, places, blocks, own_blocks, far_h, grid, *rest)
+
+
+def coarse_outer(came, cols, sides, places, blocks, own_blocks, far_h, grid, side, change, out, far, *rest):
     *sends, iterate, sems = rest
     write_row(grid, far_h, -1, came)
-    coarse_second(0, cols, places, blocks, grid, side, change, iterate, 0, None if sides else sends[0])
+    coarse_second(0, cols, places, blocks, own_blocks, grid, side, change, iterate, 0, far)
     copies = [
         send_out(iterate, n, out, place(0, COARSE_X) * BLOCK_Y + q, count, sems.at[k])
         for k, (n, q, count) in enumerate(stretches(cols))
@@ -387,22 +412,22 @@
         copy.wait()
 
 
-def coarse_left(rho, q, places, blocks, side, change):
-    return side[rho * BLOCK_Y + q] - coarse_apply(rho, q, places, blocks, change)
-
-
-def last_pair(rho, q, places, blocks, side, change):
-    return coarse_left(rho, q, places, blocks, side, change) + coarse_left(rho, q + 1, places, blocks, side, change)
-
-
-def last_inner_kernel(places, blocks, side, near_h, change_in, change, out, below, sems):
+def coarse_left(rho, q, places, blocks, own_blocks, side, change):
+    return side[rho * BLOCK_Y + q] - coarse_apply(rho, q, places, blocks, own_blocks, change)
+
+
+def last_pair(rho, q, places, blocks, own_blocks, side, change):
+    return coarse_left(rho, q, places, blocks, own_blocks, side, change) + coarse_left(rho, q + 1, places, blocks, own_blocks, side, change)
+
+
+def last_inner_kernel(places, blocks, own_blocks, side, near_h, change_in, out_in, change, out, below, sems):
     write_row(change, near_h, COARSE_X, range(-1, BLOCK_Y + 1))
     count = UNROLL // 2
 
     def body(rho, start):
         n = ((rho - 1) * BLOCK_Y + start) // 2
         for q in range(count):
-            below[n + q] = last_pair(rho, start + 2 * q, places, blocks, side, change)
+            below[n + q] = last_pair(rho, start + 2 * q, places, blocks, own_blocks, side, change)
         send_out(below, n, out, (place(rho, COARSE_X) * BLOCK_Y + start) // 2, count, sems.at[n // count])
 
     over_rows(1, COARSE_X, body)
@@ -411,11 +436,20 @@
         pltpu.make_async_copy(part, out.at[pl.ds(0, count)], sems.at[n]).wait()
 
 
-def last_outer_kernel(came, cols, places, blocks, side, far_h, change_in, out_in, change, out, below, sems):
+def last_middle_kernel(came, cols, places, blocks, own_blocks, side, far_h, change_in, *rest):
+    last_outer(came, cols, places, blocks, own_blocks, side, far_h, *rest)
+
+
+def last_ends_kernel(came, cols, places, blocks, own_blocks, side, far_h, corners_h, change_in, out_in, change, *rest):
+    write_row(change, corners_h, -1, (-1, BLOCK_Y))
+    last_outer(came, cols, places, blocks, own_blocks, side, far_h, change, *rest)
+
+
+def last_outer(came, cols, places, blocks, own_blocks, side, far_h, change, out, below, sems):
     write_row(change, far_h, -1, came)
     pairs = [q // 2 for q in cols[::2]]
     for n, q in enumerate(pairs):
-        below[n] = last_pair(0, 2 * q, places, blocks, side, change)
+        below[n] = last_pair(0, 2 * q, places, blocks, own_blocks, side, change)
     copies = [
         send_out(below, n, out, place(0, COARSE_X) * BLOCK_Y // 2 + q, count, sems.at[k])
         for k, (n, q, count) in enumerate(stretches(pairs))
@@ -425,17 +459,15 @@
 
 
 IN_VMEM = pl.BlockSpec(memory_space=pltpu.VMEM)
-IN_SMEM = pl.BlockSpec(memory_space=pltpu.SMEM)
-IN_HBM = pl.BlockSpec(memory_space=pltpu.HBM)
-
-
-def run(name, kernel, outs, args, aliases=(), scalars=(), far_args=(), far_outs=(), scratch=(), after=()):
+LONG = 10**11
+
+
+def run(name, kernel, outs, args, aliases=(), smem=(), hbm=(), hbm_outs=(), smem_outs=(), scratch=(), after=(), cost=1):
     count = len(args)
     args = list(args) + list(after)
-    specs = [IN_SMEM if n in scalars else IN_HBM if n in far_args else IN_VMEM for n in range(len(args))]
-    args = [
-        x if n in scalars or n in far_args else pltpu.with_memory_space_constraint(x, pltpu.VMEM)
-        for n, x in enumerate(args)
+    spaces = [pltpu.SMEM if n in smem else pltpu.HBM if n in hbm else pltpu.VMEM for n in range(len(args))]
+    out_spaces = [
+        pltpu.SMEM if n in smem_outs else pltpu.HBM if n in hbm_outs else pltpu.VMEM for n in range(len(outs))
     ]
 
     def body(*refs):
@@ -443,50 +475,45 @@
 
     called = pl.pallas_call(
         body,
-        out_shape=tuple(
-            (pltpu.HBM if n in far_outs else pltpu.VMEM)(shape, dtype) for n, (shape, dtype) in enumerate(outs)
-        ),
-        in_specs=specs,
-        out_specs=tuple(IN_HBM if n in far_outs else IN_VMEM for n in range(len(outs))),
+        out_shape=tuple(space(shape, dtype) for space, (shape, dtype) in zip(out_spaces, outs)),
+        in_specs=[pl.BlockSpec(memory_space=space) for space in spaces],
+        out_specs=tuple(pl.BlockSpec(memory_space=space) for space in out_spaces),
         scratch_shapes=list(scratch),
         input_output_aliases=dict(aliases),
         compiler_params=pltpu.CompilerParams(vmem_limit_bytes=8 * 2**20),
-        cost_estimate=pl.CostEstimate(flops=1, bytes_accessed=1, transcendentals=0),
+        cost_estimate=pl.CostEstimate(flops=cost, bytes_accessed=1, transcendentals=0),
         name=name,
     )
-    return called(*args)
-
-
-def coarse_blocks_call(coupling, diagonal, inverse, after):
+    return called(*(pltpu.with_memory_space_constraint(x, space) for x, space in zip(args, spaces)))
+
+
+def near_blocks_call(coupling, after):
     cells, species = coupling.shape[:2]
     part = cells // 8
     return pl.pallas_call(
-        coarse_blocks_kernel,
+        near_blocks_kernel,
         grid=(cells // part,),
-        out_shape=pltpu.VMEM((cells, species, 10 * species), BF16),
-        in_specs=[
-            pl.BlockSpec((part,) + coupling.shape[1:], lambda n: (n, 0, 0, 0)),
-            pl.BlockSpec((part,) + diagonal.shape[1:], lambda n: (n, 0, 0)),
-            pl.BlockSpec((part,) + inverse.shape[1:], lambda n: (n, 0, 0)),
-            IN_VMEM,
-        ],
+        out_shape=pltpu.VMEM((cells, species, 8 * species), BF16),
+        in_specs=[pl.BlockSpec((part,) + coupling.shape[1:], lambda n: (n, 0, 0, 0)), IN_VMEM],
         out_specs=IN_VMEM,
         compiler_params=pltpu.CompilerParams(vmem_limit_bytes=8 * 2**20),
         cost_estimate=pl.CostEstimate(flops=1, bytes_accessed=1, transcendentals=0),
-        name="coarse_blocks",
-    )(coupling, diagonal, inverse, pltpu.with_memory_space_constraint(after, pltpu.VMEM))
-
-
-def coarse_places(pattern):
-    blocks_across = lax.axis_size("gy")
-    pattern = pattern.T
+        name="near_blocks",
+    )(coupling, pltpu.with_memory_space_constraint(after, pltpu.VMEM))
+
+
+def places_kernel(across, pattern, places, made, sem):
+    number = pattern[...]
     per_block = COARSE_X * BLOCK_Y
-    owner = pattern // per_block
-    inside = pattern % per_block
-    row = owner // blocks_across * COARSE_X + inside // BLOCK_Y - lax.axis_index("gx") * COARSE_X
-    col = owner % blocks_across * BLOCK_Y + inside % BLOCK_Y - lax.axis_index("gy") * BLOCK_Y
+    owner = lax.div(number, per_block)
+    inside = lax.rem(number, per_block)
+    row = lax.div(owner, across) * COARSE_X + lax.div(inside, BLOCK_Y) - lax.axis_index("gx") * COARSE_X
+    col = lax.rem(owner, across) * BLOCK_Y + lax.rem(inside, BLOCK_Y) - lax.axis_index("gy") * BLOCK_Y
     rho = jnp.where(row_parity() == 0, row, COARSE_X - 1 - row)
-    return (rho + 1) * WIDE + col + 1
+    made[...] = (rho + 1) * WIDE + col + 1
+    copy = pltpu.make_async_copy(made, places, sem)
+    copy.start()
+    copy.wait()
 
 
 def on_device(
@@ -530,7 +557,7 @@
     coupling = jnp.transpose(fine_coupling, (1, 2, 3, 0)).reshape(species, 4 * species, cells)
     diagonal = jnp.transpose(fine_diagonal, (1, 2, 0))
     inverse = jnp.transpose(fine_inverse, (1, 2, 0))
-    places = coarse_places(coarse_pattern)
+    pattern = coarse_pattern.T
     middle, ends = len(MIDDLE), len(ENDS)
 
     blocks, grid, side, far_m, far_n = run(
@@ -538,7 +565,7 @@
         start_kernel,
         [fine_blocks, padded(BLOCK_X), field(cells), field(middle), field(ends)],
         [right_side, inverse],
-        far_args=(0, 1),
+        hbm=(0, 1),
         scratch=[pltpu.VMEM(inverse.shape, BF16), pltpu.SemaphoreType.DMA((2 + BLOCK_X,))],
     )
     far_m, far_n = far(far_m), far(far_n)
@@ -558,158 +585,179 @@
         [(3, 0)],
         after=[near_s],
     )
+    state = [padded(BLOCK_X), field(cells), padded(BLOCK_X), field(cells)]
+    grid, side, change, iterate, far_m = run(
+        "fine_middle",
+        functools.partial(fine_middle_kernel, MIDDLE),
+        state + [field(middle)],
+        [blocks, far_m, grid, side],
+        [(2, 0), (3, 1)],
+        hbm_outs=(3,),
+        scratch=row_scratch(middle),
+        after=[even_h, odd_h],
+        cost=LONG,
+    )
+    far_m = far(far_m)
     grid, side, change, iterate, near_s = run(
         "fine_inner",
         fine_inner_kernel,
-        [padded(BLOCK_X), field(cells), padded(BLOCK_X), field(cells), field(BLOCK_Y)],
-        [blocks, near_h, even_h, odd_h, grid, side],
-        [(4, 0), (5, 1)],
-        far_outs=(3,),
+        state + [field(BLOCK_Y)],
+        [blocks, near_h, even_h, odd_h, grid, side, change, iterate],
+        [(4, 0), (5, 1), (6, 2), (7, 3)],
+        hbm=(7,),
+        hbm_outs=(3,),
         scratch=row_scratch((BLOCK_X - 1) * BLOCK_Y),
     )
     near_h = near(near_s)
-    coarse_blocks = coarse_blocks_call(coarse_coupling, coarse_diagonal, coarse_inverse, near_s)
-    state = [padded(BLOCK_X), field(cells), padded(BLOCK_X), field(cells)]
-    same = [(2, 0), (3, 1), (4, 2), (5, 3)]
-    grid, side, change, iterate, far_m = run(
-        "fine_middle",
-        functools.partial(fine_outer_kernel, MIDDLE, False),
-        state + [field(middle)],
-        [blocks, far_m, grid, side, change, iterate],
-        same,
-        far_args=(5,),
-        far_outs=(3,),
-        scratch=row_scratch(middle),
-        after=[coarse_blocks],
-    )
-    far_m = far(far_m)
     grid, side, change, fine_iterate, far_n, even_s, odd_s = run(
         "fine_ends",
-        functools.partial(fine_outer_kernel, ENDS, True),
+        functools.partial(fine_ends_kernel, ENDS),
         state + [field(ends), field(BLOCK_X), field(BLOCK_X)],
         [blocks, far_n, grid, side, change, iterate],
-        same,
-        far_args=(5,),
-        far_outs=(3,),
+        [(2, 0), (3, 1), (4, 2), (5, 3)],
+        hbm=(5,),
+        hbm_outs=(3,),
         scratch=row_scratch(ends),
+    )
+    (own_blocks,) = run(
+        "own_blocks",
+        own_blocks_kernel,
+        [((coarse_cells, species, 2 * species), BF16)],
+        [coarse_diagonal, coarse_inverse],
+        after=[far_n],
     )
     far_n = far(far_n)
     even_h, odd_h = even(even_s), odd(odd_s)
 
     state = [padded(BLOCK_X), field(coarse_cells), padded(COARSE_X)]
+    change, coarse_side, coarse_grid, far_m = run(
+        "left_middle",
+        functools.partial(left_middle_kernel, MIDDLE),
+        state + [field(middle)],
+        [blocks, side, own_blocks, far_m, change],
+        [(4, 0)],
+        after=[even_h, odd_h],
+        cost=LONG,
+    )
+    far_m = far(far_m)
     change, coarse_side, coarse_grid = run(
         "left_inner",
         left_inner_kernel,
         state,
-        [blocks, side, coarse_blocks, near_h, even_h, odd_h, change],
-        [(6, 0)],
-    )
-    same = [(4, 0), (5, 1), (6, 2)]
-    change, coarse_side, coarse_grid, far_m = run(
-        "left_middle",
-        functools.partial(left_outer_kernel, MIDDLE, False),
-        state + [field(middle)],
-        [blocks, side, coarse_blocks, far_m, change, coarse_side, coarse_grid],
-        same,
-    )
-    far_m = far(far_m)
-    change, coarse_side, coarse_grid, even_s, odd_s = run(
+        [blocks, side, own_blocks, near_h, even_h, odd_h, change, coarse_side, coarse_grid],
+        [(6, 0), (7, 1), (8, 2)],
+    )
+    change, coarse_side, coarse_grid, far_n, even_s, odd_s = run(
         "left_ends",
-        functools.partial(left_outer_kernel, ENDS, True),
-        state + [field(COARSE_X), field(COARSE_X)],
-        [blocks, side, coarse_blocks, far_n, change, coarse_side, coarse_grid],
-        same,
-    )
+        functools.partial(left_ends_kernel, ENDS),
+        state + [field(ends), field(COARSE_X), field(COARSE_X)],
+        [blocks, side, own_blocks, far_n, change, coarse_side, coarse_grid],
+        [(4, 0), (5, 1), (6, 2)],
+    )
+    near_blocks = near_blocks_call(coarse_coupling, far_n)
+    (places,) = run(
+        "places",
+        functools.partial(places_kernel, cols),
+        [(pattern.shape, jnp.int32)],
+        [pattern],
+        smem_outs=(0,),
+        scratch=[pltpu.VMEM(pattern.shape, jnp.int32), pltpu.SemaphoreType.DMA],
+        after=[near_blocks],
+    )
+    far_n = far(far_n)
     even_h, odd_h = even(even_s), odd(odd_s)
-    coarse_grid, far_n, near_s = run(
+    coarse_grid, corners, near_s = run(
         "pack_first",
-        functools.partial(pack_kernel, ENDS),
-        [padded(COARSE_X), field(ends + 2), field(BLOCK_Y + 2)],
+        pack_kernel,
+        [padded(COARSE_X), field(2), field(BLOCK_Y + 2)],
         [even_h, odd_h, coarse_grid],
         [(2, 0)],
-    )
-    far_n, near_h = far(far_n), near(near_s)
+        after=[near_blocks],
+    )
+    corners, near_h = far(corners), near(near_s)
 
     state = [padded(COARSE_X), field(coarse_cells), padded(COARSE_X), field(coarse_cells)]
+    inner = MIDDLE[1:-1]
+    outer = tuple(q for q in range(BLOCK_Y) if q not in inner)
+    coarse_grid, coarse_side, coarse_change, iterate, far_m = run(
+        "coarse_middle",
+        functools.partial(coarse_middle_kernel, MIDDLE, inner),
+        state + [field(len(inner))],
+        [places, near_blocks, own_blocks, far_m, coarse_grid, coarse_side],
+        [(4, 0), (5, 1)],
+        smem=(0,),
+        hbm_outs=(3,),
+        scratch=row_scratch(len(inner)),
+        cost=LONG,
+    )
+    far_m = far(far_m)
     coarse_grid, coarse_side, coarse_change, iterate = run(
         "coarse_inner",
         coarse_inner_kernel,
         state,
-        [places, coarse_blocks, near_h, coarse_grid, coarse_side],
-        [(3, 0), (4, 1)],
-        scalars=(0,),
-        far_outs=(3,),
+        [places, near_blocks, own_blocks, near_h, coarse_grid, coarse_side, coarse_change, iterate],
+        [(4, 0), (5, 1), (6, 2), (7, 3)],
+        smem=(0,),
+        hbm=(7,),
+        hbm_outs=(3,),
         scratch=row_scratch((COARSE_X - 1) * BLOCK_Y),
     )
-    inner = MIDDLE[1:-1]
-    outer = tuple(q for q in range(BLOCK_Y) if q not in inner)
-    same = [(3, 0), (4, 1), (5, 2), (6, 3)]
-    coarse_grid, coarse_side, coarse_change, iterate, far_m = run(
-        "coarse_middle",
-        functools.partial(coarse_outer_kernel, MIDDLE, inner, False),
-        state + [field(len(inner))],
-        [places, coarse_blocks, far_m, coarse_grid, coarse_side, coarse_change, iterate],
-        same,
-        scalars=(0,),
-        far_args=(6,),
-        far_outs=(3,),
-        scratch=row_scratch(len(inner)),
-    )
-    far_m = far(far_m)
-    coarse_grid, coarse_side, coarse_change, coarse_iterate, even_s, odd_s = run(
+    coarse_grid, coarse_side, coarse_change, coarse_iterate, far_n, even_s, odd_s = run(
         "coarse_ends",
-        functools.partial(coarse_outer_kernel, ENDS + (-1, BLOCK_Y), outer, True),
-        state + [field(COARSE_X), field(COARSE_X)],
-        [places, coarse_blocks, far_n, coarse_grid, coarse_side, coarse_change, iterate],
-        same,
-        scalars=(0,),
-        far_args=(6,),
-        far_outs=(3,),
+        functools.partial(coarse_ends_kernel, ENDS, outer),
+        state + [field(len(outer)), field(COARSE_X), field(COARSE_X)],
+        [places, near_blocks, own_blocks, far_n, corners, coarse_grid, coarse_side, coarse_change, iterate],
+        [(5, 0), (6, 1), (7, 2), (8, 3)],
+        smem=(0,),
+        hbm=(8,),
+        hbm_outs=(3,),
         scratch=row_scratch(len(outer)),
     )
+    far_n = far(far_n)
     even_h, odd_h = even(even_s), odd(odd_s)
-    coarse_change, far_n, near_s = run(
+    coarse_change, corners, near_s = run(
         "pack_second",
-        functools.partial(pack_kernel, outer),
-        [padded(COARSE_X), field(len(outer) + 2), field(BLOCK_Y + 2)],
+        pack_kernel,
+        [padded(COARSE_X), field(2), field(BLOCK_Y + 2)],
         [even_h, odd_h, coarse_change],
         [(2, 0)],
     )
-    far_n, near_h = far(far_n), near(near_s)
+    corners, near_h = far(corners), near(near_s)
 
     state = [padded(COARSE_X), field(coarse_cells // 2)]
+    core = inner[1:-1]
+    rest = tuple(q for q in range(BLOCK_Y) if q not in core)
+    coarse_change, next_side = run(
+        "last_middle",
+        functools.partial(last_middle_kernel, inner, core),
+        state,
+        [places, near_blocks, own_blocks, coarse_side, far_m, coarse_change],
+        [(5, 0)],
+        smem=(0,),
+        hbm_outs=(1,),
+        scratch=row_scratch(len(core) // 2),
+        cost=LONG,
+    )
     coarse_change, next_side = run(
         "last_inner",
         last_inner_kernel,
         state,
-        [places, coarse_blocks, coarse_side, near_h, coarse_change],
-        [(4, 0)],
-        scalars=(0,),
-        far_outs=(1,),
+        [places, near_blocks, own_blocks, coarse_side, near_h, coarse_change, next_side],
+        [(5, 0), (6, 1)],
+        smem=(0,),
+        hbm=(6,),
+        hbm_outs=(1,),
         scratch=row_scratch((COARSE_X - 1) * BLOCK_Y // 2),
-    )
-    core = inner[1:-1]
-    rest = tuple(q for q in range(BLOCK_Y) if q not in core)
-    coarse_change, next_side = run(
-        "last_middle",
-        functools.partial(last_outer_kernel, inner, core),
-        state,
-        [places, coarse_blocks, coarse_side, far_m, coarse_change, next_side],
-        [(4, 0), (5, 1)],
-        scalars=(0,),
-        far_args=(5,),
-        far_outs=(1,),
-        scratch=row_scratch(len(core) // 2),
     )
     coarse_change, next_side = run(
         "last_ends",
-        functools.partial(last_outer_kernel, outer + (-1, BLOCK_Y), rest),
+        functools.partial(last_ends_kernel, outer, rest),
         state,
-        [places, coarse_blocks, coarse_side, far_n, coarse_change, next_side],
-        [(4, 0), (5, 1)],
-        scalars=(0,),
-        far_args=(5,),
-        far_outs=(1,),
+        [places, near_blocks, own_blocks, coarse_side, far_n, corners, coarse_change, next_side],
+        [(6, 0), (7, 1)],
+        smem=(0,),
+        hbm=(7,),
+        hbm_outs=(1,),
         scratch=row_scratch(len(rest) // 2),
     )
     return (fine_iterate, coarse_iterate, next_side)

time: 117 us -> 78.6 us (0.67)
  waiting for transfers between devices: 27.1 us -> 8.33 us
  local copies, waits for them, and re-layouts: 13 us -> 0.03 us
  Pallas kernels: 46.4 us -> 40 us
    unnamed x36 -> x16, local copies, waits for them, and re-layouts: 13 us -> 0.03 us
    ppermute x8 -> x10, waiting for transfers between devices: 16.5 us -> 3.92 us  [far(): return lax.ppermute(x, BOTH, far_pairs)]
    ppermute x8 -> x10, starting transfers between devices: 14.3 us -> 25.1 us  [far(): return lax.ppermute(x, BOTH, far_pairs)]
    ppermute x4, starting transfers between devices: 14.3 us -> 3.75 us  [even(): return lax.ppermute(x, BOTH, even_pairs)]
    ppermute x4, waiting for transfers between devices: 10.6 us -> 3.17 us  [even(): return lax.ppermute(x, BOTH, even_pairs)]
    pallas_call x18 -> x20, Pallas kernels: 46.4 us -> 40 us  [the longest x19 36.8 us: run(): called(*(pltpu.with_memory_space_constraint(x, space) for x, space in zip...]
    ppermute x4, waiting for transfers between devices: 0.01 us -> 1.22 us  [near(): return lax.ppermute(x, BOTH, near_pairs)]
  transfers between devices with their start and end apart: 20 -> 22, of which waited for: 7 -> 6; matrix products, arithmetic and copies ran while one was open for 0% -> 0% of each run, Pallas kernels for 29% -> 45%
where the time goes in v2:
time: 78.6 us; the launch traced here: 78.4 us
  Pallas kernels  40 us (51%)
  starting transfers between devices  29 us (37%)
  waiting for transfers between devices  8.33 us (11%)
  between operations  1.06 us (1%)
    pallas_call x19, Pallas kernels, run(): called(*(pltpu.with_memory_space_constraint(x, space) for x, space in zip...  36.8 us
    ppermute x10, starting transfers between devices, far(): return lax.ppermute(x, BOTH, far_pairs)  25.1 us
    ppermute x10, waiting for transfers between devices, far(): return lax.ppermute(x, BOTH, far_pairs)  3.92 us
    ppermute x4, starting transfers between devices, even(): return lax.ppermute(x, BOTH, even_pairs)  3.75 us
    pallas_call x1, Pallas kernels, near_blocks_call(): pl.pallas_call(near_blocks_kernel, grid=(cells // part,), out_shape=pltpu...  3.22 us
    ppermute x4, waiting for transfers between devices, even(): return lax.ppermute(x, BOTH, even_pairs)  3.17 us
  transfers between devices with their start and end apart: 22, of which 6 were waited for; matrix products, arithmetic and copies ran while one was open for 0% of the time, Pallas kernels for 45%

profile of v2, /device:TPU:0, one launch (start us, length us, event | category | flops | bytes accessed | tf_op | source)
XLA Modules:
  0.0 78.4 jit_solution(12570966963866547618)
XLA Ops:
  0.6 2.6 %start.1 = (bf16[128,64,384]{2,1,0:T(8,128)(2,1)S(1)}, bf16[204,64,256]{2,1,0:T(8,128)(2,1)S(1)}, f32[128,64,128]{2,1,0:T(8,128)S(1)}, f32[16,64,128]{2,1,0:T(8,128)S(1)}, f32[16,64,128]{2,1,0:T(8,128)S(1)}) custom-call(f32[128,64,128]{2,1,0:T(8,128)} %refs_0_.2, bf16[64,64,128]{2,1,0:T(8,128)(2,1)} %bitcast.9), custom_call_target="tpu_custom_call" | custom-call | flops 1 | bytes 1 | tf_op jit(solution)/shard_map/start/pallas_call | solution.py:487
  3.2 3.1 %collective-permute-start.4 = (f32[16,64,128]{2,1,0:T(8,128)S(1)}, f32[16,64,128]{2,1,0:T(8,128)S(1)}, u32[]{:S(2)}, u32[]{:S(2)}) collective-permute-start(f32[16,64,128]{2,1,0:T(8,128)S(1)} %get-tuple-element.73), channel_id=1, source_target_pairs={{0,2},{1,3},{2,0},{3,1},{4,6},{5,7},{6,4},{7,5},{8,16},{9,17},{10,... | collective-permute-start | bytes 1572872 | tf_op jit(solution)/shard_map/ppermute | solution.py:536
  6.3 2.0 %first.1 = (bf16[204,64,256]{2,1,0:T(8,128)(2,1)S(1)}, f32[32,64,128]{2,1,0:T(8,128)S(1)}, f32[4,64,128]{2,1,0:T(8,128)S(1)}, f32[4,64,128]{2,1,0:T(8,128)S(1)}) custom-call(f32[128,64,128]{2,1,0:T(8,128)S(1)} %get-tuple-element.67.refs_0_.refs_3_, bf16[128,64,384]{2,1,0:T(8,128)(2,1)S(1)} %get-tuple-element.66.refs_1_.refs_3_, ...), custom_call_target="tpu_custom_call", output_to_operand_aliasing={{0}: (2, {})} | custom-call | flops 1 | bytes 1 | tf_op jit(solution)/shard_map/first/pallas_call | solution.py:487
  8.3 1.6 %collective-permute-start.2 = (f32[4,64,128]{2,1,0:T(8,128)S(1)}, f32[4,64,128]{2,1,0:T(8,128)S(1)}, u32[]{:S(2)}, u32[]{:S(2)}) collective-permute-start(f32[4,64,128]{2,1,0:T(8,128)S(1)} %get-tuple-element.71), channel_id=1, source_target_pairs={{0,1},{1,0},{2,3},{3,2},{4,5},{5,4},{6,7},{7,6},{8,9},{9,8},{10,11... | collective-permute-start | bytes 393224 | tf_op jit(solution)/shard_map/ppermute | solution.py:542
  9.8 0.0 collective-permute-start.3
  9.8 2.0 %collective-permute-start = (f32[16,64,128]{2,1,0:T(8,128)S(1)}, f32[16,64,128]{2,1,0:T(8,128)S(1)}, u32[]{:S(2)}, u32[]{:S(2)}) collective-permute-start(f32[16,64,128]{2,1,0:T(8,128)S(1)} %get-tuple-element.70), channel_id=1, source_target_pairs={{0,2},{1,3},{2,0},{3,1},{4,6},{5,7},{6,4},{7,5},{8,16},{9,17},{10,... | collective-permute-start | bytes 1572872 | tf_op jit(solution)/shard_map/ppermute | solution.py:536
  11.8 0.0 collective-permute-start.1
  11.8 2.5 %fine_blocks.1.refs_0_ = bf16[128,64,384]{2,1,0:T(8,128)(2,1)S(1)} custom-call(bf16[64,256,128]{2,1,0:T(8,128)(2,1)S(1)} %bitcast.8, bf16[64,64,128]{2,1,0:T(8,128)(2,1)S(1)} %bitcast.11, bf16[64,64,128]{2,1,0:T(8,128)(2,1)S(1)} %bitcast.10, bf16[128,64,384]{2,1,0:T(8,128)(2,1)S(1)} %get-tuple-element.66.refs_1_.refs_3_, ...), custom_call_target="tpu_custom_call", output_to_operand_aliasing={{}: (3, {})} | custom-call | flops 1 | bytes 1 | tf_op jit(solution)/shard_map/fine_blocks/pallas_call | solution.py:487
  14.4 1.3 %collective-permute-done.2.refs_4_.refs_2_ = f32[4,64,128]{2,1,0:T(8,128)S(1)} collective-permute-done((f32[4,64,128]{2,1,0:T(8,128)S(1)}, f32[4,64,128]{2,1,0:T(8,128)S(1)}, u32[]{:S(2)}, u32[]{:S(2)}) %collective-permute-start.2) | collective-permute-done | bytes 131104 | tf_op jit(solution)/shard_map/ppermute | solution.py:542
  15.6 0.0 collective-permute-done.3.refs_5_.refs_3_
  15.6 0.0 collective-permute-done.4.refs_1_
  15.6 1.7 %fine_middle.1 = (bf16[204,64,256]{2,1,0:T(8,128)(2,1)S(1)}, f32[128,64,128]{2,1,0:T(8,128)S(1)}, bf16[204,64,256]{2,1,0:T(8,128)(2,1)S(1)}, f32[128,64,128]{2,1,0:T(8,128)}, f32[16,64,128]{2,1,0:T(8,128)S(1)}) custom-call(bf16[128,64,384]{2,1,0:T(8,128)(2,1)S(1)} %fine_blocks.1.refs_0_, ...), custom_call_target="tpu_custom_call", output_to_operand_aliasing={{0}: (2, {}), {1}: (3, {})} | custom-call | flops 99999997952 | bytes 1 | tf_op jit(solution)/shard_map/fine_middle/pallas_call | solution.py:487
  17.3 3.6 %collective-permute-start.9 = (f32[16,64,128]{2,1,0:T(8,128)S(1)}, f32[16,64,128]{2,1,0:T(8,128)S(1)}, u32[]{:S(2)}, u32[]{:S(2)}) collective-permute-start(f32[16,64,128]{2,1,0:T(8,128)S(1)} %get-tuple-element.89), channel_id=1, source_target_pairs={{0,2},{1,3},{2,0},{3,1},{4,6},{5,7},{6,4},{7,5},{8,16},{9,17},{10,... | collective-permute-start | bytes 1572872 | tf_op jit(solution)/shard_map/ppermute | solution.py:536
  20.9 0.0 collective-permute-done.1.refs_1_
  21.0 6.0 %fine_inner.1 = (bf16[204,64,256]{2,1,0:T(8,128)(2,1)S(1)}, f32[128,64,128]{2,1,0:T(8,128)S(1)}, bf16[204,64,256]{2,1,0:T(8,128)(2,1)S(1)}, f32[128,64,128]{2,1,0:T(8,128)}, f32[32,64,128]{2,1,0:T(8,128)S(1)}) custom-call(bf16[128,64,384]{2,1,0:T(8,128)(2,1)S(1)} %fine_blocks.1.refs_0_, ...), custom_call_target="tpu_custom_call", output_to_operand_aliasing={{0}: (4, {}), {1}: (5, {}), {2}: (6, {}), {3}: (7, {})} | custom-call | flops 1 | bytes 1 | tf_op jit(solution)/shard_map/fine_inner/pallas_call | solution.py:487
  26.9 0.0 collective-permute-done.refs_1_
  26.9 0.0 copy-start.3
  26.9 0.0 copy-start.4
  27.0 1.7 %fine_ends.1 = (bf16[204,64,256]{2,1,0:T(8,128)(2,1)S(1)}, f32[128,64,128]{2,1,0:T(8,128)S(1)}, bf16[204,64,256]{2,1,0:T(8,128)(2,1)S(1)}, f32[128,64,128]{2,1,0...) custom-call(bf16[128,64,384]{2,1,0:T(8,128)(2,1)S(1)} %fine_blocks.1, ...), custom_call_target="tpu_custom_call", output_to_operand_aliasing={{0}: (2, {}), {1}: (3, {}), {2}: (4, {}), {3}: (5, {})} | custom-call | flops 1 | bytes 1 | tf_op jit(solution)/shard_map/fine_ends/pallas_call | solution.py:487
  28.7 0.1 collective-permute-start.7
  28.8 0.0 collective-permute-start.8
  28.8 3.4 %collective-permute-start.5 = (f32[16,64,128]{2,1,0:T(8,128)S(1)}, f32[16,64,128]{2,1,0:T(8,128)S(1)}, u32[]{:S(2)}, u32[]{:S(2)}) collective-permute-start(f32[16,64,128]{2,1,0:T(8,128)S(1)} %get-tuple-element.85.refs_2_), channel_id=1, source_target_pairs={{0,2},{1,3},{2,0},{3,1},{4,6},{5,7},{6,4},{7,5},{8,16},{9,17},{10,... | collective-permute-start | bytes 1572872 | tf_op jit(solution)/shard_map/ppermute | solution.py:536
  32.2 0.0 collective-permute-start.6
  32.2 0.3 own_blocks.1.refs_2_
  32.6 0.0 collective-permute-done.9.refs_3_
  32.6 1.1 %collective-permute-done.7.refs_5_.refs_4_ = f32[4,64,128]{2,1,0:T(8,128)S(1)} collective-permute-done((f32[4,64,128]{2,1,0:T(8,128)S(1)}, f32[4,64,128]{2,1,0:T(8,128)S(1)}, u32[]{:S(2)}, u32[]{:S(2)}) %collective-permute-start.7) | collective-permute-done | bytes 131104 | tf_op jit(solution)/shard_map/ppermute | solution.py:542
  33.7 0.0 collective-permute-done.8.refs_6_.refs_5_
  33.7 1.2 %left_middle.1 = (bf16[204,64,256]{2,1,0:T(8,128)(2,1)S(1)}, f32[64,64,128]{2,1,0:T(8,128)S(1)}, bf16[136,64,256]{2,1,0:T(8,128)(2,1)S(1)}, f32[16,64,128]{2,1,0:T(8,128)S(1)}) custom-call(bf16[128,64,384]{2,1,0:T(8,128)(2,1)S(1)} %fine_blocks.1.refs_0_, f32[128,64,128]{2,1,0:T(8,128)S(1)} %get-tuple-element.84.refs_1_, ...), custom_call_target="tpu_custom_call", output_to_operand_aliasing={{0}: (4, {})} | custom-call | flops 99999997952 | bytes 1 | tf_op jit(solution)/shard_map/left_middle/pallas_call | solution.py:487
  34.9 3.0 %collective-permute-start.15 = (f32[16,64,128]{2,1,0:T(8,128)S(1)}, f32[16,64,128]{2,1,0:T(8,128)S(1)}, u32[]{:S(2)}, u32[]{:S(2)}) collective-permute-start(f32[16,64,128]{2,1,0:T(8,128)S(1)} %get-tuple-element.103), channel_id=1, source_target_pairs={{0,2},{1,3},{2,0},{3,1},{4,6},{5,7},{6,4},{7,5},{8,16},{9,17},{10,... | collective-permute-start | bytes 1572872 | tf_op jit(solution)/shard_map/ppermute | solution.py:536
  37.9 0.0 collective-permute-done.6.refs_3_
  37.9 2.9 %left_inner.1 = (bf16[204,64,256]{2,1,0:T(8,128)(2,1)S(1)}, f32[64,64,128]{2,1,0:T(8,128)S(1)}, bf16[136,64,256]{2,1,0:T(8,128)(2,1)S(1)}) custom-call(bf16[128,64,384]{2,1,0:T(8,128)(2,1)S(1)} %fine_blocks.1.refs_0_, f32[128,64,128]{2,1,0:T(8,128)S(1)} %get-tuple-element.84.refs_1_, ...), custom_call_target="tpu_custom_call", output_to_operand_aliasing={{0}: (6, {}), {1}: (7, {}), {2}: (8, {})} | custom-call | flops 1 | bytes 1 | tf_op jit(solution)/shard_map/left_inner/pallas_call | solution.py:487
  40.8 0.1 collective-permute-done.5.refs_3_
  40.8 1.2 %left_ends.1 = (bf16[204,64,256]{2,1,0:T(8,128)(2,1)S(1)}, f32[64,64,128]{2,1,0:T(8,128)S(1)}, bf16[136,64,256]{2,1,0:T(8,128)(2,1)S(1)}, f32[16,64,128]{2,1,0:T...) custom-call(bf16[128,64,384]{2,1,0:T(8,128)(2,1)S(1)} %fine_blocks.1, ...), custom_call_target="tpu_custom_call", output_to_operand_aliasing={{0}: (4, {}), {1}: (5, {}), {2}: (6, {})} | custom-call | flops 1 | bytes 1 | tf_op jit(solution)/shard_map/left_ends/pallas_call | solution.py:487
  42.0 0.7 collective-permute-start.11
  42.7 0.0 collective-permute-start.12
  42.7 2.9 %collective-permute-start.10 = (f32[16,64,128]{2,1,0:T(8,128)S(1)}, f32[16,64,128]{2,1,0:T(8,128)S(1)}, u32[]{:S(2)}, u32[]{:S(2)}) collective-permute-start(f32[16,64,128]{2,1,0:T(8,128)S(1)} %get-tuple-element.97.after), channel_id=1, source_target_pairs={{0,2},{1,3},{2,0},{3,1},{4,6},{5,7},{6,4},{7,5},{8,16},{9,17},{10,... | collective-permute-start | bytes 1572872 | tf_op jit(solution)/shard_map/ppermute | solution.py:536
  45.6 3.2 %near_blocks.1.refs_1_.refs_3_ = bf16[64,64,512]{2,1,0:T(8,128)(2,1)S(1)} custom-call(bf16[64,64,8,64]{3,2,1,0:T(8,128)(2,1)S(1)} %bitcast.7, f32[16,64,128]{2,1,0:T(8,128)S(1)} %get-tuple-element.97.after), custom_call_target="tpu_custom_call" | custom-call | flops 1 | bytes 1 | tf_op jit(solution)/shard_map/near_blocks/pallas_call | solution.py:493
  48.8 0.6 places.1.refs_0_
  49.5 0.0 collective-permute-done.11.refs_0_
  49.5 0.0 collective-permute-done.12.refs_1_
  49.5 0.2 pack_first.1
  49.7 0.1 collective-permute-start.14
  49.7 0.0 collective-permute-done.15.refs_3_
  49.7 1.9 %coarse_middle.1 = (bf16[136,64,256]{2,1,0:T(8,128)(2,1)S(1)}, f32[64,64,128]{2,1,0:T(8,128)S(1)}, bf16[136,64,256]{2,1,0:T(8,128)(2,1)S(1)}, f32[64,64,128]{2,1,0:T(8,128)}, f32[14,64,128]{2,1,0:T(8,128)S(1)}) custom-call(s32[8,64]{1,0:T(8,128)S(4)} %places.1.refs_0_, ...), custom_call_target="tpu_custom_call", output_to_operand_aliasing={{0}: (4, {}), {1}: (5, {})} | custom-call | flops 99999997952 | bytes 1 | tf_op jit(solution)/shard_map/coarse_middle/pallas_call | solution.py:487
  51.6 0.1 collective-permute-start.21
  51.7 2.0 %collective-permute-start.13 = (f32[2,64,128]{2,1,0:T(8,128)S(1)}, f32[2,64,128]{2,1,0:T(8,128)S(1)}, u32[]{:S(2)}, u32[]{:S(2)}) collective-permute-start(f32[2,64,128]{2,1,0:T(8,128)S(1)} %get-tuple-element.101), channel_id=1, source_target_pairs={{0,2},{1,3},{2,0},{3,1},{4,6},{5,7},{6,4},{7,5},{8,16},{9,17},{10,... | collective-permute-start | bytes 196616 | tf_op jit(solution)/shard_map/ppermute | solution.py:536
  53.7 0.0 collective-permute-done.14.refs_3_
  53.7 3.3 %coarse_inner.1 = (bf16[136,64,256]{2,1,0:T(8,128)(2,1)S(1)}, f32[64,64,128]{2,1,0:T(8,128)S(1)}, bf16[136,64,256]{2,1,0:T(8,128)(2,1)S(1)}, f32[64,64,128]{2,1,0:T(8,128)}) custom-call(s32[8,64]{1,0:T(8,128)S(4)} %places.1.refs_0_, ...), custom_call_target="tpu_custom_call", output_to_operand_aliasing={{0}: (4, {}), {1}: (5, {}), {2}: (6, {}), {3}: (7, {})} | custom-call | flops 1 | bytes 1 | tf_op jit(solution)/shard_map/coarse_inner/pallas_call | solution.py:487
  57.1 3.8 %collective-permute-done.13.refs_4_ = f32[2,64,128]{2,1,0:T(8,128)S(1)} collective-permute-done((f32[2,64,128]{2,1,0:T(8,128)S(1)}, f32[2,64,128]{2,1,0:T(8,128)S(1)}, u32[]{:S(2)}, u32[]{:S(2)}) %collective-permute-start.13) | collective-permute-done | bytes 65568 | tf_op jit(solution)/shard_map/ppermute | solution.py:536
  60.9 0.0 collective-permute-done.10.refs_3_
  60.9 2.2 %coarse_ends.1 = (bf16[136,64,256]{2,1,0:T(8,128)(2,1)S(1)}, f32[64,64,128]{2,1,0:T(8,128)S(1)}, bf16[136,64,256]{2,1,0:T(8,128)(2,1)S(1)}, f32[64,64,128]{2,1,0...) custom-call(s32[8,64]{1,0:T(8,128)S(4)} %places.1.refs_0_, ...), custom_call_target="tpu_custom_call", output_to_operand_aliasing={{0}: (5, {}), {1}: (6, {}), {2}: (7, {}), {3}: (8, {})} | custom-call | flops 1 | bytes 1 | tf_op jit(solution)/shard_map/coarse_ends/pallas_call | solution.py:487
  63.1 1.4 %collective-permute-start.17 = (f32[2,64,128]{2,1,0:T(8,128)S(1)}, f32[2,64,128]{2,1,0:T(8,128)S(1)}, u32[]{:S(2)}, u32[]{:S(2)}) collective-permute-start(f32[2,64,128]{2,1,0:T(8,128)S(1)} %get-tuple-element.117), channel_id=1, source_target_pairs={{0,1},{1,0},{2,3},{3,2},{4,5},{5,4},{6,7},{7,6},{8,9},{9,8},{10,11... | collective-permute-start | bytes 196616 | tf_op jit(solution)/shard_map/ppermute | solution.py:542
  64.5 0.0 collective-permute-start.18
  64.5 2.2 %collective-permute-start.16 = (f32[18,64,128]{2,1,0:T(8,128)S(1)}, f32[18,64,128]{2,1,0:T(8,128)S(1)}, u32[]{:S(2)}, u32[]{:S(2)}) collective-permute-start(f32[18,64,128]{2,1,0:T(8,128)S(1)} %get-tuple-element.116), channel_id=1, source_target_pairs={{0,2},{1,3},{2,0},{3,1},{4,6},{5,7},{6,4},{7,5},{8,16},{9,17},{10,... | collective-permute-start | bytes 1769480 | tf_op jit(solution)/shard_map/ppermute | solution.py:536
  66.7 0.8 collective-permute-done.17.refs_0_
  67.4 0.0 collective-permute-done.18.refs_1_
  67.4 0.2 pack_second.1
  67.6 2.9 %collective-permute-start.19 = (f32[2,64,128]{2,1,0:T(8,128)S(1)}, f32[2,64,128]{2,1,0:T(8,128)S(1)}, u32[]{:S(2)}, u32[]{:S(2)}) collective-permute-start(f32[2,64,128]{2,1,0:T(8,128)S(1)} %get-tuple-element.120), channel_id=1, source_target_pairs={{0,2},{1,3},{2,0},{3,1},{4,6},{5,7},{6,4},{7,5},{8,16},{9,17},{10,... | collective-permute-start | bytes 196616 | tf_op jit(solution)/shard_map/ppermute | solution.py:536
  70.5 0.0 collective-permute-done.21.refs_4_
  70.5 1.5 %last_middle.1 = (bf16[136,64,256]{2,1,0:T(8,128)(2,1)S(1)}, f32[32,64,128]{2,1,0:T(8,128)}) custom-call(s32[8,64]{1,0:T(8,128)S(4)} %places.1.refs_0_, bf16[64,64,512]{2,1,0:T(8,128)(2,1)S(1)} %near_blocks.1.refs_1_.refs_3_, bf16[64,64,128]{2,1,0:T(8,128)(2,1)S(1)} %own_blocks.1.refs_2_, ...), custom_call_target="tpu_custom_call", output_to_operand_aliasing={{0}: (5, {})} | custom-call | flops 99999997952 | bytes 1 | tf_op jit(solution)/shard_map/last_middle/pallas_call | solution.py:487
  72.1 1.2 %collective-permute-done.20.refs_4_ = f32[34,64,128]{2,1,0:T(8,128)S(1)} collective-permute-done((f32[34,64,128]{2,1,0:T(8,128)S(1)}, f32[34,64,128]{2,1,0:T(8,128)S(1)}, u32[]{:S(2)}, u32[]{:S(2)}) %collective-permute-start.20) | collective-permute-done | bytes 1114144 | tf_op jit(solution)/shard_map/ppermute | solution.py:539
  73.3 2.9 %last_inner.1 = (bf16[136,64,256]{2,1,0:T(8,128)(2,1)S(1)}, f32[32,64,128]{2,1,0:T(8,128)}) custom-call(s32[8,64]{1,0:T(8,128)S(4)} %places.1.refs_0_, bf16[64,64,512]{2,1,0:T(8,128)(2,1)S(1)} %near_blocks.1.refs_1_.refs_3_, bf16[64,64,128]{2,1,0:T(8,128)(2,1)S(1)} %own_blocks.1.refs_2_, ...), custom_call_target="tpu_custom_call", output_to_operand_aliasing={{0}: (5, {}), {1}: (6, {})} | custom-call | flops 1 | bytes 1 | tf_op jit(solution)/shard_map/last_inner/pallas_call | solution.py:487
  76.2 0.0 collective-permute-done.16.refs_4_
  76.2 2.1 %last_ends.1 = (bf16[136,64,256]{2,1,0:T(8,128)(2,1)S(1)}, f32[32,64,128]{2,1,0:T(8,128)}) custom-call(s32[8,64]{1,0:T(8,128)S(4)} %places.1.refs_0_, bf16[64,64,512]{2,1,0:T(8,128)(2,1)S(1)} %near_blocks.1.refs_1_.refs_3_, bf16[64,64,128]{2,1,0:T(8,128)(2,1)S(1)} %own_blocks.1.refs_2_, ...), custom_call_target="tpu_custom_call", output_to_operand_aliasing={{0}: (6, {}), {1}: (7, {})} | custom-call | flops 1 | bytes 1 | tf_op jit(solution)/shard_map/last_ends/pallas_call | solution.py:487
  (17 shorter events, 0.0 us)
Async XLA Ops:
  3.2 12.4 %collective-permute-start.4 = (f32[16,64,128]{2,1,0:T(8,128)S(1)}, f32[16,64,128]{2,1,0:T(8,128)S(1)}, u32[]{:S(2)}, u32[]{:S(2)}) collective-permute-start(f32[16,64,128]{2,1,0:T(8,128)S(1)} %get-tuple-element.73), channel_id=1, source_target_pairs={{0,2},{1,3},{2,0},{3,1},{4,6},{5,7},{6,4},{7,5},{8,16},{9,17},{10,... | collective-permute-start | bytes 1572872 | tf_op jit(solution)/shard_map/ppermute | solution.py:536
  6.3 5.5 %copy-start = (bf16[128,64,4,64]{0,3,2,1:T(8,128)(2,1)S(1)}, bf16[128,64,4,64]{0,3,2,1:T(8,128)(2,1)}, u32[]{:S(2)}) copy-start(bf16[128,64,4,64]{0,3,2,1:T(8,128)(2,1)} %param.9) | copy-start | bytes 12582916
  6.3 5.5 %copy-start.1 = (bf16[128,64,64]{0,2,1:T(8,128)(2,1)S(1)}, bf16[128,64,64]{0,2,1:T(8,128)(2,1)}, u32[]{:S(2)}) copy-start(bf16[128,64,64]{0,2,1:T(8,128)(2,1)} %param.11) | copy-start | bytes 3145732
  6.3 5.5 %copy-start.2 = (bf16[128,64,64]{0,2,1:T(8,128)(2,1)S(1)}, bf16[128,64,64]{0,2,1:T(8,128)(2,1)}, u32[]{:S(2)}) copy-start(bf16[128,64,64]{0,2,1:T(8,128)(2,1)} %param.10) | copy-start | bytes 3145732
  8.3 7.4 %collective-permute-start.2 = (f32[4,64,128]{2,1,0:T(8,128)S(1)}, f32[4,64,128]{2,1,0:T(8,128)S(1)}, u32[]{:S(2)}, u32[]{:S(2)}) collective-permute-start(f32[4,64,128]{2,1,0:T(8,128)S(1)} %get-tuple-element.71), channel_id=1, source_target_pairs={{0,1},{1,0},{2,3},{3,2},{4,5},{5,4},{6,7},{7,6},{8,9},{9,8},{10,11... | collective-permute-start | bytes 393224 | tf_op jit(solution)/shard_map/ppermute | solution.py:542
  9.8 5.8 %collective-permute-start.3 = (f32[4,64,128]{2,1,0:T(8,128)S(1)}, f32[4,64,128]{2,1,0:T(8,128)S(1)}, u32[]{:S(2)}, u32[]{:S(2)}) collective-permute-start(f32[4,64,128]{2,1,0:T(8,128)S(1)} %get-tuple-element.72), channel_id=1, source_target_pairs={{0,8},{1,2},{2,1},{3,4},{4,3},{5,6},{6,5},{7,15},{8,0},{9,10},{10,... | collective-permute-start | bytes 393224 | tf_op jit(solution)/shard_map/ppermute | solution.py:545
  9.8 17.1 %collective-permute-start = (f32[16,64,128]{2,1,0:T(8,128)S(1)}, f32[16,64,128]{2,1,0:T(8,128)S(1)}, u32[]{:S(2)}, u32[]{:S(2)}) collective-permute-start(f32[16,64,128]{2,1,0:T(8,128)S(1)} %get-tuple-element.70), channel_id=1, source_target_pairs={{0,2},{1,3},{2,0},{3,1},{4,6},{5,7},{6,4},{7,5},{8,16},{9,17},{10,... | collective-permute-start | bytes 1572872 | tf_op jit(solution)/shard_map/ppermute | solution.py:536
  11.8 9.1 %collective-permute-start.1 = (f32[32,64,128]{2,1,0:T(8,128)S(1)}, f32[32,64,128]{2,1,0:T(8,128)S(1)}, u32[]{:S(2)}, u32[]{:S(2)}) collective-permute-start(f32[32,64,128]{2,1,0:T(8,128)S(1)} %get-tuple-element.69.refs_4_), channel_id=1, source_target_pairs={{0,8},{1,9},{2,10},{3,11},{4,12},{5,13},{6,14},{7,15},{8,0},{9,1},... | collective-permute-start | bytes 3145736 | tf_op jit(solution)/shard_map/ppermute | solution.py:539
  17.3 15.2 %collective-permute-start.9 = (f32[16,64,128]{2,1,0:T(8,128)S(1)}, f32[16,64,128]{2,1,0:T(8,128)S(1)}, u32[]{:S(2)}, u32[]{:S(2)}) collective-permute-start(f32[16,64,128]{2,1,0:T(8,128)S(1)} %get-tuple-element.89), channel_id=1, source_target_pairs={{0,2},{1,3},{2,0},{3,1},{4,6},{5,7},{6,4},{7,5},{8,16},{9,17},{10,... | collective-permute-start | bytes 1572872 | tf_op jit(solution)/shard_map/ppermute | solution.py:536
  26.9 5.3 %copy-start.3 = (bf16[64,64,64]{2,1,0:T(8,128)(2,1)S(1)}, bf16[64,64,64]{2,1,0:T(8,128)(2,1)}, u32[]{:S(2)}) copy-start(bf16[64,64,64]{2,1,0:T(8,128)(2,1)} %refs_0_.3) | copy-start | bytes 1572868
  26.9 5.3 %copy-start.4 = (bf16[64,64,64]{2,1,0:T(8,128)(2,1)S(1)}, bf16[64,64,64]{2,1,0:T(8,128)(2,1)}, u32[]{:S(2)}) copy-start(bf16[64,64,64]{2,1,0:T(8,128)(2,1)} %refs_1_.1) | copy-start | bytes 1572868
  28.7 5.0 %collective-permute-start.7 = (f32[4,64,128]{2,1,0:T(8,128)S(1)}, f32[4,64,128]{2,1,0:T(8,128)S(1)}, u32[]{:S(2)}, u32[]{:S(2)}) collective-permute-start(f32[4,64,128]{2,1,0:T(8,128)S(1)} %get-tuple-element.87), channel_id=1, source_target_pairs={{0,1},{1,0},{2,3},{3,2},{4,5},{5,4},{6,7},{7,6},{8,9},{9,8},{10,11... | collective-permute-start | bytes 393224 | tf_op jit(solution)/shard_map/ppermute | solution.py:542
  28.8 4.9 %collective-permute-start.8 = (f32[4,64,128]{2,1,0:T(8,128)S(1)}, f32[4,64,128]{2,1,0:T(8,128)S(1)}, u32[]{:S(2)}, u32[]{:S(2)}) collective-permute-start(f32[4,64,128]{2,1,0:T(8,128)S(1)} %get-tuple-element.88), channel_id=1, source_target_pairs={{0,8},{1,2},{2,1},{3,4},{4,3},{5,6},{6,5},{7,15},{8,0},{9,10},{10,... | collective-permute-start | bytes 393224 | tf_op jit(solution)/shard_map/ppermute | solution.py:545
  28.8 12.0 %collective-permute-start.5 = (f32[16,64,128]{2,1,0:T(8,128)S(1)}, f32[16,64,128]{2,1,0:T(8,128)S(1)}, u32[]{:S(2)}, u32[]{:S(2)}) collective-permute-start(f32[16,64,128]{2,1,0:T(8,128)S(1)} %get-tuple-element.85.refs_2_), channel_id=1, source_target_pairs={{0,2},{1,3},{2,0},{3,1},{4,6},{5,7},{6,4},{7,5},{8,16},{9,17},{10,... | collective-permute-start | bytes 1572872 | tf_op jit(solution)/shard_map/ppermute | solution.py:536
  32.2 5.6 %collective-permute-start.6 = (f32[32,64,128]{2,1,0:T(8,128)S(1)}, f32[32,64,128]{2,1,0:T(8,128)S(1)}, u32[]{:S(2)}, u32[]{:S(2)}) collective-permute-start(f32[32,64,128]{2,1,0:T(8,128)S(1)} %get-tuple-element.86), channel_id=1, source_target_pairs={{0,8},{1,9},{2,10},{3,11},{4,12},{5,13},{6,14},{7,15},{8,0},{9,1},... | collective-permute-start | bytes 3145736 | tf_op jit(solution)/shard_map/ppermute | solution.py:539
  34.9 14.8 %collective-permute-start.15 = (f32[16,64,128]{2,1,0:T(8,128)S(1)}, f32[16,64,128]{2,1,0:T(8,128)S(1)}, u32[]{:S(2)}, u32[]{:S(2)}) collective-permute-start(f32[16,64,128]{2,1,0:T(8,128)S(1)} %get-tuple-element.103), channel_id=1, source_target_pairs={{0,2},{1,3},{2,0},{3,1},{4,6},{5,7},{6,4},{7,5},{8,16},{9,17},{10,... | collective-permute-start | bytes 1572872 | tf_op jit(solution)/shard_map/ppermute | solution.py:536
  40.8 4.8 %slice-start = ((s8[8388608]{0:T(1024)(128)(4,1)}), s8[4194304]{0:T(1024)(128)(4,1)S(1)}, s32[]{:S(2)}) async-start(s8[8388608]{0:T(1024)(128)(4,1)} %bitcast.6), calls=%async_computation | async-start | bytes 8388608
  40.8 4.8 %slice-start.1 = ((s8[8388608]{0:T(1024)(128)(4,1)}), s8[4194304]{0:T(1024)(128)(4,1)S(1)}, s32[]{:S(2)}) async-start(s8[8388608]{0:T(1024)(128)(4,1)} %bitcast.6), calls=%async_computation.1 | async-start | bytes 8388608
  42.0 7.4 %collective-permute-start.11 = (f32[2,64,128]{2,1,0:T(8,128)S(1)}, f32[2,64,128]{2,1,0:T(8,128)S(1)}, u32[]{:S(2)}, u32[]{:S(2)}) collective-permute-start(f32[2,64,128]{2,1,0:T(8,128)S(1)} %get-tuple-element.98), channel_id=1, source_target_pairs={{0,1},{1,0},{2,3},{3,2},{4,5},{5,4},{6,7},{7,6},{8,9},{9,8},{10,11... | collective-permute-start | bytes 196616 | tf_op jit(solution)/shard_map/ppermute | solution.py:542
  42.7 6.8 %collective-permute-start.12 = (f32[2,64,128]{2,1,0:T(8,128)S(1)}, f32[2,64,128]{2,1,0:T(8,128)S(1)}, u32[]{:S(2)}, u32[]{:S(2)}) collective-permute-start(f32[2,64,128]{2,1,0:T(8,128)S(1)} %get-tuple-element.99), channel_id=1, source_target_pairs={{0,8},{1,2},{2,1},{3,4},{4,3},{5,6},{6,5},{7,15},{8,0},{9,10},{10,... | collective-permute-start | bytes 196616 | tf_op jit(solution)/shard_map/ppermute | solution.py:545
  42.7 6.1 %copy-start.5 = (s32[64,8]{0,1:T(8,128)S(1)}, s32[64,8]{0,1:T(8,128)}, u32[]{:S(2)}) copy-start(s32[64,8]{0,1:T(8,128)} %param.15) | copy-start | bytes 6148
  42.7 18.2 %collective-permute-start.10 = (f32[16,64,128]{2,1,0:T(8,128)S(1)}, f32[16,64,128]{2,1,0:T(8,128)S(1)}, u32[]{:S(2)}, u32[]{:S(2)}) collective-permute-start(f32[16,64,128]{2,1,0:T(8,128)S(1)} %get-tuple-element.97.after), channel_id=1, source_target_pairs={{0,2},{1,3},{2,0},{3,1},{4,6},{5,7},{6,4},{7,5},{8,16},{9,17},{10,... | collective-permute-start | bytes 1572872 | tf_op jit(solution)/shard_map/ppermute | solution.py:536
  49.7 4.1 %collective-permute-start.14 = (f32[34,64,128]{2,1,0:T(8,128)S(1)}, f32[34,64,128]{2,1,0:T(8,128)S(1)}, u32[]{:S(2)}, u32[]{:S(2)}) collective-permute-start(f32[34,64,128]{2,1,0:T(8,128)S(1)} %get-tuple-element.102), channel_id=1, source_target_pairs={{0,8},{1,9},{2,10},{3,11},{4,12},{5,13},{6,14},{7,15},{8,0},{9,1},... | collective-permute-start | bytes 3342344 | tf_op jit(solution)/shard_map/ppermute | solution.py:539
  51.6 18.9 %collective-permute-start.21 = (f32[14,64,128]{2,1,0:T(8,128)S(1)}, f32[14,64,128]{2,1,0:T(8,128)S(1)}, u32[]{:S(2)}, u32[]{:S(2)}) collective-permute-start(f32[14,64,128]{2,1,0:T(8,128)S(1)} %get-tuple-element.122), channel_id=1, source_target_pairs={{0,2},{1,3},{2,0},{3,1},{4,6},{5,7},{6,4},{7,5},{8,16},{9,17},{10,... | collective-permute-start | bytes 1376264 | tf_op jit(solution)/shard_map/ppermute | solution.py:536
  51.7 9.2 %collective-permute-start.13 = (f32[2,64,128]{2,1,0:T(8,128)S(1)}, f32[2,64,128]{2,1,0:T(8,128)S(1)}, u32[]{:S(2)}, u32[]{:S(2)}) collective-permute-start(f32[2,64,128]{2,1,0:T(8,128)S(1)} %get-tuple-element.101), channel_id=1, source_target_pairs={{0,2},{1,3},{2,0},{3,1},{4,6},{5,7},{6,4},{7,5},{8,16},{9,17},{10,... | collective-permute-start | bytes 196616 | tf_op jit(solution)/shard_map/ppermute | solution.py:536
  63.1 4.3 %collective-permute-start.17 = (f32[2,64,128]{2,1,0:T(8,128)S(1)}, f32[2,64,128]{2,1,0:T(8,128)S(1)}, u32[]{:S(2)}, u32[]{:S(2)}) collective-permute-start(f32[2,64,128]{2,1,0:T(8,128)S(1)} %get-tuple-element.117), channel_id=1, source_target_pairs={{0,1},{1,0},{2,3},{3,2},{4,5},{5,4},{6,7},{7,6},{8,9},{9,8},{10,11... | collective-permute-start | bytes 196616 | tf_op jit(solution)/shard_map/ppermute | solution.py:542
  64.5 3.0 %collective-permute-start.18 = (f32[2,64,128]{2,1,0:T(8,128)S(1)}, f32[2,64,128]{2,1,0:T(8,128)S(1)}, u32[]{:S(2)}, u32[]{:S(2)}) collective-permute-start(f32[2,64,128]{2,1,0:T(8,128)S(1)} %get-tuple-element.118), channel_id=1, source_target_pairs={{0,8},{1,2},{2,1},{3,4},{4,3},{5,6},{6,5},{7,15},{8,0},{9,10},{10,... | collective-permute-start | bytes 196616 | tf_op jit(solution)/shard_map/ppermute | solution.py:545
  64.5 11.7 %collective-permute-start.16 = (f32[18,64,128]{2,1,0:T(8,128)S(1)}, f32[18,64,128]{2,1,0:T(8,128)S(1)}, u32[]{:S(2)}, u32[]{:S(2)}) collective-permute-start(f32[18,64,128]{2,1,0:T(8,128)S(1)} %get-tuple-element.116), channel_id=1, source_target_pairs={{0,2},{1,3},{2,0},{3,1},{4,6},{5,7},{6,4},{7,5},{8,16},{9,17},{10,... | collective-permute-start | bytes 1769480 | tf_op jit(solution)/shard_map/ppermute | solution.py:536
  67.6 8.6 %collective-permute-start.19 = (f32[2,64,128]{2,1,0:T(8,128)S(1)}, f32[2,64,128]{2,1,0:T(8,128)S(1)}, u32[]{:S(2)}, u32[]{:S(2)}) collective-permute-start(f32[2,64,128]{2,1,0:T(8,128)S(1)} %get-tuple-element.120), channel_id=1, source_target_pairs={{0,2},{1,3},{2,0},{3,1},{4,6},{5,7},{6,4},{7,5},{8,16},{9,17},{10,... | collective-permute-start | bytes 196616 | tf_op jit(solution)/shard_map/ppermute | solution.py:536
  70.5 2.8 %collective-permute-start.20 = (f32[34,64,128]{2,1,0:T(8,128)S(1)}, f32[34,64,128]{2,1,0:T(8,128)S(1)}, u32[]{:S(2)}, u32[]{:S(2)}) collective-permute-start(f32[34,64,128]{2,1,0:T(8,128)S(1)} %get-tuple-element.121), channel_id=1, source_target_pairs={{0,8},{1,9},{2,10},{3,11},{4,12},{5,13},{6,14},{7,15},{8,0},{9,1},... | collective-permute-start | bytes 3342344 | tf_op jit(solution)/shard_map/ppermute | solution.py:539

commit v3 on v2

v3 whole, which is shorter than its diff:
```python
import functools

import jax
import jax.numpy as jnp
from jax import lax
from jax.experimental import pallas as pl
from jax.experimental.pallas import tpu as pltpu
from jax.sharding import PartitionSpec as P

BLOCK_X = 4
BLOCK_Y = 32

WIDE = BLOCK_Y + 2
COARSE_X = BLOCK_X // 2
EDGE = BLOCK_Y // 4
MIDDLE = tuple(range(EDGE, BLOCK_Y - EDGE))
ENDS = tuple(q for q in range(BLOCK_Y) if q not in MIDDLE)
SIDES = (0, BLOCK_Y - 1)
BESIDE = (-1, BLOCK_Y)
INSIDE = tuple(range(1, BLOCK_Y - 1))

F32 = jnp.float32
BF16 = jnp.bfloat16
BOTH = ("gx", "gy")


def split(x):
    high = x.astype(BF16)
    low = (x - high.astype(F32)).astype(BF16)
    return jnp.concatenate([high, low], axis=1)


def fold(x):
    half = x.shape[1] // 2
    return x[:, :half].astype(F32) + x[:, half:].astype(F32)


def dot(*pairs):
    parts = [jnp.dot(a, b, preferred_element_type=F32) for a, b in pairs]
    return fold(functools.reduce(jnp.add, parts))


def row_parity():
    return lax.rem(lax.axis_index("gx"), 2)


def col_parity():
    return lax.rem(lax.axis_index("gy"), 2)


def place(rho, rows):
    parity = row_parity()
    return rho + parity * (rows - 1 - 2 * rho)


def spot(rho, q):
    return (rho + 1) * WIDE + q + 1


def swap_far(rows, cols, hop):
    pairs = []
    for a in range(rows):
        for b in range(cols):
            partner = a - 1 if a % 2 == 0 else a + 1
            if 0 <= partner < rows:
                pairs.append((a * cols + b, partner * cols + b))
            else:
                pairs.append((a * cols + b, a * cols + (b ^ hop)))
    return pairs


def swap_near(rows, cols):
    return [(a * cols + b, (a ^ 1) * cols + b) for a in range(rows) for b in range(cols)]


def swap_even(rows, cols):
    return [(a * cols + b, a * cols + (b ^ 1)) for a in range(rows) for b in range(cols)]


def swap_odd(rows, cols):
    pairs = []
    for a in range(rows):
        for b in range(cols):
            partner = b - 1 if b % 2 == 0 else b + 1
            if 0 <= partner < cols:
                pairs.append((a * cols + b, a * cols + partner))
            else:
                pairs.append((a * cols + b, (a ^ 1) * cols + b))
    return pairs


def far_is_inside():
    gx = lax.axis_index("gx")
    return jnp.where(row_parity() == 0, gx > 0, gx < lax.axis_size("gx") - 1)


def odd_is_inside():
    gy = lax.axis_index("gy")
    return jnp.where(col_parity() == 0, gy > 0, gy < lax.axis_size("gy") - 1)


def write_sides(grid, even_halo, odd_halo, rows):
    parity = col_parity()
    even_col = jnp.where(parity == 0, BLOCK_Y, -1)
    odd_col = BLOCK_Y - 1 - even_col
    inside = odd_is_inside()
    for rho in range(rows):
        grid[spot(rho, even_col)] = split(even_halo[rho])
        grid[spot(rho, odd_col)] = split(jnp.where(inside, odd_halo[rho], 0.0))


def read_sides(grid, even_send, odd_send, rows):
    parity = col_parity()
    even_col = jnp.where(parity == 0, BLOCK_Y - 1, 0)
    odd_col = BLOCK_Y - 1 - even_col
    for rho in range(rows):
        even_send[rho] = fold(grid[spot(rho, even_col)])
        odd_send[rho] = fold(grid[spot(rho, odd_col)])


def write_row(grid, halo, rho, cols, inside=None):
    for n, q in enumerate(cols):
        value = halo[n]
        if inside is not None:
            value = jnp.where(inside, value, 0.0)
        grid[spot(rho, q)] = split(value)


def read_row(grid, send, rho, cols):
    for n, q in enumerate(cols):
        send[n] = fold(grid[spot(rho, q)])


def over_rows(first, last, body):
    def step(rho, carry):
        body(rho)
        return carry

    lax.fori_loop(first, last, step, 0)


def stretches(cols):
    found = []
    for n, q in enumerate(cols):
        if found and found[-1][1] + found[-1][2] == q:
            found[-1][2] += 1
        else:
            found.append([n, q, 1])
    return found


def with_zeros(own, after):
    none = jnp.zeros(own.shape, BF16)
    return jnp.concatenate([own, none] if after else [none, own], axis=0)


def smoothed(blocks, cell, side):
    species = side.shape[0]
    return dot((blocks[cell, :, -2 * species :], with_zeros(split(side), False)))


def fine_cell(rho, q):
    return place(rho, BLOCK_X) * BLOCK_Y + q


def fine_apply(rho, q, blocks, grid):
    cell = fine_cell(rho, q)
    species = blocks.shape[1]
    here = spot(rho, q)
    step = WIDE * (1 - 2 * row_parity())
    near = jnp.concatenate([grid[here - step], grid[here + step], grid[here - 1], grid[here + 1]], axis=0)
    return dot(
        (blocks[cell, :, : 4 * species], near), (blocks[cell, :, 4 * species :], with_zeros(grid[here], True))
    )


def fine_second(rho, cols, blocks, grid, side, change, iterate, first, far=None):
    for q in cols:
        cell = fine_cell(rho, q)
        side[cell] = side[cell] - fine_apply(rho, q, blocks, grid)
    for m, q in enumerate(cols):
        cell = fine_cell(rho, q)
        here = spot(rho, q)
        step = smoothed(blocks, cell, side[cell])
        change[here] = split(step)
        iterate[first + q] = fold(grid[here]) + step
        if far is not None:
            far[m] = step


def fine_left(rho, q, blocks, side, change):
    return side[fine_cell(rho, q)] - fine_apply(rho, q, blocks, change)


def start_kernel(right, inverse, blocks, grid, side, far_m, far_n, inverse_here, sems):
    species = inverse.shape[0]
    part = species // 2
    loads = [
        pltpu.make_async_copy(inverse.at[pl.ds(n * part, part)], inverse_here.at[pl.ds(n * part, part)], sems.at[n])
        for n in range(2)
    ]
    for rho in range(BLOCK_X):
        row = pl.ds(fine_cell(rho, 0), BLOCK_Y)
        loads.append(pltpu.make_async_copy(right.at[row], side.at[row], sems.at[2 + rho]))
    for load in loads:
        load.start()
    for n in range(2):
        loads[n].wait()
        some = inverse_here[n * part : (n + 1) * part]
        both = jnp.concatenate([jnp.zeros(some.shape, BF16), some], axis=1)
        blocks[:, n * part : (n + 1) * part, 4 * species :] = jnp.transpose(both, (2, 0, 1))
    loads[2].wait()
    for cols, send in ((MIDDLE, far_m), (ENDS, far_n)):
        for n, q in enumerate(cols):
            cell = fine_cell(0, q)
            first = smoothed(blocks, cell, side[cell])
            grid[spot(0, q)] = split(first)
            send[n] = first
    for load in loads[3:]:
        load.wait()


def first_kernel(side, blocks, grid_in, grid, near, even, odd):
    def row(rho, near=None):
        for q in range(BLOCK_Y):
            cell = fine_cell(rho, q)
            first = smoothed(blocks, cell, side[cell])
            grid[spot(rho, q)] = split(first)
            if near is not None:
                near[q] = first

    over_rows(1, BLOCK_X - 1, row)
    row(BLOCK_X - 1, near)
    read_sides(grid, even, odd, BLOCK_X)


def fine_blocks_kernel(coupling, diagonal, inverse, blocks_in, blocks):
    species = coupling.shape[0]
    part = species // 2
    for first in range(0, species, part):
        rows = slice(first, first + part)
        blocks[:, rows, : 4 * species] = jnp.transpose(coupling[rows], (2, 0, 1))
        both = jnp.concatenate([diagonal[rows], inverse[rows]], axis=1)
        blocks[:, rows, 4 * species :] = jnp.transpose(both, (2, 0, 1))


def fine_inner_kernel(
    blocks, near_h, even_h, odd_h, grid_in, side_in, change_in, grid, side, change, out, last, near, made, sems
):
    write_row(grid, near_h, BLOCK_X, range(BLOCK_Y))
    write_sides(grid, even_h, odd_h, BLOCK_X)

    def leave(rho):
        source = made.at[pl.ds((rho - 1) * BLOCK_Y, BLOCK_Y)]
        return pltpu.make_async_copy(source, out.at[pl.ds(fine_cell(rho, 0), BLOCK_Y)], sems.at[rho - 1])

    def body(rho):
        fine_second(rho, range(BLOCK_Y), blocks, grid, side, change, made, (rho - 1) * BLOCK_Y)
        leave(rho).start()

    over_rows(1, BLOCK_X - 1, body)
    fine_second(BLOCK_X - 1, range(BLOCK_Y), blocks, grid, side, change, last, 0, near)
    for rho in range(1, BLOCK_X - 1):
        leave(rho).wait()


def fine_middle_kernel(cols, blocks, far_h, grid_in, side_in, grid, side, change, iterate, far):
    write_row(grid, far_h, -1, cols, far_is_inside())
    fine_second(0, cols, blocks, grid, side, change, iterate, 0, far)


def fine_ends_kernel(
    cols, blocks, far_h, grid_in, side_in, change_in, iterate_in, grid, side, change, iterate, far, even, odd
):
    write_row(grid, far_h, -1, cols, far_is_inside())
    fine_second(0, cols, blocks, grid, side, change, iterate, 0, far)
    read_sides(change, even, odd, BLOCK_X)


def left_pair(rho, cols, blocks, side, change, coarse_side, own_blocks, coarse_grid, far=None, shift=0):
    for q in cols:
        upper = fine_left(2 * rho, q, blocks, side, change)
        coarse_side[rho * BLOCK_Y + q] = upper + fine_left(2 * rho + 1, q, blocks, side, change)
    for n, q in enumerate(cols):
        cell = place(rho, COARSE_X) * BLOCK_Y + q
        first = smoothed(own_blocks, cell, coarse_side[rho * BLOCK_Y + q])
        coarse_grid[spot(rho, q)] = split(first)
        if far is not None:
            far[n + shift] = first


def left_middle_kernel(cols, blocks, side, own_blocks, far_h, change_in, change, coarse_side, coarse_grid, far):
    write_row(change, far_h, -1, cols, far_is_inside())
    left_pair(0, cols, blocks, side, change, coarse_side, own_blocks, coarse_grid, far)


def left_ends_kernel(
    cols,
    blocks,
    side,
    own_blocks,
    far_h,
    near_h,
    even_h,
    odd_h,
    change_in,
    coarse_in,
    grid_in,
    change,
    coarse_side,
    coarse_grid,
    far,
    even,
    odd,
):
    write_row(change, far_h, -1, cols, far_is_inside())
    write_row(change, near_h, BLOCK_X, range(BLOCK_Y))
    write_sides(change, even_h, odd_h, BLOCK_X)
    left_pair(0, cols, blocks, side, change, coarse_side, own_blocks, coarse_grid, far)
    for rho in range(1, COARSE_X):
        left_pair(rho, SIDES, blocks, side, change, coarse_side, own_blocks, coarse_grid)
    read_sides(coarse_grid, even, odd, COARSE_X)


def left_inner_kernel(blocks, side, own_blocks, change, coarse_in, grid_in, coarse_side, coarse_grid, near):
    for rho in range(1, COARSE_X):
        last = near if rho == COARSE_X - 1 else None
        left_pair(rho, INSIDE, blocks, side, change, coarse_side, own_blocks, coarse_grid, last, INSIDE[0])
    for q in SIDES:
        near[q] = fold(coarse_grid[spot(COARSE_X - 1, q)])


def near_blocks_kernel(coupling, first_row, last_row, out_in, blocks, out, sems):
    species = coupling.shape[1]
    step, count = pl.program_id(0), coupling.shape[0]
    copies = []
    for n, (rho, source) in enumerate(((0, first_row), (BLOCK_X - 1, last_row))):
        target = out.at[pl.ds(fine_cell(rho, 0), BLOCK_Y)]
        copies.append(pltpu.make_async_copy(source, target, sems.at[n]))

    @pl.when(step == 0)
    def _():
        for copy in copies:
            copy.start()

    for n in range(count):
        blocks[step * count + n] = coupling[n].reshape(species, 8 * species)

    @pl.when(step == pl.num_programs(0) - 1)
    def _():
        for copy in copies:
            copy.wait()


def coarse_apply(rho, q, places, blocks, own_blocks, grid):
    cell = place(rho, COARSE_X) * BLOCK_Y + q
    near = jnp.concatenate([grid[places[k, cell]] for k in range(8)], axis=0)
    return dot((blocks[cell], near), (own_blocks[cell], with_zeros(grid[spot(rho, q)], True)))


def coarse_second(rho, cols, places, blocks, own_blocks, grid, side, change, iterate, far=None, shift=0):
    for q in cols:
        here = rho * BLOCK_Y + q
        side[here] = side[here] - coarse_apply(rho, q, places, blocks, own_blocks, grid)
    for m, q in enumerate(cols):
        here = spot(rho, q)
        cell = place(rho, COARSE_X) * BLOCK_Y + q
        step = smoothed(own_blocks, cell, side[rho * BLOCK_Y + q])
        change[here] = split(step)
        iterate[cell] = fold(grid[here]) + step
        if far is not None:
            far[m + shift] = step


def pack_kernel(even_h, odd_h, grid_in, grid, far, near):
    write_sides(grid, even_h, odd_h, COARSE_X)
    read_row(grid, far, 0, BESIDE)
    read_row(grid, near, COARSE_X - 1, BESIDE)


def row_out(source, out, rho, sem):
    some = pl.ds(place(rho, COARSE_X) * BLOCK_Y, BLOCK_Y)
    return pltpu.make_async_copy(source.at[some], out.at[some], sem)


def coarse_inner_kernel(
    places, blocks, own_blocks, grid, side_in, change_in, iterate_in, side, change, iterate, near, out, sem
):
    leave = row_out(iterate, out, 0, sem)
    leave.start()
    for rho in range(1, COARSE_X):
        last = near if rho == COARSE_X - 1 else None
        coarse_second(rho, INSIDE, places, blocks, own_blocks, grid, side, change, iterate, last, INSIDE[0])
    for q in SIDES:
        near[q] = fold(change[spot(COARSE_X - 1, q)])
    leave.wait()


def coarse_middle_kernel(
    came, cols, places, blocks, own_blocks, far_h, grid_in, side_in, grid, side, change, iterate, far
):
    write_row(grid, far_h, -1, came)
    coarse_second(0, cols, places, blocks, own_blocks, grid, side, change, iterate, far)


def coarse_ends_kernel(
    came,
    cols,
    places,
    blocks,
    own_blocks,
    far_h,
    corners_h,
    near_h,
    beside_h,
    grid_in,
    side_in,
    change_in,
    iterate_in,
    grid,
    side,
    change,
    iterate,
    far,
    even,
    odd,
):
    write_row(grid, far_h, -1, came)
    write_row(grid, corners_h, -1, BESIDE)
    write_row(grid, near_h, COARSE_X, range(BLOCK_Y))
    write_row(grid, beside_h, COARSE_X, BESIDE)
    coarse_second(0, cols, places, blocks, own_blocks, grid, side, change, iterate, far)
    for rho in range(1, COARSE_X):
        coarse_second(rho, SIDES, places, blocks, own_blocks, grid, side, change, iterate)
    read_sides(change, even, odd, COARSE_X)


def last_pairs(rho, pairs, places, blocks, own_blocks, side, change, below):
    first = place(rho, COARSE_X) * (BLOCK_Y // 2)
    for pair in pairs:
        q = 2 * pair
        total = side[rho * BLOCK_Y + q] + side[rho * BLOCK_Y + q + 1]
        total = total - coarse_apply(rho, q, places, blocks, own_blocks, change)
        total = total - coarse_apply(rho, q + 1, places, blocks, own_blocks, change)
        below[first + pair] = total


def last_middle_kernel(came, pairs, places, blocks, own_blocks, side, far_h, change_in, change, below):
    write_row(change, far_h, -1, came)
    last_pairs(0, pairs, places, blocks, own_blocks, side, change, below)


def last_inner_kernel(
    pairs, places, blocks, own_blocks, side, near_h, iterate, change_in, below_in, out_in, change, below, out, sems
):
    leave = [row_out(iterate, out, rho, sems.at[rho]) for rho in range(1, COARSE_X)]
    for copy in leave:
        copy.start()
    write_row(change, near_h, COARSE_X, range(BLOCK_Y))
    for rho in range(1, COARSE_X):
        last_pairs(rho, pairs, places, blocks, own_blocks, side, change, below)
    for copy in leave:
        copy.wait()


def last_ends_kernel(
    came,
    done,
    todo,
    places,
    blocks,
    own_blocks,
    side,
    far_h,
    corners_h,
    beside_h,
    change_in,
    below,
    change,
    out,
    made,
    sems,
):
    copies = []

    def send(source, rho, first, count):
        some = pl.ds(place(rho, COARSE_X) * (BLOCK_Y // 2) + first, count)
        copies.append(pltpu.make_async_copy(source.at[some], out.at[some], sems.at[len(copies)]))
        copies[-1].start()

    for rho in range(COARSE_X):
        for _, first, count in stretches(done[rho]):
            send(below, rho, first, count)
    write_row(change, far_h, -1, came)
    write_row(change, corners_h, -1, BESIDE)
    write_row(change, beside_h, COARSE_X, BESIDE)
    for rho in reversed(range(COARSE_X)):
        for _, first, count in stretches(todo[rho]):
            last_pairs(rho, range(first, first + count), places, blocks, own_blocks, side, change, made)
            send(made, rho, first, count)
    for copy in copies:
        copy.wait()


IN_VMEM = pl.BlockSpec(memory_space=pltpu.VMEM)
IN_HBM = pl.BlockSpec(memory_space=pltpu.HBM)
LONG = 10**11


def run(name, kernel, outs, args, aliases=(), smem=(), hbm=(), hbm_outs=(), smem_outs=(), scratch=(), after=(), cost=1, room=2):
    count = len(args)
    args = list(args) + list(after)
    spaces = [pltpu.SMEM if n in smem else pltpu.HBM if n in hbm else pltpu.VMEM for n in range(len(args))]
    out_spaces = [
        pltpu.SMEM if n in smem_outs else pltpu.HBM if n in hbm_outs else pltpu.VMEM for n in range(len(outs))
    ]

    def body(*refs):
        kernel(*refs[:count], *refs[len(args) :])

    called = pl.pallas_call(
        body,
        out_shape=tuple(space(shape, dtype) for space, (shape, dtype) in zip(out_spaces, outs)),
        in_specs=[pl.BlockSpec(memory_space=space) for space in spaces],
        out_specs=tuple(pl.BlockSpec(memory_space=space) for space in out_spaces),
        scratch_shapes=list(scratch),
        input_output_aliases=dict(aliases),
        compiler_params=pltpu.CompilerParams(vmem_limit_bytes=room * 2**20),
        cost_estimate=pl.CostEstimate(flops=cost, bytes_accessed=1, transcendentals=0),
        name=name,
    )
    return called(*(pltpu.with_memory_space_constraint(x, space) for x, space in zip(args, spaces)))


def near_blocks_call(coupling, first_row, last_row, out):
    cells, species = coupling.shape[:2]
    part = cells // 8
    here = [pltpu.with_memory_space_constraint(x, pltpu.VMEM) for x in (first_row, last_row)]
    return pl.pallas_call(
        near_blocks_kernel,
        grid=(cells // part,),
        out_shape=(pltpu.VMEM((cells, species, 8 * species), BF16), pltpu.HBM(out.shape, out.dtype)),
        in_specs=[
            pl.BlockSpec((part,) + coupling.shape[1:], lambda n: (n, 0, 0, 0)),
            IN_VMEM,
            IN_VMEM,
            IN_HBM,
        ],
        out_specs=(IN_VMEM, IN_HBM),
        scratch_shapes=[pltpu.SemaphoreType.DMA((2,))],
        input_output_aliases={3: 1},
        compiler_params=pltpu.CompilerParams(vmem_limit_bytes=5 * 2**20),
        cost_estimate=pl.CostEstimate(flops=1, bytes_accessed=1, transcendentals=0),
        name="near_blocks",
    )(coupling, *here, pltpu.with_memory_space_constraint(out, pltpu.HBM))


def own_blocks_kernel(across, diagonal, inverse, pattern, blocks, places, made, sem):
    number = pattern[...]
    per_block = COARSE_X * BLOCK_Y
    owner = lax.div(number, per_block)
    inside = lax.rem(number, per_block)
    row = lax.div(owner, across) * COARSE_X + lax.div(inside, BLOCK_Y) - lax.axis_index("gx") * COARSE_X
    col = lax.rem(owner, across) * BLOCK_Y + lax.rem(inside, BLOCK_Y) - lax.axis_index("gy") * BLOCK_Y
    rho = jnp.where(row_parity() == 0, row, COARSE_X - 1 - row)
    made[...] = (rho + 1) * WIDE + col + 1
    copy = pltpu.make_async_copy(made, places, sem)
    copy.start()
    for cell in range(diagonal.shape[0]):
        blocks[cell] = jnp.concatenate([diagonal[cell], inverse[cell]], axis=1)
    copy.wait()


def on_device(
    right_side,
    fine_coupling,
    fine_diagonal,
    fine_inverse,
    coarse_coupling,
    coarse_diagonal,
    coarse_inverse,
    coarse_pattern,
):
    cells, species, vectors = right_side.shape
    coarse_cells = coarse_coupling.shape[0]
    rows, cols = lax.axis_size("gx"), lax.axis_size("gy")
    far_pairs, near_pairs = swap_far(rows, cols, 2 if cols % 4 == 0 else 1), swap_near(rows, cols)
    corner_pairs = swap_far(rows, cols, 1)
    even_pairs, odd_pairs = swap_even(rows, cols), swap_odd(rows, cols)

    def far(x):
        return lax.ppermute(x, BOTH, far_pairs)

    def near(x):
        return lax.ppermute(x, BOTH, near_pairs)

    def even(x):
        return lax.ppermute(x, BOTH, even_pairs)

    def odd(x):
        return lax.ppermute(x, BOTH, odd_pairs)

    def field(count):
        return ((count, species, vectors), F32)

    def padded(count):
        return (((count + 2) * WIDE, species, 2 * vectors), BF16)

    fine_blocks = ((cells, species, 6 * species), BF16)
    coupling = jnp.transpose(fine_coupling, (1, 2, 3, 0)).reshape(species, 4 * species, cells)
    diagonal = jnp.transpose(fine_diagonal, (1, 2, 0))
    inverse = jnp.transpose(fine_inverse, (1, 2, 0))
    pattern = coarse_pattern.T
    middle, ends = len(MIDDLE), len(ENDS)

    blocks, grid, side, far_m, far_n = run(
        "start",
        start_kernel,
        [fine_blocks, padded(BLOCK_X), field(cells), field(middle), field(ends)],
        [right_side, inverse],
        hbm=(0, 1),
        scratch=[pltpu.VMEM(inverse.shape, BF16), pltpu.SemaphoreType.DMA((2 + BLOCK_X,))],
        room=6,
    )
    far_m, far_n = far(far_m), far(far_n)
    grid, near_s, even_s, odd_s = run(
        "first",
        first_kernel,
        [padded(BLOCK_X), field(BLOCK_Y), field(BLOCK_X), field(BLOCK_X)],
        [side, blocks, grid],
        [(2, 0)],
    )
    near_h, even_h, odd_h = near(near_s), even(even_s), odd(odd_s)
    (blocks,) = run(
        "fine_blocks",
        fine_blocks_kernel,
        [fine_blocks],
        [coupling, diagonal, inverse, blocks],
        [(3, 0)],
        after=[near_s],
        room=6,
    )
    own_blocks, places = run(
        "own_blocks",
        functools.partial(own_blocks_kernel, cols),
        [((coarse_cells, species, 2 * species), BF16), (pattern.shape, jnp.int32)],
        [coarse_diagonal, coarse_inverse, pattern],
        smem_outs=(1,),
        scratch=[pltpu.VMEM(pattern.shape, jnp.int32), pltpu.SemaphoreType.DMA],
        after=[blocks],
    )
    state = [padded(BLOCK_X), field(cells), padded(BLOCK_X)]
    grid, side, change, iterate, far_m = run(
        "fine_middle",
        functools.partial(fine_middle_kernel, MIDDLE),
        state + [field(BLOCK_Y), field(middle)],
        [blocks, far_m, grid, side],
        [(2, 0), (3, 1)],
        after=[even_h, odd_h, own_blocks],
        cost=LONG,
    )
    far_m = far(far_m)
    grid, side, change, fine_iterate, last_row, near_s = run(
        "fine_inner",
        fine_inner_kernel,
        state + [field(cells), field(BLOCK_Y), field(BLOCK_Y)],
        [blocks, near_h, even_h, odd_h, grid, side, change],
        [(4, 0), (5, 1), (6, 2)],
        hbm_outs=(3,),
        scratch=[
            pltpu.VMEM(((BLOCK_X - 2) * BLOCK_Y, species, vectors), F32),
            pltpu.SemaphoreType.DMA((BLOCK_X - 2,)),
        ],
        room=4,
    )
    near_h = near(near_s)
    grid, side, change, iterate, far_n, even_s, odd_s = run(
        "fine_ends",
        functools.partial(fine_ends_kernel, ENDS),
        state + [field(BLOCK_Y), field(ends), field(BLOCK_X), field(BLOCK_X)],
        [blocks, far_n, grid, side, change, iterate],
        [(2, 0), (3, 1), (4, 2), (5, 3)],
    )
    near_blocks, fine_iterate = near_blocks_call(coarse_coupling, iterate, last_row, fine_iterate)
    far_n = far(far_n)
    even_h, odd_h = even(even_s), odd(odd_s)

    state = [padded(BLOCK_X), field(coarse_cells), padded(COARSE_X)]
    change, coarse_side, coarse_grid, far_m = run(
        "left_middle",
        functools.partial(left_middle_kernel, MIDDLE),
        state + [field(middle)],
        [blocks, side, own_blocks, far_m, change],
        [(4, 0)],
        after=[even_h, odd_h, near_blocks],
        cost=LONG,
    )
    far_m = far(far_m)
    change, coarse_side, coarse_grid, far_n, even_s, odd_s = run(
        "left_ends",
        functools.partial(left_ends_kernel, ENDS),
        state + [field(ends), field(COARSE_X), field(COARSE_X)],
        [blocks, side, own_blocks, far_n, near_h, even_h, odd_h, change, coarse_side, coarse_grid],
        [(7, 0), (8, 1), (9, 2)],
        cost=LONG,
    )
    coarse_side, coarse_grid, near_s = run(
        "left_inner",
        left_inner_kernel,
        state[1:] + [field(BLOCK_Y)],
        [blocks, side, own_blocks, change, coarse_side, coarse_grid],
        [(4, 0), (5, 1)],
    )
    far_n = far(far_n)
    even_h, odd_h = even(even_s), odd(odd_s)
    near_h = near(near_s)
    coarse_grid, corners, beside = run(
        "pack_first",
        pack_kernel,
        [padded(COARSE_X), field(2), field(2)],
        [even_h, odd_h, coarse_grid],
        [(2, 0)],
    )
    corners, beside = lax.ppermute(corners, BOTH, corner_pairs), near(beside)

    state = [padded(COARSE_X), field(coarse_cells), padded(COARSE_X), field(coarse_cells)]
    inner = MIDDLE[1:-1]
    outer = tuple(q for q in range(BLOCK_Y) if q not in inner)
    coarse_grid, coarse_side, coarse_change, iterate, far_m = run(
        "coarse_middle",
        functools.partial(coarse_middle_kernel, MIDDLE, inner),
        state + [field(len(inner))],
        [places, near_blocks, own_blocks, far_m, coarse_grid, coarse_side],
        [(4, 0), (5, 1)],
        smem=(0,),
        cost=LONG,
    )
    far_m = far(far_m)
    coarse_grid, coarse_side, coarse_change, iterate, far_n, even_s, odd_s = run(
        "coarse_ends",
        functools.partial(coarse_ends_kernel, ENDS, outer),
        state + [field(len(outer)), field(COARSE_X), field(COARSE_X)],
        [places, near_blocks, own_blocks, far_n, corners, near_h, beside]
        + [coarse_grid, coarse_side, coarse_change, iterate],
        [(7, 0), (8, 1), (9, 2), (10, 3)],
        smem=(0,),
        cost=LONG,
    )
    coarse_side, coarse_change, iterate, near_s, coarse_iterate = run(
        "coarse_inner",
        coarse_inner_kernel,
        state[1:] + [field(BLOCK_Y), field(coarse_cells)],
        [places, near_blocks, own_blocks, coarse_grid, coarse_side, coarse_change, iterate],
        [(4, 0), (5, 1), (6, 2)],
        smem=(0,),
        hbm_outs=(4,),
        scratch=[pltpu.SemaphoreType.DMA],
    )
    far_n = far(far_n)
    even_h, odd_h = even(even_s), odd(odd_s)
    near_h = near(near_s)
    coarse_change, corners, beside = run(
        "pack_second",
        pack_kernel,
        [padded(COARSE_X), field(2), field(2)],
        [even_h, odd_h, coarse_change],
        [(2, 0)],
    )
    corners, beside = lax.ppermute(corners, BOTH, corner_pairs), near(beside)

    state = [padded(COARSE_X), field(coarse_cells // 2)]
    half = BLOCK_Y // 2
    core = tuple(q // 2 for q in inner[1:-1:2])
    pairs = tuple(range(1, half - 1))
    todo = [tuple(q for q in range(half) if q not in core)] + [(0, half - 1)] * (COARSE_X - 1)
    coarse_change, below = run(
        "last_middle",
        functools.partial(last_middle_kernel, inner, core),
        state,
        [places, near_blocks, own_blocks, coarse_side, far_m, coarse_change],
        [(5, 0)],
        smem=(0,),
        cost=LONG,
    )
    coarse_change, below, coarse_iterate = run(
        "last_inner",
        functools.partial(last_inner_kernel, pairs),
        state + [field(coarse_cells)],
        [places, near_blocks, own_blocks, coarse_side, near_h, iterate, coarse_change, below, coarse_iterate],
        [(6, 0), (7, 1), (8, 2)],
        smem=(0,),
        hbm=(8,),
        hbm_outs=(2,),
        scratch=[pltpu.SemaphoreType.DMA((COARSE_X,))],
    )
    coarse_change, next_side = run(
        "last_ends",
        functools.partial(last_ends_kernel, outer, [core] + [pairs] * (COARSE_X - 1), todo),
        state,
        [places, near_blocks, own_blocks, coarse_side, far_n, corners, beside, coarse_change, below],
        [(7, 0)],
        smem=(0,),
        hbm_outs=(1,),
        scratch=[pltpu.VMEM(state[1][0], F32), pltpu.SemaphoreType.DMA((4 * COARSE_X,))],
        room=3,
    )
    return (fine_iterate, coarse_iterate, next_side)


def solution(mesh):
    placed = (
        P(BOTH, None, None),
        P(BOTH, None, None, None),
        P(BOTH, None, None),
        P(BOTH, None, None),
        P(BOTH, None, None, None),
        P(BOTH, None, None),
        P(BOTH, None, None),
        P(BOTH, None),
    )
    return jax.shard_map(
        on_device,
        mesh=mesh,
        in_specs=placed,
        out_specs=(P(BOTH, None, None), P(BOTH, None, None), P(BOTH, None, None)),
        check_vma=False,
    )
```

time: 78.6 us -> 67.5 us (0.86)
  Pallas kernels: 40 us -> 33.6 us
  waiting for transfers between devices: 8.33 us -> 5.72 us
  starting transfers between devices: 29 us -> 26.8 us
    pallas_call x19 -> x18, Pallas kernels: 36.8 us -> 30.4 us  [run(): called(*(pltpu.with_memory_space_constraint(x, space) for x, space in zip...]
    ppermute x10 -> x8, starting transfers between devices: 25.1 us -> 20.2 us  [far(): return lax.ppermute(x, BOTH, far_pairs)]
    ppermute x0 -> x2, starting transfers between devices: none -> 3.42 us  [on_device(): corners, beside = (lax.ppermute(corners, BOTH, corner_pairs), near(beside))]
    ppermute x4, waiting for transfers between devices: 3.17 us -> 0.01 us  [even(): return lax.ppermute(x, BOTH, even_pairs)]
    ppermute x4 -> x6, waiting for transfers between devices: 1.22 us -> 0.02 us  [near(): return lax.ppermute(x, BOTH, near_pairs)]
    ppermute x0 -> x2, waiting for transfers between devices: none -> 1.17 us  [on_device(): corners, beside = (lax.ppermute(corners, BOTH, corner_pairs), near(beside))]
    ppermute x4, starting transfers between devices: 3.75 us -> 2.86 us  [even(): return lax.ppermute(x, BOTH, even_pairs)]
    ppermute x10 -> x8, waiting for transfers between devices: 3.92 us -> 4.51 us  [far(): return lax.ppermute(x, BOTH, far_pairs)]
  transfers between devices with their start and end apart: 22 -> 24, of which waited for: 6 -> 5; matrix products, arithmetic and copies ran while one was open for 0% -> 0% of each run, Pallas kernels for 45% -> 43%
where the time goes in v3:
time: 67.5 us; the launch traced here: 67.4 us
  Pallas kernels  33.6 us (50%)
  starting transfers between devices  26.8 us (40%)
  waiting for transfers between devices  5.72 us (8%)
  between operations  1.15 us (2%)
    pallas_call x18, Pallas kernels, run(): called(*(pltpu.with_memory_space_constraint(x, space) for x, space in zip...  30.4 us
    ppermute x8, starting transfers between devices, far(): return lax.ppermute(x, BOTH, far_pairs)  20.2 us
    ppermute x8, waiting for transfers between devices, far(): return lax.ppermute(x, BOTH, far_pairs)  4.51 us
    ppermute x2, starting transfers between devices, on_device(): corners, beside = (lax.ppermute(corners, BOTH, corner_pairs), near(beside))  3.42 us
    pallas_call x1, Pallas kernels, near_blocks_call(): pl.pallas_call(near_blocks_kernel, grid=(cells // part,), out_shape=(pltp...  3.27 us
    ppermute x4, starting transfers between devices, even(): return lax.ppermute(x, BOTH, even_pairs)  2.86 us
  transfers between devices with their start and end apart: 24, of which 5 were waited for; matrix products, arithmetic and copies ran while one was open for 0% of the time, Pallas kernels for 43%

profile of v3, /device:TPU:0, one launch (start us, length us, event | category | flops | bytes accessed | tf_op | source)
XLA Modules:
  0.0 67.4 jit_solution(1771662528347038150)
XLA Ops:
  0.6 2.6 %start.1 = (bf16[128,64,384]{2,1,0:T(8,128)(2,1)S(1)}, bf16[204,64,256]{2,1,0:T(8,128)(2,1)S(1)}, f32[128,64,128]{2,1,0:T(8,128)S(1)}, f32[16,64,128]{2,1,0:T(8,128)S(1)}, f32[16,64,128]{2,1,0:T(8,128)S(1)}) custom-call(f32[128,64,128]{2,1,0:T(8,128)} %refs_0_.2, bf16[64,64,128]{2,1,0:T(8,128)(2,1)} %bitcast.9), custom_call_target="tpu_custom_call" | custom-call | flops 1 | bytes 1 | tf_op jit(solution)/shard_map/start/pallas_call | solution.py:532
  3.2 3.1 %collective-permute-start.4 = (f32[16,64,128]{2,1,0:T(8,128)S(1)}, f32[16,64,128]{2,1,0:T(8,128)S(1)}, u32[]{:S(2)}, u32[]{:S(2)}) collective-permute-start(f32[16,64,128]{2,1,0:T(8,128)S(1)} %get-tuple-element.82), channel_id=1, source_target_pairs={{0,2},{1,3},{2,0},{3,1},{4,6},{5,7},{6,4},{7,5},{8,16},{9,17},{10,... | collective-permute-start | bytes 1572872 | tf_op jit(solution)/shard_map/ppermute | solution.py:592
  6.3 1.3 %first.1 = (bf16[204,64,256]{2,1,0:T(8,128)(2,1)S(1)}, f32[32,64,128]{2,1,0:T(8,128)S(1)}, f32[4,64,128]{2,1,0:T(8,128)S(1)}, f32[4,64,128]{2,1,0:T(8,128)S(1)}) custom-call(f32[128,64,128]{2,1,0:T(8,128)S(1)} %get-tuple-element.76.refs_0_.refs_3_, bf16[128,64,384]{2,1,0:T(8,128)(2,1)S(1)} %get-tuple-element.75.refs_1_.refs_3_, ...), custom_call_target="tpu_custom_call", output_to_operand_aliasing={{0}: (2, {})} | custom-call | flops 1 | bytes 1 | tf_op jit(solution)/shard_map/first/pallas_call | solution.py:532
  7.6 1.6 %collective-permute-start.2 = (f32[4,64,128]{2,1,0:T(8,128)S(1)}, f32[4,64,128]{2,1,0:T(8,128)S(1)}, u32[]{:S(2)}, u32[]{:S(2)}) collective-permute-start(f32[4,64,128]{2,1,0:T(8,128)S(1)} %get-tuple-element.80), channel_id=1, source_target_pairs={{0,1},{1,0},{2,3},{3,2},{4,5},{5,4},{6,7},{7,6},{8,9},{9,8},{10,11... | collective-permute-start | bytes 393224 | tf_op jit(solution)/shard_map/ppermute | solution.py:598
  9.2 0.0 collective-permute-start.3
  9.2 2.0 %collective-permute-start = (f32[16,64,128]{2,1,0:T(8,128)S(1)}, f32[16,64,128]{2,1,0:T(8,128)S(1)}, u32[]{:S(2)}, u32[]{:S(2)}) collective-permute-start(f32[16,64,128]{2,1,0:T(8,128)S(1)} %get-tuple-element.79), channel_id=1, source_target_pairs={{0,2},{1,3},{2,0},{3,1},{4,6},{5,7},{6,4},{7,5},{8,16},{9,17},{10,... | collective-permute-start | bytes 1572872 | tf_op jit(solution)/shard_map/ppermute | solution.py:592
  11.2 0.0 collective-permute-start.1
  11.2 0.0 copy-start.3
  11.2 0.0 copy-start.4
  11.2 0.0 copy-start.5
  11.2 2.5 %fine_blocks.1.refs_3_.refs_0_ = bf16[128,64,384]{2,1,0:T(8,128)(2,1)S(1)} custom-call(bf16[64,256,128]{2,1,0:T(8,128)(2,1)S(1)} %bitcast.8, bf16[64,64,128]{2,1,0:T(8,128)(2,1)S(1)} %bitcast.11, bf16[64,64,128]{2,1,0:T(8,128)(2,1)S(1)} %bitcast.10, bf16[128,64,384]{2,1,0:T(8,128)(2,1)S(1)} %get-tuple-element.75.refs_1_.refs_3_, ...), custom_call_target="tpu_custom_call", output_to_operand_aliasing={{}: (3, {})} | custom-call | flops 1 | bytes 1 | tf_op jit(solution)/shard_map/fine_blocks/pallas_call | solution.py:532
  13.8 0.9 %own_blocks.1 = (bf16[64,64,128]{2,1,0:T(8,128)(2,1)S(1)}, s32[8,64]{1,0:T(8,128)S(4)}) custom-call(bf16[64,64,64]{2,1,0:T(8,128)(2,1)S(1)} %copy-done.3, bf16[64,64,64]{2,1,0:T(8,128)(2,1)S(1)} %copy-done.4, s32[8,64]{1,0:T(8,128)S(1)} %bitcast.12, bf16[128,64,384]{2,1,0:T(8,128)(2,1)S(1)} %fine_blocks.1.refs_3_.refs_0_), custom_call_target="tpu_custom_call" | custom-call | flops 1 | bytes 1 | tf_op jit(solution)/shard_map/own_blocks/pallas_call | solution.py:532
  14.7 0.0 collective-permute-done.3.refs_5_.refs_3_
  14.7 0.1 collective-permute-done.4.refs_1_
  14.8 0.9 %fine_middle.1 = (bf16[204,64,256]{2,1,0:T(8,128)(2,1)S(1)}, f32[128,64,128]{2,1,0:T(8,128)S(1)}, bf16[204,64,256]{2,1,0:T(8,128)(2,1)S(1)}, f32[32,64,128]{2,1,0:T(8,128)S(1)}, f32[16,64,128]{2,1,0:T(8,128)S(1)}) custom-call(bf16[128,64,384]{2,1,0:T(8,128)(2,1)S(1)} %fine_blocks.1.refs_3_.refs_0_, ...), custom_call_target="tpu_custom_call", output_to_operand_aliasing={{0}: (2, {}), {1}: (3, {})} | custom-call | flops 99999997952 | bytes 1 | tf_op jit(solution)/shard_map/fine_middle/pallas_call | solution.py:532
  15.7 4.4 %collective-permute-start.9 = (f32[16,64,128]{2,1,0:T(8,128)S(1)}, f32[16,64,128]{2,1,0:T(8,128)S(1)}, u32[]{:S(2)}, u32[]{:S(2)}) collective-permute-start(f32[16,64,128]{2,1,0:T(8,128)S(1)} %get-tuple-element.103), channel_id=1, source_target_pairs={{0,2},{1,3},{2,0},{3,1},{4,6},{5,7},{6,4},{7,5},{8,16},{9,17},{10,... | collective-permute-start | bytes 1572872 | tf_op jit(solution)/shard_map/ppermute | solution.py:592
  20.1 4.6 %fine_inner.1 = (bf16[204,64,256]{2,1,0:T(8,128)(2,1)S(1)}, f32[128,64,128]{2,1,0:T(8,128)S(1)}, bf16[204,64,256]{2,1,0:T(8,128)(2,1)S(1)}, f32[128,64,128]{2,1,...) custom-call(bf16[128,64,384]{2,1,0:T(8,128)(2,1)S(1)} %fine_blocks.1, ...), custom_call_target="tpu_custom_call", output_to_operand_aliasing={{0}: (4, {}), {1}: (5, {}), {2}: (6, {})} | custom-call | flops 1 | bytes 1 | tf_op jit(solution)/shard_map/fine_inner/pallas_call | solution.py:532
  24.8 0.0 collective-permute-done.refs_1_
  24.8 0.0 slice-start
  24.8 0.0 slice-start.1
  24.8 0.9 %fine_ends.1 = (bf16[204,64,256]{2,1,0:T(8,128)(2,1)S(1)}, f32[128,64,128]{2,1,0:T(8,128)S(1)}, bf16[204,64,256]{2,1,0:T(8,128)(2,1)S(1)}, f32[32,64,128]{2,1,0:...) custom-call(bf16[128,64,384]{2,1,0:T(8,128)(2,1)S(1)} %fine_blocks.1, ...), custom_call_target="tpu_custom_call", output_to_operand_aliasing={{0}: (2, {}), {1}: (3, {}), {2}: (4, {}), {3}: (5, {})} | custom-call | flops 1 | bytes 1 | tf_op jit(solution)/shard_map/fine_ends/pallas_call | solution.py:532
  25.7 0.1 collective-permute-start.7
  25.8 0.1 collective-permute-start.8
  25.9 3.4 %collective-permute-start.5 = (f32[16,64,128]{2,1,0:T(8,128)S(1)}, f32[16,64,128]{2,1,0:T(8,128)S(1)}, u32[]{:S(2)}, u32[]{:S(2)}) collective-permute-start(f32[16,64,128]{2,1,0:T(8,128)S(1)} %get-tuple-element.99), channel_id=1, source_target_pairs={{0,2},{1,3},{2,0},{3,1},{4,6},{5,7},{6,4},{7,5},{8,16},{9,17},{10,... | collective-permute-start | bytes 1572872 | tf_op jit(solution)/shard_map/ppermute | solution.py:592
  29.3 3.3 %near_blocks.1 = (bf16[64,64,512]{2,1,0:T(8,128)(2,1)S(1)}, f32[128,64,128]{2,1,0:T(8,128)}) custom-call(bf16[64,64,8,64]{3,2,1,0:T(8,128)(2,1)S(1)} %bitcast.7, f32[32,64,128]{2,1,0:T(8,128)S(1)} %get-tuple-element.92.first_row, f32[32,64,128]{2,1,0:T(8,128)S(1)} %get-tuple-element.93.last_row, ...), custom_call_target="tpu_custom_call", output_to_operand_aliasing={{1}: (3, {})} | custom-call | flops 1 | bytes 1 | tf_op jit(solution)/shard_map/near_blocks/pallas_call | solution.py:539
  32.6 0.0 collective-permute-done.9.refs_3_
  32.6 0.0 collective-permute-done.8.refs_6_
  32.6 1.2 %left_middle.1 = (bf16[204,64,256]{2,1,0:T(8,128)(2,1)S(1)}, f32[64,64,128]{2,1,0:T(8,128)S(1)}, bf16[136,64,256]{2,1,0:T(8,128)(2,1)S(1)}, f32[16,64,128]{2,1,0:T(8,128)S(1)}) custom-call(bf16[128,64,384]{2,1,0:T(8,128)(2,1)S(1)} %fine_blocks.1.refs_3_.refs_0_, f32[128,64,128]{2,1,0:T(8,128)S(1)} %get-tuple-element.98.refs_1_, ...), custom_call_target="tpu_custom_call", output_to_operand_aliasing={{0}: (4, {})} | custom-call | flops 99999997952 | bytes 1 | tf_op jit(solution)/shard_map/left_middle/pallas_call | solution.py:532
  33.8 0.9 %collective-permute-start.16 = (f32[16,64,128]{2,1,0:T(8,128)S(1)}, f32[16,64,128]{2,1,0:T(8,128)S(1)}, u32[]{:S(2)}, u32[]{:S(2)}) collective-permute-start(f32[16,64,128]{2,1,0:T(8,128)S(1)} %get-tuple-element.118), channel_id=1, source_target_pairs={{0,2},{1,3},{2,0},{3,1},{4,6},{5,7},{6,4},{7,5},{8,16},{9,17},{10,... | collective-permute-start | bytes 1572872 | tf_op jit(solution)/shard_map/ppermute | solution.py:592
  34.7 3.1 %collective-permute-done.5.refs_3_ = f32[16,64,128]{2,1,0:T(8,128)S(1)} collective-permute-done((f32[16,64,128]{2,1,0:T(8,128)S(1)}, f32[16,64,128]{2,1,0:T(8,128)S(1)}, u32[]{:S(2)}, u32[]{:S(2)}) %collective-permute-start.5) | collective-permute-done | bytes 524320 | tf_op jit(solution)/shard_map/ppermute | solution.py:592
  37.8 0.0 collective-permute-done.6.refs_4_
  37.9 1.8 %left_ends.1 = (bf16[204,64,256]{2,1,0:T(8,128)(2,1)S(1)}, f32[64,64,128]{2,1,0:T(8,128)S(1)}, bf16[136,64,256]{2,1,0:T(8,128)(2,1)S(1)}, f32[16,64,128]{2,1,0:T...) custom-call(bf16[128,64,384]{2,1,0:T(8,128)(2,1)S(1)} %fine_blocks.1, ...), custom_call_target="tpu_custom_call", output_to_operand_aliasing={{0}: (7, {}), {1}: (8, {}), {2}: (9, {})} | custom-call | flops 99999997952 | bytes 1 | tf_op jit(solution)/shard_map/left_ends/pallas_call | solution.py:532
  39.6 0.1 collective-permute-start.11
  39.7 0.1 collective-permute-start.12
  39.8 3.4 %collective-permute-start.10 = (f32[16,64,128]{2,1,0:T(8,128)S(1)}, f32[16,64,128]{2,1,0:T(8,128)S(1)}, u32[]{:S(2)}, u32[]{:S(2)}) collective-permute-start(f32[16,64,128]{2,1,0:T(8,128)S(1)} %get-tuple-element.108), channel_id=1, source_target_pairs={{0,2},{1,3},{2,0},{3,1},{4,6},{5,7},{6,4},{7,5},{8,16},{9,17},{10,... | collective-permute-start | bytes 1572872 | tf_op jit(solution)/shard_map/ppermute | solution.py:592
  43.2 2.3 %left_inner.1 = (f32[64,64,128]{2,1,0:T(8,128)S(1)}, bf16[136,64,256]{2,1,0:T(8,128)(2,1)S(1)}, f32[32,64,128]{2,1,0:T(8,128)S(1)}) custom-call(bf16[128,64,384]{2,1,0:T(8,128)(2,1)S(1)} %fine_blocks.1.refs_3_.refs_0_, f32[128,64,128]{2,1,0:T(8,128)S(1)} %get-tuple-element.98.refs_1_, ...), custom_call_target="tpu_custom_call", output_to_operand_aliasing={{0}: (4, {}), {1}: (5, {})} | custom-call | flops 1 | bytes 1 | tf_op jit(solution)/shard_map/left_inner/pallas_call | solution.py:532
  45.5 0.1 collective-permute-start.14
  45.6 0.0 collective-permute-done.11.refs_0_
  45.6 0.0 collective-permute-done.12.refs_1_
  45.6 0.1 pack_first.1
  45.7 1.3 %collective-permute-start.13 = (f32[2,64,128]{2,1,0:T(8,128)S(1)}, f32[2,64,128]{2,1,0:T(8,128)S(1)}, u32[]{:S(2)}, u32[]{:S(2)}) collective-permute-start(f32[2,64,128]{2,1,0:T(8,128)S(1)} %get-tuple-element.115), channel_id=1, source_target_pairs={{0,1},{1,0},{2,3},{3,2},{4,5},{5,4},{6,7},{7,6},{8,16},{9,17},{10,... | collective-permute-start | bytes 196616 | tf_op jit(solution)/shard_map/ppermute | solution.py:724
  47.0 0.0 collective-permute-start.15
  47.0 0.0 collective-permute-done.16.refs_3_
  47.0 1.1 %coarse_middle.1 = (bf16[136,64,256]{2,1,0:T(8,128)(2,1)S(1)}, f32[64,64,128]{2,1,0:T(8,128)S(1)}, bf16[136,64,256]{2,1,0:T(8,128)(2,1)S(1)}, f32[64,64,128]{2,1,0:T(8,128)S(1)}, f32[14,64,128]{2,1,0:T(8,128)S(1)}) custom-call(s32[8,64]{1,0:T(8,128)S(4)} %get-tuple-element.96.refs_0_, ...), custom_call_target="tpu_custom_call", output_to_operand_aliasing={{0}: (4, {}), {1}: (5, {})} | custom-call | flops 99999997952 | bytes 1 | tf_op jit(solution)/shard_map/coarse_middle/pallas_call | solution.py:532
  48.1 0.7 %collective-permute-start.18 = (f32[14,64,128]{2,1,0:T(8,128)S(1)}, f32[14,64,128]{2,1,0:T(8,128)S(1)}, u32[]{:S(2)}, u32[]{:S(2)}) collective-permute-start(f32[14,64,128]{2,1,0:T(8,128)S(1)} %get-tuple-element.132), channel_id=1, source_target_pairs={{0,2},{1,3},{2,0},{3,1},{4,6},{5,7},{6,4},{7,5},{8,16},{9,17},{10,... | collective-permute-start | bytes 1376264 | tf_op jit(solution)/shard_map/ppermute | solution.py:592
  48.8 1.2 %collective-permute-done.13.refs_4_ = f32[2,64,128]{2,1,0:T(8,128)S(1)} collective-permute-done((f32[2,64,128]{2,1,0:T(8,128)S(1)}, f32[2,64,128]{2,1,0:T(8,128)S(1)}, u32[]{:S(2)}, u32[]{:S(2)}) %collective-permute-start.13) | collective-permute-done | bytes 65568 | tf_op jit(solution)/shard_map/ppermute | solution.py:724
  50.0 0.0 collective-permute-done.15.refs_6_
  50.0 1.0 %collective-permute-done.10.refs_3_ = f32[16,64,128]{2,1,0:T(8,128)S(1)} collective-permute-done((f32[16,64,128]{2,1,0:T(8,128)S(1)}, f32[16,64,128]{2,1,0:T(8,128)S(1)}, u32[]{:S(2)}, u32[]{:S(2)}) %collective-permute-start.10) | collective-permute-done | bytes 524320 | tf_op jit(solution)/shard_map/ppermute | solution.py:592
  51.0 0.0 collective-permute-done.14.refs_5_
  51.0 1.8 %coarse_ends.1 = (bf16[136,64,256]{2,1,0:T(8,128)(2,1)S(1)}, f32[64,64,128]{2,1,0:T(8,128)S(1)}, bf16[136,64,256]{2,1,0:T(8,128)(2,1)S(1)}, f32[64,64,128]{2,1,0...) custom-call(s32[8,64]{1,0:T(8,128)S(4)} %get-tuple-element.96.refs_0, ...), custom_call_target="tpu_custom_call", output_to_operand_aliasing={{0}: (7, {}), {1}: (8, {}), {2}: (9, {}), {3}: (10, {})} | custom-call | flops 99999997952 | bytes 1 | tf_op jit(solution)/shard_map/coarse_ends/pallas_call | solution.py:532
  52.8 1.2 %collective-permute-start.19 = (f32[2,64,128]{2,1,0:T(8,128)S(1)}, f32[2,64,128]{2,1,0:T(8,128)S(1)}, u32[]{:S(2)}, u32[]{:S(2)}) collective-permute-start(f32[2,64,128]{2,1,0:T(8,128)S(1)} %get-tuple-element.133), channel_id=1, source_target_pairs={{0,1},{1,0},{2,3},{3,2},{4,5},{5,4},{6,7},{7,6},{8,9},{9,8},{10,11... | collective-permute-start | bytes 196616 | tf_op jit(solution)/shard_map/ppermute | solution.py:598
  54.0 0.0 collective-permute-start.20
  54.0 2.4 %collective-permute-start.21 = (f32[18,64,128]{2,1,0:T(8,128)S(1)}, f32[18,64,128]{2,1,0:T(8,128)S(1)}, u32[]{:S(2)}, u32[]{:S(2)}) collective-permute-start(f32[18,64,128]{2,1,0:T(8,128)S(1)} %get-tuple-element.141), channel_id=1, source_target_pairs={{0,2},{1,3},{2,0},{3,1},{4,6},{5,7},{6,4},{7,5},{8,16},{9,17},{10,... | collective-permute-start | bytes 1769480 | tf_op jit(solution)/shard_map/ppermute | solution.py:592
  56.4 2.7 %coarse_inner.1 = (f32[64,64,128]{2,1,0:T(8,128)S(1)}, bf16[136,64,256]{2,1,0:T(8,128)(2,1)S(1)}, f32[64,64,128]{2,1,0:T(8,128)S(1)}, f32[32,64,128]{2,1,0:T(8,128)S(1)}, f32[64,64,128]{2,1,0:T(8,128)}) custom-call(s32[8,64]{1,0:T(8,128)S(4)} %get-tuple-element.96.refs_0_, ...), custom_call_target="tpu_custom_call", output_to_operand_aliasing={{0}: (4, {}), {1}: (5, {}), {2}: (6, {})} | custom-call | flops 1 | bytes 1 | tf_op jit(solution)/shard_map/coarse_inner/pallas_call | solution.py:532
  59.0 0.1 collective-permute-start.17
  59.1 0.0 collective-permute-done.20.refs_1_
  59.1 0.1 pack_second.1
  59.2 2.1 %collective-permute-start.22 = (f32[2,64,128]{2,1,0:T(8,128)S(1)}, f32[2,64,128]{2,1,0:T(8,128)S(1)}, u32[]{:S(2)}, u32[]{:S(2)}) collective-permute-start(f32[2,64,128]{2,1,0:T(8,128)S(1)} %get-tuple-element.142), channel_id=1, source_target_pairs={{0,1},{1,0},{2,3},{3,2},{4,5},{5,4},{6,7},{7,6},{8,16},{9,17},{10,... | collective-permute-start | bytes 196616 | tf_op jit(solution)/shard_map/ppermute | solution.py:769
  61.3 0.0 collective-permute-done.18.refs_4_
  61.3 0.8 %last_middle.1 = (bf16[136,64,256]{2,1,0:T(8,128)(2,1)S(1)}, f32[32,64,128]{2,1,0:T(8,128)S(1)}) custom-call(s32[8,64]{1,0:T(8,128)S(4)} %get-tuple-element.96.refs_0_, bf16[64,64,512]{2,1,0:T(8,128)(2,1)S(1)} %get-tuple-element.97.refs_7_.refs_1_, bf16[64,64,128]{2,1,0:T(8,128)(2,1)S(1)} %get-tuple-element.84.refs_6_.refs_2_, ...), custom_call_target="tpu_custom_call", output_to_operand_aliasing={{0}: (5, {})} | custom-call | flops 99999997952 | bytes 1 | tf_op jit(solution)/shard_map/last_middle/pallas_call | solution.py:532
  62.1 2.6 %last_inner.1 = (bf16[136,64,256]{2,1,0:T(8,128)(2,1)S(1)}, f32[32,64,128]{2,1,0:T(8,128)S(1)}, f32[64,64,128]{2,1,0:T(8,128)}) custom-call(s32[8,64]{1,0:T(8,128)S(4)} %get-tuple-element.96.refs_0_, bf16[64,64,512]{2,1,0:T(8,128)(2,1)S(1)} %get-tuple-element.97.refs_7_.refs_1_, ...), custom_call_target="tpu_custom_call", output_to_operand_aliasing={{0}: (6, {}), {1}: (7, {}), {2}: (8, {})} | custom-call | flops 1 | bytes 1 | tf_op jit(solution)/shard_map/last_inner/pallas_call | solution.py:532
  64.8 0.0 collective-permute-done.23.refs_6_
  64.8 0.2 collective-permute-done.21.refs_4_
  64.9 2.3 %last_ends.1 = (bf16[136,64,256]{2,1,0:T(8,128)(2,1)S(1)}, f32[32,64,128]{2,1,0:T(8,128)}) custom-call(s32[8,64]{1,0:T(8,128)S(4)} %get-tuple-element.96.refs_0_, bf16[64,64,512]{2,1,0:T(8,128)(2,1)S(1)} %get-tuple-element.97.refs_7_.refs_1_, bf16[64,64,128]{2,1,0:T(8,128)(2,1)S(1)} %get-tuple-element.84.refs_6_.refs_2_, ...), custom_call_target="tpu_custom_call", output_to_operand_aliasing={{0}: (7, {})} | custom-call | flops 1 | bytes 1 | tf_op jit(solution)/shard_map/last_ends/pallas_call | solution.py:532
  (20 shorter events, 0.0 us)
Async XLA Ops:
  3.2 11.7 %collective-permute-start.4 = (f32[16,64,128]{2,1,0:T(8,128)S(1)}, f32[16,64,128]{2,1,0:T(8,128)S(1)}, u32[]{:S(2)}, u32[]{:S(2)}) collective-permute-start(f32[16,64,128]{2,1,0:T(8,128)S(1)} %get-tuple-element.82), channel_id=1, source_target_pairs={{0,2},{1,3},{2,0},{3,1},{4,6},{5,7},{6,4},{7,5},{8,16},{9,17},{10,... | collective-permute-start | bytes 1572872 | tf_op jit(solution)/shard_map/ppermute | solution.py:592
  6.3 4.9 %copy-start = (bf16[128,64,4,64]{0,3,2,1:T(8,128)(2,1)S(1)}, bf16[128,64,4,64]{0,3,2,1:T(8,128)(2,1)}, u32[]{:S(2)}) copy-start(bf16[128,64,4,64]{0,3,2,1:T(8,128)(2,1)} %param.9) | copy-start | bytes 12582916
  6.3 4.9 %copy-start.1 = (bf16[128,64,64]{0,2,1:T(8,128)(2,1)S(1)}, bf16[128,64,64]{0,2,1:T(8,128)(2,1)}, u32[]{:S(2)}) copy-start(bf16[128,64,64]{0,2,1:T(8,128)(2,1)} %param.11) | copy-start | bytes 3145732
  6.3 4.9 %copy-start.2 = (bf16[128,64,64]{0,2,1:T(8,128)(2,1)S(1)}, bf16[128,64,64]{0,2,1:T(8,128)(2,1)}, u32[]{:S(2)}) copy-start(bf16[128,64,64]{0,2,1:T(8,128)(2,1)} %param.10) | copy-start | bytes 3145732
  7.6 7.1 %collective-permute-start.2 = (f32[4,64,128]{2,1,0:T(8,128)S(1)}, f32[4,64,128]{2,1,0:T(8,128)S(1)}, u32[]{:S(2)}, u32[]{:S(2)}) collective-permute-start(f32[4,64,128]{2,1,0:T(8,128)S(1)} %get-tuple-element.80), channel_id=1, source_target_pairs={{0,1},{1,0},{2,3},{3,2},{4,5},{5,4},{6,7},{7,6},{8,9},{9,8},{10,11... | collective-permute-start | bytes 393224 | tf_op jit(solution)/shard_map/ppermute | solution.py:598
  9.2 5.5 %collective-permute-start.3 = (f32[4,64,128]{2,1,0:T(8,128)S(1)}, f32[4,64,128]{2,1,0:T(8,128)S(1)}, u32[]{:S(2)}, u32[]{:S(2)}) collective-permute-start(f32[4,64,128]{2,1,0:T(8,128)S(1)} %get-tuple-element.81), channel_id=1, source_target_pairs={{0,8},{1,2},{2,1},{3,4},{4,3},{5,6},{6,5},{7,15},{8,0},{9,10},{10,... | collective-permute-start | bytes 393224 | tf_op jit(solution)/shard_map/ppermute | solution.py:601
  9.2 15.6 %collective-permute-start = (f32[16,64,128]{2,1,0:T(8,128)S(1)}, f32[16,64,128]{2,1,0:T(8,128)S(1)}, u32[]{:S(2)}, u32[]{:S(2)}) collective-permute-start(f32[16,64,128]{2,1,0:T(8,128)S(1)} %get-tuple-element.79), channel_id=1, source_target_pairs={{0,2},{1,3},{2,0},{3,1},{4,6},{5,7},{6,4},{7,5},{8,16},{9,17},{10,... | collective-permute-start | bytes 1572872 | tf_op jit(solution)/shard_map/ppermute | solution.py:592
  11.2 9.0 %collective-permute-start.1 = (f32[32,64,128]{2,1,0:T(8,128)S(1)}, f32[32,64,128]{2,1,0:T(8,128)S(1)}, u32[]{:S(2)}, u32[]{:S(2)}) collective-permute-start(f32[32,64,128]{2,1,0:T(8,128)S(1)} %get-tuple-element.78.refs_4_), channel_id=1, source_target_pairs={{0,8},{1,9},{2,10},{3,11},{4,12},{5,13},{6,14},{7,15},{8,0},{9,1},... | collective-permute-start | bytes 3145736 | tf_op jit(solution)/shard_map/ppermute | solution.py:595
  11.2 2.6 %copy-start.3 = (bf16[64,64,64]{2,1,0:T(8,128)(2,1)S(1)}, bf16[64,64,64]{2,1,0:T(8,128)(2,1)}, u32[]{:S(2)}) copy-start(bf16[64,64,64]{2,1,0:T(8,128)(2,1)} %refs_0_.3) | copy-start | bytes 1572868
  11.2 2.6 %copy-start.4 = (bf16[64,64,64]{2,1,0:T(8,128)(2,1)S(1)}, bf16[64,64,64]{2,1,0:T(8,128)(2,1)}, u32[]{:S(2)}) copy-start(bf16[64,64,64]{2,1,0:T(8,128)(2,1)} %refs_1_.1) | copy-start | bytes 1572868
  11.2 2.6 %copy-start.5 = (s32[64,8]{0,1:T(8,128)S(1)}, s32[64,8]{0,1:T(8,128)}, u32[]{:S(2)}) copy-start(s32[64,8]{0,1:T(8,128)} %param.15) | copy-start | bytes 6148
  15.7 16.9 %collective-permute-start.9 = (f32[16,64,128]{2,1,0:T(8,128)S(1)}, f32[16,64,128]{2,1,0:T(8,128)S(1)}, u32[]{:S(2)}, u32[]{:S(2)}) collective-permute-start(f32[16,64,128]{2,1,0:T(8,128)S(1)} %get-tuple-element.103), channel_id=1, source_target_pairs={{0,2},{1,3},{2,0},{3,1},{4,6},{5,7},{6,4},{7,5},{8,16},{9,17},{10,... | collective-permute-start | bytes 1572872 | tf_op jit(solution)/shard_map/ppermute | solution.py:592
  24.8 4.5 %slice-start = ((s8[8388608]{0:T(1024)(128)(4,1)}), s8[4194304]{0:T(1024)(128)(4,1)S(1)}, s32[]{:S(2)}) async-start(s8[8388608]{0:T(1024)(128)(4,1)} %bitcast.6), calls=%async_computation | async-start | bytes 8388608
  24.8 4.5 %slice-start.1 = ((s8[8388608]{0:T(1024)(128)(4,1)}), s8[4194304]{0:T(1024)(128)(4,1)S(1)}, s32[]{:S(2)}) async-start(s8[8388608]{0:T(1024)(128)(4,1)} %bitcast.6), calls=%async_computation.1 | async-start | bytes 8388608
  25.7 6.9 %collective-permute-start.7 = (f32[4,64,128]{2,1,0:T(8,128)S(1)}, f32[4,64,128]{2,1,0:T(8,128)S(1)}, u32[]{:S(2)}, u32[]{:S(2)}) collective-permute-start(f32[4,64,128]{2,1,0:T(8,128)S(1)} %get-tuple-element.101), channel_id=1, source_target_pairs={{0,1},{1,0},{2,3},{3,2},{4,5},{5,4},{6,7},{7,6},{8,9},{9,8},{10,11... | collective-permute-start | bytes 393224 | tf_op jit(solution)/shard_map/ppermute | solution.py:598
  25.8 6.8 %collective-permute-start.8 = (f32[4,64,128]{2,1,0:T(8,128)S(1)}, f32[4,64,128]{2,1,0:T(8,128)S(1)}, u32[]{:S(2)}, u32[]{:S(2)}) collective-permute-start(f32[4,64,128]{2,1,0:T(8,128)S(1)} %get-tuple-element.102), channel_id=1, source_target_pairs={{0,8},{1,2},{2,1},{3,4},{4,3},{5,6},{6,5},{7,15},{8,0},{9,10},{10,... | collective-permute-start | bytes 393224 | tf_op jit(solution)/shard_map/ppermute | solution.py:601
  25.9 12.0 %collective-permute-start.5 = (f32[16,64,128]{2,1,0:T(8,128)S(1)}, f32[16,64,128]{2,1,0:T(8,128)S(1)}, u32[]{:S(2)}, u32[]{:S(2)}) collective-permute-start(f32[16,64,128]{2,1,0:T(8,128)S(1)} %get-tuple-element.99), channel_id=1, source_target_pairs={{0,2},{1,3},{2,0},{3,1},{4,6},{5,7},{6,4},{7,5},{8,16},{9,17},{10,... | collective-permute-start | bytes 1572872 | tf_op jit(solution)/shard_map/ppermute | solution.py:592
  29.3 8.6 %collective-permute-start.6 = (f32[32,64,128]{2,1,0:T(8,128)S(1)}, f32[32,64,128]{2,1,0:T(8,128)S(1)}, u32[]{:S(2)}, u32[]{:S(2)}) collective-permute-start(f32[32,64,128]{2,1,0:T(8,128)S(1)} %get-tuple-element.100), channel_id=1, source_target_pairs={{0,8},{1,9},{2,10},{3,11},{4,12},{5,13},{6,14},{7,15},{8,0},{9,1},... | collective-permute-start | bytes 3145736 | tf_op jit(solution)/shard_map/ppermute | solution.py:595
  33.8 13.2 %collective-permute-start.16 = (f32[16,64,128]{2,1,0:T(8,128)S(1)}, f32[16,64,128]{2,1,0:T(8,128)S(1)}, u32[]{:S(2)}, u32[]{:S(2)}) collective-permute-start(f32[16,64,128]{2,1,0:T(8,128)S(1)} %get-tuple-element.118), channel_id=1, source_target_pairs={{0,2},{1,3},{2,0},{3,1},{4,6},{5,7},{6,4},{7,5},{8,16},{9,17},{10,... | collective-permute-start | bytes 1572872 | tf_op jit(solution)/shard_map/ppermute | solution.py:592
  39.6 6.0 %collective-permute-start.11 = (f32[2,64,128]{2,1,0:T(8,128)S(1)}, f32[2,64,128]{2,1,0:T(8,128)S(1)}, u32[]{:S(2)}, u32[]{:S(2)}) collective-permute-start(f32[2,64,128]{2,1,0:T(8,128)S(1)} %get-tuple-element.109), channel_id=1, source_target_pairs={{0,1},{1,0},{2,3},{3,2},{4,5},{5,4},{6,7},{7,6},{8,9},{9,8},{10,11... | collective-permute-start | bytes 196616 | tf_op jit(solution)/shard_map/ppermute | solution.py:598
  39.7 5.9 %collective-permute-start.12 = (f32[2,64,128]{2,1,0:T(8,128)S(1)}, f32[2,64,128]{2,1,0:T(8,128)S(1)}, u32[]{:S(2)}, u32[]{:S(2)}) collective-permute-start(f32[2,64,128]{2,1,0:T(8,128)S(1)} %get-tuple-element.110), channel_id=1, source_target_pairs={{0,8},{1,2},{2,1},{3,4},{4,3},{5,6},{6,5},{7,15},{8,0},{9,10},{10,... | collective-permute-start | bytes 196616 | tf_op jit(solution)/shard_map/ppermute | solution.py:601
  39.8 11.3 %collective-permute-start.10 = (f32[16,64,128]{2,1,0:T(8,128)S(1)}, f32[16,64,128]{2,1,0:T(8,128)S(1)}, u32[]{:S(2)}, u32[]{:S(2)}) collective-permute-start(f32[16,64,128]{2,1,0:T(8,128)S(1)} %get-tuple-element.108), channel_id=1, source_target_pairs={{0,2},{1,3},{2,0},{3,1},{4,6},{5,7},{6,4},{7,5},{8,16},{9,17},{10,... | collective-permute-start | bytes 1572872 | tf_op jit(solution)/shard_map/ppermute | solution.py:592
  45.5 5.5 %collective-permute-start.14 = (f32[32,64,128]{2,1,0:T(8,128)S(1)}, f32[32,64,128]{2,1,0:T(8,128)S(1)}, u32[]{:S(2)}, u32[]{:S(2)}) collective-permute-start(f32[32,64,128]{2,1,0:T(8,128)S(1)} %get-tuple-element.116), channel_id=1, source_target_pairs={{0,8},{1,9},{2,10},{3,11},{4,12},{5,13},{6,14},{7,15},{8,0},{9,1},... | collective-permute-start | bytes 3145736 | tf_op jit(solution)/shard_map/ppermute | solution.py:595
  45.7 4.3 %collective-permute-start.13 = (f32[2,64,128]{2,1,0:T(8,128)S(1)}, f32[2,64,128]{2,1,0:T(8,128)S(1)}, u32[]{:S(2)}, u32[]{:S(2)}) collective-permute-start(f32[2,64,128]{2,1,0:T(8,128)S(1)} %get-tuple-element.115), channel_id=1, source_target_pairs={{0,1},{1,0},{2,3},{3,2},{4,5},{5,4},{6,7},{7,6},{8,16},{9,17},{10,... | collective-permute-start | bytes 196616 | tf_op jit(solution)/shard_map/ppermute | solution.py:724
  47.0 3.0 %collective-permute-start.15 = (f32[2,64,128]{2,1,0:T(8,128)S(1)}, f32[2,64,128]{2,1,0:T(8,128)S(1)}, u32[]{:S(2)}, u32[]{:S(2)}) collective-permute-start(f32[2,64,128]{2,1,0:T(8,128)S(1)} %get-tuple-element.117), channel_id=1, source_target_pairs={{0,8},{1,9},{2,10},{3,11},{4,12},{5,13},{6,14},{7,15},{8,0},{9,1},... | collective-permute-start | bytes 196616 | tf_op jit(solution)/shard_map/ppermute | solution.py:595
  48.1 13.1 %collective-permute-start.18 = (f32[14,64,128]{2,1,0:T(8,128)S(1)}, f32[14,64,128]{2,1,0:T(8,128)S(1)}, u32[]{:S(2)}, u32[]{:S(2)}) collective-permute-start(f32[14,64,128]{2,1,0:T(8,128)S(1)} %get-tuple-element.132), channel_id=1, source_target_pairs={{0,2},{1,3},{2,0},{3,1},{4,6},{5,7},{6,4},{7,5},{8,16},{9,17},{10,... | collective-permute-start | bytes 1376264 | tf_op jit(solution)/shard_map/ppermute | solution.py:592
  52.8 6.3 %collective-permute-start.19 = (f32[2,64,128]{2,1,0:T(8,128)S(1)}, f32[2,64,128]{2,1,0:T(8,128)S(1)}, u32[]{:S(2)}, u32[]{:S(2)}) collective-permute-start(f32[2,64,128]{2,1,0:T(8,128)S(1)} %get-tuple-element.133), channel_id=1, source_target_pairs={{0,1},{1,0},{2,3},{3,2},{4,5},{5,4},{6,7},{7,6},{8,9},{9,8},{10,11... | collective-permute-start | bytes 196616 | tf_op jit(solution)/shard_map/ppermute | solution.py:598
  54.0 5.2 %collective-permute-start.20 = (f32[2,64,128]{2,1,0:T(8,128)S(1)}, f32[2,64,128]{2,1,0:T(8,128)S(1)}, u32[]{:S(2)}, u32[]{:S(2)}) collective-permute-start(f32[2,64,128]{2,1,0:T(8,128)S(1)} %get-tuple-element.134), channel_id=1, source_target_pairs={{0,8},{1,2},{2,1},{3,4},{4,3},{5,6},{6,5},{7,15},{8,0},{9,10},{10,... | collective-permute-start | bytes 196616 | tf_op jit(solution)/shard_map/ppermute | solution.py:601
  54.0 10.9 %collective-permute-start.21 = (f32[18,64,128]{2,1,0:T(8,128)S(1)}, f32[18,64,128]{2,1,0:T(8,128)S(1)}, u32[]{:S(2)}, u32[]{:S(2)}) collective-permute-start(f32[18,64,128]{2,1,0:T(8,128)S(1)} %get-tuple-element.141), channel_id=1, source_target_pairs={{0,2},{1,3},{2,0},{3,1},{4,6},{5,7},{6,4},{7,5},{8,16},{9,17},{10,... | collective-permute-start | bytes 1769480 | tf_op jit(solution)/shard_map/ppermute | solution.py:592
  59.0 3.1 %collective-permute-start.17 = (f32[32,64,128]{2,1,0:T(8,128)S(1)}, f32[32,64,128]{2,1,0:T(8,128)S(1)}, u32[]{:S(2)}, u32[]{:S(2)}) collective-permute-start(f32[32,64,128]{2,1,0:T(8,128)S(1)} %get-tuple-element.130), channel_id=1, source_target_pairs={{0,8},{1,9},{2,10},{3,11},{4,12},{5,13},{6,14},{7,15},{8,0},{9,1},... | collective-permute-start | bytes 3145736 | tf_op jit(solution)/shard_map/ppermute | solution.py:595
  59.2 5.5 %collective-permute-start.22 = (f32[2,64,128]{2,1,0:T(8,128)S(1)}, f32[2,64,128]{2,1,0:T(8,128)S(1)}, u32[]{:S(2)}, u32[]{:S(2)}) collective-permute-start(f32[2,64,128]{2,1,0:T(8,128)S(1)} %get-tuple-element.142), channel_id=1, source_target_pairs={{0,1},{1,0},{2,3},{3,2},{4,5},{5,4},{6,7},{7,6},{8,16},{9,17},{10,... | collective-permute-start | bytes 196616 | tf_op jit(solution)/shard_map/ppermute | solution.py:769
  61.3 3.5 %collective-permute-start.23 = (f32[2,64,128]{2,1,0:T(8,128)S(1)}, f32[2,64,128]{2,1,0:T(8,128)S(1)}, u32[]{:S(2)}, u32[]{:S(2)}) collective-permute-start(f32[2,64,128]{2,1,0:T(8,128)S(1)} %get-tuple-element.143), channel_id=1, source_target_pairs={{0,8},{1,9},{2,10},{3,11},{4,12},{5,13},{6,14},{7,15},{8,0},{9,1},... | collective-permute-start | bytes 196616 | tf_op jit(solution)/shard_map/ppermute | solution.py:595

commit v4 on v3

--- a/solution.py
+++ b/solution.py
@@ -64,7 +64,7 @@
             partner = a - 1 if a % 2 == 0 else a + 1
             if 0 <= partner < rows:
                 pairs.append((a * cols + b, partner * cols + b))
-            else:
+            elif hop:
                 pairs.append((a * cols + b, a * cols + (b ^ hop)))
     return pairs
 
@@ -139,16 +139,6 @@
     lax.fori_loop(first, last, step, 0)
 
 
-def stretches(cols):
-    found = []
-    for n, q in enumerate(cols):
-        if found and found[-1][1] + found[-1][2] == q:
-            found[-1][2] += 1
-        else:
-            found.append([n, q, 1])
-    return found
-
-
 def with_zeros(own, after):
     none = jnp.zeros(own.shape, BF16)
     return jnp.concatenate([own, none] if after else [none, own], axis=0)
@@ -175,15 +165,19 @@
 
 
 def fine_second(rho, cols, blocks, grid, side, change, iterate, first, far=None):
-    for q in cols:
+    fine_cells([(rho, q, first + q) for q in cols], blocks, grid, side, change, iterate, far)
+
+
+def fine_cells(cells, blocks, grid, side, change, iterate, far=None):
+    for rho, q, _ in cells:
         cell = fine_cell(rho, q)
         side[cell] = side[cell] - fine_apply(rho, q, blocks, grid)
-    for m, q in enumerate(cols):
+    for m, (rho, q, n) in enumerate(cells):
         cell = fine_cell(rho, q)
         here = spot(rho, q)
         step = smoothed(blocks, cell, side[cell])
         change[here] = split(step)
-        iterate[first + q] = fold(grid[here]) + step
+        iterate[n] = fold(grid[here]) + step
         if far is not None:
             far[m] = step
 
@@ -234,7 +228,7 @@
     read_sides(grid, even, odd, BLOCK_X)
 
 
-def fine_blocks_kernel(coupling, diagonal, inverse, blocks_in, blocks):
+def fine_blocks_kernel(coupling, diagonal, inverse, blocks_in, near_in, blocks, near):
     species = coupling.shape[0]
     part = species // 2
     for first in range(0, species, part):
@@ -244,36 +238,46 @@
         blocks[:, rows, 4 * species :] = jnp.transpose(both, (2, 0, 1))
 
 
-def fine_inner_kernel(
-    blocks, near_h, even_h, odd_h, grid_in, side_in, change_in, grid, side, change, out, last, near, made, sems
+def fine_inner_kernel(blocks, grid, side_in, side, change, held):
+    for rho in range(1, BLOCK_X - 1):
+        fine_second(rho, INSIDE, blocks, grid, side, change, held, (rho - 1) * BLOCK_Y)
+
+
+def fine_middle_kernel(cols, blocks, far_h, grid_in, side_in, change_in, grid, side, change, iterate, far):
+    write_row(grid, far_h, -1, cols, far_is_inside())
+    fine_second(0, cols, blocks, grid, side, change, iterate, 0, far)
+
+
+def fine_last_kernel(
+    blocks, near_h, even_h, odd_h, grid_in, side_in, change_in, grid, side, change, last, near
 ):
     write_row(grid, near_h, BLOCK_X, range(BLOCK_Y))
     write_sides(grid, even_h, odd_h, BLOCK_X)
-
-    def leave(rho):
-        source = made.at[pl.ds((rho - 1) * BLOCK_Y, BLOCK_Y)]
-        return pltpu.make_async_copy(source, out.at[pl.ds(fine_cell(rho, 0), BLOCK_Y)], sems.at[rho - 1])
-
-    def body(rho):
-        fine_second(rho, range(BLOCK_Y), blocks, grid, side, change, made, (rho - 1) * BLOCK_Y)
-        leave(rho).start()
-
-    over_rows(1, BLOCK_X - 1, body)
     fine_second(BLOCK_X - 1, range(BLOCK_Y), blocks, grid, side, change, last, 0, near)
-    for rho in range(1, BLOCK_X - 1):
-        leave(rho).wait()
-
-
-def fine_middle_kernel(cols, blocks, far_h, grid_in, side_in, grid, side, change, iterate, far):
-    write_row(grid, far_h, -1, cols, far_is_inside())
-    fine_second(0, cols, blocks, grid, side, change, iterate, 0, far)
 
 
 def fine_ends_kernel(
-    cols, blocks, far_h, grid_in, side_in, change_in, iterate_in, grid, side, change, iterate, far, even, odd
+    cols,
+    blocks,
+    far_h,
+    grid_in,
+    side_in,
+    change_in,
+    iterate_in,
+    held_in,
+    grid,
+    side,
+    change,
+    iterate,
+    held,
+    far,
+    even,
+    odd,
 ):
     write_row(grid, far_h, -1, cols, far_is_inside())
     fine_second(0, cols, blocks, grid, side, change, iterate, 0, far)
+    others = [(rho, q, (rho - 1) * BLOCK_Y + q) for rho in range(1, BLOCK_X - 1) for q in SIDES]
+    fine_cells(others, blocks, grid, side, change, held)
     read_sides(change, even, odd, BLOCK_X)
 
 
@@ -294,15 +298,17 @@
     left_pair(0, cols, blocks, side, change, coarse_side, own_blocks, coarse_grid, far)
 
 
+def left_halo_kernel(near_h, even_h, odd_h, change_in, change):
+    write_row(change, near_h, BLOCK_X, range(BLOCK_Y))
+    write_sides(change, even_h, odd_h, BLOCK_X)
+
+
 def left_ends_kernel(
     cols,
     blocks,
     side,
     own_blocks,
     far_h,
-    near_h,
-    even_h,
-    odd_h,
     change_in,
     coarse_in,
     grid_in,
@@ -314,8 +320,6 @@
     odd,
 ):
     write_row(change, far_h, -1, cols, far_is_inside())
-    write_row(change, near_h, BLOCK_X, range(BLOCK_Y))
-    write_sides(change, even_h, odd_h, BLOCK_X)
     left_pair(0, cols, blocks, side, change, coarse_side, own_blocks, coarse_grid, far)
     for rho in range(1, COARSE_X):
         left_pair(rho, SIDES, blocks, side, change, coarse_side, own_blocks, coarse_grid)
@@ -330,13 +334,16 @@
         near[q] = fold(coarse_grid[spot(COARSE_X - 1, q)])
 
 
-def near_blocks_kernel(coupling, first_row, last_row, out_in, blocks, out, sems):
+def near_blocks_kernel(coupling, first_row, held, last_row, blocks, out, sems):
     species = coupling.shape[1]
     step, count = pl.program_id(0), coupling.shape[0]
     copies = []
-    for n, (rho, source) in enumerate(((0, first_row), (BLOCK_X - 1, last_row))):
+    for rho in range(BLOCK_X):
+        source = first_row if rho == 0 else last_row
+        if 0 < rho < BLOCK_X - 1:
+            source = held.at[pl.ds((rho - 1) * BLOCK_Y, BLOCK_Y)]
         target = out.at[pl.ds(fine_cell(rho, 0), BLOCK_Y)]
-        copies.append(pltpu.make_async_copy(source, target, sems.at[n]))
+        copies.append(pltpu.make_async_copy(source, target, sems.at[rho]))
 
     @pl.when(step == 0)
     def _():
@@ -396,11 +403,28 @@
     leave.wait()
 
 
+def coarse_halo_kernel(near_h, beside_h, grid_in, grid):
+    write_row(grid, near_h, COARSE_X, range(BLOCK_Y))
+    write_row(grid, beside_h, COARSE_X, BESIDE)
+
+
 def coarse_middle_kernel(
     came, cols, places, blocks, own_blocks, far_h, grid_in, side_in, grid, side, change, iterate, far
 ):
     write_row(grid, far_h, -1, came)
     coarse_second(0, cols, places, blocks, own_blocks, grid, side, change, iterate, far)
+
+
+class InTwo:
+    def __init__(self, low, high):
+        self.low, self.high = low, high
+
+    def __setitem__(self, n, value):
+        count = self.low.shape[0]
+        if n < count:
+            self.low[n] = value
+        else:
+            self.high[n - count] = value
 
 
 def coarse_ends_kernel(
@@ -411,8 +435,6 @@
     own_blocks,
     far_h,
     corners_h,
-    near_h,
-    beside_h,
     grid_in,
     side_in,
     change_in,
@@ -421,14 +443,14 @@
     side,
     change,
     iterate,
-    far,
+    low,
+    high,
     even,
     odd,
 ):
+    far = InTwo(low, high)
     write_row(grid, far_h, -1, came)
     write_row(grid, corners_h, -1, BESIDE)
-    write_row(grid, near_h, COARSE_X, range(BLOCK_Y))
-    write_row(grid, beside_h, COARSE_X, BESIDE)
     coarse_second(0, cols, places, blocks, own_blocks, grid, side, change, iterate, far)
     for rho in range(1, COARSE_X):
         coarse_second(rho, SIDES, places, blocks, own_blocks, grid, side, change, iterate)
@@ -463,41 +485,35 @@
         copy.wait()
 
 
-def last_ends_kernel(
-    came,
-    done,
-    todo,
-    places,
-    blocks,
-    own_blocks,
-    side,
-    far_h,
-    corners_h,
-    beside_h,
-    change_in,
-    below,
-    change,
-    out,
-    made,
-    sems,
+def last_sides_kernel(todo, places, blocks, own_blocks, side, beside_h, change_in, below_in, change, below):
+    write_row(change, beside_h, COARSE_X, BESIDE)
+    for rho in range(1, COARSE_X):
+        last_pairs(rho, todo, places, blocks, own_blocks, side, change, below)
+
+
+def last_low_kernel(
+    came, todo, places, blocks, own_blocks, side, far_h, corners_h, change_in, below_in, change, below
 ):
+    write_row(change, far_h, -1, came)
+    write_row(change, corners_h, -1, BESIDE)
+    last_pairs(0, todo, places, blocks, own_blocks, side, change, below)
+
+
+def last_high_kernel(came, todo, places, blocks, own_blocks, side, far_h, change_in, below, change, out, made, sems):
+    half = BLOCK_Y // 2
     copies = []
 
     def send(source, rho, first, count):
-        some = pl.ds(place(rho, COARSE_X) * (BLOCK_Y // 2) + first, count)
+        some = pl.ds(place(rho, COARSE_X) * half + first, count)
         copies.append(pltpu.make_async_copy(source.at[some], out.at[some], sems.at[len(copies)]))
         copies[-1].start()
 
-    for rho in range(COARSE_X):
-        for _, first, count in stretches(done[rho]):
-            send(below, rho, first, count)
+    for rho in range(1, COARSE_X):
+        send(below, rho, 0, half)
+    send(below, 0, 0, todo[0])
     write_row(change, far_h, -1, came)
-    write_row(change, corners_h, -1, BESIDE)
-    write_row(change, beside_h, COARSE_X, BESIDE)
-    for rho in reversed(range(COARSE_X)):
-        for _, first, count in stretches(todo[rho]):
-            last_pairs(rho, range(first, first + count), places, blocks, own_blocks, side, change, made)
-            send(made, rho, first, count)
+    last_pairs(0, todo, places, blocks, own_blocks, side, change, made)
+    send(made, 0, todo[0], len(todo))
     for copy in copies:
         copy.wait()
 
@@ -532,27 +548,29 @@
     return called(*(pltpu.with_memory_space_constraint(x, space) for x, space in zip(args, spaces)))
 
 
-def near_blocks_call(coupling, first_row, last_row, out):
+def near_blocks_call(coupling, first_row, held, last_row, count):
     cells, species = coupling.shape[:2]
     part = cells // 8
-    here = [pltpu.with_memory_space_constraint(x, pltpu.VMEM) for x in (first_row, last_row)]
+    here = [pltpu.with_memory_space_constraint(x, pltpu.VMEM) for x in (first_row, held, last_row)]
     return pl.pallas_call(
         near_blocks_kernel,
         grid=(cells // part,),
-        out_shape=(pltpu.VMEM((cells, species, 8 * species), BF16), pltpu.HBM(out.shape, out.dtype)),
+        out_shape=(
+            pltpu.VMEM((cells, species, 8 * species), BF16),
+            pltpu.HBM((count,) + first_row.shape[1:], F32),
+        ),
         in_specs=[
             pl.BlockSpec((part,) + coupling.shape[1:], lambda n: (n, 0, 0, 0)),
             IN_VMEM,
             IN_VMEM,
-            IN_HBM,
+            IN_VMEM,
         ],
         out_specs=(IN_VMEM, IN_HBM),
-        scratch_shapes=[pltpu.SemaphoreType.DMA((2,))],
-        input_output_aliases={3: 1},
+        scratch_shapes=[pltpu.SemaphoreType.DMA((BLOCK_X,))],
         compiler_params=pltpu.CompilerParams(vmem_limit_bytes=5 * 2**20),
         cost_estimate=pl.CostEstimate(flops=1, bytes_accessed=1, transcendentals=0),
         name="near_blocks",
-    )(coupling, *here, pltpu.with_memory_space_constraint(out, pltpu.HBM))
+    )(coupling, *here)
 
 
 def own_blocks_kernel(across, diagonal, inverse, pattern, blocks, places, made, sem):
@@ -622,7 +640,7 @@
         scratch=[pltpu.VMEM(inverse.shape, BF16), pltpu.SemaphoreType.DMA((2 + BLOCK_X,))],
         room=6,
     )
-    far_m, far_n = far(far_m), far(far_n)
+    far_m, far_n = lax.ppermute(far_m, BOTH, swap_far(rows, cols, 0)), far(far_n)
     grid, near_s, even_s, odd_s = run(
         "first",
         first_kernel,
@@ -630,15 +648,49 @@
         [side, blocks, grid],
         [(2, 0)],
     )
-    near_h, even_h, odd_h = near(near_s), even(even_s), odd(odd_s)
-    (blocks,) = run(
+    even_h, odd_h = even(even_s), odd(odd_s)
+    blocks, near_s = run(
         "fine_blocks",
         fine_blocks_kernel,
-        [fine_blocks],
-        [coupling, diagonal, inverse, blocks],
-        [(3, 0)],
-        after=[near_s],
+        [fine_blocks, field(BLOCK_Y)],
+        [coupling, diagonal, inverse, blocks, near_s],
+        [(3, 0), (4, 1)],
         room=6,
+    )
+    near_h = near(near_s)
+    state = [padded(BLOCK_X), field(cells), padded(BLOCK_X)]
+    side, change, held = run(
+        "fine_inner",
+        fine_inner_kernel,
+        state[1:] + [field((BLOCK_X - 2) * BLOCK_Y)],
+        [blocks, grid, side],
+        [(2, 0)],
+    )
+    grid, side, change, iterate, far_m = run(
+        "fine_middle",
+        functools.partial(fine_middle_kernel, MIDDLE),
+        state + [field(BLOCK_Y), field(middle)],
+        [blocks, far_m, grid, side, change],
+        [(2, 0), (3, 1), (4, 2)],
+        after=[even_h, odd_h],
+        cost=LONG,
+    )
+    far_m = far(far_m)
+    grid, side, change, last_row, near_s = run(
+        "fine_last",
+        fine_last_kernel,
+        state + [field(BLOCK_Y), field(BLOCK_Y)],
+        [blocks, near_h, even_h, odd_h, grid, side, change],
+        [(4, 0), (5, 1), (6, 2)],
+    )
+    near_h = near(near_s)
+    grid, side, change, iterate, held, far_n, even_s, odd_s = run(
+        "fine_ends",
+        functools.partial(fine_ends_kernel, ENDS),
+        state
+        + [field(BLOCK_Y), field((BLOCK_X - 2) * BLOCK_Y), field(ends), field(BLOCK_X), field(BLOCK_X)],
+        [blocks, far_n, grid, side, change, iterate, held],
+        [(2, 0), (3, 1), (4, 2), (5, 3), (6, 4)],
     )
     own_blocks, places = run(
         "own_blocks",
@@ -647,41 +699,9 @@
         [coarse_diagonal, coarse_inverse, pattern],
         smem_outs=(1,),
         scratch=[pltpu.VMEM(pattern.shape, jnp.int32), pltpu.SemaphoreType.DMA],
-        after=[blocks],
-    )
-    state = [padded(BLOCK_X), field(cells), padded(BLOCK_X)]
-    grid, side, change, iterate, far_m = run(
-        "fine_middle",
-        functools.partial(fine_middle_kernel, MIDDLE),
-        state + [field(BLOCK_Y), field(middle)],
-        [blocks, far_m, grid, side],
-        [(2, 0), (3, 1)],
-        after=[even_h, odd_h, own_blocks],
-        cost=LONG,
-    )
-    far_m = far(far_m)
-    grid, side, change, fine_iterate, last_row, near_s = run(
-        "fine_inner",
-        fine_inner_kernel,
-        state + [field(cells), field(BLOCK_Y), field(BLOCK_Y)],
-        [blocks, near_h, even_h, odd_h, grid, side, change],
-        [(4, 0), (5, 1), (6, 2)],
-        hbm_outs=(3,),
-        scratch=[
-            pltpu.VMEM(((BLOCK_X - 2) * BLOCK_Y, species, vectors), F32),
-            pltpu.SemaphoreType.DMA((BLOCK_X - 2,)),
-        ],
-        room=4,
-    )
-    near_h = near(near_s)
-    grid, side, change, iterate, far_n, even_s, odd_s = run(
-        "fine_ends",
-        functools.partial(fine_ends_kernel, ENDS),
-        state + [field(BLOCK_Y), field(ends), field(BLOCK_X), field(BLOCK_X)],
-        [blocks, far_n, grid, side, change, iterate],
-        [(2, 0), (3, 1), (4, 2), (5, 3)],
-    )
-    near_blocks, fine_iterate = near_blocks_call(coarse_coupling, iterate, last_row, fine_iterate)
+        after=[far_n],
+    )
+    near_blocks, fine_iterate = near_blocks_call(coarse_coupling, iterate, held, last_row, cells)
     far_n = far(far_n)
     even_h, odd_h = even(even_s), odd(odd_s)
 
@@ -696,12 +716,15 @@
         cost=LONG,
     )
     far_m = far(far_m)
+    (change,) = run(
+        "left_halo", left_halo_kernel, [padded(BLOCK_X)], [near_h, even_h, odd_h, change], [(3, 0)]
+    )
     change, coarse_side, coarse_grid, far_n, even_s, odd_s = run(
         "left_ends",
         functools.partial(left_ends_kernel, ENDS),
         state + [field(ends), field(COARSE_X), field(COARSE_X)],
-        [blocks, side, own_blocks, far_n, near_h, even_h, odd_h, change, coarse_side, coarse_grid],
-        [(7, 0), (8, 1), (9, 2)],
+        [blocks, side, own_blocks, far_n, change, coarse_side, coarse_grid],
+        [(4, 0), (5, 1), (6, 2)],
         cost=LONG,
     )
     coarse_side, coarse_grid, near_s = run(
@@ -736,13 +759,16 @@
         cost=LONG,
     )
     far_m = far(far_m)
-    coarse_grid, coarse_side, coarse_change, iterate, far_n, even_s, odd_s = run(
+    (coarse_grid,) = run(
+        "coarse_halo", coarse_halo_kernel, [padded(COARSE_X)], [near_h, beside, coarse_grid], [(2, 0)]
+    )
+    low, high = (tuple(q for q in outer if (q < inner[0]) == first) for first in (True, False))
+    coarse_grid, coarse_side, coarse_change, iterate, far_low, far_high, even_s, odd_s = run(
         "coarse_ends",
         functools.partial(coarse_ends_kernel, ENDS, outer),
-        state + [field(len(outer)), field(COARSE_X), field(COARSE_X)],
-        [places, near_blocks, own_blocks, far_n, corners, near_h, beside]
-        + [coarse_grid, coarse_side, coarse_change, iterate],
-        [(7, 0), (8, 1), (9, 2), (10, 3)],
+        state + [field(len(low)), field(len(high)), field(COARSE_X), field(COARSE_X)],
+        [places, near_blocks, own_blocks, far_n, corners, coarse_grid, coarse_side, coarse_change, iterate],
+        [(5, 0), (6, 1), (7, 2), (8, 3)],
         smem=(0,),
         cost=LONG,
     )
@@ -756,7 +782,7 @@
         hbm_outs=(4,),
         scratch=[pltpu.SemaphoreType.DMA],
     )
-    far_n = far(far_n)
+    far_low, far_high = far(far_low), far(far_high)
     even_h, odd_h = even(even_s), odd(odd_s)
     near_h = near(near_s)
     coarse_change, corners, beside = run(
@@ -772,7 +798,6 @@
     half = BLOCK_Y // 2
     core = tuple(q // 2 for q in inner[1:-1:2])
     pairs = tuple(range(1, half - 1))
-    todo = [tuple(q for q in range(half) if q not in core)] + [(0, half - 1)] * (COARSE_X - 1)
     coarse_change, below = run(
         "last_middle",
         functools.partial(last_middle_kernel, inner, core),
@@ -793,15 +818,31 @@
         hbm_outs=(2,),
         scratch=[pltpu.SemaphoreType.DMA((COARSE_X,))],
     )
+    coarse_change, below = run(
+        "last_sides",
+        functools.partial(last_sides_kernel, (0, half - 1)),
+        state,
+        [places, near_blocks, own_blocks, coarse_side, beside, coarse_change, below],
+        [(5, 0), (6, 1)],
+        smem=(0,),
+    )
+    coarse_change, below = run(
+        "last_low",
+        functools.partial(last_low_kernel, low, tuple(range(core[0]))),
+        state,
+        [places, near_blocks, own_blocks, coarse_side, far_low, corners, coarse_change, below],
+        [(6, 0), (7, 1)],
+        smem=(0,),
+    )
     coarse_change, next_side = run(
-        "last_ends",
-        functools.partial(last_ends_kernel, outer, [core] + [pairs] * (COARSE_X - 1), todo),
+        "last_high",
+        functools.partial(last_high_kernel, high, tuple(range(core[-1] + 1, half))),
         state,
-        [places, near_blocks, own_blocks, coarse_side, far_n, corners, beside, coarse_change, below],
-        [(7, 0)],
+        [places, near_blocks, own_blocks, coarse_side, far_high, coarse_change, below],
+        [(5, 0)],
         smem=(0,),
         hbm_outs=(1,),
-        scratch=[pltpu.VMEM(state[1][0], F32), pltpu.SemaphoreType.DMA((4 * COARSE_X,))],
+        scratch=[pltpu.VMEM(state[1][0], F32), pltpu.SemaphoreType.DMA((COARSE_X + 1,))],
         room=3,
     )
     return (fine_iterate, coarse_iterate, next_side)

time: 67.5 us -> 67.1 us (level)
  waiting for transfers between devices: 5.72 us -> 0.73 us
  starting transfers between devices: 26.8 us -> 31.3 us
    ppermute x4, starting transfers between devices: 2.86 us -> 10.7 us  [even(): return lax.ppermute(x, BOTH, even_pairs)]
    ppermute x8, starting transfers between devices: 20.2 us -> 13.1 us  [far(): return lax.ppermute(x, BOTH, far_pairs)]
    ppermute x8, waiting for transfers between devices: 4.51 us -> 0.69 us  [far(): return lax.ppermute(x, BOTH, far_pairs)]
    ppermute x4, starting transfers between devices: 0.15 us -> 2.57 us  [odd(): return lax.ppermute(x, BOTH, odd_pairs)]
    ppermute x2, waiting for transfers between devices: 1.17 us -> 0.01 us  [on_device(): corners, beside = (lax.ppermute(corners, BOTH, corner_pairs), near(beside))]
    ppermute x0 -> x1, starting transfers between devices: none -> 0.69 us  [on_device(): lax.ppermute(far_m, BOTH, swap_far(rows, cols, 0))]
    pallas_call x18 -> x23, Pallas kernels: 30.4 us -> 30.4 us  [run(): called(*(pltpu.with_memory_space_constraint(x, space) for x, space in zip...]
  transfers between devices with their start and end apart: 24 -> 25, of which waited for: 5 -> 2; matrix products, arithmetic and copies ran while one was open for 0% -> 0% of each run, Pallas kernels for 43% -> 44%
where the time goes in v4:
time: 67.1 us; the launch traced here: 66.9 us
  Pallas kernels  33.7 us (50%)
  starting transfers between devices  31.3 us (47%)
  between operations  1.19 us (2%)
  waiting for transfers between devices  0.73 us (1%)
    pallas_call x23, Pallas kernels, run(): called(*(pltpu.with_memory_space_constraint(x, space) for x, space in zip...  30.4 us
    ppermute x8, starting transfers between devices, far(): return lax.ppermute(x, BOTH, far_pairs)  13.1 us
    ppermute x4, starting transfers between devices, even(): return lax.ppermute(x, BOTH, even_pairs)  10.7 us
    ppermute x2, starting transfers between devices, on_device(): corners, beside = (lax.ppermute(corners, BOTH, corner_pairs), near(beside))  3.54 us
    pallas_call x1, Pallas kernels, near_blocks_call(): pl.pallas_call(near_blocks_kernel, grid=(cells // part,), out_shape=(pltp...  3.31 us
    ppermute x4, starting transfers between devices, odd(): return lax.ppermute(x, BOTH, odd_pairs)  2.57 us
  transfers between devices with their start and end apart: 25, of which 2 were waited for; matrix products, arithmetic and copies ran while one was open for 0% of the time, Pallas kernels for 44%

profile of v4, /device:TPU:0, one launch (start us, length us, event | category | flops | bytes accessed | tf_op | source)
XLA Modules:
  0.0 66.9 jit_solution(16322408432472145442)
XLA Ops:
  0.6 2.6 %start.1 = (bf16[128,64,384]{2,1,0:T(8,128)(2,1)S(1)}, bf16[204,64,256]{2,1,0:T(8,128)(2,1)S(1)}, f32[128,64,128]{2,1,0:T(8,128)S(1)}, f32[16,64,128]{2,1,0:T(8,128)S(1)}, f32[16,64,128]{2,1,0:T(8,128)S(1)}) custom-call(f32[128,64,128]{2,1,0:T(8,128)} %refs_0_.2, bf16[64,64,128]{2,1,0:T(8,128)(2,1)} %bitcast.9), custom_call_target="tpu_custom_call" | custom-call | flops 1 | bytes 1 | tf_op jit(solution)/shard_map/start/pallas_call | solution.py:548
  3.2 0.7 %collective-permute-start.4 = (f32[16,64,128]{2,1,0:T(8,128)S(1)}, f32[16,64,128]{2,1,0:T(8,128)S(1)}, u32[]{:S(2)}, u32[]{:S(2)}) collective-permute-start(f32[16,64,128]{2,1,0:T(8,128)S(1)} %get-tuple-element.94), channel_id=1, source_target_pairs={{8,16},{9,17},{10,18},{11,19},{12,20},{13,21},{14,22},{15,23},{16,... | collective-permute-start | bytes 1572872 | tf_op jit(solution)/shard_map/ppermute | solution.py:643
  3.9 0.0 copy-start
  3.9 0.0 copy-start.1
  3.9 0.0 copy-start.4
  3.9 1.4 %first.1 = (bf16[204,64,256]{2,1,0:T(8,128)(2,1)S(1)}, f32[32,64,128]{2,1,0:T(8,128)S(1)}, f32[4,64,128]{2,1,0:T(8,128)S(1)}, f32[4,64,128]{2,1,0:T(8,128)S(1)}) custom-call(f32[128,64,128]{2,1,0:T(8,128)S(1)} %get-tuple-element.86.refs_0_.refs_2_, bf16[128,64,384]{2,1,0:T(8,128)(2,1)S(1)} %get-tuple-element.85.refs_1_.refs_3_, ...), custom_call_target="tpu_custom_call", output_to_operand_aliasing={{0}: (2, {})} | custom-call | flops 1 | bytes 1 | tf_op jit(solution)/shard_map/first/pallas_call | solution.py:548
  5.3 3.0 %collective-permute-start.2 = (f32[4,64,128]{2,1,0:T(8,128)S(1)}, f32[4,64,128]{2,1,0:T(8,128)S(1)}, u32[]{:S(2)}, u32[]{:S(2)}) collective-permute-start(f32[4,64,128]{2,1,0:T(8,128)S(1)} %get-tuple-element.92), channel_id=1, source_target_pairs={{0,1},{1,0},{2,3},{3,2},{4,5},{5,4},{6,7},{7,6},{8,9},{9,8},{10,11... | collective-permute-start | bytes 393224 | tf_op jit(solution)/shard_map/ppermute | solution.py:616
  8.3 2.6 %collective-permute-start.3 = (f32[4,64,128]{2,1,0:T(8,128)S(1)}, f32[4,64,128]{2,1,0:T(8,128)S(1)}, u32[]{:S(2)}, u32[]{:S(2)}) collective-permute-start(f32[4,64,128]{2,1,0:T(8,128)S(1)} %get-tuple-element.93), channel_id=1, source_target_pairs={{0,8},{1,2},{2,1},{3,4},{4,3},{5,6},{6,5},{7,15},{8,0},{9,10},{10,... | collective-permute-start | bytes 393224 | tf_op jit(solution)/shard_map/ppermute | solution.py:619
  10.9 2.5 %fine_blocks.1 = (bf16[128,64,384]{2,1,0:T(8,128)(2,1)S(1)}, f32[32,64,128]{2,1,0:T(8,128)S(1)}) custom-call(bf16[64,256,128]{2,1,0:T(8,128)(2,1)S(1)} %bitcast.8, bf16[64,64,128]{2,1,0:T(8,128)(2,1)S(1)} %bitcast.11, bf16[64,64,128]{2,1,0:T(8,128)(2,1)S(1)} %bitcast.10, ...), custom_call_target="tpu_custom_call", output_to_operand_aliasing={{0}: (3, {}), {1}: (4, {})} | custom-call | flops 1 | bytes 1 | tf_op jit(solution)/shard_map/fine_blocks/pallas_call | solution.py:548
  13.4 0.3 collective-permute-start.1
  13.7 2.7 %fine_inner.1 = (f32[128,64,128]{2,1,0:T(8,128)S(1)}, bf16[204,64,256]{2,1,0:T(8,128)(2,1)S(1)}, f32[64,64,128]{2,1,0:T(8,128)S(1)}) custom-call(bf16[128,64,384]{2,1,0:T(8,128)(2,1)S(1)} %get-tuple-element.89.refs_0_, bf16[204,64,256]{2,1,0:T(8,128)(2,1)S(1)} %get-tuple-element.95.refs_1_.refs_2_, ...), custom_call_target="tpu_custom_call", output_to_operand_aliasing={{0}: (2, {})} | custom-call | flops 1 | bytes 1 | tf_op jit(solution)/shard_map/fine_inner/pallas_call | solution.py:548
  16.5 0.0 collective-permute-done.2.refs_5_.refs_2_
  16.5 0.0 collective-permute-done.4.refs_1_
  16.5 0.9 %fine_middle.1 = (bf16[204,64,256]{2,1,0:T(8,128)(2,1)S(1)}, f32[128,64,128]{2,1,0:T(8,128)S(1)}, bf16[204,64,256]{2,1,0:T(8,128)(2,1)S(1)}, f32[32,64,128]{2,1,0:T(8,128)S(1)}, f32[16,64,128]{2,1,0:T(8,128)S(1)}) custom-call(bf16[128,64,384]{2,1,0:T(8,128)(2,1)S(1)} %get-tuple-element.89.refs_0_, ...), custom_call_target="tpu_custom_call", output_to_operand_aliasing={{0}: (2, {}), {1}: (3, {}), {2}: (4, {})} | custom-call | flops 99999997952 | bytes 1 | tf_op jit(solution)/shard_map/fine_middle/pallas_call | solution.py:548
  17.4 2.1 %collective-permute-start.9 = (f32[16,64,128]{2,1,0:T(8,128)S(1)}, f32[16,64,128]{2,1,0:T(8,128)S(1)}, u32[]{:S(2)}, u32[]{:S(2)}) collective-permute-start(f32[16,64,128]{2,1,0:T(8,128)S(1)} %get-tuple-element.118), channel_id=1, source_target_pairs={{0,2},{1,3},{2,0},{3,1},{4,6},{5,7},{6,4},{7,5},{8,16},{9,17},{10,... | collective-permute-start | bytes 1572872 | tf_op jit(solution)/shard_map/ppermute | solution.py:610
  19.4 0.0 collective-permute-done.1.refs_1_
  19.4 1.4 %fine_last.1 = (bf16[204,64,256]{2,1,0:T(8,128)(2,1)S(1)}, f32[128,64,128]{2,1,0:T(8,128)S(1)}, bf16[204,64,256]{2,1,0:T(8,128)(2,1)S(1)}, f32[32,64,128]{2,1,0:T(8,128)S(1)}, f32[32,64,128]{2,1,0:T(8,128)S(1)}) custom-call(bf16[128,64,384]{2,1,0:T(8,128)(2,1)S(1)} %get-tuple-element.89.refs_0_, ...), custom_call_target="tpu_custom_call", output_to_operand_aliasing={{0}: (4, {}), {1}: (5, {}), {2}: (6, {})} | custom-call | flops 1 | bytes 1 | tf_op jit(solution)/shard_map/fine_last/pallas_call | solution.py:548
  20.9 0.0 slice-start
  20.9 0.0 copy-start.2
  20.9 0.0 copy-start.3
  20.9 0.0 copy-start.5
  21.0 1.2 %fine_ends.1 = (bf16[204,64,256]{2,1,0:T(8,128)(2,1)S(1)}, f32[128,64,128]{2,1,0:T(8,128)S(1)}, bf16[204,64,256]{2,1,0:T(8,128)(2,1)S(1)}, f32[32,64,128]{2,1,0:...) custom-call(bf16[128,64,384]{2,1,0:T(8,128)(2,1)S(1)} %get-tuple-ele, ...), custom_call_target="tpu_custom_call", output_to_operand_aliasing={{0}: (2, {}), {1}: (3, {}), {2}: (4, {}), {3}: (5, {}), {4}... | custom-call | flops 1 | bytes 1 | tf_op jit(solution)/shard_map/fine_ends/pallas_call | solution.py:548
  22.1 2.7 %collective-permute-start.7 = (f32[4,64,128]{2,1,0:T(8,128)S(1)}, f32[4,64,128]{2,1,0:T(8,128)S(1)}, u32[]{:S(2)}, u32[]{:S(2)}) collective-permute-start(f32[4,64,128]{2,1,0:T(8,128)S(1)} %get-tuple-element.116), channel_id=1, source_target_pairs={{0,1},{1,0},{2,3},{3,2},{4,5},{5,4},{6,7},{7,6},{8,9},{9,8},{10,11... | collective-permute-start | bytes 393224 | tf_op jit(solution)/shard_map/ppermute | solution.py:616
  24.8 1.5 %collective-permute-start.5 = (f32[16,64,128]{2,1,0:T(8,128)S(1)}, f32[16,64,128]{2,1,0:T(8,128)S(1)}, u32[]{:S(2)}, u32[]{:S(2)}) collective-permute-start(f32[16,64,128]{2,1,0:T(8,128)S(1)} %get-tuple-element.110.refs_3_), channel_id=1, source_target_pairs={{0,2},{1,3},{2,0},{3,1},{4,6},{5,7},{6,4},{7,5},{8,16},{9,17},{10,... | collective-permute-start | bytes 1572872 | tf_op jit(solution)/shard_map/ppermute | solution.py:610
  26.4 0.9 %own_blocks.1 = (bf16[64,64,128]{2,1,0:T(8,128)(2,1)S(1)}, s32[8,64]{1,0:T(8,128)S(4)}) custom-call(bf16[64,64,64]{2,1,0:T(8,128)(2,1)S(1)} %copy-done.2, bf16[64,64,64]{2,1,0:T(8,128)(2,1)S(1)} %copy-done.3, s32[8,64]{1,0:T(8,128)S(1)} %bitcast.12, f32[16,64,128]{2,1,0:T(8,128)S(1)} %get-tuple-element.110.refs_3_), custom_call_target="tpu_custom_call" | custom-call | flops 1 | bytes 1 | tf_op jit(solution)/shard_map/own_blocks/pallas_call | solution.py:548
  27.3 3.3 %near_blocks.1 = (bf16[64,64,512]{2,1,0:T(8,128)(2,1)S(1)}, f32[128,64,128]{2,1,0:T(8,128)}) custom-call(bf16[64,64,8,64]{3,2,1,0:T(8,128)(2,1)S(1)} %bitcast.7, f32[32,64,128]{2,1,0:T(8,128)S(1)} %get-tuple-element.106.first_row, f32[64,64,128]{2,1,0:T(8,128)S(1)} %get-tuple-element.107.held, f32[32,64,128]{2,1,0:T(8,128)S(1)} %get-tuple-element.108.last_row), custom_call_target="tpu_custom_call" | custom-call | flops 1 | bytes 1 | tf_op jit(solution)/shard_map/near_blocks/pallas_call | solution.py:555
  30.6 0.0 collective-permute-done.7.refs_5_.refs_1_
  30.7 0.0 collective-permute-done.8.refs_6_.refs_2_
  30.7 1.2 %left_middle.1 = (bf16[204,64,256]{2,1,0:T(8,128)(2,1)S(1)}, f32[64,64,128]{2,1,0:T(8,128)S(1)}, bf16[136,64,256]{2,1,0:T(8,128)(2,1)S(1)}, f32[16,64,128]{2,1,0:T(8,128)S(1)}) custom-call(bf16[128,64,384]{2,1,0:T(8,128)(2,1)S(1)} %get-tuple-element.89.refs_0_, f32[128,64,128]{2,1,0:T(8,128)S(1)} %get-tuple-element.114.refs_1_, ...), custom_call_target="tpu_custom_call", output_to_operand_aliasing={{0}: (4, {})} | custom-call | flops 99999997952 | bytes 1 | tf_op jit(solution)/shard_map/left_middle/pallas_call | solution.py:548
  31.9 2.9 %collective-permute-start.16 = (f32[16,64,128]{2,1,0:T(8,128)S(1)}, f32[16,64,128]{2,1,0:T(8,128)S(1)}, u32[]{:S(2)}, u32[]{:S(2)}) collective-permute-start(f32[16,64,128]{2,1,0:T(8,128)S(1)} %get-tuple-element.133), channel_id=1, source_target_pairs={{0,2},{1,3},{2,0},{3,1},{4,6},{5,7},{6,4},{7,5},{8,16},{9,17},{10,... | collective-permute-start | bytes 1572872 | tf_op jit(solution)/shard_map/ppermute | solution.py:610
  34.7 0.0 collective-permute-done.6.refs_0_
  34.7 0.2 left_halo.1.refs_4_
  34.9 0.2 collective-permute-done.5.refs_3_
  35.1 1.5 %left_ends.1 = (bf16[204,64,256]{2,1,0:T(8,128)(2,1)S(1)}, f32[64,64,128]{2,1,0:T(8,128)S(1)}, bf16[136,64,256]{2,1,0:T(8,128)(2,1)S(1)}, f32[16,64,128]{2,1,0:T...) custom-call(bf16[128,64,384]{2,1,0:T(8,128)(2,1)S(1)} %get-tuple-ele, ...), custom_call_target="tpu_custom_call", output_to_operand_aliasing={{0}: (4, {}), {1}: (5, {}), {2}: (6, {})} | custom-call | flops 99999997952 | bytes 1 | tf_op jit(solution)/shard_map/left_ends/pallas_call | solution.py:548
  36.6 2.1 %collective-permute-start.11 = (f32[2,64,128]{2,1,0:T(8,128)S(1)}, f32[2,64,128]{2,1,0:T(8,128)S(1)}, u32[]{:S(2)}, u32[]{:S(2)}) collective-permute-start(f32[2,64,128]{2,1,0:T(8,128)S(1)} %get-tuple-element.124), channel_id=1, source_target_pairs={{0,1},{1,0},{2,3},{3,2},{4,5},{5,4},{6,7},{7,6},{8,9},{9,8},{10,11... | collective-permute-start | bytes 196616 | tf_op jit(solution)/shard_map/ppermute | solution.py:616
  38.7 0.0 collective-permute-start.12
  38.7 2.5 %collective-permute-start.10 = (f32[16,64,128]{2,1,0:T(8,128)S(1)}, f32[16,64,128]{2,1,0:T(8,128)S(1)}, u32[]{:S(2)}, u32[]{:S(2)}) collective-permute-start(f32[16,64,128]{2,1,0:T(8,128)S(1)} %get-tuple-element.123), channel_id=1, source_target_pairs={{0,2},{1,3},{2,0},{3,1},{4,6},{5,7},{6,4},{7,5},{8,16},{9,17},{10,... | collective-permute-start | bytes 1572872 | tf_op jit(solution)/shard_map/ppermute | solution.py:610
  41.2 2.3 %left_inner.1 = (f32[64,64,128]{2,1,0:T(8,128)S(1)}, bf16[136,64,256]{2,1,0:T(8,128)(2,1)S(1)}, f32[32,64,128]{2,1,0:T(8,128)S(1)}) custom-call(bf16[128,64,384]{2,1,0:T(8,128)(2,1)S(1)} %get-tuple-element.89.refs_0_, f32[128,64,128]{2,1,0:T(8,128)S(1)} %get-tuple-element.114.refs_1_, ...), custom_call_target="tpu_custom_call", output_to_operand_aliasing={{0}: (4, {}), {1}: (5, {})} | custom-call | flops 1 | bytes 1 | tf_op jit(solution)/shard_map/left_inner/pallas_call | solution.py:548
  43.5 0.1 collective-permute-start.14
  43.6 0.0 collective-permute-done.12.refs_1_
  43.6 0.1 pack_first.1
  43.7 1.5 %collective-permute-start.13 = (f32[2,64,128]{2,1,0:T(8,128)S(1)}, f32[2,64,128]{2,1,0:T(8,128)S(1)}, u32[]{:S(2)}, u32[]{:S(2)}) collective-permute-start(f32[2,64,128]{2,1,0:T(8,128)S(1)} %get-tuple-element.130), channel_id=1, source_target_pairs={{0,1},{1,0},{2,3},{3,2},{4,5},{5,4},{6,7},{7,6},{8,16},{9,17},{10,... | collective-permute-start | bytes 196616 | tf_op jit(solution)/shard_map/ppermute | solution.py:747
  45.2 0.0 collective-permute-start.15
  45.2 0.0 collective-permute-done.16.refs_3_
  45.2 1.1 %coarse_middle.1 = (bf16[136,64,256]{2,1,0:T(8,128)(2,1)S(1)}, f32[64,64,128]{2,1,0:T(8,128)S(1)}, bf16[136,64,256]{2,1,0:T(8,128)(2,1)S(1)}, f32[64,64,128]{2,1,0:T(8,128)S(1)}, f32[14,64,128]{2,1,0:T(8,128)S(1)}) custom-call(s32[8,64]{1,0:T(8,128)S(4)} %get-tuple-element.111.refs_0_, ...), custom_call_target="tpu_custom_call", output_to_operand_aliasing={{0}: (4, {}), {1}: (5, {})} | custom-call | flops 99999997952 | bytes 1 | tf_op jit(solution)/shard_map/coarse_middle/pallas_call | solution.py:548
  46.3 2.1 %collective-permute-start.18 = (f32[14,64,128]{2,1,0:T(8,128)S(1)}, f32[14,64,128]{2,1,0:T(8,128)S(1)}, u32[]{:S(2)}, u32[]{:S(2)}) collective-permute-start(f32[14,64,128]{2,1,0:T(8,128)S(1)} %get-tuple-element.147), channel_id=1, source_target_pairs={{0,2},{1,3},{2,0},{3,1},{4,6},{5,7},{6,4},{7,5},{8,16},{9,17},{10,... | collective-permute-start | bytes 1376264 | tf_op jit(solution)/shard_map/ppermute | solution.py:610
  48.4 0.1 coarse_halo.1.refs_5_
  48.6 0.0 collective-permute-done.13.refs_4_
  48.6 0.5 collective-permute-done.10.refs_3_
  49.0 1.6 %coarse_ends.1 = (bf16[136,64,256]{2,1,0:T(8,128)(2,1)S(1)}, f32[64,64,128]{2,1,0:T(8,128)S(1)}, bf16[136,64,256]{2,1,0:T(8,128)(2,1)S(1)}, f32[64,64,128]{2,1,0...) custom-call(s32[8,64]{1,0:T(8,128)S(4)} %get-tuple-element.111.refs_, ...), custom_call_target="tpu_custom_call", output_to_operand_aliasing={{0}: (5, {}), {1}: (6, {}), {2}: (7, {}), {3}: (8, {})} | custom-call | flops 99999997952 | bytes 1 | tf_op jit(solution)/shard_map/coarse_ends/pallas_call | solution.py:548
  50.7 2.9 %collective-permute-start.19 = (f32[2,64,128]{2,1,0:T(8,128)S(1)}, f32[2,64,128]{2,1,0:T(8,128)S(1)}, u32[]{:S(2)}, u32[]{:S(2)}) collective-permute-start(f32[2,64,128]{2,1,0:T(8,128)S(1)} %get-tuple-element.148), channel_id=1, source_target_pairs={{0,1},{1,0},{2,3},{3,2},{4,5},{5,4},{6,7},{7,6},{8,9},{9,8},{10,11... | collective-permute-start | bytes 196616 | tf_op jit(solution)/shard_map/ppermute | solution.py:616
  53.5 0.0 collective-permute-start.20
  53.5 1.5 %collective-permute-start.21 = (f32[9,64,128]{2,1,0:T(8,128)S(1)}, f32[9,64,128]{2,1,0:T(8,128)S(1)}, u32[]{:S(2)}, u32[]{:S(2)}) collective-permute-start(f32[9,64,128]{2,1,0:T(8,128)S(1)} %get-tuple-element.156), channel_id=1, source_target_pairs={{0,2},{1,3},{2,0},{3,1},{4,6},{5,7},{6,4},{7,5},{8,16},{9,17},{10,... | collective-permute-start | bytes 884744 | tf_op jit(solution)/shard_map/ppermute | solution.py:610
  55.1 0.5 collective-permute-start.22
  55.6 2.7 %coarse_inner.1 = (f32[64,64,128]{2,1,0:T(8,128)S(1)}, bf16[136,64,256]{2,1,0:T(8,128)(2,1)S(1)}, f32[64,64,128]{2,1,0:T(8,128)S(1)}, f32[32,64,128]{2,1,0:T(8,128)S(1)}, f32[64,64,128]{2,1,0:T(8,128)}) custom-call(s32[8,64]{1,0:T(8,128)S(4)} %get-tuple-element.111.refs_0_, ...), custom_call_target="tpu_custom_call", output_to_operand_aliasing={{0}: (4, {}), {1}: (5, {}), {2}: (6, {})} | custom-call | flops 1 | bytes 1 | tf_op jit(solution)/shard_map/coarse_inner/pallas_call | solution.py:548
  58.3 0.0 collective-permute-done.19.refs_0_
  58.3 0.3 collective-permute-start.17
  58.6 0.1 pack_second.1
  58.6 2.0 %collective-permute-start.23 = (f32[2,64,128]{2,1,0:T(8,128)S(1)}, f32[2,64,128]{2,1,0:T(8,128)S(1)}, u32[]{:S(2)}, u32[]{:S(2)}) collective-permute-start(f32[2,64,128]{2,1,0:T(8,128)S(1)} %get-tuple-element.158), channel_id=1, source_target_pairs={{0,1},{1,0},{2,3},{3,2},{4,5},{5,4},{6,7},{7,6},{8,16},{9,17},{10,... | collective-permute-start | bytes 196616 | tf_op jit(solution)/shard_map/ppermute | solution.py:795
  60.6 0.8 %last_middle.1 = (bf16[136,64,256]{2,1,0:T(8,128)(2,1)S(1)}, f32[32,64,128]{2,1,0:T(8,128)S(1)}) custom-call(s32[8,64]{1,0:T(8,128)S(4)} %get-tuple-element.111.refs_0_, bf16[64,64,512]{2,1,0:T(8,128)(2,1)S(1)} %get-tuple-element.112.refs_7_.refs_1_, bf16[64,64,128]{2,1,0:T(8,128)(2,1)S(1)} %get-tuple-element.113.refs_2_, ...), custom_call_target="tpu_custom_call", output_to_operand_aliasing={{0}: (5, {})} | custom-call | flops 99999997952 | bytes 1 | tf_op jit(solution)/shard_map/last_middle/pallas_call | solution.py:548
  61.5 2.6 %last_inner.1 = (bf16[136,64,256]{2,1,0:T(8,128)(2,1)S(1)}, f32[32,64,128]{2,1,0:T(8,128)S(1)}, f32[64,64,128]{2,1,0:T(8,128)}) custom-call(s32[8,64]{1,0:T(8,128)S(4)} %get-tuple-element.111.refs_0_, bf16[64,64,512]{2,1,0:T(8,128)(2,1)S(1)} %get-tuple-element.112.refs_7_.refs_1_, ...), custom_call_target="tpu_custom_call", output_to_operand_aliasing={{0}: (6, {}), {1}: (7, {}), {2}: (8, {})} | custom-call | flops 1 | bytes 1 | tf_op jit(solution)/shard_map/last_inner/pallas_call | solution.py:548
  64.1 0.4 last_sides.1
  64.5 0.7 %last_low.1 = (bf16[136,64,256]{2,1,0:T(8,128)(2,1)S(1)}, f32[32,64,128]{2,1,0:T(8,128)S(1)}) custom-call(s32[8,64]{1,0:T(8,128)S(4)} %get-tuple-element.111.refs_0_, bf16[64,64,512]{2,1,0:T(8,128)(2,1)S(1)} %get-tuple-element.112.refs_7_.refs_1_, bf16[64,64,128]{2,1,0:T(8,128)(2,1)S(1)} %get-tuple-element.113.refs_2_, ...), custom_call_target="tpu_custom_call", output_to_operand_aliasing={{0}: (6, {}), {1}: (7, {})} | custom-call | flops 1 | bytes 1 | tf_op jit(solution)/shard_map/last_low/pallas_call | solution.py:548
  65.2 1.5 %last_high.1 = (bf16[136,64,256]{2,1,0:T(8,128)(2,1)S(1)}, f32[32,64,128]{2,1,0:T(8,128)}) custom-call(s32[8,64]{1,0:T(8,128)S(4)} %get-tuple-element.111.refs_0_, bf16[64,64,512]{2,1,0:T(8,128)(2,1)S(1)} %get-tuple-element.112.refs_7_.refs_1_, bf16[64,64,128]{2,1,0:T(8,128)(2,1)S(1)} %get-tuple-element.113.refs_2_, ...), custom_call_target="tpu_custom_call", output_to_operand_aliasing={{0}: (5, {})} | custom-call | flops 1 | bytes 1 | tf_op jit(solution)/shard_map/last_high/pallas_call | solution.py:548
  (27 shorter events, 0.1 us)
Async XLA Ops:
  3.2 13.3 %collective-permute-start.4 = (f32[16,64,128]{2,1,0:T(8,128)S(1)}, f32[16,64,128]{2,1,0:T(8,128)S(1)}, u32[]{:S(2)}, u32[]{:S(2)}) collective-permute-start(f32[16,64,128]{2,1,0:T(8,128)S(1)} %get-tuple-element.94), channel_id=1, source_target_pairs={{8,16},{9,17},{10,18},{11,19},{12,20},{13,21},{14,22},{15,23},{16,... | collective-permute-start | bytes 1572872 | tf_op jit(solution)/shard_map/ppermute | solution.py:643
  3.9 7.0 %copy-start = (bf16[128,64,4,64]{0,3,2,1:T(8,128)(2,1)S(1)}, bf16[128,64,4,64]{0,3,2,1:T(8,128)(2,1)}, u32[]{:S(2)}) copy-start(bf16[128,64,4,64]{0,3,2,1:T(8,128)(2,1)} %param.9) | copy-start | bytes 12582916
  3.9 7.0 %copy-start.1 = (bf16[128,64,64]{0,2,1:T(8,128)(2,1)S(1)}, bf16[128,64,64]{0,2,1:T(8,128)(2,1)}, u32[]{:S(2)}) copy-start(bf16[128,64,64]{0,2,1:T(8,128)(2,1)} %param.11) | copy-start | bytes 3145732
  3.9 6.9 %copy-start.4 = (bf16[128,64,64]{0,2,1:T(8,128)(2,1)S(1)}, bf16[128,64,64]{0,2,1:T(8,128)(2,1)}, u32[]{:S(2)}) copy-start(bf16[128,64,64]{0,2,1:T(8,128)(2,1)} %param.10) | copy-start | bytes 3145732
  5.3 11.2 %collective-permute-start.2 = (f32[4,64,128]{2,1,0:T(8,128)S(1)}, f32[4,64,128]{2,1,0:T(8,128)S(1)}, u32[]{:S(2)}, u32[]{:S(2)}) collective-permute-start(f32[4,64,128]{2,1,0:T(8,128)S(1)} %get-tuple-element.92), channel_id=1, source_target_pairs={{0,1},{1,0},{2,3},{3,2},{4,5},{5,4},{6,7},{7,6},{8,9},{9,8},{10,11... | collective-permute-start | bytes 393224 | tf_op jit(solution)/shard_map/ppermute | solution.py:616
  8.3 8.2 %collective-permute-start.3 = (f32[4,64,128]{2,1,0:T(8,128)S(1)}, f32[4,64,128]{2,1,0:T(8,128)S(1)}, u32[]{:S(2)}, u32[]{:S(2)}) collective-permute-start(f32[4,64,128]{2,1,0:T(8,128)S(1)} %get-tuple-element.93), channel_id=1, source_target_pairs={{0,8},{1,2},{2,1},{3,4},{4,3},{5,6},{6,5},{7,15},{8,0},{9,10},{10,... | collective-permute-start | bytes 393224 | tf_op jit(solution)/shard_map/ppermute | solution.py:619
  10.9 10.0 %collective-permute-start = (f32[16,64,128]{2,1,0:T(8,128)S(1)}, f32[16,64,128]{2,1,0:T(8,128)S(1)}, u32[]{:S(2)}, u32[]{:S(2)}) collective-permute-start(f32[16,64,128]{2,1,0:T(8,128)S(1)} %get-tuple-element.90), channel_id=1, source_target_pairs={{0,2},{1,3},{2,0},{3,1},{4,6},{5,7},{6,4},{7,5},{8,16},{9,17},{10,... | collective-permute-start | bytes 1572872 | tf_op jit(solution)/shard_map/ppermute | solution.py:610
  13.4 6.0 %collective-permute-start.1 = (f32[32,64,128]{2,1,0:T(8,128)S(1)}, f32[32,64,128]{2,1,0:T(8,128)S(1)}, u32[]{:S(2)}, u32[]{:S(2)}) collective-permute-start(f32[32,64,128]{2,1,0:T(8,128)S(1)} %get-tuple-element.91), channel_id=1, source_target_pairs={{0,8},{1,9},{2,10},{3,11},{4,12},{5,13},{6,14},{7,15},{8,0},{9,1},... | collective-permute-start | bytes 3145736 | tf_op jit(solution)/shard_map/ppermute | solution.py:613
  17.4 13.3 %collective-permute-start.9 = (f32[16,64,128]{2,1,0:T(8,128)S(1)}, f32[16,64,128]{2,1,0:T(8,128)S(1)}, u32[]{:S(2)}, u32[]{:S(2)}) collective-permute-start(f32[16,64,128]{2,1,0:T(8,128)S(1)} %get-tuple-element.118), channel_id=1, source_target_pairs={{0,2},{1,3},{2,0},{3,1},{4,6},{5,7},{6,4},{7,5},{8,16},{9,17},{10,... | collective-permute-start | bytes 1572872 | tf_op jit(solution)/shard_map/ppermute | solution.py:610
  20.9 6.4 %slice-start = ((s8[8388608]{0:T(1024)(128)(4,1)}), s8[4194304]{0:T(1024)(128)(4,1)S(1)}, s32[]{:S(2)}) async-start(s8[8388608]{0:T(1024)(128)(4,1)} %bitcast.6), calls=%async_computation | async-start | bytes 8388608
  20.9 5.5 %copy-start.2 = (bf16[64,64,64]{2,1,0:T(8,128)(2,1)S(1)}, bf16[64,64,64]{2,1,0:T(8,128)(2,1)}, u32[]{:S(2)}) copy-start(bf16[64,64,64]{2,1,0:T(8,128)(2,1)} %refs_0_.3) | copy-start | bytes 1572868
  20.9 5.5 %copy-start.3 = (bf16[64,64,64]{2,1,0:T(8,128)(2,1)S(1)}, bf16[64,64,64]{2,1,0:T(8,128)(2,1)}, u32[]{:S(2)}) copy-start(bf16[64,64,64]{2,1,0:T(8,128)(2,1)} %refs_1_.1) | copy-start | bytes 1572868
  20.9 5.4 %copy-start.5 = (s32[64,8]{0,1:T(8,128)S(1)}, s32[64,8]{0,1:T(8,128)}, u32[]{:S(2)}) copy-start(s32[64,8]{0,1:T(8,128)} %param.15) | copy-start | bytes 6148
  20.9 6.4 %slice-start.1 = ((s8[8388608]{0:T(1024)(128)(4,1)}), s8[4194304]{0:T(1024)(128)(4,1)S(1)}, s32[]{:S(2)}) async-start(s8[8388608]{0:T(1024)(128)(4,1)} %bitcast.6), calls=%async_computation.1 | async-start | bytes 8388608
  22.1 8.5 %collective-permute-start.7 = (f32[4,64,128]{2,1,0:T(8,128)S(1)}, f32[4,64,128]{2,1,0:T(8,128)S(1)}, u32[]{:S(2)}, u32[]{:S(2)}) collective-permute-start(f32[4,64,128]{2,1,0:T(8,128)S(1)} %get-tuple-element.116), channel_id=1, source_target_pairs={{0,1},{1,0},{2,3},{3,2},{4,5},{5,4},{6,7},{7,6},{8,9},{9,8},{10,11... | collective-permute-start | bytes 393224 | tf_op jit(solution)/shard_map/ppermute | solution.py:616
  24.8 5.8 %collective-permute-start.8 = (f32[4,64,128]{2,1,0:T(8,128)S(1)}, f32[4,64,128]{2,1,0:T(8,128)S(1)}, u32[]{:S(2)}, u32[]{:S(2)}) collective-permute-start(f32[4,64,128]{2,1,0:T(8,128)S(1)} %get-tuple-element.117), channel_id=1, source_target_pairs={{0,8},{1,2},{2,1},{3,4},{4,3},{5,6},{6,5},{7,15},{8,0},{9,10},{10,... | collective-permute-start | bytes 393224 | tf_op jit(solution)/shard_map/ppermute | solution.py:619
  24.8 10.3 %collective-permute-start.5 = (f32[16,64,128]{2,1,0:T(8,128)S(1)}, f32[16,64,128]{2,1,0:T(8,128)S(1)}, u32[]{:S(2)}, u32[]{:S(2)}) collective-permute-start(f32[16,64,128]{2,1,0:T(8,128)S(1)} %get-tuple-element.110.refs_3_), channel_id=1, source_target_pairs={{0,2},{1,3},{2,0},{3,1},{4,6},{5,7},{6,4},{7,5},{8,16},{9,17},{10,... | collective-permute-start | bytes 1572872 | tf_op jit(solution)/shard_map/ppermute | solution.py:610
  26.4 8.4 %collective-permute-start.6 = (f32[32,64,128]{2,1,0:T(8,128)S(1)}, f32[32,64,128]{2,1,0:T(8,128)S(1)}, u32[]{:S(2)}, u32[]{:S(2)}) collective-permute-start(f32[32,64,128]{2,1,0:T(8,128)S(1)} %get-tuple-element.115), channel_id=1, source_target_pairs={{0,8},{1,9},{2,10},{3,11},{4,12},{5,13},{6,14},{7,15},{8,0},{9,1},... | collective-permute-start | bytes 3145736 | tf_op jit(solution)/shard_map/ppermute | solution.py:613
  31.9 13.3 %collective-permute-start.16 = (f32[16,64,128]{2,1,0:T(8,128)S(1)}, f32[16,64,128]{2,1,0:T(8,128)S(1)}, u32[]{:S(2)}, u32[]{:S(2)}) collective-permute-start(f32[16,64,128]{2,1,0:T(8,128)S(1)} %get-tuple-element.133), channel_id=1, source_target_pairs={{0,2},{1,3},{2,0},{3,1},{4,6},{5,7},{6,4},{7,5},{8,16},{9,17},{10,... | collective-permute-start | bytes 1572872 | tf_op jit(solution)/shard_map/ppermute | solution.py:610
  36.6 7.0 %collective-permute-start.11 = (f32[2,64,128]{2,1,0:T(8,128)S(1)}, f32[2,64,128]{2,1,0:T(8,128)S(1)}, u32[]{:S(2)}, u32[]{:S(2)}) collective-permute-start(f32[2,64,128]{2,1,0:T(8,128)S(1)} %get-tuple-element.124), channel_id=1, source_target_pairs={{0,1},{1,0},{2,3},{3,2},{4,5},{5,4},{6,7},{7,6},{8,9},{9,8},{10,11... | collective-permute-start | bytes 196616 | tf_op jit(solution)/shard_map/ppermute | solution.py:616
  38.7 4.9 %collective-permute-start.12 = (f32[2,64,128]{2,1,0:T(8,128)S(1)}, f32[2,64,128]{2,1,0:T(8,128)S(1)}, u32[]{:S(2)}, u32[]{:S(2)}) collective-permute-start(f32[2,64,128]{2,1,0:T(8,128)S(1)} %get-tuple-element.125), channel_id=1, source_target_pairs={{0,8},{1,2},{2,1},{3,4},{4,3},{5,6},{6,5},{7,15},{8,0},{9,10},{10,... | collective-permute-start | bytes 196616 | tf_op jit(solution)/shard_map/ppermute | solution.py:619
  38.7 10.3 %collective-permute-start.10 = (f32[16,64,128]{2,1,0:T(8,128)S(1)}, f32[16,64,128]{2,1,0:T(8,128)S(1)}, u32[]{:S(2)}, u32[]{:S(2)}) collective-permute-start(f32[16,64,128]{2,1,0:T(8,128)S(1)} %get-tuple-element.123), channel_id=1, source_target_pairs={{0,2},{1,3},{2,0},{3,1},{4,6},{5,7},{6,4},{7,5},{8,16},{9,17},{10,... | collective-permute-start | bytes 1572872 | tf_op jit(solution)/shard_map/ppermute | solution.py:610
  43.5 4.9 %collective-permute-start.14 = (f32[32,64,128]{2,1,0:T(8,128)S(1)}, f32[32,64,128]{2,1,0:T(8,128)S(1)}, u32[]{:S(2)}, u32[]{:S(2)}) collective-permute-start(f32[32,64,128]{2,1,0:T(8,128)S(1)} %get-tuple-element.131), channel_id=1, source_target_pairs={{0,8},{1,9},{2,10},{3,11},{4,12},{5,13},{6,14},{7,15},{8,0},{9,1},... | collective-permute-start | bytes 3145736 | tf_op jit(solution)/shard_map/ppermute | solution.py:613
  43.7 4.9 %collective-permute-start.13 = (f32[2,64,128]{2,1,0:T(8,128)S(1)}, f32[2,64,128]{2,1,0:T(8,128)S(1)}, u32[]{:S(2)}, u32[]{:S(2)}) collective-permute-start(f32[2,64,128]{2,1,0:T(8,128)S(1)} %get-tuple-element.130), channel_id=1, source_target_pairs={{0,1},{1,0},{2,3},{3,2},{4,5},{5,4},{6,7},{7,6},{8,16},{9,17},{10,... | collective-permute-start | bytes 196616 | tf_op jit(solution)/shard_map/ppermute | solution.py:747
  45.2 3.2 %collective-permute-start.15 = (f32[2,64,128]{2,1,0:T(8,128)S(1)}, f32[2,64,128]{2,1,0:T(8,128)S(1)}, u32[]{:S(2)}, u32[]{:S(2)}) collective-permute-start(f32[2,64,128]{2,1,0:T(8,128)S(1)} %get-tuple-element.132), channel_id=1, source_target_pairs={{0,8},{1,9},{2,10},{3,11},{4,12},{5,13},{6,14},{7,15},{8,0},{9,1},... | collective-permute-start | bytes 196616 | tf_op jit(solution)/shard_map/ppermute | solution.py:613
  46.3 14.3 %collective-permute-start.18 = (f32[14,64,128]{2,1,0:T(8,128)S(1)}, f32[14,64,128]{2,1,0:T(8,128)S(1)}, u32[]{:S(2)}, u32[]{:S(2)}) collective-permute-start(f32[14,64,128]{2,1,0:T(8,128)S(1)} %get-tuple-element.147), channel_id=1, source_target_pairs={{0,2},{1,3},{2,0},{3,1},{4,6},{5,7},{6,4},{7,5},{8,16},{9,17},{10,... | collective-permute-start | bytes 1376264 | tf_op jit(solution)/shard_map/ppermute | solution.py:610
  50.7 7.6 %collective-permute-start.19 = (f32[2,64,128]{2,1,0:T(8,128)S(1)}, f32[2,64,128]{2,1,0:T(8,128)S(1)}, u32[]{:S(2)}, u32[]{:S(2)}) collective-permute-start(f32[2,64,128]{2,1,0:T(8,128)S(1)} %get-tuple-element.148), channel_id=1, source_target_pairs={{0,1},{1,0},{2,3},{3,2},{4,5},{5,4},{6,7},{7,6},{8,9},{9,8},{10,11... | collective-permute-start | bytes 196616 | tf_op jit(solution)/shard_map/ppermute | solution.py:616
  53.5 5.0 %collective-permute-start.20 = (f32[2,64,128]{2,1,0:T(8,128)S(1)}, f32[2,64,128]{2,1,0:T(8,128)S(1)}, u32[]{:S(2)}, u32[]{:S(2)}) collective-permute-start(f32[2,64,128]{2,1,0:T(8,128)S(1)} %get-tuple-element.149), channel_id=1, source_target_pairs={{0,8},{1,2},{2,1},{3,4},{4,3},{5,6},{6,5},{7,15},{8,0},{9,10},{10,... | collective-permute-start | bytes 196616 | tf_op jit(solution)/shard_map/ppermute | solution.py:619
  53.5 11.7 %collective-permute-start.21 = (f32[9,64,128]{2,1,0:T(8,128)S(1)}, f32[9,64,128]{2,1,0:T(8,128)S(1)}, u32[]{:S(2)}, u32[]{:S(2)}) collective-permute-start(f32[9,64,128]{2,1,0:T(8,128)S(1)} %get-tuple-element.156), channel_id=1, source_target_pairs={{0,2},{1,3},{2,0},{3,1},{4,6},{5,7},{6,4},{7,5},{8,16},{9,17},{10,... | collective-permute-start | bytes 884744 | tf_op jit(solution)/shard_map/ppermute | solution.py:610
  55.1 9.4 %collective-permute-start.22 = (f32[9,64,128]{2,1,0:T(8,128)S(1)}, f32[9,64,128]{2,1,0:T(8,128)S(1)}, u32[]{:S(2)}, u32[]{:S(2)}) collective-permute-start(f32[9,64,128]{2,1,0:T(8,128)S(1)} %get-tuple-element.157), channel_id=1, source_target_pairs={{0,2},{1,3},{2,0},{3,1},{4,6},{5,7},{6,4},{7,5},{8,16},{9,17},{10,... | collective-permute-start | bytes 884744 | tf_op jit(solution)/shard_map/ppermute | solution.py:610
  58.3 3.2 %collective-permute-start.17 = (f32[32,64,128]{2,1,0:T(8,128)S(1)}, f32[32,64,128]{2,1,0:T(8,128)S(1)}, u32[]{:S(2)}, u32[]{:S(2)}) collective-permute-start(f32[32,64,128]{2,1,0:T(8,128)S(1)} %get-tuple-element.145), channel_id=1, source_target_pairs={{0,8},{1,9},{2,10},{3,11},{4,12},{5,13},{6,14},{7,15},{8,0},{9,1},... | collective-permute-start | bytes 3145736 | tf_op jit(solution)/shard_map/ppermute | solution.py:613
  58.6 5.9 %collective-permute-start.23 = (f32[2,64,128]{2,1,0:T(8,128)S(1)}, f32[2,64,128]{2,1,0:T(8,128)S(1)}, u32[]{:S(2)}, u32[]{:S(2)}) collective-permute-start(f32[2,64,128]{2,1,0:T(8,128)S(1)} %get-tuple-element.158), channel_id=1, source_target_pairs={{0,1},{1,0},{2,3},{3,2},{4,5},{5,4},{6,7},{7,6},{8,16},{9,17},{10,... | collective-permute-start | bytes 196616 | tf_op jit(solution)/shard_map/ppermute | solution.py:795
  60.6 3.5 %collective-permute-start.24 = (f32[2,64,128]{2,1,0:T(8,128)S(1)}, f32[2,64,128]{2,1,0:T(8,128)S(1)}, u32[]{:S(2)}, u32[]{:S(2)}) collective-permute-start(f32[2,64,128]{2,1,0:T(8,128)S(1)} %get-tuple-element.159), channel_id=1, source_target_pairs={{0,8},{1,9},{2,10},{3,11},{4,12},{5,13},{6,14},{7,15},{8,0},{9,1},... | collective-permute-start | bytes 196616 | tf_op jit(solution)/shard_map/ppermute | solution.py:613

commit v5 on v4

--- a/solution.py
+++ b/solution.py
@@ -17,6 +17,7 @@
 ENDS = tuple(q for q in range(BLOCK_Y) if q not in MIDDLE)
 SIDES = (0, BLOCK_Y - 1)
 BESIDE = (-1, BLOCK_Y)
+BORDER = (-1, 0, BLOCK_Y - 1, BLOCK_Y)
 INSIDE = tuple(range(1, BLOCK_Y - 1))
 
 F32 = jnp.float32
@@ -228,7 +229,7 @@
     read_sides(grid, even, odd, BLOCK_X)
 
 
-def fine_blocks_kernel(coupling, diagonal, inverse, blocks_in, near_in, blocks, near):
+def fine_blocks_kernel(coupling, diagonal, inverse, blocks_in, blocks):
     species = coupling.shape[0]
     part = species // 2
     for first in range(0, species, part):
@@ -329,9 +330,7 @@
 def left_inner_kernel(blocks, side, own_blocks, change, coarse_in, grid_in, coarse_side, coarse_grid, near):
     for rho in range(1, COARSE_X):
         last = near if rho == COARSE_X - 1 else None
-        left_pair(rho, INSIDE, blocks, side, change, coarse_side, own_blocks, coarse_grid, last, INSIDE[0])
-    for q in SIDES:
-        near[q] = fold(coarse_grid[spot(COARSE_X - 1, q)])
+        left_pair(rho, INSIDE, blocks, side, change, coarse_side, own_blocks, coarse_grid, last)
 
 
 def near_blocks_kernel(coupling, first_row, held, last_row, blocks, out, sems):
@@ -382,30 +381,18 @@
 def pack_kernel(even_h, odd_h, grid_in, grid, far, near):
     write_sides(grid, even_h, odd_h, COARSE_X)
     read_row(grid, far, 0, BESIDE)
-    read_row(grid, near, COARSE_X - 1, BESIDE)
-
-
-def row_out(source, out, rho, sem):
-    some = pl.ds(place(rho, COARSE_X) * BLOCK_Y, BLOCK_Y)
-    return pltpu.make_async_copy(source.at[some], out.at[some], sem)
-
-
-def coarse_inner_kernel(
-    places, blocks, own_blocks, grid, side_in, change_in, iterate_in, side, change, iterate, near, out, sem
-):
-    leave = row_out(iterate, out, 0, sem)
-    leave.start()
+    read_row(grid, near, COARSE_X - 1, BORDER)
+
+
+def coarse_inner_kernel(places, blocks, own_blocks, grid, side_in, change_in, iterate_in, side, change, iterate, near):
     for rho in range(1, COARSE_X):
         last = near if rho == COARSE_X - 1 else None
-        coarse_second(rho, INSIDE, places, blocks, own_blocks, grid, side, change, iterate, last, INSIDE[0])
-    for q in SIDES:
-        near[q] = fold(change[spot(COARSE_X - 1, q)])
-    leave.wait()
+        coarse_second(rho, INSIDE, places, blocks, own_blocks, grid, side, change, iterate, last)
 
 
 def coarse_halo_kernel(near_h, beside_h, grid_in, grid):
-    write_row(grid, near_h, COARSE_X, range(BLOCK_Y))
-    write_row(grid, beside_h, COARSE_X, BESIDE)
+    write_row(grid, near_h, COARSE_X, INSIDE)
+    write_row(grid, beside_h, COARSE_X, BORDER)
 
 
 def coarse_middle_kernel(
@@ -467,39 +454,36 @@
         below[first + pair] = total
 
 
-def last_middle_kernel(came, pairs, places, blocks, own_blocks, side, far_h, change_in, change, below):
+def last_middle_kernel(came, pairs, places, blocks, own_blocks, side, far_h, change_in, below_in, change, below):
     write_row(change, far_h, -1, came)
     last_pairs(0, pairs, places, blocks, own_blocks, side, change, below)
 
 
 def last_inner_kernel(
-    pairs, places, blocks, own_blocks, side, near_h, iterate, change_in, below_in, out_in, change, below, out, sems
+    pairs, places, blocks, own_blocks, side, near_h, iterate, change_in, change, below, out, sem
 ):
-    leave = [row_out(iterate, out, rho, sems.at[rho]) for rho in range(1, COARSE_X)]
-    for copy in leave:
-        copy.start()
-    write_row(change, near_h, COARSE_X, range(BLOCK_Y))
+    leave = pltpu.make_async_copy(iterate, out, sem)
+    leave.start()
+    write_row(change, near_h, COARSE_X, INSIDE)
     for rho in range(1, COARSE_X):
         last_pairs(rho, pairs, places, blocks, own_blocks, side, change, below)
-    for copy in leave:
-        copy.wait()
+    leave.wait()
 
 
 def last_sides_kernel(todo, places, blocks, own_blocks, side, beside_h, change_in, below_in, change, below):
-    write_row(change, beside_h, COARSE_X, BESIDE)
+    write_row(change, beside_h, COARSE_X, BORDER)
     for rho in range(1, COARSE_X):
         last_pairs(rho, todo, places, blocks, own_blocks, side, change, below)
 
 
-def last_low_kernel(
-    came, todo, places, blocks, own_blocks, side, far_h, corners_h, change_in, below_in, change, below
+def last_low_kernel(came, todo, places, blocks, own_blocks, side, far_h, change_in, below_in, change, below):
+    write_row(change, far_h, -1, came)
+    last_pairs(0, todo, places, blocks, own_blocks, side, change, below)
+
+
+def last_high_kernel(
+    came, todo, places, blocks, own_blocks, side, change_in, below, corners_h, far_h, change, out, made, sems
 ):
-    write_row(change, far_h, -1, came)
-    write_row(change, corners_h, -1, BESIDE)
-    last_pairs(0, todo, places, blocks, own_blocks, side, change, below)
-
-
-def last_high_kernel(came, todo, places, blocks, own_blocks, side, far_h, change_in, below, change, out, made, sems):
     half = BLOCK_Y // 2
     copies = []
 
@@ -510,9 +494,11 @@
 
     for rho in range(1, COARSE_X):
         send(below, rho, 0, half)
-    send(below, 0, 0, todo[0])
+    send(below, 0, 1, todo[0] - 1)
+    write_row(change, corners_h, -1, BESIDE)
     write_row(change, far_h, -1, came)
-    last_pairs(0, todo, places, blocks, own_blocks, side, change, made)
+    last_pairs(0, (0,) + todo, places, blocks, own_blocks, side, change, made)
+    send(made, 0, 0, 1)
     send(made, 0, todo[0], len(todo))
     for copy in copies:
         copy.wait()
@@ -648,16 +634,16 @@
         [side, blocks, grid],
         [(2, 0)],
     )
-    even_h, odd_h = even(even_s), odd(odd_s)
-    blocks, near_s = run(
+    near_h, even_h, odd_h = near(near_s), even(even_s), odd(odd_s)
+    (blocks,) = run(
         "fine_blocks",
         fine_blocks_kernel,
-        [fine_blocks, field(BLOCK_Y)],
-        [coupling, diagonal, inverse, blocks, near_s],
-        [(3, 0), (4, 1)],
+        [fine_blocks],
+        [coupling, diagonal, inverse, blocks],
+        [(3, 0)],
+        after=[near_s],
         room=6,
     )
-    near_h = near(near_s)
     state = [padded(BLOCK_X), field(cells), padded(BLOCK_X)]
     side, change, held = run(
         "fine_inner",
@@ -719,6 +705,14 @@
     (change,) = run(
         "left_halo", left_halo_kernel, [padded(BLOCK_X)], [near_h, even_h, odd_h, change], [(3, 0)]
     )
+    coarse_side, coarse_grid, near_s = run(
+        "left_inner",
+        left_inner_kernel,
+        state[1:] + [field(len(INSIDE))],
+        [blocks, side, own_blocks, change, coarse_side, coarse_grid],
+        [(4, 0), (5, 1)],
+    )
+    near_h = near(near_s)
     change, coarse_side, coarse_grid, far_n, even_s, odd_s = run(
         "left_ends",
         functools.partial(left_ends_kernel, ENDS),
@@ -727,20 +721,12 @@
         [(4, 0), (5, 1), (6, 2)],
         cost=LONG,
     )
-    coarse_side, coarse_grid, near_s = run(
-        "left_inner",
-        left_inner_kernel,
-        state[1:] + [field(BLOCK_Y)],
-        [blocks, side, own_blocks, change, coarse_side, coarse_grid],
-        [(4, 0), (5, 1)],
-    )
     far_n = far(far_n)
     even_h, odd_h = even(even_s), odd(odd_s)
-    near_h = near(near_s)
     coarse_grid, corners, beside = run(
         "pack_first",
         pack_kernel,
-        [padded(COARSE_X), field(2), field(2)],
+        [padded(COARSE_X), field(2), field(len(BORDER))],
         [even_h, odd_h, coarse_grid],
         [(2, 0)],
     )
@@ -762,6 +748,15 @@
     (coarse_grid,) = run(
         "coarse_halo", coarse_halo_kernel, [padded(COARSE_X)], [near_h, beside, coarse_grid], [(2, 0)]
     )
+    coarse_side, coarse_change, iterate, near_s = run(
+        "coarse_inner",
+        coarse_inner_kernel,
+        state[1:] + [field(len(INSIDE))],
+        [places, near_blocks, own_blocks, coarse_grid, coarse_side, coarse_change, iterate],
+        [(4, 0), (5, 1), (6, 2)],
+        smem=(0,),
+    )
+    near_h = near(near_s)
     low, high = (tuple(q for q in outer if (q < inner[0]) == first) for first in (True, False))
     coarse_grid, coarse_side, coarse_change, iterate, far_low, far_high, even_s, odd_s = run(
         "coarse_ends",
@@ -772,51 +767,38 @@
         smem=(0,),
         cost=LONG,
     )
-    coarse_side, coarse_change, iterate, near_s, coarse_iterate = run(
-        "coarse_inner",
-        coarse_inner_kernel,
-        state[1:] + [field(BLOCK_Y), field(coarse_cells)],
-        [places, near_blocks, own_blocks, coarse_grid, coarse_side, coarse_change, iterate],
-        [(4, 0), (5, 1), (6, 2)],
-        smem=(0,),
-        hbm_outs=(4,),
-        scratch=[pltpu.SemaphoreType.DMA],
-    )
     far_low, far_high = far(far_low), far(far_high)
     even_h, odd_h = even(even_s), odd(odd_s)
-    near_h = near(near_s)
+    state = [padded(COARSE_X), field(coarse_cells // 2)]
+    half = BLOCK_Y // 2
+    core = tuple(q // 2 for q in inner[1:-1:2])
+    coarse_change, below, coarse_iterate = run(
+        "last_inner",
+        functools.partial(last_inner_kernel, tuple(range(1, half - 1))),
+        state + [field(coarse_cells)],
+        [places, near_blocks, own_blocks, coarse_side, near_h, iterate, coarse_change],
+        [(6, 0)],
+        smem=(0,),
+        hbm_outs=(2,),
+        scratch=[pltpu.SemaphoreType.DMA],
+    )
     coarse_change, corners, beside = run(
         "pack_second",
         pack_kernel,
-        [padded(COARSE_X), field(2), field(2)],
+        [padded(COARSE_X), field(2), field(len(BORDER))],
         [even_h, odd_h, coarse_change],
         [(2, 0)],
     )
     corners, beside = lax.ppermute(corners, BOTH, corner_pairs), near(beside)
 
-    state = [padded(COARSE_X), field(coarse_cells // 2)]
-    half = BLOCK_Y // 2
-    core = tuple(q // 2 for q in inner[1:-1:2])
-    pairs = tuple(range(1, half - 1))
     coarse_change, below = run(
         "last_middle",
         functools.partial(last_middle_kernel, inner, core),
         state,
-        [places, near_blocks, own_blocks, coarse_side, far_m, coarse_change],
-        [(5, 0)],
+        [places, near_blocks, own_blocks, coarse_side, far_m, coarse_change, below],
+        [(5, 0), (6, 1)],
         smem=(0,),
         cost=LONG,
-    )
-    coarse_change, below, coarse_iterate = run(
-        "last_inner",
-        functools.partial(last_inner_kernel, pairs),
-        state + [field(coarse_cells)],
-        [places, near_blocks, own_blocks, coarse_side, near_h, iterate, coarse_change, below, coarse_iterate],
-        [(6, 0), (7, 1), (8, 2)],
-        smem=(0,),
-        hbm=(8,),
-        hbm_outs=(2,),
-        scratch=[pltpu.SemaphoreType.DMA((COARSE_X,))],
     )
     coarse_change, below = run(
         "last_sides",
@@ -828,21 +810,21 @@
     )
     coarse_change, below = run(
         "last_low",
-        functools.partial(last_low_kernel, low, tuple(range(core[0]))),
+        functools.partial(last_low_kernel, low, tuple(range(1, core[0]))),
         state,
-        [places, near_blocks, own_blocks, coarse_side, far_low, corners, coarse_change, below],
-        [(6, 0), (7, 1)],
+        [places, near_blocks, own_blocks, coarse_side, far_low, coarse_change, below],
+        [(5, 0), (6, 1)],
         smem=(0,),
     )
     coarse_change, next_side = run(
         "last_high",
         functools.partial(last_high_kernel, high, tuple(range(core[-1] + 1, half))),
         state,
-        [places, near_blocks, own_blocks, coarse_side, far_high, coarse_change, below],
-        [(5, 0)],
+        [places, near_blocks, own_blocks, coarse_side, coarse_change, below, corners, far_high],
+        [(4, 0)],
         smem=(0,),
         hbm_outs=(1,),
-        scratch=[pltpu.VMEM(state[1][0], F32), pltpu.SemaphoreType.DMA((COARSE_X + 1,))],
+        scratch=[pltpu.VMEM(state[1][0], F32), pltpu.SemaphoreType.DMA((COARSE_X + 2,))],
         room=3,
     )
     return (fine_iterate, coarse_iterate, next_side)

time: 67.1 us -> 66.5 us (level)
  starting transfers between devices: 31.3 us -> 28.9 us
  waiting for transfers between devices: 0.73 us -> 2.73 us
    ppermute x4, starting transfers between devices: 10.7 us -> 7.83 us  [even(): return lax.ppermute(x, BOTH, even_pairs)]
    ppermute x2, starting transfers between devices: 3.54 us -> 4.79 us  [on_device(): corners, beside = (lax.ppermute(corners, BOTH, corner_pairs), near(beside))]
    ppermute x4, waiting for transfers between devices: 0.01 us -> 0.78 us  [even(): return lax.ppermute(x, BOTH, even_pairs)]
    ppermute x8, waiting for transfers between devices: 0.69 us -> 1.42 us  [far(): return lax.ppermute(x, BOTH, far_pairs)]
  transfers between devices with their start and end apart: 25 -> 25, of which waited for: 2 -> 3; matrix products, arithmetic and copies ran while one was open for 0% -> 0% of each run, Pallas kernels for 44% -> 44%
where the time goes in v5:
time: 66.5 us; the launch traced here: 66.3 us
  Pallas kernels  33.5 us (50%)
  starting transfers between devices  28.9 us (43%)
  waiting for transfers between devices  2.73 us (4%)
  between operations  1.16 us (2%)
    pallas_call x23, Pallas kernels, run(): called(*(pltpu.with_memory_space_constraint(x, space) for x, space in zip...  30.1 us
    ppermute x8, starting transfers between devices, far(): return lax.ppermute(x, BOTH, far_pairs)  12.5 us
    ppermute x4, starting transfers between devices, even(): return lax.ppermute(x, BOTH, even_pairs)  7.83 us
    ppermute x2, starting transfers between devices, on_device(): corners, beside = (lax.ppermute(corners, BOTH, corner_pairs), near(beside))  4.79 us
    pallas_call x1, Pallas kernels, near_blocks_call(): pl.pallas_call(near_blocks_kernel, grid=(cells // part,), out_shape=(pltp...  3.31 us
    ppermute x4, starting transfers between devices, odd(): return lax.ppermute(x, BOTH, odd_pairs)  2.78 us
    ppermute x8, waiting for transfers between devices, far(): return lax.ppermute(x, BOTH, far_pairs)  1.42 us
  transfers between devices with their start and end apart: 25, of which 3 were waited for; matrix products, arithmetic and copies ran while one was open for 0% of the time, Pallas kernels for 44%

profile of v5, /device:TPU:0, one launch (start us, length us, event | category | flops | bytes accessed | tf_op | source)
XLA Modules:
  0.0 66.3 jit_solution(7928686151134688300)
XLA Ops:
  0.6 2.6 %start.1 = (bf16[128,64,384]{2,1,0:T(8,128)(2,1)S(1)}, bf16[204,64,256]{2,1,0:T(8,128)(2,1)S(1)}, f32[128,64,128]{2,1,0:T(8,128)S(1)}, f32[16,64,128]{2,1,0:T(8,128)S(1)}, f32[16,64,128]{2,1,0:T(8,128)S(1)}) custom-call(f32[128,64,128]{2,1,0:T(8,128)} %refs_0_.2, bf16[64,64,128]{2,1,0:T(8,128)(2,1)} %bitcast.9), custom_call_target="tpu_custom_call" | custom-call | flops 1 | bytes 1 | tf_op jit(solution)/shard_map/start/pallas_call | solution.py:534
  3.2 0.7 %collective-permute-start.4 = (f32[16,64,128]{2,1,0:T(8,128)S(1)}, f32[16,64,128]{2,1,0:T(8,128)S(1)}, u32[]{:S(2)}, u32[]{:S(2)}) collective-permute-start(f32[16,64,128]{2,1,0:T(8,128)S(1)} %get-tuple-element.87), channel_id=1, source_target_pairs={{8,16},{9,17},{10,18},{11,19},{12,20},{13,21},{14,22},{15,23},{16,... | collective-permute-start | bytes 1572872 | tf_op jit(solution)/shard_map/ppermute | solution.py:629
  3.9 0.0 copy-start
  3.9 0.0 copy-start.1
  3.9 0.0 copy-start.2
  3.9 1.4 %first.1 = (bf16[204,64,256]{2,1,0:T(8,128)(2,1)S(1)}, f32[32,64,128]{2,1,0:T(8,128)S(1)}, f32[4,64,128]{2,1,0:T(8,128)S(1)}, f32[4,64,128]{2,1,0:T(8,128)S(1)}) custom-call(f32[128,64,128]{2,1,0:T(8,128)S(1)} %get-tuple-element.81.refs_0_.refs_2_, bf16[128,64,384]{2,1,0:T(8,128)(2,1)S(1)} %get-tuple-element.80.refs_1_.refs_3_, ...), custom_call_target="tpu_custom_call", output_to_operand_aliasing={{0}: (2, {})} | custom-call | flops 1 | bytes 1 | tf_op jit(solution)/shard_map/first/pallas_call | solution.py:534
  5.3 3.0 %collective-permute-start.2 = (f32[4,64,128]{2,1,0:T(8,128)S(1)}, f32[4,64,128]{2,1,0:T(8,128)S(1)}, u32[]{:S(2)}, u32[]{:S(2)}) collective-permute-start(f32[4,64,128]{2,1,0:T(8,128)S(1)} %get-tuple-element.85), channel_id=1, source_target_pairs={{0,1},{1,0},{2,3},{3,2},{4,5},{5,4},{6,7},{7,6},{8,9},{9,8},{10,11... | collective-permute-start | bytes 393224 | tf_op jit(solution)/shard_map/ppermute | solution.py:602
  8.3 2.6 %collective-permute-start.3 = (f32[4,64,128]{2,1,0:T(8,128)S(1)}, f32[4,64,128]{2,1,0:T(8,128)S(1)}, u32[]{:S(2)}, u32[]{:S(2)}) collective-permute-start(f32[4,64,128]{2,1,0:T(8,128)S(1)} %get-tuple-element.86), channel_id=1, source_target_pairs={{0,8},{1,2},{2,1},{3,4},{4,3},{5,6},{6,5},{7,15},{8,0},{9,10},{10,... | collective-permute-start | bytes 393224 | tf_op jit(solution)/shard_map/ppermute | solution.py:605
  10.9 0.3 collective-permute-start.1
  11.2 2.5 %fine_blocks.1.refs_0_ = bf16[128,64,384]{2,1,0:T(8,128)(2,1)S(1)} custom-call(bf16[64,256,128]{2,1,0:T(8,128)(2,1)S(1)} %bitcast.8, bf16[64,64,128]{2,1,0:T(8,128)(2,1)S(1)} %bitcast.11, bf16[64,64,128]{2,1,0:T(8,128)(2,1)S(1)} %bitcast.10, bf16[128,64,384]{2,1,0:T(8,128)(2,1)S(1)} %get-tuple-element.80.refs_1_.refs_3_, ...), custom_call_target="tpu_custom_call", output_to_operand_aliasing={{}: (3, {})} | custom-call | flops 1 | bytes 1 | tf_op jit(solution)/shard_map/fine_blocks/pallas_call | solution.py:534
  13.7 2.7 %fine_inner.1 = (f32[128,64,128]{2,1,0:T(8,128)S(1)}, bf16[204,64,256]{2,1,0:T(8,128)(2,1)S(1)}, f32[64,64,128]{2,1,0:T(8,128)S(1)}) custom-call(bf16[128,64,384]{2,1,0:T(8,128)(2,1)S(1)} %fine_blocks.1.refs_0_, bf16[204,64,256]{2,1,0:T(8,128)(2,1)S(1)} %get-tuple-element.88.refs_1_.refs_2_, ...), custom_call_target="tpu_custom_call", output_to_operand_aliasing={{0}: (2, {})} | custom-call | flops 1 | bytes 1 | tf_op jit(solution)/shard_map/fine_inner/pallas_call | solution.py:534
  16.4 0.0 collective-permute-done.2.refs_5_.refs_2_
  16.4 0.0 collective-permute-done.3.refs_6_.refs_3_
  16.4 0.9 %fine_middle.1 = (bf16[204,64,256]{2,1,0:T(8,128)(2,1)S(1)}, f32[128,64,128]{2,1,0:T(8,128)S(1)}, bf16[204,64,256]{2,1,0:T(8,128)(2,1)S(1)}, f32[32,64,128]{2,1,0:T(8,128)S(1)}, f32[16,64,128]{2,1,0:T(8,128)S(1)}) custom-call(bf16[128,64,384]{2,1,0:T(8,128)(2,1)S(1)} %fine_blocks.1.refs_0_, ...), custom_call_target="tpu_custom_call", output_to_operand_aliasing={{0}: (2, {}), {1}: (3, {}), {2}: (4, {})} | custom-call | flops 99999997952 | bytes 1 | tf_op jit(solution)/shard_map/fine_middle/pallas_call | solution.py:534
  17.3 2.1 %collective-permute-start.9 = (f32[16,64,128]{2,1,0:T(8,128)S(1)}, f32[16,64,128]{2,1,0:T(8,128)S(1)}, u32[]{:S(2)}, u32[]{:S(2)}) collective-permute-start(f32[16,64,128]{2,1,0:T(8,128)S(1)} %get-tuple-element.111), channel_id=1, source_target_pairs={{0,2},{1,3},{2,0},{3,1},{4,6},{5,7},{6,4},{7,5},{8,16},{9,17},{10,... | collective-permute-start | bytes 1572872 | tf_op jit(solution)/shard_map/ppermute | solution.py:596
  19.4 0.0 collective-permute-done.1.refs_1_
  19.4 1.4 %fine_last.1 = (bf16[204,64,256]{2,1,0:T(8,128)(2,1)S(1)}, f32[128,64,128]{2,1,0:T(8,128)S(1)}, bf16[204,64,256]{2,1,0:T(8,128)(2,1)S(1)}, f32[32,64,128]{2,1,0:T(8,128)S(1)}, f32[32,64,128]{2,1,0:T(8,128)S(1)}) custom-call(bf16[128,64,384]{2,1,0:T(8,128)(2,1)S(1)} %fine_blocks.1.refs_0_, ...), custom_call_target="tpu_custom_call", output_to_operand_aliasing={{0}: (4, {}), {1}: (5, {}), {2}: (6, {})} | custom-call | flops 1 | bytes 1 | tf_op jit(solution)/shard_map/fine_last/pallas_call | solution.py:534
  20.8 0.0 collective-permute-done.refs_1_
  20.8 0.0 slice-start
  20.9 0.0 copy-start.3
  20.9 0.0 copy-start.4
  20.9 0.0 copy-start.5
  20.9 0.0 slice-start.1
  20.9 1.2 %fine_ends.1 = (bf16[204,64,256]{2,1,0:T(8,128)(2,1)S(1)}, f32[128,64,128]{2,1,0:T(8,128)S(1)}, bf16[204,64,256]{2,1,0:T(8,128)(2,1)S(1)}, f32[32,64,128]{2,1,0:...) custom-call(bf16[128,64,384]{2,1,0:T(8,128)(2,1)S(1)} %fine_blocks.1, ...), custom_call_target="tpu_custom_call", output_to_operand_aliasing={{0}: (2, {}), {1}: (3, {}), {2}: (4, {}), {3}: (5, {}), {4}... | custom-call | flops 1 | bytes 1 | tf_op jit(solution)/shard_map/fine_ends/pallas_call | solution.py:534
  22.1 2.7 %collective-permute-start.7 = (f32[4,64,128]{2,1,0:T(8,128)S(1)}, f32[4,64,128]{2,1,0:T(8,128)S(1)}, u32[]{:S(2)}, u32[]{:S(2)}) collective-permute-start(f32[4,64,128]{2,1,0:T(8,128)S(1)} %get-tuple-element.109), channel_id=1, source_target_pairs={{0,1},{1,0},{2,3},{3,2},{4,5},{5,4},{6,7},{7,6},{8,9},{9,8},{10,11... | collective-permute-start | bytes 393224 | tf_op jit(solution)/shard_map/ppermute | solution.py:602
  24.8 1.5 %collective-permute-start.5 = (f32[16,64,128]{2,1,0:T(8,128)S(1)}, f32[16,64,128]{2,1,0:T(8,128)S(1)}, u32[]{:S(2)}, u32[]{:S(2)}) collective-permute-start(f32[16,64,128]{2,1,0:T(8,128)S(1)} %get-tuple-element.103.refs_3_), channel_id=1, source_target_pairs={{0,2},{1,3},{2,0},{3,1},{4,6},{5,7},{6,4},{7,5},{8,16},{9,17},{10,... | collective-permute-start | bytes 1572872 | tf_op jit(solution)/shard_map/ppermute | solution.py:596
  26.4 0.9 %own_blocks.1 = (bf16[64,64,128]{2,1,0:T(8,128)(2,1)S(1)}, s32[8,64]{1,0:T(8,128)S(4)}) custom-call(bf16[64,64,64]{2,1,0:T(8,128)(2,1)S(1)} %copy-done.3, bf16[64,64,64]{2,1,0:T(8,128)(2,1)S(1)} %copy-done.4, s32[8,64]{1,0:T(8,128)S(1)} %bitcast.12, f32[16,64,128]{2,1,0:T(8,128)S(1)} %get-tuple-element.103.refs_3_), custom_call_target="tpu_custom_call" | custom-call | flops 1 | bytes 1 | tf_op jit(solution)/shard_map/own_blocks/pallas_call | solution.py:534
  27.3 3.3 %near_blocks.1 = (bf16[64,64,512]{2,1,0:T(8,128)(2,1)S(1)}, f32[128,64,128]{2,1,0:T(8,128)}) custom-call(bf16[64,64,8,64]{3,2,1,0:T(8,128)(2,1)S(1)} %bitcast.7, f32[32,64,128]{2,1,0:T(8,128)S(1)} %get-tuple-element.99.first_row, f32[64,64,128]{2,1,0:T(8,128)S(1)} %get-tuple-element.100.held, f32[32,64,128]{2,1,0:T(8,128)S(1)} %get-tuple-element.101.last_row), custom_call_target="tpu_custom_call" | custom-call | flops 1 | bytes 1 | tf_op jit(solution)/shard_map/near_blocks/pallas_call | solution.py:541
  30.6 0.0 collective-permute-done.7.refs_5_.refs_1_
  30.6 0.0 collective-permute-done.8.refs_6_.refs_2_
  30.6 1.2 %left_middle.1 = (bf16[204,64,256]{2,1,0:T(8,128)(2,1)S(1)}, f32[64,64,128]{2,1,0:T(8,128)S(1)}, bf16[136,64,256]{2,1,0:T(8,128)(2,1)S(1)}, f32[16,64,128]{2,1,0:T(8,128)S(1)}) custom-call(bf16[128,64,384]{2,1,0:T(8,128)(2,1)S(1)} %fine_blocks.1.refs_0_, f32[128,64,128]{2,1,0:T(8,128)S(1)} %get-tuple-element.107.refs_1_, ...), custom_call_target="tpu_custom_call", output_to_operand_aliasing={{0}: (4, {})} | custom-call | flops 99999997952 | bytes 1 | tf_op jit(solution)/shard_map/left_middle/pallas_call | solution.py:534
  31.8 2.8 %collective-permute-start.16 = (f32[16,64,128]{2,1,0:T(8,128)S(1)}, f32[16,64,128]{2,1,0:T(8,128)S(1)}, u32[]{:S(2)}, u32[]{:S(2)}) collective-permute-start(f32[16,64,128]{2,1,0:T(8,128)S(1)} %get-tuple-element.125), channel_id=1, source_target_pairs={{0,2},{1,3},{2,0},{3,1},{4,6},{5,7},{6,4},{7,5},{8,16},{9,17},{10,... | collective-permute-start | bytes 1572872 | tf_op jit(solution)/shard_map/ppermute | solution.py:596
  34.7 0.0 collective-permute-done.6.refs_0_
  34.7 0.2 left_halo.1.refs_3_.refs_4_
  34.8 2.3 %left_inner.1 = (f32[64,64,128]{2,1,0:T(8,128)S(1)}, bf16[136,64,256]{2,1,0:T(8,128)(2,1)S(1)}, f32[30,64,128]{2,1,0:T(8,128)S(1)}) custom-call(bf16[128,64,384]{2,1,0:T(8,128)(2,1)S(1)} %fine_blocks.1.refs_0_, f32[128,64,128]{2,1,0:T(8,128)S(1)} %get-tuple-element.107.refs_1_, ...), custom_call_target="tpu_custom_call", output_to_operand_aliasing={{0}: (4, {}), {1}: (5, {})} | custom-call | flops 1 | bytes 1 | tf_op jit(solution)/shard_map/left_inner/pallas_call | solution.py:534
  37.2 0.0 collective-permute-done.5.refs_3_
  37.2 1.5 %left_ends.1 = (bf16[204,64,256]{2,1,0:T(8,128)(2,1)S(1)}, f32[64,64,128]{2,1,0:T(8,128)S(1)}, bf16[136,64,256]{2,1,0:T(8,128)(2,1)S(1)}, f32[16,64,128]{2,1,0:T...) custom-call(bf16[128,64,384]{2,1,0:T(8,128)(2,1)S(1)} %fine_blocks.1, ...), custom_call_target="tpu_custom_call", output_to_operand_aliasing={{0}: (4, {}), {1}: (5, {}), {2}: (6, {})} | custom-call | flops 99999997952 | bytes 1 | tf_op jit(solution)/shard_map/left_ends/pallas_call | solution.py:534
  38.6 0.8 %collective-permute-start.11 = (f32[2,64,128]{2,1,0:T(8,128)S(1)}, f32[2,64,128]{2,1,0:T(8,128)S(1)}, u32[]{:S(2)}, u32[]{:S(2)}) collective-permute-start(f32[2,64,128]{2,1,0:T(8,128)S(1)} %get-tuple-element.119), channel_id=1, source_target_pairs={{0,1},{1,0},{2,3},{3,2},{4,5},{5,4},{6,7},{7,6},{8,9},{9,8},{10,11... | collective-permute-start | bytes 196616 | tf_op jit(solution)/shard_map/ppermute | solution.py:602
  39.5 0.0 collective-permute-start.12
  39.5 2.7 %collective-permute-start.10 = (f32[16,64,128]{2,1,0:T(8,128)S(1)}, f32[16,64,128]{2,1,0:T(8,128)S(1)}, u32[]{:S(2)}, u32[]{:S(2)}) collective-permute-start(f32[16,64,128]{2,1,0:T(8,128)S(1)} %get-tuple-element.118), channel_id=1, source_target_pairs={{0,2},{1,3},{2,0},{3,1},{4,6},{5,7},{6,4},{7,5},{8,16},{9,17},{10,... | collective-permute-start | bytes 1572872 | tf_op jit(solution)/shard_map/ppermute | solution.py:596
  42.2 0.0 collective-permute-start.14
  42.2 0.8 %collective-permute-done.11.refs_0_ = f32[2,64,128]{2,1,0:T(8,128)S(1)} collective-permute-done((f32[2,64,128]{2,1,0:T(8,128)S(1)}, f32[2,64,128]{2,1,0:T(8,128)S(1)}, u32[]{:S(2)}, u32[]{:S(2)}) %collective-permute-start.11) | collective-permute-done | bytes 65568 | tf_op jit(solution)/shard_map/ppermute | solution.py:602
  43.0 0.0 collective-permute-done.12.refs_1_
  43.0 0.1 pack_first.1
  43.0 3.0 %collective-permute-start.13 = (f32[2,64,128]{2,1,0:T(8,128)S(1)}, f32[2,64,128]{2,1,0:T(8,128)S(1)}, u32[]{:S(2)}, u32[]{:S(2)}) collective-permute-start(f32[2,64,128]{2,1,0:T(8,128)S(1)} %get-tuple-element.122), channel_id=1, source_target_pairs={{0,1},{1,0},{2,3},{3,2},{4,5},{5,4},{6,7},{7,6},{8,16},{9,17},{10,... | collective-permute-start | bytes 196616 | tf_op jit(solution)/shard_map/ppermute | solution.py:733
  46.0 1.1 %coarse_middle.1 = (bf16[136,64,256]{2,1,0:T(8,128)(2,1)S(1)}, f32[64,64,128]{2,1,0:T(8,128)S(1)}, bf16[136,64,256]{2,1,0:T(8,128)(2,1)S(1)}, f32[64,64,128]{2,1,0:T(8,128)S(1)}, f32[14,64,128]{2,1,0:T(8,128)S(1)}) custom-call(s32[8,64]{1,0:T(8,128)S(4)} %get-tuple-element.104.refs_0_, ...), custom_call_target="tpu_custom_call", output_to_operand_aliasing={{0}: (4, {}), {1}: (5, {})} | custom-call | flops 99999997952 | bytes 1 | tf_op jit(solution)/shard_map/coarse_middle/pallas_call | solution.py:534
  47.1 1.2 %collective-permute-start.22 = (f32[14,64,128]{2,1,0:T(8,128)S(1)}, f32[14,64,128]{2,1,0:T(8,128)S(1)}, u32[]{:S(2)}, u32[]{:S(2)}) collective-permute-start(f32[14,64,128]{2,1,0:T(8,128)S(1)} %get-tuple-element.145), channel_id=1, source_target_pairs={{0,2},{1,3},{2,0},{3,1},{4,6},{5,7},{6,4},{7,5},{8,16},{9,17},{10,... | collective-permute-start | bytes 1376264 | tf_op jit(solution)/shard_map/ppermute | solution.py:596
  48.4 0.1 coarse_halo.1.refs_3_.refs_5_
  48.5 2.1 %coarse_inner.1 = (f32[64,64,128]{2,1,0:T(8,128)S(1)}, bf16[136,64,256]{2,1,0:T(8,128)(2,1)S(1)}, f32[64,64,128]{2,1,0:T(8,128)S(1)}, f32[30,64,128]{2,1,0:T(8,128)S(1)}) custom-call(s32[8,64]{1,0:T(8,128)S(4)} %get-tuple-element.104.refs_0_, ...), custom_call_target="tpu_custom_call", output_to_operand_aliasing={{0}: (4, {}), {1}: (5, {}), {2}: (6, {})} | custom-call | flops 1 | bytes 1 | tf_op jit(solution)/shard_map/coarse_inner/pallas_call | solution.py:534
  50.6 0.1 collective-permute-start.17
  50.7 1.6 %coarse_ends.1 = (bf16[136,64,256]{2,1,0:T(8,128)(2,1)S(1)}, f32[64,64,128]{2,1,0:T(8,128)S(1)}, bf16[136,64,256]{2,1,0:T(8,128)(2,1)S(1)}, f32[64,64,128]{2,1,0...) custom-call(s32[8,64]{1,0:T(8,128)S(4)} %get-tuple-element.104.refs_, ...), custom_call_target="tpu_custom_call", output_to_operand_aliasing={{0}: (5, {}), {1}: (6, {}), {2}: (7, {}), {3}: (8, {})} | custom-call | flops 99999997952 | bytes 1 | tf_op jit(solution)/shard_map/coarse_ends/pallas_call | solution.py:534
  52.4 1.3 %collective-permute-start.19 = (f32[2,64,128]{2,1,0:T(8,128)S(1)}, f32[2,64,128]{2,1,0:T(8,128)S(1)}, u32[]{:S(2)}, u32[]{:S(2)}) collective-permute-start(f32[2,64,128]{2,1,0:T(8,128)S(1)} %get-tuple-element.141), channel_id=1, source_target_pairs={{0,1},{1,0},{2,3},{3,2},{4,5},{5,4},{6,7},{7,6},{8,9},{9,8},{10,11... | collective-permute-start | bytes 196616 | tf_op jit(solution)/shard_map/ppermute | solution.py:602
  53.7 0.2 collective-permute-start.20
  53.9 2.0 %collective-permute-start.18 = (f32[9,64,128]{2,1,0:T(8,128)S(1)}, f32[9,64,128]{2,1,0:T(8,128)S(1)}, u32[]{:S(2)}, u32[]{:S(2)}) collective-permute-start(f32[9,64,128]{2,1,0:T(8,128)S(1)} %get-tuple-element.140), channel_id=1, source_target_pairs={{0,2},{1,3},{2,0},{3,1},{4,6},{5,7},{6,4},{7,5},{8,16},{9,17},{10,... | collective-permute-start | bytes 884744 | tf_op jit(solution)/shard_map/ppermute | solution.py:596
  56.0 0.0 collective-permute-start.24
  56.0 2.9 %last_inner.1 = (bf16[136,64,256]{2,1,0:T(8,128)(2,1)S(1)}, f32[32,64,128]{2,1,0:T(8,128)S(1)}, f32[64,64,128]{2,1,0:T(8,128)}) custom-call(s32[8,64]{1,0:T(8,128)S(4)} %get-tuple-element.104.refs_0_, bf16[64,64,512]{2,1,0:T(8,128)(2,1)S(1)} %get-tuple-element.105.refs_7_.refs_1_, ...), custom_call_target="tpu_custom_call", output_to_operand_aliasing={{0}: (6, {})} | custom-call | flops 1 | bytes 1 | tf_op jit(solution)/shard_map/last_inner/pallas_call | solution.py:534
  58.9 0.1 pack_second.1
  59.0 1.8 %collective-permute-start.23 = (f32[2,64,128]{2,1,0:T(8,128)S(1)}, f32[2,64,128]{2,1,0:T(8,128)S(1)}, u32[]{:S(2)}, u32[]{:S(2)}) collective-permute-start(f32[2,64,128]{2,1,0:T(8,128)S(1)} %get-tuple-element.154), channel_id=1, source_target_pairs={{0,1},{1,0},{2,3},{3,2},{4,5},{5,4},{6,7},{7,6},{8,16},{9,17},{10,... | collective-permute-start | bytes 196616 | tf_op jit(solution)/shard_map/ppermute | solution.py:792
  60.8 0.8 %last_middle.1 = (bf16[136,64,256]{2,1,0:T(8,128)(2,1)S(1)}, f32[32,64,128]{2,1,0:T(8,128)S(1)}) custom-call(s32[8,64]{1,0:T(8,128)S(4)} %get-tuple-element.104.refs_0_, bf16[64,64,512]{2,1,0:T(8,128)(2,1)S(1)} %get-tuple-element.105.refs_7_.refs_1_, ...), custom_call_target="tpu_custom_call", output_to_operand_aliasing={{0}: (5, {}), {1}: (6, {})} | custom-call | flops 99999997952 | bytes 1 | tf_op jit(solution)/shard_map/last_middle/pallas_call | solution.py:534
  61.6 0.5 collective-permute-done.21.refs_4_
  62.1 0.4 last_sides.1
  62.5 0.6 last_low.1
  63.1 1.4 %collective-permute-done.24.refs_7_ = f32[9,64,128]{2,1,0:T(8,128)S(1)} collective-permute-done((f32[9,64,128]{2,1,0:T(8,128)S(1)}, f32[9,64,128]{2,1,0:T(8,128)S(1)}, u32[]{:S(2)}, u32[]{:S(2)}) %collective-permute-start.24) | collective-permute-done | bytes 294944 | tf_op jit(solution)/shard_map/ppermute | solution.py:596
  64.5 1.6 %last_high.1 = (bf16[136,64,256]{2,1,0:T(8,128)(2,1)S(1)}, f32[32,64,128]{2,1,0:T(8,128)}) custom-call(s32[8,64]{1,0:T(8,128)S(4)} %get-tuple-element.104.refs_0_, bf16[64,64,512]{2,1,0:T(8,128)(2,1)S(1)} %get-tuple-element.105.refs_7_.refs_1_, bf16[64,64,128]{2,1,0:T(8,128)(2,1)S(1)} %get-tuple-element.106.refs_2_, ...), custom_call_target="tpu_custom_call", output_to_operand_aliasing={{0}: (4, {})} | custom-call | flops 1 | bytes 1 | tf_op jit(solution)/shard_map/last_high/pallas_call | solution.py:534
  (27 shorter events, 0.1 us)
Async XLA Ops:
  3.2 13.2 %collective-permute-start.4 = (f32[16,64,128]{2,1,0:T(8,128)S(1)}, f32[16,64,128]{2,1,0:T(8,128)S(1)}, u32[]{:S(2)}, u32[]{:S(2)}) collective-permute-start(f32[16,64,128]{2,1,0:T(8,128)S(1)} %get-tuple-element.87), channel_id=1, source_target_pairs={{8,16},{9,17},{10,18},{11,19},{12,20},{13,21},{14,22},{15,23},{16,... | collective-permute-start | bytes 1572872 | tf_op jit(solution)/shard_map/ppermute | solution.py:629
  3.9 7.3 %copy-start = (bf16[128,64,4,64]{0,3,2,1:T(8,128)(2,1)S(1)}, bf16[128,64,4,64]{0,3,2,1:T(8,128)(2,1)}, u32[]{:S(2)}) copy-start(bf16[128,64,4,64]{0,3,2,1:T(8,128)(2,1)} %param.9) | copy-start | bytes 12582916
  3.9 7.2 %copy-start.1 = (bf16[128,64,64]{0,2,1:T(8,128)(2,1)S(1)}, bf16[128,64,64]{0,2,1:T(8,128)(2,1)}, u32[]{:S(2)}) copy-start(bf16[128,64,64]{0,2,1:T(8,128)(2,1)} %param.11) | copy-start | bytes 3145732
  3.9 7.2 %copy-start.2 = (bf16[128,64,64]{0,2,1:T(8,128)(2,1)S(1)}, bf16[128,64,64]{0,2,1:T(8,128)(2,1)}, u32[]{:S(2)}) copy-start(bf16[128,64,64]{0,2,1:T(8,128)(2,1)} %param.10) | copy-start | bytes 3145732
  5.3 11.1 %collective-permute-start.2 = (f32[4,64,128]{2,1,0:T(8,128)S(1)}, f32[4,64,128]{2,1,0:T(8,128)S(1)}, u32[]{:S(2)}, u32[]{:S(2)}) collective-permute-start(f32[4,64,128]{2,1,0:T(8,128)S(1)} %get-tuple-element.85), channel_id=1, source_target_pairs={{0,1},{1,0},{2,3},{3,2},{4,5},{5,4},{6,7},{7,6},{8,9},{9,8},{10,11... | collective-permute-start | bytes 393224 | tf_op jit(solution)/shard_map/ppermute | solution.py:602
  8.3 8.1 %collective-permute-start.3 = (f32[4,64,128]{2,1,0:T(8,128)S(1)}, f32[4,64,128]{2,1,0:T(8,128)S(1)}, u32[]{:S(2)}, u32[]{:S(2)}) collective-permute-start(f32[4,64,128]{2,1,0:T(8,128)S(1)} %get-tuple-element.86), channel_id=1, source_target_pairs={{0,8},{1,2},{2,1},{3,4},{4,3},{5,6},{6,5},{7,15},{8,0},{9,10},{10,... | collective-permute-start | bytes 393224 | tf_op jit(solution)/shard_map/ppermute | solution.py:605
  10.9 10.0 %collective-permute-start = (f32[16,64,128]{2,1,0:T(8,128)S(1)}, f32[16,64,128]{2,1,0:T(8,128)S(1)}, u32[]{:S(2)}, u32[]{:S(2)}) collective-permute-start(f32[16,64,128]{2,1,0:T(8,128)S(1)} %get-tuple-element.84), channel_id=1, source_target_pairs={{0,2},{1,3},{2,0},{3,1},{4,6},{5,7},{6,4},{7,5},{8,16},{9,17},{10,... | collective-permute-start | bytes 1572872 | tf_op jit(solution)/shard_map/ppermute | solution.py:596
  10.9 8.5 %collective-permute-start.1 = (f32[32,64,128]{2,1,0:T(8,128)S(1)}, f32[32,64,128]{2,1,0:T(8,128)S(1)}, u32[]{:S(2)}, u32[]{:S(2)}) collective-permute-start(f32[32,64,128]{2,1,0:T(8,128)S(1)} %get-tuple-element.83.refs_4_), channel_id=1, source_target_pairs={{0,8},{1,9},{2,10},{3,11},{4,12},{5,13},{6,14},{7,15},{8,0},{9,1},... | collective-permute-start | bytes 3145736 | tf_op jit(solution)/shard_map/ppermute | solution.py:599
  17.3 13.3 %collective-permute-start.9 = (f32[16,64,128]{2,1,0:T(8,128)S(1)}, f32[16,64,128]{2,1,0:T(8,128)S(1)}, u32[]{:S(2)}, u32[]{:S(2)}) collective-permute-start(f32[16,64,128]{2,1,0:T(8,128)S(1)} %get-tuple-element.111), channel_id=1, source_target_pairs={{0,2},{1,3},{2,0},{3,1},{4,6},{5,7},{6,4},{7,5},{8,16},{9,17},{10,... | collective-permute-start | bytes 1572872 | tf_op jit(solution)/shard_map/ppermute | solution.py:596
  20.8 6.4 %slice-start = ((s8[8388608]{0:T(1024)(128)(4,1)}), s8[4194304]{0:T(1024)(128)(4,1)S(1)}, s32[]{:S(2)}) async-start(s8[8388608]{0:T(1024)(128)(4,1)} %bitcast.6), calls=%async_computation | async-start | bytes 8388608
  20.9 5.5 %copy-start.3 = (bf16[64,64,64]{2,1,0:T(8,128)(2,1)S(1)}, bf16[64,64,64]{2,1,0:T(8,128)(2,1)}, u32[]{:S(2)}) copy-start(bf16[64,64,64]{2,1,0:T(8,128)(2,1)} %refs_0_.3) | copy-start | bytes 1572868
  20.9 5.5 %copy-start.4 = (bf16[64,64,64]{2,1,0:T(8,128)(2,1)S(1)}, bf16[64,64,64]{2,1,0:T(8,128)(2,1)}, u32[]{:S(2)}) copy-start(bf16[64,64,64]{2,1,0:T(8,128)(2,1)} %refs_1_.1) | copy-start | bytes 1572868
  20.9 5.5 %copy-start.5 = (s32[64,8]{0,1:T(8,128)S(1)}, s32[64,8]{0,1:T(8,128)}, u32[]{:S(2)}) copy-start(s32[64,8]{0,1:T(8,128)} %param.15) | copy-start | bytes 6148
  20.9 6.4 %slice-start.1 = ((s8[8388608]{0:T(1024)(128)(4,1)}), s8[4194304]{0:T(1024)(128)(4,1)S(1)}, s32[]{:S(2)}) async-start(s8[8388608]{0:T(1024)(128)(4,1)} %bitcast.6), calls=%async_computation.1 | async-start | bytes 8388608
  22.1 8.5 %collective-permute-start.7 = (f32[4,64,128]{2,1,0:T(8,128)S(1)}, f32[4,64,128]{2,1,0:T(8,128)S(1)}, u32[]{:S(2)}, u32[]{:S(2)}) collective-permute-start(f32[4,64,128]{2,1,0:T(8,128)S(1)} %get-tuple-element.109), channel_id=1, source_target_pairs={{0,1},{1,0},{2,3},{3,2},{4,5},{5,4},{6,7},{7,6},{8,9},{9,8},{10,11... | collective-permute-start | bytes 393224 | tf_op jit(solution)/shard_map/ppermute | solution.py:602
  24.8 5.8 %collective-permute-start.8 = (f32[4,64,128]{2,1,0:T(8,128)S(1)}, f32[4,64,128]{2,1,0:T(8,128)S(1)}, u32[]{:S(2)}, u32[]{:S(2)}) collective-permute-start(f32[4,64,128]{2,1,0:T(8,128)S(1)} %get-tuple-element.110), channel_id=1, source_target_pairs={{0,8},{1,2},{2,1},{3,4},{4,3},{5,6},{6,5},{7,15},{8,0},{9,10},{10,... | collective-permute-start | bytes 393224 | tf_op jit(solution)/shard_map/ppermute | solution.py:605
  24.8 12.4 %collective-permute-start.5 = (f32[16,64,128]{2,1,0:T(8,128)S(1)}, f32[16,64,128]{2,1,0:T(8,128)S(1)}, u32[]{:S(2)}, u32[]{:S(2)}) collective-permute-start(f32[16,64,128]{2,1,0:T(8,128)S(1)} %get-tuple-element.103.refs_3_), channel_id=1, source_target_pairs={{0,2},{1,3},{2,0},{3,1},{4,6},{5,7},{6,4},{7,5},{8,16},{9,17},{10,... | collective-permute-start | bytes 1572872 | tf_op jit(solution)/shard_map/ppermute | solution.py:596
  26.3 8.3 %collective-permute-start.6 = (f32[32,64,128]{2,1,0:T(8,128)S(1)}, f32[32,64,128]{2,1,0:T(8,128)S(1)}, u32[]{:S(2)}, u32[]{:S(2)}) collective-permute-start(f32[32,64,128]{2,1,0:T(8,128)S(1)} %get-tuple-element.108), channel_id=1, source_target_pairs={{0,8},{1,9},{2,10},{3,11},{4,12},{5,13},{6,14},{7,15},{8,0},{9,1},... | collective-permute-start | bytes 3145736 | tf_op jit(solution)/shard_map/ppermute | solution.py:599
  31.8 14.2 %collective-permute-start.16 = (f32[16,64,128]{2,1,0:T(8,128)S(1)}, f32[16,64,128]{2,1,0:T(8,128)S(1)}, u32[]{:S(2)}, u32[]{:S(2)}) collective-permute-start(f32[16,64,128]{2,1,0:T(8,128)S(1)} %get-tuple-element.125), channel_id=1, source_target_pairs={{0,2},{1,3},{2,0},{3,1},{4,6},{5,7},{6,4},{7,5},{8,16},{9,17},{10,... | collective-permute-start | bytes 1572872 | tf_op jit(solution)/shard_map/ppermute | solution.py:596
  38.6 4.3 %collective-permute-start.11 = (f32[2,64,128]{2,1,0:T(8,128)S(1)}, f32[2,64,128]{2,1,0:T(8,128)S(1)}, u32[]{:S(2)}, u32[]{:S(2)}) collective-permute-start(f32[2,64,128]{2,1,0:T(8,128)S(1)} %get-tuple-element.119), channel_id=1, source_target_pairs={{0,1},{1,0},{2,3},{3,2},{4,5},{5,4},{6,7},{7,6},{8,9},{9,8},{10,11... | collective-permute-start | bytes 196616 | tf_op jit(solution)/shard_map/ppermute | solution.py:602
  39.5 3.5 %collective-permute-start.12 = (f32[2,64,128]{2,1,0:T(8,128)S(1)}, f32[2,64,128]{2,1,0:T(8,128)S(1)}, u32[]{:S(2)}, u32[]{:S(2)}) collective-permute-start(f32[2,64,128]{2,1,0:T(8,128)S(1)} %get-tuple-element.120), channel_id=1, source_target_pairs={{0,8},{1,2},{2,1},{3,4},{4,3},{5,6},{6,5},{7,15},{8,0},{9,10},{10,... | collective-permute-start | bytes 196616 | tf_op jit(solution)/shard_map/ppermute | solution.py:605
  39.5 11.3 %collective-permute-start.10 = (f32[16,64,128]{2,1,0:T(8,128)S(1)}, f32[16,64,128]{2,1,0:T(8,128)S(1)}, u32[]{:S(2)}, u32[]{:S(2)}) collective-permute-start(f32[16,64,128]{2,1,0:T(8,128)S(1)} %get-tuple-element.118), channel_id=1, source_target_pairs={{0,2},{1,3},{2,0},{3,1},{4,6},{5,7},{6,4},{7,5},{8,16},{9,17},{10,... | collective-permute-start | bytes 1572872 | tf_op jit(solution)/shard_map/ppermute | solution.py:596
  42.2 6.2 %collective-permute-start.14 = (f32[30,64,128]{2,1,0:T(8,128)S(1)}, f32[30,64,128]{2,1,0:T(8,128)S(1)}, u32[]{:S(2)}, u32[]{:S(2)}) collective-permute-start(f32[30,64,128]{2,1,0:T(8,128)S(1)} %get-tuple-element.123), channel_id=1, source_target_pairs={{0,8},{1,9},{2,10},{3,11},{4,12},{5,13},{6,14},{7,15},{8,0},{9,1},... | collective-permute-start | bytes 2949128 | tf_op jit(solution)/shard_map/ppermute | solution.py:599
  43.0 7.7 %collective-permute-start.13 = (f32[2,64,128]{2,1,0:T(8,128)S(1)}, f32[2,64,128]{2,1,0:T(8,128)S(1)}, u32[]{:S(2)}, u32[]{:S(2)}) collective-permute-start(f32[2,64,128]{2,1,0:T(8,128)S(1)} %get-tuple-element.122), channel_id=1, source_target_pairs={{0,1},{1,0},{2,3},{3,2},{4,5},{5,4},{6,7},{7,6},{8,16},{9,17},{10,... | collective-permute-start | bytes 196616 | tf_op jit(solution)/shard_map/ppermute | solution.py:733
  46.0 2.4 %collective-permute-start.15 = (f32[4,64,128]{2,1,0:T(8,128)S(1)}, f32[4,64,128]{2,1,0:T(8,128)S(1)}, u32[]{:S(2)}, u32[]{:S(2)}) collective-permute-start(f32[4,64,128]{2,1,0:T(8,128)S(1)} %get-tuple-element.124), channel_id=1, source_target_pairs={{0,8},{1,9},{2,10},{3,11},{4,12},{5,13},{6,14},{7,15},{8,0},{9,1},... | collective-permute-start | bytes 393224 | tf_op jit(solution)/shard_map/ppermute | solution.py:599
  47.1 13.7 %collective-permute-start.22 = (f32[14,64,128]{2,1,0:T(8,128)S(1)}, f32[14,64,128]{2,1,0:T(8,128)S(1)}, u32[]{:S(2)}, u32[]{:S(2)}) collective-permute-start(f32[14,64,128]{2,1,0:T(8,128)S(1)} %get-tuple-element.145), channel_id=1, source_target_pairs={{0,2},{1,3},{2,0},{3,1},{4,6},{5,7},{6,4},{7,5},{8,16},{9,17},{10,... | collective-permute-start | bytes 1376264 | tf_op jit(solution)/shard_map/ppermute | solution.py:596
  50.6 5.3 %collective-permute-start.17 = (f32[30,64,128]{2,1,0:T(8,128)S(1)}, f32[30,64,128]{2,1,0:T(8,128)S(1)}, u32[]{:S(2)}, u32[]{:S(2)}) collective-permute-start(f32[30,64,128]{2,1,0:T(8,128)S(1)} %get-tuple-element.136), channel_id=1, source_target_pairs={{0,8},{1,9},{2,10},{3,11},{4,12},{5,13},{6,14},{7,15},{8,0},{9,1},... | collective-permute-start | bytes 2949128 | tf_op jit(solution)/shard_map/ppermute | solution.py:599
  52.4 6.5 %collective-permute-start.19 = (f32[2,64,128]{2,1,0:T(8,128)S(1)}, f32[2,64,128]{2,1,0:T(8,128)S(1)}, u32[]{:S(2)}, u32[]{:S(2)}) collective-permute-start(f32[2,64,128]{2,1,0:T(8,128)S(1)} %get-tuple-element.141), channel_id=1, source_target_pairs={{0,1},{1,0},{2,3},{3,2},{4,5},{5,4},{6,7},{7,6},{8,9},{9,8},{10,11... | collective-permute-start | bytes 196616 | tf_op jit(solution)/shard_map/ppermute | solution.py:602
  53.7 5.2 %collective-permute-start.20 = (f32[2,64,128]{2,1,0:T(8,128)S(1)}, f32[2,64,128]{2,1,0:T(8,128)S(1)}, u32[]{:S(2)}, u32[]{:S(2)}) collective-permute-start(f32[2,64,128]{2,1,0:T(8,128)S(1)} %get-tuple-element.142), channel_id=1, source_target_pairs={{0,8},{1,2},{2,1},{3,4},{4,3},{5,6},{6,5},{7,15},{8,0},{9,10},{10,... | collective-permute-start | bytes 196616 | tf_op jit(solution)/shard_map/ppermute | solution.py:605
  53.9 8.6 %collective-permute-start.18 = (f32[9,64,128]{2,1,0:T(8,128)S(1)}, f32[9,64,128]{2,1,0:T(8,128)S(1)}, u32[]{:S(2)}, u32[]{:S(2)}) collective-permute-start(f32[9,64,128]{2,1,0:T(8,128)S(1)} %get-tuple-element.140), channel_id=1, source_target_pairs={{0,2},{1,3},{2,0},{3,1},{4,6},{5,7},{6,4},{7,5},{8,16},{9,17},{10,... | collective-permute-start | bytes 884744 | tf_op jit(solution)/shard_map/ppermute | solution.py:596
  56.0 8.6 %collective-permute-start.24 = (f32[9,64,128]{2,1,0:T(8,128)S(1)}, f32[9,64,128]{2,1,0:T(8,128)S(1)}, u32[]{:S(2)}, u32[]{:S(2)}) collective-permute-start(f32[9,64,128]{2,1,0:T(8,128)S(1)} %get-tuple-element.155), channel_id=1, source_target_pairs={{0,2},{1,3},{2,0},{3,1},{4,6},{5,7},{6,4},{7,5},{8,16},{9,17},{10,... | collective-permute-start | bytes 884744 | tf_op jit(solution)/shard_map/ppermute | solution.py:596
  59.0 5.5 %collective-permute-start.23 = (f32[2,64,128]{2,1,0:T(8,128)S(1)}, f32[2,64,128]{2,1,0:T(8,128)S(1)}, u32[]{:S(2)}, u32[]{:S(2)}) collective-permute-start(f32[2,64,128]{2,1,0:T(8,128)S(1)} %get-tuple-element.154), channel_id=1, source_target_pairs={{0,1},{1,0},{2,3},{3,2},{4,5},{5,4},{6,7},{7,6},{8,16},{9,17},{10,... | collective-permute-start | bytes 196616 | tf_op jit(solution)/shard_map/ppermute | solution.py:792
  60.8 1.3 %collective-permute-start.21 = (f32[4,64,128]{2,1,0:T(8,128)S(1)}, f32[4,64,128]{2,1,0:T(8,128)S(1)}, u32[]{:S(2)}, u32[]{:S(2)}) collective-permute-start(f32[4,64,128]{2,1,0:T(8,128)S(1)} %get-tuple-element.144), channel_id=1, source_target_pairs={{0,8},{1,9},{2,10},{3,11},{4,12},{5,13},{6,14},{7,15},{8,0},{9,1},... | collective-permute-start | bytes 393224 | tf_op jit(solution)/shard_map/ppermute | solution.py:599

commit v6 on v5

--- a/solution.py
+++ b/solution.py
@@ -536,7 +536,7 @@
 
 def near_blocks_call(coupling, first_row, held, last_row, count):
     cells, species = coupling.shape[:2]
-    part = cells // 8
+    part = cells // 4
     here = [pltpu.with_memory_space_constraint(x, pltpu.VMEM) for x in (first_row, held, last_row)]
     return pl.pallas_call(
         near_blocks_kernel,
@@ -553,7 +553,7 @@
         ],
         out_specs=(IN_VMEM, IN_HBM),
         scratch_shapes=[pltpu.SemaphoreType.DMA((BLOCK_X,))],
-        compiler_params=pltpu.CompilerParams(vmem_limit_bytes=5 * 2**20),
+        compiler_params=pltpu.CompilerParams(vmem_limit_bytes=7 * 2**20),
         cost_estimate=pl.CostEstimate(flops=1, bytes_accessed=1, transcendentals=0),
         name="near_blocks",
     )(coupling, *here)
@@ -767,7 +767,7 @@
         smem=(0,),
         cost=LONG,
     )
-    far_low, far_high = far(far_low), far(far_high)
+    far_low, far_high = (lax.ppermute(x, BOTH, corner_pairs) for x in (far_low, far_high))
     even_h, odd_h = even(even_s), odd(odd_s)
     state = [padded(COARSE_X), field(coarse_cells // 2)]
     half = BLOCK_Y // 2

time: 66.5 us -> 66.5 us (level)
    ppermute x0 -> x2, starting transfers between devices: none -> 2.03 us  [on_device(): lax.ppermute(x, BOTH, corner_pairs)]
    ppermute x8 -> x6, starting transfers between devices: 12.5 us -> 10.5 us  [far(): return lax.ppermute(x, BOTH, far_pairs)]
    ppermute x8 -> x6, waiting for transfers between devices: 1.42 us -> 0.02 us  [far(): return lax.ppermute(x, BOTH, far_pairs)]
    ppermute x2, waiting for transfers between devices: 0.01 us -> 0.7 us  [on_device(): corners, beside = (lax.ppermute(corners, BOTH, corner_pairs), near(beside))]
    ppermute x0 -> x2, waiting for transfers between devices: none -> 0.69 us  [on_device(): lax.ppermute(x, BOTH, corner_pairs)]
  transfers between devices with their start and end apart: 25 -> 25, of which waited for: 3 -> 4; matrix products, arithmetic and copies ran while one was open for 0% -> 0% of each run, Pallas kernels for 44% -> 44%
where the time goes in v6:
time: 66.5 us; the launch traced here: 66.3 us
  Pallas kernels  33.3 us (50%)
  starting transfers between devices  29.1 us (44%)
  waiting for transfers between devices  2.72 us (4%)
  between operations  1.16 us (2%)
    pallas_call x23, Pallas kernels, run(): called(*(pltpu.with_memory_space_constraint(x, space) for x, space in zip...  30.1 us
    ppermute x6, starting transfers between devices, far(): return lax.ppermute(x, BOTH, far_pairs)  10.5 us
    ppermute x4, starting transfers between devices, even(): return lax.ppermute(x, BOTH, even_pairs)  7.87 us
    ppermute x2, starting transfers between devices, on_device(): corners, beside = (lax.ppermute(corners, BOTH, corner_pairs), near(beside))  4.83 us
    pallas_call x1, Pallas kernels, near_blocks_call(): pl.pallas_call(near_blocks_kernel, grid=(cells // part,), out_shape=(pltp...  3.16 us
    ppermute x4, starting transfers between devices, odd(): return lax.ppermute(x, BOTH, odd_pairs)  2.78 us
    ppermute x2, starting transfers between devices, on_device(): lax.ppermute(x, BOTH, corner_pairs)  2.03 us
  transfers between devices with their start and end apart: 25, of which 4 were waited for; matrix products, arithmetic and copies ran while one was open for 0% of the time, Pallas kernels for 44%

profile of v6, /device:TPU:0, one launch (start us, length us, event | category | flops | bytes accessed | tf_op | source)
XLA Modules:
  0.0 66.3 jit_solution(8197832605665404801)
XLA Ops:
  0.6 2.6 %start.1 = (bf16[128,64,384]{2,1,0:T(8,128)(2,1)S(1)}, bf16[204,64,256]{2,1,0:T(8,128)(2,1)S(1)}, f32[128,64,128]{2,1,0:T(8,128)S(1)}, f32[16,64,128]{2,1,0:T(8,128)S(1)}, f32[16,64,128]{2,1,0:T(8,128)S(1)}) custom-call(f32[128,64,128]{2,1,0:T(8,128)} %refs_0_.2, bf16[64,64,128]{2,1,0:T(8,128)(2,1)} %bitcast.9), custom_call_target="tpu_custom_call" | custom-call | flops 1 | bytes 1 | tf_op jit(solution)/shard_map/start/pallas_call | solution.py:534
  3.2 0.7 %collective-permute-start.4 = (f32[16,64,128]{2,1,0:T(8,128)S(1)}, f32[16,64,128]{2,1,0:T(8,128)S(1)}, u32[]{:S(2)}, u32[]{:S(2)}) collective-permute-start(f32[16,64,128]{2,1,0:T(8,128)S(1)} %get-tuple-element.87), channel_id=1, source_target_pairs={{8,16},{9,17},{10,18},{11,19},{12,20},{13,21},{14,22},{15,23},{16,... | collective-permute-start | bytes 1572872 | tf_op jit(solution)/shard_map/ppermute | solution.py:629
  3.9 0.0 copy-start
  3.9 0.0 copy-start.1
  3.9 0.0 copy-start.2
  3.9 1.4 %first.1 = (bf16[204,64,256]{2,1,0:T(8,128)(2,1)S(1)}, f32[32,64,128]{2,1,0:T(8,128)S(1)}, f32[4,64,128]{2,1,0:T(8,128)S(1)}, f32[4,64,128]{2,1,0:T(8,128)S(1)}) custom-call(f32[128,64,128]{2,1,0:T(8,128)S(1)} %get-tuple-element.81.refs_0_.refs_2_, bf16[128,64,384]{2,1,0:T(8,128)(2,1)S(1)} %get-tuple-element.80.refs_1_.refs_3_, ...), custom_call_target="tpu_custom_call", output_to_operand_aliasing={{0}: (2, {})} | custom-call | flops 1 | bytes 1 | tf_op jit(solution)/shard_map/first/pallas_call | solution.py:534
  5.3 3.0 %collective-permute-start.2 = (f32[4,64,128]{2,1,0:T(8,128)S(1)}, f32[4,64,128]{2,1,0:T(8,128)S(1)}, u32[]{:S(2)}, u32[]{:S(2)}) collective-permute-start(f32[4,64,128]{2,1,0:T(8,128)S(1)} %get-tuple-element.85), channel_id=1, source_target_pairs={{0,1},{1,0},{2,3},{3,2},{4,5},{5,4},{6,7},{7,6},{8,9},{9,8},{10,11... | collective-permute-start | bytes 393224 | tf_op jit(solution)/shard_map/ppermute | solution.py:602
  8.3 2.6 %collective-permute-start.3 = (f32[4,64,128]{2,1,0:T(8,128)S(1)}, f32[4,64,128]{2,1,0:T(8,128)S(1)}, u32[]{:S(2)}, u32[]{:S(2)}) collective-permute-start(f32[4,64,128]{2,1,0:T(8,128)S(1)} %get-tuple-element.86), channel_id=1, source_target_pairs={{0,8},{1,2},{2,1},{3,4},{4,3},{5,6},{6,5},{7,15},{8,0},{9,10},{10,... | collective-permute-start | bytes 393224 | tf_op jit(solution)/shard_map/ppermute | solution.py:605
  10.9 0.0 collective-permute-start
  10.9 0.3 collective-permute-start.1
  11.2 2.5 %fine_blocks.1.refs_0_ = bf16[128,64,384]{2,1,0:T(8,128)(2,1)S(1)} custom-call(bf16[64,256,128]{2,1,0:T(8,128)(2,1)S(1)} %bitcast.8, bf16[64,64,128]{2,1,0:T(8,128)(2,1)S(1)} %bitcast.11, bf16[64,64,128]{2,1,0:T(8,128)(2,1)S(1)} %bitcast.10, bf16[128,64,384]{2,1,0:T(8,128)(2,1)S(1)} %get-tuple-element.80.refs_1_.refs_3_, ...), custom_call_target="tpu_custom_call", output_to_operand_aliasing={{}: (3, {})} | custom-call | flops 1 | bytes 1 | tf_op jit(solution)/shard_map/fine_blocks/pallas_call | solution.py:534
  13.7 2.7 %fine_inner.1 = (f32[128,64,128]{2,1,0:T(8,128)S(1)}, bf16[204,64,256]{2,1,0:T(8,128)(2,1)S(1)}, f32[64,64,128]{2,1,0:T(8,128)S(1)}) custom-call(bf16[128,64,384]{2,1,0:T(8,128)(2,1)S(1)} %fine_blocks.1.refs_0_, bf16[204,64,256]{2,1,0:T(8,128)(2,1)S(1)} %get-tuple-element.88.refs_1_.refs_2_, ...), custom_call_target="tpu_custom_call", output_to_operand_aliasing={{0}: (2, {})} | custom-call | flops 1 | bytes 1 | tf_op jit(solution)/shard_map/fine_inner/pallas_call | solution.py:534
  16.4 0.0 collective-permute-done.3.refs_6_.refs_3_
  16.4 0.0 collective-permute-done.4.refs_1_
  16.4 0.9 %fine_middle.1 = (bf16[204,64,256]{2,1,0:T(8,128)(2,1)S(1)}, f32[128,64,128]{2,1,0:T(8,128)S(1)}, bf16[204,64,256]{2,1,0:T(8,128)(2,1)S(1)}, f32[32,64,128]{2,1,0:T(8,128)S(1)}, f32[16,64,128]{2,1,0:T(8,128)S(1)}) custom-call(bf16[128,64,384]{2,1,0:T(8,128)(2,1)S(1)} %fine_blocks.1.refs_0_, ...), custom_call_target="tpu_custom_call", output_to_operand_aliasing={{0}: (2, {}), {1}: (3, {}), {2}: (4, {})} | custom-call | flops 99999997952 | bytes 1 | tf_op jit(solution)/shard_map/fine_middle/pallas_call | solution.py:534
  17.3 2.1 %collective-permute-start.9 = (f32[16,64,128]{2,1,0:T(8,128)S(1)}, f32[16,64,128]{2,1,0:T(8,128)S(1)}, u32[]{:S(2)}, u32[]{:S(2)}) collective-permute-start(f32[16,64,128]{2,1,0:T(8,128)S(1)} %get-tuple-element.111), channel_id=1, source_target_pairs={{0,2},{1,3},{2,0},{3,1},{4,6},{5,7},{6,4},{7,5},{8,16},{9,17},{10,... | collective-permute-start | bytes 1572872 | tf_op jit(solution)/shard_map/ppermute | solution.py:596
  19.4 0.0 collective-permute-done.1.refs_1_
  19.4 1.4 %fine_last.1 = (bf16[204,64,256]{2,1,0:T(8,128)(2,1)S(1)}, f32[128,64,128]{2,1,0:T(8,128)S(1)}, bf16[204,64,256]{2,1,0:T(8,128)(2,1)S(1)}, f32[32,64,128]{2,1,0:T(8,128)S(1)}, f32[32,64,128]{2,1,0:T(8,128)S(1)}) custom-call(bf16[128,64,384]{2,1,0:T(8,128)(2,1)S(1)} %fine_blocks.1.refs_0_, ...), custom_call_target="tpu_custom_call", output_to_operand_aliasing={{0}: (4, {}), {1}: (5, {}), {2}: (6, {})} | custom-call | flops 1 | bytes 1 | tf_op jit(solution)/shard_map/fine_last/pallas_call | solution.py:534
  20.8 0.0 slice-start
  20.9 0.0 copy-start.3
  20.9 0.0 copy-start.4
  20.9 0.0 copy-start.5
  20.9 1.2 %fine_ends.1 = (bf16[204,64,256]{2,1,0:T(8,128)(2,1)S(1)}, f32[128,64,128]{2,1,0:T(8,128)S(1)}, bf16[204,64,256]{2,1,0:T(8,128)(2,1)S(1)}, f32[32,64,128]{2,1,0:...) custom-call(bf16[128,64,384]{2,1,0:T(8,128)(2,1)S(1)} %fine_blocks.1, ...), custom_call_target="tpu_custom_call", output_to_operand_aliasing={{0}: (2, {}), {1}: (3, {}), {2}: (4, {}), {3}: (5, {}), {4}... | custom-call | flops 1 | bytes 1 | tf_op jit(solution)/shard_map/fine_ends/pallas_call | solution.py:534
  22.1 2.7 %collective-permute-start.7 = (f32[4,64,128]{2,1,0:T(8,128)S(1)}, f32[4,64,128]{2,1,0:T(8,128)S(1)}, u32[]{:S(2)}, u32[]{:S(2)}) collective-permute-start(f32[4,64,128]{2,1,0:T(8,128)S(1)} %get-tuple-element.109), channel_id=1, source_target_pairs={{0,1},{1,0},{2,3},{3,2},{4,5},{5,4},{6,7},{7,6},{8,9},{9,8},{10,11... | collective-permute-start | bytes 393224 | tf_op jit(solution)/shard_map/ppermute | solution.py:602
  24.8 0.0 collective-permute-start.8
  24.8 1.5 %collective-permute-start.5 = (f32[16,64,128]{2,1,0:T(8,128)S(1)}, f32[16,64,128]{2,1,0:T(8,128)S(1)}, u32[]{:S(2)}, u32[]{:S(2)}) collective-permute-start(f32[16,64,128]{2,1,0:T(8,128)S(1)} %get-tuple-element.103.refs_3_), channel_id=1, source_target_pairs={{0,2},{1,3},{2,0},{3,1},{4,6},{5,7},{6,4},{7,5},{8,16},{9,17},{10,... | collective-permute-start | bytes 1572872 | tf_op jit(solution)/shard_map/ppermute | solution.py:596
  26.3 0.0 collective-permute-start.6
  26.4 0.9 %own_blocks.1 = (bf16[64,64,128]{2,1,0:T(8,128)(2,1)S(1)}, s32[8,64]{1,0:T(8,128)S(4)}) custom-call(bf16[64,64,64]{2,1,0:T(8,128)(2,1)S(1)} %copy-done.3, bf16[64,64,64]{2,1,0:T(8,128)(2,1)S(1)} %copy-done.4, s32[8,64]{1,0:T(8,128)S(1)} %bitcast.12, f32[16,64,128]{2,1,0:T(8,128)S(1)} %get-tuple-element.103.refs_3_), custom_call_target="tpu_custom_call" | custom-call | flops 1 | bytes 1 | tf_op jit(solution)/shard_map/own_blocks/pallas_call | solution.py:534
  27.3 3.2 %near_blocks.1 = (bf16[64,64,512]{2,1,0:T(8,128)(2,1)S(1)}, f32[128,64,128]{2,1,0:T(8,128)}) custom-call(bf16[64,64,8,64]{3,2,1,0:T(8,128)(2,1)S(1)} %bitcast.7, f32[32,64,128]{2,1,0:T(8,128)S(1)} %get-tuple-element.99.first_row, f32[64,64,128]{2,1,0:T(8,128)S(1)} %get-tuple-element.100.held, f32[32,64,128]{2,1,0:T(8,128)S(1)} %get-tuple-element.101.last_row), custom_call_target="tpu_custom_call" | custom-call | flops 1 | bytes 1 | tf_op jit(solution)/shard_map/near_blocks/pallas_call | solution.py:541
  30.5 0.0 collective-permute-done.9.refs_3_
  30.5 0.0 collective-permute-done.7.refs_5_.refs_1_
  30.5 1.2 %left_middle.1 = (bf16[204,64,256]{2,1,0:T(8,128)(2,1)S(1)}, f32[64,64,128]{2,1,0:T(8,128)S(1)}, bf16[136,64,256]{2,1,0:T(8,128)(2,1)S(1)}, f32[16,64,128]{2,1,0:T(8,128)S(1)}) custom-call(bf16[128,64,384]{2,1,0:T(8,128)(2,1)S(1)} %fine_blocks.1.refs_0_, f32[128,64,128]{2,1,0:T(8,128)S(1)} %get-tuple-element.107.refs_1_, ...), custom_call_target="tpu_custom_call", output_to_operand_aliasing={{0}: (4, {})} | custom-call | flops 99999997952 | bytes 1 | tf_op jit(solution)/shard_map/left_middle/pallas_call | solution.py:534
  31.7 3.0 %collective-permute-start.16 = (f32[16,64,128]{2,1,0:T(8,128)S(1)}, f32[16,64,128]{2,1,0:T(8,128)S(1)}, u32[]{:S(2)}, u32[]{:S(2)}) collective-permute-start(f32[16,64,128]{2,1,0:T(8,128)S(1)} %get-tuple-element.125), channel_id=1, source_target_pairs={{0,2},{1,3},{2,0},{3,1},{4,6},{5,7},{6,4},{7,5},{8,16},{9,17},{10,... | collective-permute-start | bytes 1572872 | tf_op jit(solution)/shard_map/ppermute | solution.py:596
  34.7 0.0 collective-permute-done.6.refs_0_
  34.7 0.2 left_halo.1.refs_3_.refs_4_
  34.8 2.3 %left_inner.1 = (f32[64,64,128]{2,1,0:T(8,128)S(1)}, bf16[136,64,256]{2,1,0:T(8,128)(2,1)S(1)}, f32[30,64,128]{2,1,0:T(8,128)S(1)}) custom-call(bf16[128,64,384]{2,1,0:T(8,128)(2,1)S(1)} %fine_blocks.1.refs_0_, f32[128,64,128]{2,1,0:T(8,128)S(1)} %get-tuple-element.107.refs_1_, ...), custom_call_target="tpu_custom_call", output_to_operand_aliasing={{0}: (4, {}), {1}: (5, {})} | custom-call | flops 1 | bytes 1 | tf_op jit(solution)/shard_map/left_inner/pallas_call | solution.py:534
  37.2 0.0 collective-permute-done.5.refs_3_
  37.2 1.5 %left_ends.1 = (bf16[204,64,256]{2,1,0:T(8,128)(2,1)S(1)}, f32[64,64,128]{2,1,0:T(8,128)S(1)}, bf16[136,64,256]{2,1,0:T(8,128)(2,1)S(1)}, f32[16,64,128]{2,1,0:T...) custom-call(bf16[128,64,384]{2,1,0:T(8,128)(2,1)S(1)} %fine_blocks.1, ...), custom_call_target="tpu_custom_call", output_to_operand_aliasing={{0}: (4, {}), {1}: (5, {}), {2}: (6, {})} | custom-call | flops 99999997952 | bytes 1 | tf_op jit(solution)/shard_map/left_ends/pallas_call | solution.py:534
  38.6 0.8 %collective-permute-start.11 = (f32[2,64,128]{2,1,0:T(8,128)S(1)}, f32[2,64,128]{2,1,0:T(8,128)S(1)}, u32[]{:S(2)}, u32[]{:S(2)}) collective-permute-start(f32[2,64,128]{2,1,0:T(8,128)S(1)} %get-tuple-element.119), channel_id=1, source_target_pairs={{0,1},{1,0},{2,3},{3,2},{4,5},{5,4},{6,7},{7,6},{8,9},{9,8},{10,11... | collective-permute-start | bytes 196616 | tf_op jit(solution)/shard_map/ppermute | solution.py:602
  39.5 0.0 collective-permute-start.12
  39.5 2.7 %collective-permute-start.10 = (f32[16,64,128]{2,1,0:T(8,128)S(1)}, f32[16,64,128]{2,1,0:T(8,128)S(1)}, u32[]{:S(2)}, u32[]{:S(2)}) collective-permute-start(f32[16,64,128]{2,1,0:T(8,128)S(1)} %get-tuple-element.118), channel_id=1, source_target_pairs={{0,2},{1,3},{2,0},{3,1},{4,6},{5,7},{6,4},{7,5},{8,16},{9,17},{10,... | collective-permute-start | bytes 1572872 | tf_op jit(solution)/shard_map/ppermute | solution.py:596
  42.2 0.8 %collective-permute-done.11.refs_0_ = f32[2,64,128]{2,1,0:T(8,128)S(1)} collective-permute-done((f32[2,64,128]{2,1,0:T(8,128)S(1)}, f32[2,64,128]{2,1,0:T(8,128)S(1)}, u32[]{:S(2)}, u32[]{:S(2)}) %collective-permute-start.11) | collective-permute-done | bytes 65568 | tf_op jit(solution)/shard_map/ppermute | solution.py:602
  43.0 0.1 pack_first.1
  43.0 3.0 %collective-permute-start.13 = (f32[2,64,128]{2,1,0:T(8,128)S(1)}, f32[2,64,128]{2,1,0:T(8,128)S(1)}, u32[]{:S(2)}, u32[]{:S(2)}) collective-permute-start(f32[2,64,128]{2,1,0:T(8,128)S(1)} %get-tuple-element.122), channel_id=1, source_target_pairs={{0,1},{1,0},{2,3},{3,2},{4,5},{5,4},{6,7},{7,6},{8,16},{9,17},{10,... | collective-permute-start | bytes 196616 | tf_op jit(solution)/shard_map/ppermute | solution.py:733
  46.0 1.1 %coarse_middle.1 = (bf16[136,64,256]{2,1,0:T(8,128)(2,1)S(1)}, f32[64,64,128]{2,1,0:T(8,128)S(1)}, bf16[136,64,256]{2,1,0:T(8,128)(2,1)S(1)}, f32[64,64,128]{2,1,0:T(8,128)S(1)}, f32[14,64,128]{2,1,0:T(8,128)S(1)}) custom-call(s32[8,64]{1,0:T(8,128)S(4)} %get-tuple-element.104.refs_0_, ...), custom_call_target="tpu_custom_call", output_to_operand_aliasing={{0}: (4, {}), {1}: (5, {})} | custom-call | flops 99999997952 | bytes 1 | tf_op jit(solution)/shard_map/coarse_middle/pallas_call | solution.py:534
  47.1 1.2 %collective-permute-start.22 = (f32[14,64,128]{2,1,0:T(8,128)S(1)}, f32[14,64,128]{2,1,0:T(8,128)S(1)}, u32[]{:S(2)}, u32[]{:S(2)}) collective-permute-start(f32[14,64,128]{2,1,0:T(8,128)S(1)} %get-tuple-element.145), channel_id=1, source_target_pairs={{0,2},{1,3},{2,0},{3,1},{4,6},{5,7},{6,4},{7,5},{8,16},{9,17},{10,... | collective-permute-start | bytes 1376264 | tf_op jit(solution)/shard_map/ppermute | solution.py:596
  48.4 0.1 coarse_halo.1.refs_3_.refs_5_
  48.5 2.1 %coarse_inner.1 = (f32[64,64,128]{2,1,0:T(8,128)S(1)}, bf16[136,64,256]{2,1,0:T(8,128)(2,1)S(1)}, f32[64,64,128]{2,1,0:T(8,128)S(1)}, f32[30,64,128]{2,1,0:T(8,128)S(1)}) custom-call(s32[8,64]{1,0:T(8,128)S(4)} %get-tuple-element.104.refs_0_, ...), custom_call_target="tpu_custom_call", output_to_operand_aliasing={{0}: (4, {}), {1}: (5, {}), {2}: (6, {})} | custom-call | flops 1 | bytes 1 | tf_op jit(solution)/shard_map/coarse_inner/pallas_call | solution.py:534
  50.6 0.1 collective-permute-start.17
  50.7 1.6 %coarse_ends.1 = (bf16[136,64,256]{2,1,0:T(8,128)(2,1)S(1)}, f32[64,64,128]{2,1,0:T(8,128)S(1)}, bf16[136,64,256]{2,1,0:T(8,128)(2,1)S(1)}, f32[64,64,128]{2,1,0...) custom-call(s32[8,64]{1,0:T(8,128)S(4)} %get-tuple-element.104.refs_, ...), custom_call_target="tpu_custom_call", output_to_operand_aliasing={{0}: (5, {}), {1}: (6, {}), {2}: (7, {}), {3}: (8, {})} | custom-call | flops 99999997952 | bytes 1 | tf_op jit(solution)/shard_map/coarse_ends/pallas_call | solution.py:534
  52.4 1.4 %collective-permute-start.19 = (f32[2,64,128]{2,1,0:T(8,128)S(1)}, f32[2,64,128]{2,1,0:T(8,128)S(1)}, u32[]{:S(2)}, u32[]{:S(2)}) collective-permute-start(f32[2,64,128]{2,1,0:T(8,128)S(1)} %get-tuple-element.141), channel_id=1, source_target_pairs={{0,1},{1,0},{2,3},{3,2},{4,5},{5,4},{6,7},{7,6},{8,9},{9,8},{10,11... | collective-permute-start | bytes 196616 | tf_op jit(solution)/shard_map/ppermute | solution.py:602
  53.7 0.2 collective-permute-start.20
  53.9 1.8 %collective-permute-start.18 = (f32[9,64,128]{2,1,0:T(8,128)S(1)}, f32[9,64,128]{2,1,0:T(8,128)S(1)}, u32[]{:S(2)}, u32[]{:S(2)}) collective-permute-start(f32[9,64,128]{2,1,0:T(8,128)S(1)} %get-tuple-element.140), channel_id=1, source_target_pairs={{0,1},{1,0},{2,3},{3,2},{4,5},{5,4},{6,7},{7,6},{8,16},{9,17},{10,... | collective-permute-start | bytes 884744 | tf_op jit(solution)/shard_map/ppermute | solution.py:770
  55.7 0.3 collective-permute-start.24
  55.9 2.9 %last_inner.1 = (bf16[136,64,256]{2,1,0:T(8,128)(2,1)S(1)}, f32[32,64,128]{2,1,0:T(8,128)S(1)}, f32[64,64,128]{2,1,0:T(8,128)}) custom-call(s32[8,64]{1,0:T(8,128)S(4)} %get-tuple-element.104.refs_0_, bf16[64,64,512]{2,1,0:T(8,128)(2,1)S(1)} %get-tuple-element.105.refs_7_.refs_1_, ...), custom_call_target="tpu_custom_call", output_to_operand_aliasing={{0}: (6, {})} | custom-call | flops 1 | bytes 1 | tf_op jit(solution)/shard_map/last_inner/pallas_call | solution.py:534
  58.9 0.1 pack_second.1
  59.0 1.8 %collective-permute-start.23 = (f32[2,64,128]{2,1,0:T(8,128)S(1)}, f32[2,64,128]{2,1,0:T(8,128)S(1)}, u32[]{:S(2)}, u32[]{:S(2)}) collective-permute-start(f32[2,64,128]{2,1,0:T(8,128)S(1)} %get-tuple-element.154), channel_id=1, source_target_pairs={{0,1},{1,0},{2,3},{3,2},{4,5},{5,4},{6,7},{7,6},{8,16},{9,17},{10,... | collective-permute-start | bytes 196616 | tf_op jit(solution)/shard_map/ppermute | solution.py:792
  60.8 0.8 %last_middle.1 = (bf16[136,64,256]{2,1,0:T(8,128)(2,1)S(1)}, f32[32,64,128]{2,1,0:T(8,128)S(1)}) custom-call(s32[8,64]{1,0:T(8,128)S(4)} %get-tuple-element.104.refs_0_, bf16[64,64,512]{2,1,0:T(8,128)(2,1)S(1)} %get-tuple-element.105.refs_7_.refs_1_, ...), custom_call_target="tpu_custom_call", output_to_operand_aliasing={{0}: (5, {}), {1}: (6, {})} | custom-call | flops 99999997952 | bytes 1 | tf_op jit(solution)/shard_map/last_middle/pallas_call | solution.py:534
  61.6 0.5 collective-permute-done.21.refs_4_
  62.1 0.4 last_sides.1
  62.5 0.6 last_low.1
  63.1 0.7 %collective-permute-done.24.refs_7_ = f32[9,64,128]{2,1,0:T(8,128)S(1)} collective-permute-done((f32[9,64,128]{2,1,0:T(8,128)S(1)}, f32[9,64,128]{2,1,0:T(8,128)S(1)}, u32[]{:S(2)}, u32[]{:S(2)}) %collective-permute-start.24) | collective-permute-done | bytes 294944 | tf_op jit(solution)/shard_map/ppermute | solution.py:770
  63.8 0.7 %collective-permute-done.23.refs_6_ = f32[2,64,128]{2,1,0:T(8,128)S(1)} collective-permute-done((f32[2,64,128]{2,1,0:T(8,128)S(1)}, f32[2,64,128]{2,1,0:T(8,128)S(1)}, u32[]{:S(2)}, u32[]{:S(2)}) %collective-permute-start.23) | collective-permute-done | bytes 65568 | tf_op jit(solution)/shard_map/ppermute | solution.py:792
  64.5 1.6 %last_high.1 = (bf16[136,64,256]{2,1,0:T(8,128)(2,1)S(1)}, f32[32,64,128]{2,1,0:T(8,128)}) custom-call(s32[8,64]{1,0:T(8,128)S(4)} %get-tuple-element.104.refs_0_, bf16[64,64,512]{2,1,0:T(8,128)(2,1)S(1)} %get-tuple-element.105.refs_7_.refs_1_, bf16[64,64,128]{2,1,0:T(8,128)(2,1)S(1)} %get-tuple-element.106.refs_2_, ...), custom_call_target="tpu_custom_call", output_to_operand_aliasing={{0}: (4, {})} | custom-call | flops 1 | bytes 1 | tf_op jit(solution)/shard_map/last_high/pallas_call | solution.py:534
  (27 shorter events, 0.1 us)
Async XLA Ops:
  3.2 13.2 %collective-permute-start.4 = (f32[16,64,128]{2,1,0:T(8,128)S(1)}, f32[16,64,128]{2,1,0:T(8,128)S(1)}, u32[]{:S(2)}, u32[]{:S(2)}) collective-permute-start(f32[16,64,128]{2,1,0:T(8,128)S(1)} %get-tuple-element.87), channel_id=1, source_target_pairs={{8,16},{9,17},{10,18},{11,19},{12,20},{13,21},{14,22},{15,23},{16,... | collective-permute-start | bytes 1572872 | tf_op jit(solution)/shard_map/ppermute | solution.py:629
  3.9 7.3 %copy-start = (bf16[128,64,4,64]{0,3,2,1:T(8,128)(2,1)S(1)}, bf16[128,64,4,64]{0,3,2,1:T(8,128)(2,1)}, u32[]{:S(2)}) copy-start(bf16[128,64,4,64]{0,3,2,1:T(8,128)(2,1)} %param.9) | copy-start | bytes 12582916
  3.9 7.2 %copy-start.1 = (bf16[128,64,64]{0,2,1:T(8,128)(2,1)S(1)}, bf16[128,64,64]{0,2,1:T(8,128)(2,1)}, u32[]{:S(2)}) copy-start(bf16[128,64,64]{0,2,1:T(8,128)(2,1)} %param.11) | copy-start | bytes 3145732
  3.9 7.2 %copy-start.2 = (bf16[128,64,64]{0,2,1:T(8,128)(2,1)S(1)}, bf16[128,64,64]{0,2,1:T(8,128)(2,1)}, u32[]{:S(2)}) copy-start(bf16[128,64,64]{0,2,1:T(8,128)(2,1)} %param.10) | copy-start | bytes 3145732
  5.3 11.1 %collective-permute-start.2 = (f32[4,64,128]{2,1,0:T(8,128)S(1)}, f32[4,64,128]{2,1,0:T(8,128)S(1)}, u32[]{:S(2)}, u32[]{:S(2)}) collective-permute-start(f32[4,64,128]{2,1,0:T(8,128)S(1)} %get-tuple-element.85), channel_id=1, source_target_pairs={{0,1},{1,0},{2,3},{3,2},{4,5},{5,4},{6,7},{7,6},{8,9},{9,8},{10,11... | collective-permute-start | bytes 393224 | tf_op jit(solution)/shard_map/ppermute | solution.py:602
  8.3 8.1 %collective-permute-start.3 = (f32[4,64,128]{2,1,0:T(8,128)S(1)}, f32[4,64,128]{2,1,0:T(8,128)S(1)}, u32[]{:S(2)}, u32[]{:S(2)}) collective-permute-start(f32[4,64,128]{2,1,0:T(8,128)S(1)} %get-tuple-element.86), channel_id=1, source_target_pairs={{0,8},{1,2},{2,1},{3,4},{4,3},{5,6},{6,5},{7,15},{8,0},{9,10},{10,... | collective-permute-start | bytes 393224 | tf_op jit(solution)/shard_map/ppermute | solution.py:605
  10.9 10.0 %collective-permute-start = (f32[16,64,128]{2,1,0:T(8,128)S(1)}, f32[16,64,128]{2,1,0:T(8,128)S(1)}, u32[]{:S(2)}, u32[]{:S(2)}) collective-permute-start(f32[16,64,128]{2,1,0:T(8,128)S(1)} %get-tuple-element.84), channel_id=1, source_target_pairs={{0,2},{1,3},{2,0},{3,1},{4,6},{5,7},{6,4},{7,5},{8,16},{9,17},{10,... | collective-permute-start | bytes 1572872 | tf_op jit(solution)/shard_map/ppermute | solution.py:596
  10.9 8.5 %collective-permute-start.1 = (f32[32,64,128]{2,1,0:T(8,128)S(1)}, f32[32,64,128]{2,1,0:T(8,128)S(1)}, u32[]{:S(2)}, u32[]{:S(2)}) collective-permute-start(f32[32,64,128]{2,1,0:T(8,128)S(1)} %get-tuple-element.83.refs_4_), channel_id=1, source_target_pairs={{0,8},{1,9},{2,10},{3,11},{4,12},{5,13},{6,14},{7,15},{8,0},{9,1},... | collective-permute-start | bytes 3145736 | tf_op jit(solution)/shard_map/ppermute | solution.py:599
  17.3 13.2 %collective-permute-start.9 = (f32[16,64,128]{2,1,0:T(8,128)S(1)}, f32[16,64,128]{2,1,0:T(8,128)S(1)}, u32[]{:S(2)}, u32[]{:S(2)}) collective-permute-start(f32[16,64,128]{2,1,0:T(8,128)S(1)} %get-tuple-element.111), channel_id=1, source_target_pairs={{0,2},{1,3},{2,0},{3,1},{4,6},{5,7},{6,4},{7,5},{8,16},{9,17},{10,... | collective-permute-start | bytes 1572872 | tf_op jit(solution)/shard_map/ppermute | solution.py:596
  20.8 6.4 %slice-start = ((s8[8388608]{0:T(1024)(128)(4,1)}), s8[4194304]{0:T(1024)(128)(4,1)S(1)}, s32[]{:S(2)}) async-start(s8[8388608]{0:T(1024)(128)(4,1)} %bitcast.6), calls=%async_computation | async-start | bytes 8388608
  20.9 5.5 %copy-start.3 = (bf16[64,64,64]{2,1,0:T(8,128)(2,1)S(1)}, bf16[64,64,64]{2,1,0:T(8,128)(2,1)}, u32[]{:S(2)}) copy-start(bf16[64,64,64]{2,1,0:T(8,128)(2,1)} %refs_0_.3) | copy-start | bytes 1572868
  20.9 5.5 %copy-start.4 = (bf16[64,64,64]{2,1,0:T(8,128)(2,1)S(1)}, bf16[64,64,64]{2,1,0:T(8,128)(2,1)}, u32[]{:S(2)}) copy-start(bf16[64,64,64]{2,1,0:T(8,128)(2,1)} %refs_1_.1) | copy-start | bytes 1572868
  20.9 5.5 %copy-start.5 = (s32[64,8]{0,1:T(8,128)S(1)}, s32[64,8]{0,1:T(8,128)}, u32[]{:S(2)}) copy-start(s32[64,8]{0,1:T(8,128)} %param.15) | copy-start | bytes 6148
  20.9 6.4 %slice-start.1 = ((s8[8388608]{0:T(1024)(128)(4,1)}), s8[4194304]{0:T(1024)(128)(4,1)S(1)}, s32[]{:S(2)}) async-start(s8[8388608]{0:T(1024)(128)(4,1)} %bitcast.6), calls=%async_computation.1 | async-start | bytes 8388608
  22.1 8.3 %collective-permute-start.7 = (f32[4,64,128]{2,1,0:T(8,128)S(1)}, f32[4,64,128]{2,1,0:T(8,128)S(1)}, u32[]{:S(2)}, u32[]{:S(2)}) collective-permute-start(f32[4,64,128]{2,1,0:T(8,128)S(1)} %get-tuple-element.109), channel_id=1, source_target_pairs={{0,1},{1,0},{2,3},{3,2},{4,5},{5,4},{6,7},{7,6},{8,9},{9,8},{10,11... | collective-permute-start | bytes 393224 | tf_op jit(solution)/shard_map/ppermute | solution.py:602
  24.8 5.7 %collective-permute-start.8 = (f32[4,64,128]{2,1,0:T(8,128)S(1)}, f32[4,64,128]{2,1,0:T(8,128)S(1)}, u32[]{:S(2)}, u32[]{:S(2)}) collective-permute-start(f32[4,64,128]{2,1,0:T(8,128)S(1)} %get-tuple-element.110), channel_id=1, source_target_pairs={{0,8},{1,2},{2,1},{3,4},{4,3},{5,6},{6,5},{7,15},{8,0},{9,10},{10,... | collective-permute-start | bytes 393224 | tf_op jit(solution)/shard_map/ppermute | solution.py:605
  24.8 12.4 %collective-permute-start.5 = (f32[16,64,128]{2,1,0:T(8,128)S(1)}, f32[16,64,128]{2,1,0:T(8,128)S(1)}, u32[]{:S(2)}, u32[]{:S(2)}) collective-permute-start(f32[16,64,128]{2,1,0:T(8,128)S(1)} %get-tuple-element.103.refs_3_), channel_id=1, source_target_pairs={{0,2},{1,3},{2,0},{3,1},{4,6},{5,7},{6,4},{7,5},{8,16},{9,17},{10,... | collective-permute-start | bytes 1572872 | tf_op jit(solution)/shard_map/ppermute | solution.py:596
  26.3 8.3 %collective-permute-start.6 = (f32[32,64,128]{2,1,0:T(8,128)S(1)}, f32[32,64,128]{2,1,0:T(8,128)S(1)}, u32[]{:S(2)}, u32[]{:S(2)}) collective-permute-start(f32[32,64,128]{2,1,0:T(8,128)S(1)} %get-tuple-element.108), channel_id=1, source_target_pairs={{0,8},{1,9},{2,10},{3,11},{4,12},{5,13},{6,14},{7,15},{8,0},{9,1},... | collective-permute-start | bytes 3145736 | tf_op jit(solution)/shard_map/ppermute | solution.py:599
  31.7 14.3 %collective-permute-start.16 = (f32[16,64,128]{2,1,0:T(8,128)S(1)}, f32[16,64,128]{2,1,0:T(8,128)S(1)}, u32[]{:S(2)}, u32[]{:S(2)}) collective-permute-start(f32[16,64,128]{2,1,0:T(8,128)S(1)} %get-tuple-element.125), channel_id=1, source_target_pairs={{0,2},{1,3},{2,0},{3,1},{4,6},{5,7},{6,4},{7,5},{8,16},{9,17},{10,... | collective-permute-start | bytes 1572872 | tf_op jit(solution)/shard_map/ppermute | solution.py:596
  38.6 4.3 %collective-permute-start.11 = (f32[2,64,128]{2,1,0:T(8,128)S(1)}, f32[2,64,128]{2,1,0:T(8,128)S(1)}, u32[]{:S(2)}, u32[]{:S(2)}) collective-permute-start(f32[2,64,128]{2,1,0:T(8,128)S(1)} %get-tuple-element.119), channel_id=1, source_target_pairs={{0,1},{1,0},{2,3},{3,2},{4,5},{5,4},{6,7},{7,6},{8,9},{9,8},{10,11... | collective-permute-start | bytes 196616 | tf_op jit(solution)/shard_map/ppermute | solution.py:602
  39.5 3.5 %collective-permute-start.12 = (f32[2,64,128]{2,1,0:T(8,128)S(1)}, f32[2,64,128]{2,1,0:T(8,128)S(1)}, u32[]{:S(2)}, u32[]{:S(2)}) collective-permute-start(f32[2,64,128]{2,1,0:T(8,128)S(1)} %get-tuple-element.120), channel_id=1, source_target_pairs={{0,8},{1,2},{2,1},{3,4},{4,3},{5,6},{6,5},{7,15},{8,0},{9,10},{10,... | collective-permute-start | bytes 196616 | tf_op jit(solution)/shard_map/ppermute | solution.py:605
  39.5 11.2 %collective-permute-start.10 = (f32[16,64,128]{2,1,0:T(8,128)S(1)}, f32[16,64,128]{2,1,0:T(8,128)S(1)}, u32[]{:S(2)}, u32[]{:S(2)}) collective-permute-start(f32[16,64,128]{2,1,0:T(8,128)S(1)} %get-tuple-element.118), channel_id=1, source_target_pairs={{0,2},{1,3},{2,0},{3,1},{4,6},{5,7},{6,4},{7,5},{8,16},{9,17},{10,... | collective-permute-start | bytes 1572872 | tf_op jit(solution)/shard_map/ppermute | solution.py:596
  42.2 6.2 %collective-permute-start.14 = (f32[30,64,128]{2,1,0:T(8,128)S(1)}, f32[30,64,128]{2,1,0:T(8,128)S(1)}, u32[]{:S(2)}, u32[]{:S(2)}) collective-permute-start(f32[30,64,128]{2,1,0:T(8,128)S(1)} %get-tuple-element.123), channel_id=1, source_target_pairs={{0,8},{1,9},{2,10},{3,11},{4,12},{5,13},{6,14},{7,15},{8,0},{9,1},... | collective-permute-start | bytes 2949128 | tf_op jit(solution)/shard_map/ppermute | solution.py:599
  43.0 7.6 %collective-permute-start.13 = (f32[2,64,128]{2,1,0:T(8,128)S(1)}, f32[2,64,128]{2,1,0:T(8,128)S(1)}, u32[]{:S(2)}, u32[]{:S(2)}) collective-permute-start(f32[2,64,128]{2,1,0:T(8,128)S(1)} %get-tuple-element.122), channel_id=1, source_target_pairs={{0,1},{1,0},{2,3},{3,2},{4,5},{5,4},{6,7},{7,6},{8,16},{9,17},{10,... | collective-permute-start | bytes 196616 | tf_op jit(solution)/shard_map/ppermute | solution.py:733
  46.0 2.3 %collective-permute-start.15 = (f32[4,64,128]{2,1,0:T(8,128)S(1)}, f32[4,64,128]{2,1,0:T(8,128)S(1)}, u32[]{:S(2)}, u32[]{:S(2)}) collective-permute-start(f32[4,64,128]{2,1,0:T(8,128)S(1)} %get-tuple-element.124), channel_id=1, source_target_pairs={{0,8},{1,9},{2,10},{3,11},{4,12},{5,13},{6,14},{7,15},{8,0},{9,1},... | collective-permute-start | bytes 393224 | tf_op jit(solution)/shard_map/ppermute | solution.py:599
  47.1 13.7 %collective-permute-start.22 = (f32[14,64,128]{2,1,0:T(8,128)S(1)}, f32[14,64,128]{2,1,0:T(8,128)S(1)}, u32[]{:S(2)}, u32[]{:S(2)}) collective-permute-start(f32[14,64,128]{2,1,0:T(8,128)S(1)} %get-tuple-element.145), channel_id=1, source_target_pairs={{0,2},{1,3},{2,0},{3,1},{4,6},{5,7},{6,4},{7,5},{8,16},{9,17},{10,... | collective-permute-start | bytes 1376264 | tf_op jit(solution)/shard_map/ppermute | solution.py:596
  50.6 5.1 %collective-permute-start.17 = (f32[30,64,128]{2,1,0:T(8,128)S(1)}, f32[30,64,128]{2,1,0:T(8,128)S(1)}, u32[]{:S(2)}, u32[]{:S(2)}) collective-permute-start(f32[30,64,128]{2,1,0:T(8,128)S(1)} %get-tuple-element.136), channel_id=1, source_target_pairs={{0,8},{1,9},{2,10},{3,11},{4,12},{5,13},{6,14},{7,15},{8,0},{9,1},... | collective-permute-start | bytes 2949128 | tf_op jit(solution)/shard_map/ppermute | solution.py:599
  52.4 6.5 %collective-permute-start.19 = (f32[2,64,128]{2,1,0:T(8,128)S(1)}, f32[2,64,128]{2,1,0:T(8,128)S(1)}, u32[]{:S(2)}, u32[]{:S(2)}) collective-permute-start(f32[2,64,128]{2,1,0:T(8,128)S(1)} %get-tuple-element.141), channel_id=1, source_target_pairs={{0,1},{1,0},{2,3},{3,2},{4,5},{5,4},{6,7},{7,6},{8,9},{9,8},{10,11... | collective-permute-start | bytes 196616 | tf_op jit(solution)/shard_map/ppermute | solution.py:602
  53.7 5.2 %collective-permute-start.20 = (f32[2,64,128]{2,1,0:T(8,128)S(1)}, f32[2,64,128]{2,1,0:T(8,128)S(1)}, u32[]{:S(2)}, u32[]{:S(2)}) collective-permute-start(f32[2,64,128]{2,1,0:T(8,128)S(1)} %get-tuple-element.142), channel_id=1, source_target_pairs={{0,8},{1,2},{2,1},{3,4},{4,3},{5,6},{6,5},{7,15},{8,0},{9,10},{10,... | collective-permute-start | bytes 196616 | tf_op jit(solution)/shard_map/ppermute | solution.py:605
  53.9 8.6 %collective-permute-start.18 = (f32[9,64,128]{2,1,0:T(8,128)S(1)}, f32[9,64,128]{2,1,0:T(8,128)S(1)}, u32[]{:S(2)}, u32[]{:S(2)}) collective-permute-start(f32[9,64,128]{2,1,0:T(8,128)S(1)} %get-tuple-element.140), channel_id=1, source_target_pairs={{0,1},{1,0},{2,3},{3,2},{4,5},{5,4},{6,7},{7,6},{8,16},{9,17},{10,... | collective-permute-start | bytes 884744 | tf_op jit(solution)/shard_map/ppermute | solution.py:770
  55.7 8.1 %collective-permute-start.24 = (f32[9,64,128]{2,1,0:T(8,128)S(1)}, f32[9,64,128]{2,1,0:T(8,128)S(1)}, u32[]{:S(2)}, u32[]{:S(2)}) collective-permute-start(f32[9,64,128]{2,1,0:T(8,128)S(1)} %get-tuple-element.155), channel_id=1, source_target_pairs={{0,1},{1,0},{2,3},{3,2},{4,5},{5,4},{6,7},{7,6},{8,16},{9,17},{10,... | collective-permute-start | bytes 884744 | tf_op jit(solution)/shard_map/ppermute | solution.py:770
  59.0 5.5 %collective-permute-start.23 = (f32[2,64,128]{2,1,0:T(8,128)S(1)}, f32[2,64,128]{2,1,0:T(8,128)S(1)}, u32[]{:S(2)}, u32[]{:S(2)}) collective-permute-start(f32[2,64,128]{2,1,0:T(8,128)S(1)} %get-tuple-element.154), channel_id=1, source_target_pairs={{0,1},{1,0},{2,3},{3,2},{4,5},{5,4},{6,7},{7,6},{8,16},{9,17},{10,... | collective-permute-start | bytes 196616 | tf_op jit(solution)/shard_map/ppermute | solution.py:792
  60.8 1.3 %collective-permute-start.21 = (f32[4,64,128]{2,1,0:T(8,128)S(1)}, f32[4,64,128]{2,1,0:T(8,128)S(1)}, u32[]{:S(2)}, u32[]{:S(2)}) collective-permute-start(f32[4,64,128]{2,1,0:T(8,128)S(1)} %get-tuple-element.144), channel_id=1, source_target_pairs={{0,8},{1,9},{2,10},{3,11},{4,12},{5,13},{6,14},{7,15},{8,0},{9,1},... | collective-permute-start | bytes 393224 | tf_op jit(solution)/shard_map/ppermute | solution.py:599
